TPU v7x, 256 devices: a whole 4x4x8 slice. The times are simulated.
256 devices in a mesh: dp: 4 (over y), mp: 64 (over x, z, core).
Axes of the slice: x: 4, y: 4, z: 8, core: 2. Of those that a mesh axis runs over, the one named last changes fastest.
Arguments:
- gate: bfloat16 [2048, 14336], P('dp', 'mp'), may hold values from -6 to 6
- upward: bfloat16 [2048, 14336], P('dp', 'mp'), may hold values from -6 to 6
- cotangent: bfloat16 [2048, 8192], P('dp', 'mp'), may hold values from -4 to 4
- down_weight: bfloat16 [14336, 8192], P('mp'), may hold values from -0.046875 to 0.046875
- error_buffer: bfloat16 [4, 14336, 8192], P('dp', 'mp'), may hold values from -24 to 24
- start_q: float32 [14336, 32], P('mp'), may hold values from -0.046875 to 0.046875
Outputs:
- d_gate: bfloat16 [2048, 14336], P('dp', 'mp')
- d_up: bfloat16 [2048, 14336], P('dp', 'mp')
- new_error: bfloat16 [4, 14336, 8192], P('dp', 'mp')
- next_q: float32 [14336, 32], P('mp')
All inputs are finite; a program needn't handle non-finite values.
Results may differ from a plain program's by a relative error of at most 0.0065.
Values may be sent and summed in bfloat16 or wider, within the bound.
No kernel may reach another device: no remote copies, remote signals or barrier semaphores. Data moves between devices by JAX's collectives and lax.ppermute only.
A program may use at most 128 MiB of HBM per device.

v0:
```python
import jax
import jax.numpy as jnp
from jax import lax
from jax.sharding import PartitionSpec as P


def orthonormal(basis):
    gram = jnp.dot(basis, basis.T, precision=lax.Precision.HIGHEST)
    lower = jnp.linalg.cholesky(gram)
    return lax.linalg.triangular_solve(lower, basis, left_side=True, lower=True)


def local(gate, upward, cotangent, down_weight, error_buffer, start_q):
    groups = lax.axis_size("dp")
    gate_f = gate.astype(jnp.float32)
    up_f = upward.astype(jnp.float32)
    sigma = jax.nn.sigmoid(gate_f)
    silu = gate_f * sigma
    hidden = (silu * up_f).astype(jnp.bfloat16)
    start_matrix = error_buffer[0].astype(jnp.float32)
    piece = lax.all_gather(cotangent, "mp", axis=1, tiled=True)
    matrix = start_matrix
    d_part = jnp.dot(piece, down_weight.T, preferred_element_type=jnp.float32)
    block = matrix
    block = block + jnp.dot(hidden.T, piece, preferred_element_type=jnp.float32)
    matrix = block
    d_hidden, matrix = (d_part, matrix)
    d_gate = (d_hidden * up_f * sigma * (1.0 + gate_f * (1.0 - sigma))).astype(jnp.bfloat16)
    d_up = (d_hidden * silu).astype(jnp.bfloat16)
    partial_basis = jnp.dot(start_q.T, matrix, precision=lax.Precision.HIGHEST)
    basis = lax.psum(partial_basis, ("dp", "mp")) / groups
    basis_hat = orthonormal(basis)
    local_q = jnp.dot(matrix, basis_hat.T, precision=lax.Precision.HIGHEST)
    next_q = lax.psum(local_q, "dp") / groups
    approx = jnp.dot(next_q, basis_hat, precision=lax.Precision.HIGHEST)
    new_error = (matrix - approx).astype(jnp.bfloat16)[None]
    return (d_gate, d_up, new_error, next_q)


def solution(mesh):
    in_specs = (
        P("dp", "mp"),
        P("dp", "mp"),
        P("dp", "mp"),
        P("mp", None),
        P("dp", "mp", None),
        P("mp", None),
    )
    out_specs = (P("dp", "mp"), P("dp", "mp"), P("dp", "mp", None), P("mp", None))
    return jax.shard_map(local, mesh=mesh, in_specs=in_specs, out_specs=out_specs, check_vma=False)
```

profile of v0, /device:TPU:1, one launch (start us, length us, event | category | flops | bytes accessed | tf_op | source)
XLA Modules:
  0.0 420.2 jit_solution(11203735086870340042)
XLA Ops:
  7.2 0.0 copy-start
  7.2 0.0 all-gather.2.cloned.1.call-start
  7.2 0.7 all-gather.2.cloned.1.call-update
  7.9 0.0 all-reduce.2.cloned.1.call-start
  8.0 92.3 %all-gather.2.cloned.1.call-done = bf16[512,8192]{1,0:T(8,128)(2,1)} async-done(((bf16[512,128]{1,0:T(8,128)(2,1)}), bf16[512,8192]{1,0:T(8,128)(2,1)}) %all-gather.2.cloned.1.call-update) | async-done | bytes 8388624 | tf_op jit(solution)/shard_map/all_gather | solution.py:21
  100.3 6.9 %convolution_add_fusion = f32[224,8192]{1,0:T(8,128)S(1)} fusion(bf16[512,8192]{1,0:T(8,128)(2,1)} %all-gather.2.cloned.1.call-done, bf16[1,224,8192]{2,1,0:T(8,128)(2,1)} %param.10, bf16[512,224]{0,1:T(8,128)(2,1)} %param.7, bf16[512,224]{0,1:T(8,128)(2,1)} %param.6), kind=kOutput, calls=%fused_computation.1 | convolution fusion | flops 1883635712 | bytes 19857408 | tf_op jit(solution)/shard_map/dot_general | solution.py:25
  107.1 0.0 copy-start.1
  107.1 3.0 copy-done.1
  110.1 0.0 copy-done
  110.1 0.0 copy-start.2
  110.1 0.0 copy-start.3
  110.1 5.6 %convolution_bitcast_fusion = f32[32,8192]{1,0:T(8,128)} fusion(f32[224,8192]{1,0:T(8,128)S(1)} %convolution_add_fusion, f32[224,32]{0,1:T(8,128)S(1)} %copy-done), kind=kOutput, calls=%fused_computation.4 | convolution fusion | flops 704643072 | bytes 8417280 | tf_op jit(solution)/shard_map/dot_general | solution.py:30
  115.7 0.0 all-reduce.2.cloned.1.call-update
  115.7 0.0 copy-done.2
  115.8 0.0 copy-done.3
  115.8 8.0 %multiply_convert_fusion = (bf16[512,224]{0,1:T(8,128)(2,1)}, bf16[512,224]{0,1:T(8,128)(2,1)}) fusion(bf16[512,224]{0,1:T(8,128)(2,1)S(1)} %copy-done.2, bf16[512,224]{0,1:T(8,128)(2,1)S(1)} %copy-done.3, bf16[512,8192]{1,0:T(8,128)(2,1)} %all-gather.2.cloned.1.call-done, bf16[224,8192]{1,0:T(8,128)(2,1)} %param.9), kind=kOutput, calls=%fused_computation.24 | convolution fusion | flops 1880768512 | bytes 12976128 | tf_op jit(solution)/shard_map/dot_general | solution.py:23
  123.8 246.3 %all-reduce.2.cloned.1.call-done = f32[32,8192]{1,0:T(8,128)} async-done(((f32[32,8192]{1,0:T(8,128)}), f32[32,8192]{1,0:T(8,128)}) %all-reduce.2.cloned.1.call-update) | async-done | bytes 1048592 | tf_op jit(solution)/shard_map/psum | solution.py:31
  370.1 2.6 fusion.4
  372.7 0.1 copy.10
  372.8 2.9 cholesky.16
  375.7 0.6 compare_reduce_fusion
  376.4 0.7 fusion.17
  377.0 2.4 custom-call.6
  379.5 2.3 fusion.2
  381.7 8.8 %fusion.23 = f32[224,32]{0,1:T(8,128)S(1)} fusion(f32[224,8192]{1,0:T(8,128)} %copy-done.1, f32[32,8192]{1,0:T(8,128)S(1)} %fusion.2), kind=kOutput, calls=%fused_computation.38 | convolution fusion | flops 704643072 | bytes 8417280 | tf_op jit(solution)/shard_map/dot_general | solution.py:33
  390.5 13.2 %psum.15 = f32[224,32]{0,1:T(8,128)S(1)} all-reduce(f32[224,32]{0,1:T(8,128)S(1)} %fusion.23), channel_id=1, replica_groups=mesh['dp'=4,'mp'=64] {'dp'}, use_global_device_ids=true, to_apply=%region_3.4 | all-reduce | flops 7168 | bytes 57344 | tf_op jit(solution)/shard_map/psum | solution.py:34
  403.8 0.0 copy-start.4
  403.8 9.6 %fusion.1 = bf16[1,224,8192]{2,1,0:T(8,128)(2,1)} fusion(f32[224,8192]{1,0:T(8,128)} %copy-done.1, f32[224,32]{0,1:T(8,128)S(1)} %broadcast_multiply_fusion, f32[32,8192]{1,0:T(8,128)S(1)} %fusion.2), kind=kOutput, calls=%fused_computation.3 | convolution fusion | flops 708313088 | bytes 12087296 | tf_op jit(solution)/shard_map/dot_general | solution.py:35
  413.4 0.0 copy-done.4
  (3 shorter events, 0.0 us)
Async XLA Ops:
  7.2 103.0 %copy-start = (f32[224,32]{0,1:T(8,128)S(1)}, f32[224,32]{0,1:T(8,128)}, u32[]{:S(2)}) copy-start(f32[224,32]{0,1:T(8,128)} %param.11) | copy-start | bytes 86020
  7.2 93.1 %all-gather.2.cloned.1.call-start = ((), (), s32[]{:S(2)}) async-start(), calls=%async_computation | async-start | bytes 8519680 | tf_op jit(solution)/shard_map/all_gather | solution.py:21
  7.9 362.2 %all-reduce.2.cloned.1.call-start = ((), (), s32[]{:S(2)}) async-start(), calls=%async_computation.1 | async-start | bytes 2097152 | tf_op jit(solution)/shard_map/psum | solution.py:31
  107.1 3.0 copy-start.1
  110.1 5.6 %copy-start.2 = (bf16[512,224]{0,1:T(8,128)(2,1)S(1)}, bf16[512,224]{0,1:T(8,128)(2,1)}, u32[]{:S(2)}) copy-start(bf16[512,224]{0,1:T(8,128)(2,1)} %param.6) | copy-start | bytes 688132
  110.1 5.6 %copy-start.3 = (bf16[512,224]{0,1:T(8,128)(2,1)S(1)}, bf16[512,224]{0,1:T(8,128)(2,1)}, u32[]{:S(2)}) copy-start(bf16[512,224]{0,1:T(8,128)(2,1)} %param.7) | copy-start | bytes 688132
  403.8 9.6 %copy-start.4 = (f32[224,32]{0,1:T(8,128)}, f32[224,32]{0,1:T(8,128)S(1)}, u32[]{:S(2)}) copy-start(f32[224,32]{0,1:T(8,128)S(1)} %broadcast_multiply_fusion) | copy-start | bytes 86020
Sparse Core Ops, SparseCore 0:
  10.6 89.6 all-gather.1
  115.9 254.1 all-reduce.1
where the time goes:
time: 424 us; the launch traced here: 420 us
  waiting for transfers between devices  339 us (80%)
  matrix products  43.7 us (10%)
  between operations  14.1 us (3%)
  blocking collectives  13.2 us (3%)
  other arithmetic  6.69 us (2%)
    psum x1, waiting for transfers between devices, local(): basis = lax.psum(partial_basis, ('dp', 'mp')) / groups  246 us
    all_gather x1, waiting for transfers between devices, local(): piece = lax.all_gather(cotangent, 'mp', axis=1, tiled=True)  92.3 us
    psum x1, blocking collectives, local(): next_q = lax.psum(local_q, 'dp') / groups  13.2 us
    dot_general x1, matrix products, local(): approx = jnp.dot(next_q, basis_hat, precision=lax.Precision.HIGHEST)  9.55 us
    dot_general x1, matrix products, local(): local_q = jnp.dot(matrix, basis_hat.T, precision=lax.Precision.HIGHEST)  8.79 us
  transfers between devices with their start and end apart: 2, of which 2 were waited for; matrix products, arithmetic and copies ran while one was open for 2% of the time, Pallas kernels for 0%

commit v1 on v0

v1 whole, which is shorter than its diff:
```python
import jax
import jax.numpy as jnp
from jax import lax
from jax.sharding import Mesh, PartitionSpec as P

BF = jnp.bfloat16
F32 = jnp.float32
X, Z, CORES = 4, 8, 2
PLANE = ("x", "z", "core")


def dot(a, b):
    return jnp.dot(a, b, preferred_element_type=F32)


def split(a):
    high = a.astype(BF)
    return high, (a - high.astype(F32)).astype(BF)


def spread(a, n):
    return jnp.broadcast_to(a[None], (n,) + a.shape)


def total(a, axis, n):
    return lax.all_to_all(spread(a, n), axis, 0, 0).astype(F32).sum(0)


def local(gate, upward, cotangent, down_weight, error_buffer, start_q):
    groups = lax.axis_size("dp")
    rank = start_q.shape[1]
    error = error_buffer[0]
    piece = lax.all_gather(cotangent, PLANE, axis=1, tiled=True)

    gate_f = gate.T.astype(F32)
    up_f = upward.T.astype(F32)
    sigma = jax.nn.sigmoid(gate_f)
    silu = gate_f * sigma
    hidden = (silu * up_f).astype(BF)

    q_parts = jnp.concatenate(split(start_q.T), axis=0)

    left = dot(q_parts, hidden)
    left = (left[:rank] + left[rank:]).astype(BF)
    swapped = lax.ppermute(left, "core", [(0, 1), (1, 0)])
    left = (left.astype(F32) + swapped.astype(F32)).astype(BF)
    left = total(left, "x", X).astype(BF)
    left = total(left, "z", Z).astype(BF)

    part = dot(q_parts, error)
    part = (part[:rank] + part[rank:]).astype(BF)
    part = part.reshape(rank, X * Z * CORES, -1).transpose(1, 0, 2)
    part = lax.all_to_all(part, PLANE, 0, 0).astype(F32).sum(0)

    mine = (part + dot(left, cotangent)) / groups
    mine = total(mine, "dp", groups).astype(BF)
    basis = lax.all_to_all(spread(mine, X * Z * CORES), PLANE, 0, 0)
    basis = basis.transpose(1, 0, 2).reshape(rank, -1)

    matrix = error.astype(F32) + dot(hidden, piece)
    gram = lax.dot_general(basis, basis, (((1,), (1,)), ((), ())), preferred_element_type=F32)
    lower = jnp.linalg.cholesky(gram)
    inverse = lax.linalg.triangular_solve(lower, jnp.eye(rank, dtype=F32), left_side=True, lower=True)

    turned = lax.dot_general(basis, matrix.astype(BF), (((1,), (1,)), ((), ())), preferred_element_type=F32)
    turned = total(turned, "dp", groups) / groups
    next_qt = jnp.dot(inverse, turned, precision=lax.Precision.HIGHEST)
    factor = jnp.dot(inverse.T, next_qt, precision=lax.Precision.HIGHEST)
    factor = jnp.concatenate(split(factor), axis=0)
    approx = lax.dot_general(factor, jnp.concatenate([basis, basis], axis=0), (((0,), (0,)), ((), ())), preferred_element_type=F32)
    new_error = (matrix - approx).astype(BF)[None]

    d_hidden = lax.dot_general(down_weight, piece, (((1,), (1,)), ((), ())), preferred_element_type=F32)
    d_gate = (d_hidden * up_f * sigma * (1.0 + gate_f * (1.0 - sigma))).astype(BF).T
    d_up = (d_hidden * silu).astype(BF).T
    return (d_gate, d_up, new_error, next_qt.T)


def solution(mesh):
    mesh = Mesh(mesh.devices.reshape(mesh.shape["dp"], X, Z, CORES), ("dp",) + PLANE)
    in_specs = (
        P("dp", PLANE),
        P("dp", PLANE),
        P("dp", PLANE),
        P(PLANE, None),
        P("dp", PLANE, None),
        P(PLANE, None),
    )
    out_specs = (P("dp", PLANE), P("dp", PLANE), P("dp", PLANE, None), P(PLANE, None))
    return jax.shard_map(local, mesh=mesh, in_specs=in_specs, out_specs=out_specs, check_vma=False)
```

time: 424 us -> 152 us (0.36)
  waiting for transfers between devices: 339 us -> 29.9 us
  blocking collectives: 13.2 us -> 44.9 us
  starting transfers between devices: 0.08 us -> 22.6 us
  matrix products: 43.7 us -> 25.7 us
    psum x1 -> x0, waiting for transfers between devices: 246 us -> none  [local(): basis = lax.psum(partial_basis, ('dp', 'mp')) / groups]
    all_gather x1, waiting for transfers between devices: 92.3 us -> 3.38 us  [local(): piece = lax.all_gather(cotangent, PLANE, axis=1, tiled=True)]
    all_to_all x0 -> x3, blocking collectives: none -> 44.9 us  [the longest x1 29 us: local(): basis = lax.all_to_all(spread(mine, X * Z * CORES), PLANE, 0, 0)]
    all_to_all x0 -> x3, waiting for transfers between devices: none -> 25 us  [the longest x1 17.6 us: local(): part = lax.all_to_all(part, PLANE, 0, 0).astype(F32).sum(0)]
    all_to_all x0 -> x3, starting transfers between devices: none -> 19.2 us  [the longest x2 12 us: total(): return lax.all_to_all(spread(a, n), axis, 0, 0).astype(F32).sum(0)]
    dot_general x6 -> x10, matrix products: 41.4 us -> 25.5 us  [the longest x4 9.63 us: dot(): return jnp.dot(a, b, preferred_element_type=F32)]
    psum x1 -> x0, blocking collectives: 13.2 us -> none  [local(): next_q = lax.psum(local_q, 'dp') / groups]
  transfers between devices with their start and end apart: 2 -> 5, of which waited for: 2 -> 4; matrix products, arithmetic and copies ran while one was open for 2% -> 15% of each run, Pallas kernels for 0% -> 0%
where the time goes in v1:
time: 152 us; the launch traced here: 151 us
  blocking collectives  44.9 us (30%)
  waiting for transfers between devices  29.9 us (20%)
  matrix products  25.7 us (17%)
  starting transfers between devices  22.6 us (15%)
  between operations  14.2 us (9%)
  other arithmetic  10.6 us (7%)
  local copies, waits for them, and re-layouts  3.39 us (2%)
    all_to_all x1, blocking collectives, local(): basis = lax.all_to_all(spread(mine, X * Z * CORES), PLANE, 0, 0)  29 us
    all_to_all x1, waiting for transfers between devices, local(): part = lax.all_to_all(part, PLANE, 0, 0).astype(F32).sum(0)  17.6 us
    all_to_all x2, blocking collectives, total(): return lax.all_to_all(spread(a, n), axis, 0, 0).astype(F32).sum(0)  15.9 us
    all_to_all x2, starting transfers between devices, total(): return lax.all_to_all(spread(a, n), axis, 0, 0).astype(F32).sum(0)  12 us
    dot_general x4, matrix products, dot(): return jnp.dot(a, b, preferred_element_type=F32)  9.63 us
    dot_general x1, matrix products, local(): lax.dot_general(down_weight, piece, (((1,), (1,)), ((), ())), preferred_e...  7.97 us
    all_to_all x2, waiting for transfers between devices, total(): return lax.all_to_all(spread(a, n), axis, 0, 0).astype(F32).sum(0)  7.35 us
    all_to_all x1, starting transfers between devices, local(): part = lax.all_to_all(part, PLANE, 0, 0).astype(F32).sum(0)  7.16 us
  transfers between devices with their start and end apart: 5, of which 4 were waited for; matrix products, arithmetic and copies ran while one was open for 15% of the time, Pallas kernels for 0%

profile of v1, /device:TPU:1, one launch (start us, length us, event | category | flops | bytes accessed | tf_op | source)
XLA Modules:
  0.0 151.3 jit_solution(14827394284469674011)
XLA Ops:
  7.2 0.0 all-gather.2.cloned.1.call-start
  7.2 0.7 all-gather.2.cloned.1.call-update
  7.9 0.8 fusion.33
  8.7 0.8 bitcast_convert_fusion
  9.4 1.2 fusion.19
  10.6 0.1 fusion.36
  10.8 3.3 %collective-permute-start = (bf16[32,512]{1,0:T(8,128)(2,1)S(1)}, bf16[32,512]{1,0:T(8,128)(2,1)S(1)}, u32[]{:S(2)}, u32[]{:S(2)}) collective-permute-start(bf16[32,512]{1,0:T(8,128)(2,1)S(1)} %fusion.29), channel_id=1, source_target_pairs={{0,1},{1,0},{2,3},{3,2},{4,5},{5,4},{6,7},{7,6},{8,9},{9,8},{10,11... | collective-permute-start | bytes 98312 | tf_op jit(solution)/shard_map/ppermute | solution.py:45
  14.1 0.9 collective-permute-done
  15.0 7.2 %all_to_all.30 = bf16[4,32,512]{2,1,0:T(8,128)(2,1)S(1)} all-to-all(bf16[4,32,512]{2,1,0:T(8,128)(2,1)S(1)} %broadcast_in_dim.13), channel_id=1, replica_groups=mesh['dp'=4,'x'=4,'z'=8,'core'=2] {'x'}, dimensions={0} | all-to-all | bytes 262144 | tf_op jit(solution)/shard_map/all_to_all | solution.py:26
  22.3 0.7 broadcast_in_dim.14
  23.0 7.9 %all-to-all-start.2 = ((bf16[8,32,512]{2,1,0:T(8,128)(2,1)}), bf16[8,32,512]{2,1,0:T(8,128)(2,1)S(1)}, u32[]{:S(2)}, u32[]{:S(2)}) async-start(bf16[8,32,512]{2,1,0:T(8,128)(2,1)} %broadcast_in_dim.14), calls=%async_computation.2 | async-start | bytes 524288 | tf_op jit(solution)/shard_map/all_to_all | solution.py:26
  30.9 2.8 %fusion.2 = f32[64,8192]{1,0:T(8,128)S(1)} fusion(bf16[1,224,8192]{2,1,0:T(8,128)(2,1)} %param.10, bf16[32,224]{1,0:T(8,128)(2,1)S(1)} %fusion.33, bf16[32,224]{1,0:T(8,128)(2,1)S(1)} %bitcast_convert_fusion), kind=kOutput, calls=%fused_computation.4 | convolution fusion | flops 234938368 | bytes 5795840 | tf_op jit(solution)/shard_map/dot_general | solution.py:13
  33.7 0.0 copy-start.1
  33.7 0.9 bitcast_bitcast_fusion
  34.6 7.3 %all-to-all-done.2 = bf16[8,32,512]{2,1,0:T(8,128)(2,1)S(1)} async-done(((bf16[8,32,512]{2,1,0:T(8,128)(2,1)}), bf16[8,32,512]{2,1,0:T(8,128)(2,1)S(1)}, u32[]{:S(2)}, u32[]{:S(2)}) %all-to-all-start.2) | async-done | bytes 262176 | tf_op jit(solution)/shard_map/all_to_all | solution.py:26
  42.0 7.2 %all-to-all-start = ((bf16[64,32,128]{2,1,0:T(8,128)(2,1)}), bf16[64,32,128]{2,1,0:T(8,128)(2,1)S(1)}, u32[]{:S(2)}, u32[]{:S(2)}) async-start(bf16[64,32,128]{2,1,0:T(8,128)(2,1)} %bitcast_bitcast_fusion), calls=%async_computation | async-start | bytes 1048576 | tf_op jit(solution)/shard_map/all_to_all | solution.py:53
  49.2 17.6 %all-to-all-done = bf16[64,32,128]{2,1,0:T(8,128)(2,1)S(1)} async-done(((bf16[64,32,128]{2,1,0:T(8,128)(2,1)}), bf16[64,32,128]{2,1,0:T(8,128)(2,1)S(1)}, u32[]{:S(2)}, u32[]{:S(2)}) %all-to-all-start) | async-done | bytes 524320 | tf_op jit(solution)/shard_map/all_to_all | solution.py:53
  66.8 0.1 convert_reduce_fusion
  66.9 0.0 copy-done.1
  66.9 0.1 fusion.6
  67.1 8.7 %all_to_all.31 = f32[4,32,128]{2,1,0:T(8,128)S(1)} all-to-all(f32[4,32,128]{2,1,0:T(8,128)S(1)} %broadcast_in_dim.15), channel_id=1, replica_groups=mesh['dp'=4,'x'=4,'z'=8,'core'=2] {'dp'}, dimensions={0} | all-to-all | bytes 131072 | tf_op jit(solution)/shard_map/all_to_all | solution.py:26
  75.8 0.1 broadcast_in_dim.16
  75.9 29.0 %all_to_all.32 = bf16[64,32,128]{2,1,0:T(8,128)(2,1)S(1)} all-to-all(bf16[64,32,128]{2,1,0:T(8,128)(2,1)S(1)} %broadcast_in_dim.16), channel_id=1, replica_groups=mesh['dp'=4,'x'=4,'z'=8,'core'=2] {'x','z','core'}, dimensions={0} | all-to-all | bytes 1048576 | tf_op jit(solution)/shard_map/all_to_all | solution.py:57
  104.9 0.3 convolution_bitcast_fusion
  105.1 0.1 copy.17
  105.2 2.9 %cholesky.17 = f32[32,32]{1,0:T(8,128)S(1)} custom-call(f32[32,32]{1,0:T(8,128)S(1)} %fusion.40), custom_call_target="Cholesky" | custom-call | tf_op jit(solution)/shard_map/jit(cholesky)/cholesky | solution.py:62
  108.2 0.6 compare_reduce_fusion
  108.8 0.7 fusion.37
  109.5 2.5 %custom-call.6 = f32[1,32,32]{1,2,0:T(8,128)S(1)} custom-call(f32[1,32,32]{2,1,0:T(8,128)S(1)} %fusion.37), custom_call_target="InvertDiagBlocksLowerTriangular" | custom-call | tf_op jit(solution)/shard_map/triangular_solve | solution.py:63
  111.9 0.2 fusion.38
  112.2 3.4 %all-gather.2.cloned.1.call-done = bf16[512,8192]{1,0:T(8,128)(2,1)} async-done(((bf16[512,128]{1,0:T(8,128)(2,1)}), bf16[512,8192]{1,0:T(8,128)(2,1)}) %all-gather.2.cloned.1.call-update) | async-done | bytes 8388624 | tf_op jit(solution)/shard_map/all_gather | solution.py:33
  115.6 6.5 %convolution_add_fusion = f32[224,8192]{1,0:T(8,128)S(1)} fusion(bf16[224,512]{1,0:T(8,128)(2,1)S(1)} %fusion.19, bf16[512,8192]{1,0:T(8,128)(2,1)} %all-gather.2.cloned.1.call-done, bf16[1,224,8192]{2,1,0:T(8,128)(2,1)} %param.10), kind=kOutput, calls=%fused_computation.1 | convolution fusion | flops 1882718208 | bytes 19628032 | tf_op jit(solution)/shard_map/dot_general | solution.py:13
  122.1 0.0 copy-start
  122.1 0.0 copy-start.2
  122.1 0.0 copy-start.3
  122.1 1.2 fusion.4
  123.3 1.8 %copy-done = f32[224,8192]{1,0:T(8,128)} copy-done((f32[224,8192]{1,0:T(8,128)}, f32[224,8192]{1,0:T(8,128)S(1)}, u32[]{:S(2)}) %copy-start) | copy-done | bytes 7340056
  125.1 0.7 broadcast_in_dim.18
  125.8 4.2 %all-to-all-start.5 = ((f32[4,32,224]{2,1,0:T(8,128)}), f32[4,32,224]{2,1,0:T(8,128)S(1)}, u32[]{:S(2)}, u32[]{:S(2)}) async-start(f32[4,32,224]{2,1,0:T(8,128)} %broadcast_in_dim.18), calls=%async_computation.5 | async-start | bytes 262144 | tf_op jit(solution)/shard_map/all_to_all | solution.py:26
  129.9 0.0 copy-done.2
  130.0 0.0 copy-done.3
  130.0 8.0 %fusion.28 = (bf16[512,224]{0,1:T(8,128)(2,1)}, bf16[512,224]{0,1:T(8,128)(2,1)}) fusion(bf16[512,224]{0,1:T(8,128)(2,1)S(1)} %copy-done.2, bf16[512,224]{0,1:T(8,128)(2,1)S(1)} %copy-done.3, bf16[512,8192]{1,0:T(8,128)(2,1)} %all-gather.2.cloned.1.call-done, bf16[224,8192]{1,0:T(8,128)(2,1)} %param.9), kind=kOutput, calls=%fused_computation.42 | convolution fusion | flops 1880768512 | bytes 12976128 | tf_op jit(solution)/shard_map/dot_general | solution.py:73
  137.9 0.0 all-to-all-done.5
  137.9 0.2 fusion.34
  138.1 0.0 copy-start.4
  138.1 0.2 subtract_convert_fusion
  138.4 6.1 %fusion.1 = bf16[1,224,8192]{2,1,0:T(8,128)(2,1)} fusion(f32[224,8192]{1,0:T(8,128)} %copy-done, bf16[32,8192]{1,0:T(8,128)(2,1)S(1)} %copy_bitcast_fusion, bf16[32,224]{1,0:T(8,128)(2,1)S(1)} %get-tuple-element.4, bf16[32,224]{1,0:T(8,128)(2,1)S(1)} %get-tuple-element.5), kind=kOutput, calls=%fused_computation.3 | convolution fusion | flops 240705536 | bytes 11563008 | tf_op jit(solution)/shard_map/dot_general | solution.py:70
  144.4 0.0 copy-done.4
  (11 shorter events, 0.2 us)
Async XLA Ops:
  7.2 108.4 %all-gather.2.cloned.1.call-start = ((), (), s32[]{:S(2)}) async-start(), calls=%async_computation.6 | async-start | bytes 8519680 | tf_op jit(solution)/shard_map/all_gather | solution.py:33
  10.8 4.2 %collective-permute-start = (bf16[32,512]{1,0:T(8,128)(2,1)S(1)}, bf16[32,512]{1,0:T(8,128)(2,1)S(1)}, u32[]{:S(2)}, u32[]{:S(2)}) collective-permute-start(bf16[32,512]{1,0:T(8,128)(2,1)S(1)} %fusion.29), channel_id=1, source_target_pairs={{0,1},{1,0},{2,3},{3,2},{4,5},{5,4},{6,7},{7,6},{8,9},{9,8},{10,11... | collective-permute-start | bytes 98312 | tf_op jit(solution)/shard_map/ppermute | solution.py:45
  23.0 19.0 %all-to-all-start.2 = ((bf16[8,32,512]{2,1,0:T(8,128)(2,1)}), bf16[8,32,512]{2,1,0:T(8,128)(2,1)S(1)}, u32[]{:S(2)}, u32[]{:S(2)}) async-start(bf16[8,32,512]{2,1,0:T(8,128)(2,1)} %broadcast_in_dim.14), calls=%async_computation.2 | async-start | bytes 524288 | tf_op jit(solution)/shard_map/all_to_all | solution.py:26
  33.7 33.2 %copy-start.1 = (bf16[512,128]{1,0:T(8,128)(2,1)S(1)}, bf16[512,128]{1,0:T(8,128)(2,1)}, u32[]{:S(2)}) copy-start(bf16[512,128]{1,0:T(8,128)(2,1)} %param.8) | copy-start | bytes 393220
  42.0 24.9 %all-to-all-start = ((bf16[64,32,128]{2,1,0:T(8,128)(2,1)}), bf16[64,32,128]{2,1,0:T(8,128)(2,1)S(1)}, u32[]{:S(2)}, u32[]{:S(2)}) async-start(bf16[64,32,128]{2,1,0:T(8,128)(2,1)} %bitcast_bitcast_fusion), calls=%async_computation | async-start | bytes 1048576 | tf_op jit(solution)/shard_map/all_to_all | solution.py:53
  122.1 3.0 %copy-start = (f32[224,8192]{1,0:T(8,128)}, f32[224,8192]{1,0:T(8,128)S(1)}, u32[]{:S(2)}) copy-start(f32[224,8192]{1,0:T(8,128)S(1)} %convolution_add_fusion) | copy-start | bytes 22020100
  122.1 7.8 %copy-start.2 = (bf16[512,224]{0,1:T(8,128)(2,1)S(1)}, bf16[512,224]{0,1:T(8,128)(2,1)}, u32[]{:S(2)}) copy-start(bf16[512,224]{0,1:T(8,128)(2,1)} %param.6) | copy-start | bytes 688132
  122.1 7.8 %copy-start.3 = (bf16[512,224]{0,1:T(8,128)(2,1)S(1)}, bf16[512,224]{0,1:T(8,128)(2,1)}, u32[]{:S(2)}) copy-start(bf16[512,224]{0,1:T(8,128)(2,1)} %param.7) | copy-start | bytes 688132
  125.8 12.2 %all-to-all-start.5 = ((f32[4,32,224]{2,1,0:T(8,128)}), f32[4,32,224]{2,1,0:T(8,128)S(1)}, u32[]{:S(2)}, u32[]{:S(2)}) async-start(f32[4,32,224]{2,1,0:T(8,128)} %broadcast_in_dim.18), calls=%async_computation.5 | async-start | bytes 262144 | tf_op jit(solution)/shard_map/all_to_all | solution.py:26
  138.1 6.3 %copy-start.4 = (f32[32,224]{1,0:T(8,128)}, f32[32,224]{1,0:T(8,128)S(1)}, u32[]{:S(2)}) copy-start(f32[32,224]{1,0:T(8,128)S(1)} %fusion.34) | copy-start | bytes 86020
Sparse Core Ops, SparseCore 0:
  10.6 104.9 all-gather.1

commit v2 on v1

v2 whole, which is shorter than its diff:
```python
import jax
import jax.numpy as jnp
from jax import lax
from jax.experimental import pallas as pl
from jax.experimental.pallas import tpu as pltpu
from jax.sharding import Mesh, PartitionSpec as P

BF = jnp.bfloat16
F32 = jnp.float32
X, Z, CORES = 4, 8, 2
PLANE = ("x", "z", "core")
NT = (((1,), (1,)), ((), ()))
TN = (((0,), (0,)), ((), ()))


def dot(a, b):
    return jnp.dot(a, b, preferred_element_type=F32)


def split(a):
    high = a.astype(BF)
    return high, (a - high.astype(F32)).astype(BF)


def spread(a, n):
    return jnp.broadcast_to(a[None], (n,) + a.shape)


def total(a, axis, n):
    return lax.all_to_all(spread(a, n), axis, 0, 0).astype(F32).sum(0)


def shift(a, axis, step, n):
    return lax.ppermute(a, axis, [(i, (i + step) % n) for i in range(n)])


def piece_kernel(at_ref, own_ref, other_ref, hidden_ref, error_ref, weight_ref, matrix_in, d_in, matrix_ref, d_ref):
    del matrix_in
    first = at_ref[1] == 0
    own, other = own_ref[0], other_ref[0]
    block = jnp.concatenate([jnp.where(first, own, other), jnp.where(first, other, own)], axis=1)
    matrix_ref[...] = error_ref[...].astype(F32) + dot(hidden_ref[...], block)
    term = lax.dot_general(weight_ref[...], block, NT, preferred_element_type=F32)

    @pl.when(pl.program_id(0) == 0)
    def _():
        d_ref[...] = d_in[...] + term

    @pl.when(pl.program_id(0) > 0)
    def _():
        d_ref[...] += term


def add_piece(z, core, own, other, hidden, error, weight, matrix, d_hidden):
    tokens, wide = own.shape[1], own.shape[2]
    rows = hidden.shape[0]
    column = lambda i, at: (0, i * Z + at[0])
    whole = lambda i, at: (0, 0)
    slab = pl.BlockSpec((rows, CORES * wide), column)
    return pl.pallas_call(
        piece_kernel,
        grid_spec=pltpu.PrefetchScalarGridSpec(
            num_scalar_prefetch=1,
            grid=(X,),
            in_specs=[
                pl.BlockSpec((1, tokens, wide), lambda i, at: (i, 0, 0)),
                pl.BlockSpec((1, tokens, wide), lambda i, at: (i, 0, 0)),
                pl.BlockSpec((rows, tokens), whole),
                slab,
                slab,
                pl.BlockSpec(memory_space=pl.ANY),
                pl.BlockSpec((rows, tokens), whole),
            ],
            out_specs=[slab, pl.BlockSpec((rows, tokens), whole)],
        ),
        out_shape=[
            jax.ShapeDtypeStruct(matrix.shape, F32),
            jax.ShapeDtypeStruct(d_hidden.shape, F32),
        ],
        input_output_aliases={6: 0, 7: 1},
        cost_estimate=pl.CostEstimate(flops=4 * rows * tokens * X * CORES * wide, bytes_accessed=6 << 20, transcendentals=0),
        compiler_params=pltpu.CompilerParams(vmem_limit_bytes=24 << 20),
    )(jnp.stack([z, core]), own, other, hidden, error, weight, matrix, d_hidden)


def final_kernel(matrix_ref, factor_ref, basis_ref, out_ref):
    basis = basis_ref[...]
    approx = lax.dot_general(factor_ref[...], jnp.concatenate([basis, basis], axis=0), TN, preferred_element_type=F32)
    out_ref[...] = (matrix_ref[...] - approx).astype(BF)


def finish(matrix, factor, basis):
    rows, columns = matrix.shape
    step = 1024
    block = pl.BlockSpec((rows, step), lambda i: (0, i))
    return pl.pallas_call(
        final_kernel,
        grid=(columns // step,),
        in_specs=[block, pl.BlockSpec(factor.shape, lambda i: (0, 0)), pl.BlockSpec((basis.shape[0], step), lambda i: (0, i))],
        out_specs=block,
        out_shape=jax.ShapeDtypeStruct(matrix.shape, BF),
        cost_estimate=pl.CostEstimate(flops=2 * rows * columns * 64, bytes_accessed=12 << 20, transcendentals=0),
        compiler_params=pltpu.CompilerParams(vmem_limit_bytes=16 << 20),
    )(matrix, factor, basis)


def local(gate, upward, cotangent, down_weight, error_buffer, start_q):
    groups = lax.axis_size("dp")
    z, core = lax.axis_index("z"), lax.axis_index("core")
    rank = start_q.shape[1]
    tokens, wide = cotangent.shape
    error = error_buffer[0]
    rows, columns = error.shape

    pieces = {0: lax.all_to_all(spread(cotangent, X), "x", 0, 0)}

    gate_f = gate.T.astype(F32)
    up_f = upward.T.astype(F32)
    sigma = jax.nn.sigmoid(gate_f)
    silu = gate_f * sigma
    hidden = (silu * up_f).astype(BF)

    q_parts = jnp.concatenate(split(start_q.T), axis=0)

    left = dot(q_parts, hidden)
    left = (left[:rank] + left[rank:]).astype(BF)
    part = dot(q_parts, error)
    part = (part[:rank] + part[rank:]).astype(BF).reshape(rank, X, Z, CORES, wide)
    mine = lax.dynamic_index_in_dim(part, core, 3, False).reshape(rank, -1)
    theirs = lax.dynamic_index_in_dim(part, 1 - core, 3, False).reshape(rank, -1)
    theirs = shift(jnp.concatenate([left, theirs], axis=1), "core", 1, CORES)
    both = jnp.concatenate([left, mine], axis=1).astype(F32) + theirs.astype(F32)
    both = both.astype(BF)

    left, part = both[:, :tokens], both[:, tokens:].reshape(rank, X, Z * wide).transpose(1, 0, 2)
    both = jnp.concatenate([spread(left, X), part], axis=2)
    both = lax.all_to_all(both, "x", 0, 0).astype(F32).sum(0).astype(BF)
    left, part = both[:, :tokens], both[:, tokens:].reshape(rank, Z, wide).transpose(1, 0, 2)
    both = jnp.concatenate([spread(left, Z), part], axis=2)
    both = lax.all_to_all(both, "z", 0, 0).astype(F32).sum(0)
    left, part = both[:, :tokens].astype(BF), both[:, tokens:]

    mine = (part + dot(left, cotangent)) / groups
    mine = total(mine, "dp", groups).astype(BF)
    mine = lax.all_to_all(spread(mine, X * Z), ("x", "z"), 0, 0)
    theirs = shift(mine, "core", 1, CORES)
    first = core == 0
    basis = jnp.stack([jnp.where(first, mine, theirs), jnp.where(first, theirs, mine)], axis=1)
    basis = basis.transpose(2, 0, 1, 3).reshape(rank, columns)

    up, down = pieces[0], pieces[0]
    half = tokens // 2
    for step in range(1, Z // 2):
        up, down = shift(up, "z", 1, Z), shift(down, "z", Z - 1, Z)
        pieces[step], pieces[Z - step] = up, down
    up, down = shift(up[:, :half], "z", 1, Z), shift(down[:, half:], "z", Z - 1, Z)
    pieces[Z // 2] = jnp.concatenate([up, down], axis=1)

    matrix = jnp.zeros((rows, columns), F32)
    d_hidden = jnp.zeros((rows, tokens), F32)
    for step in (0, 1, 7, 2, 6, 3, 5, 4):
        own = pieces[step]
        other = shift(own, "core", 1, CORES)
        matrix, d_hidden = add_piece((z - step) % Z, core, own, other, hidden, error, down_weight, matrix, d_hidden)

    d_gate = (d_hidden * up_f * sigma * (1.0 + gate_f * (1.0 - sigma))).astype(BF).T
    d_up = (d_hidden * silu).astype(BF).T

    turned = lax.dot_general(basis, matrix.astype(BF), NT, preferred_element_type=F32)
    basis, turned = lax.optimization_barrier((basis, turned))
    turned = total(turned, "dp", groups) / groups
    gram = lax.dot_general(basis, basis, NT, preferred_element_type=F32)
    lower = jnp.linalg.cholesky(gram)
    inverse = lax.linalg.triangular_solve(lower, jnp.eye(rank, dtype=F32), left_side=True, lower=True)
    next_qt = jnp.dot(inverse, turned, precision=lax.Precision.HIGHEST)
    factor = jnp.dot(inverse.T, next_qt, precision=lax.Precision.HIGHEST)
    factor = jnp.concatenate(split(factor), axis=0)
    new_error = finish(matrix, factor, basis)[None]
    return (d_gate, d_up, new_error, next_qt.T)


def solution(mesh):
    mesh = Mesh(mesh.devices.reshape(mesh.shape["dp"], X, Z, CORES), ("dp",) + PLANE)
    in_specs = (
        P("dp", PLANE),
        P("dp", PLANE),
        P("dp", PLANE),
        P(PLANE, None),
        P("dp", PLANE, None),
        P(PLANE, None),
    )
    out_specs = (P("dp", PLANE), P("dp", PLANE), P("dp", PLANE, None), P(PLANE, None))
    return jax.shard_map(local, mesh=mesh, in_specs=in_specs, out_specs=out_specs, check_vma=False)
```

time: 152 us -> 178 us (1.17)
  blocking collectives: 44.9 us -> 0 us
  local copies, waits for them, and re-layouts: 3.39 us -> 40.4 us
  Pallas kernels: 0 us -> 34.2 us
  starting transfers between devices: 22.6 us -> 56.5 us
  matrix products: 25.7 us -> 5.14 us
  between operations: 14.2 us -> 1.21 us
  waiting for transfers between devices: 29.9 us -> 26.3 us
  other arithmetic: 10.6 us -> 13 us
    all_to_all x3 -> x0, blocking collectives: 44.9 us -> none  [the longest x1 29 us: local(): basis = lax.all_to_all(spread(mine, X * Z * CORES), PLANE, 0, 0)]
    pallas_call x0 -> x9, Pallas kernels: none -> 34.2 us  [the longest x8 29.3 us: add_piece(): pl.pallas_call(piece_kernel, grid_spec=pltpu.PrefetchScalarGridSpec(num_s...]
    unnamed x10 -> x41, local copies, waits for them, and re-layouts: 1.78 us -> 29.6 us
    ppermute x1 -> x18, starting transfers between devices: 3.33 us -> 29.6 us  [shift(): return lax.ppermute(a, axis, [(i, (i + step) % n) for i in range(n)])]
    dot_general x4 -> x2, matrix products: 15.5 us -> 1.48 us  [the longest x1 1.22 us: local(): lax.dot_general(basis, matrix.astype(BF), NT, preferred_element_type=F32)]
    all_to_all x1 -> x4, starting transfers between devices: 7.16 us -> 19.4 us  [the longest x1 6.35 us: local(): both = lax.all_to_all(both, 'z', 0, 0).astype(F32).sum(0)]
    ppermute x1 -> x18, waiting for transfers between devices: 0.86 us -> 11.3 us  [shift(): return lax.ppermute(a, axis, [(i, (i + step) % n) for i in range(n)])]
    dot_general x4 -> x3, matrix products: 9.63 us -> 3.09 us  [dot(): return jnp.dot(a, b, preferred_element_type=F32)]
  transfers between devices with their start and end apart: 5 -> 24, of which waited for: 4 -> 6; matrix products, arithmetic and copies ran while one was open for 15% -> 11% of each run, Pallas kernels for 0% -> 15%
where the time goes in v2:
time: 178 us; the launch traced here: 177 us
  starting transfers between devices  56.5 us (32%)
  local copies, waits for them, and re-layouts  40.4 us (23%)
  Pallas kernels  34.2 us (19%)
  waiting for transfers between devices  26.3 us (15%)
  other arithmetic  13 us (7%)
  matrix products  5.14 us (3%)
    unnamed x41, local copies, waits for them, and re-layouts  29.6 us
    ppermute x18, starting transfers between devices, shift(): return lax.ppermute(a, axis, [(i, (i + step) % n) for i in range(n)])  29.6 us
    pallas_call x8, Pallas kernels, add_piece(): pl.pallas_call(piece_kernel, grid_spec=pltpu.PrefetchScalarGridSpec(num_s...  29.3 us
    ppermute x18, waiting for transfers between devices, shift(): return lax.ppermute(a, axis, [(i, (i + step) % n) for i in range(n)])  11.3 us
    all_to_all x1, waiting for transfers between devices, local(): pieces = {0: lax.all_to_all(spread(cotangent, X), 'x', 0, 0)}  8.51 us
    all_to_all x2, starting transfers between devices, total(): return lax.all_to_all(spread(a, n), axis, 0, 0).astype(F32).sum(0)  7.51 us
    all_to_all x1, starting transfers between devices, local(): both = lax.all_to_all(both, 'z', 0, 0).astype(F32).sum(0)  6.35 us
    all_to_all x1, starting transfers between devices, local(): mine = lax.all_to_all(spread(mine, X * Z), ('x', 'z'), 0, 0)  6.1 us
  transfers between devices with their start and end apart: 24, of which 6 were waited for; matrix products, arithmetic and copies ran while one was open for 11% of the time, Pallas kernels for 15%

profile of v2, /device:TPU:1, one launch (start us, length us, event | category | flops | bytes accessed | tf_op | source)
XLA Modules:
  0.0 176.7 jit_solution(7313867215980822010)
XLA Ops:
  2.3 2.8 %fusion.18 = f32[64,8192]{1,0:T(8,128)S(1)} fusion(bf16[32,224]{1,0:T(8,128)(2,1)S(1)} %fusion.15, bf16[32,224]{1,0:T(8,128)(2,1)S(1)} %bitcast_convert_fusion, bf16[1,224,8192]{2,1,0:T(8,128)(2,1)} %param.10), kind=kOutput, calls=%fused_computation.48 | convolution fusion | flops 234938368 | bytes 5795840 | tf_op jit(solution)/shard_map/dot_general | solution.py:17
  5.5 3.1 %dynamic-slice_reduce_fusion.1 = (bf16[32,4,8,128]{3,2,1,0:T(8,128)(2,1)S(1)}, bf16[32,4,8,128]{3,2,1,0:T(8,128)(2,1)S(1)}) fusion(bf16[32,4,8,2,128]{4,3,2,1,0:T(2,128)(2,1)S(1)} %reshape.45, s32[]{:T(128)S(6)} %select_n.67, s32[]{:T(128)S(6)} %select_n.68), kind=kLoop, calls=%fused_computation.10 | loop fusion | bytes 1048584 | tf_op jit(solution)/shard_map/jit(dynamic_index_in_dim)/dynamic_slice | solution.py:129
  9.2 3.3 %collective-permute-start.16 = (bf16[32,4608]{1,0:T(8,128)(2,1)S(1)}, bf16[32,4608]{1,0:T(8,128)(2,1)S(1)}, u32[]{:S(2)}, u32[]{:S(2)}) collective-permute-start(bf16[32,4608]{1,0:T(8,128)(2,1)S(1)} %pad_maximum_fusion.1), channel_id=1, source_target_pairs={{0,1},{1,0},{2,3},{3,2},{4,5},{5,4},{6,7},{7,6},{8,9},{9,8},{10,11... | collective-permute-start | bytes 884744 | tf_op jit(solution)/shard_map/ppermute | solution.py:34
  13.3 3.5 %all-to-all-start = ((bf16[4,512,128]{2,1,0:T(8,128)(2,1)}), bf16[4,512,128]{2,1,0:T(8,128)(2,1)S(1)}, u32[]{:S(2)}, u32[]{:S(2)}) async-start(bf16[4,512,128]{2,1,0:T(8,128)(2,1)} %broadcast_in_dim.19), calls=%async_computation | async-start | bytes 1048576 | tf_op jit(solution)/shard_map/all_to_all | solution.py:115
  17.9 8.5 %all-to-all-done.own_ref = bf16[4,512,128]{2,1,0:T(8,128)(2,1)S(1)} async-done(((bf16[4,512,128]{2,1,0:T(8,128)(2,1)}), bf16[4,512,128]{2,1,0:T(8,128)(2,1)S(1)}, u32[]{:S(2)}, u32[]{:S(2)}) %all-to-all-start) | async-done | bytes 524320 | tf_op jit(solution)/shard_map/all_to_all | solution.py:115
  26.4 3.5 %all-to-all-start.1 = ((bf16[4,32,1536]{2,1,0:T(8,128)(2,1)}), bf16[4,32,1536]{2,1,0:T(8,128)(2,1)S(1)}, u32[]{:S(2)}, u32[]{:S(2)}) async-start(bf16[4,32,1536]{2,1,0:T(8,128)(2,1)} %pad_maximum_fusion), calls=%async_computation.1 | async-start | bytes 786432 | tf_op jit(solution)/shard_map/all_to_all | solution.py:137
  30.1 4.0 %collective-permute-start.4 = (bf16[4,512,128]{2,1,0:T(8,128)(2,1)S(1)}, bf16[4,512,128]{2,1,0:T(8,128)(2,1)S(1)}, u32[]{:S(2)}, u32[]{:S(2)}) collective-permute-start(bf16[4,512,128]{2,1,0:T(8,128)(2,1)S(1)} %all-to-all-done.own_ref), channel_id=1, source_target_pairs={{0,14},{2,0},{4,2},{6,4},{8,6},{10,8},{12,10},{14,12},{1,15},{3,1}... | collective-permute-start | bytes 1572872 | tf_op jit(solution)/shard_map/ppermute | solution.py:34
  34.1 2.7 %all-to-all-done.1 = bf16[4,32,1536]{2,1,0:T(8,128)(2,1)S(1)} async-done(((bf16[4,32,1536]{2,1,0:T(8,128)(2,1)}), bf16[4,32,1536]{2,1,0:T(8,128)(2,1)S(1)}, u32[]{:S(2)}, u32[]{:S(2)}) %all-to-all-start.1) | async-done | bytes 393248 | tf_op jit(solution)/shard_map/all_to_all | solution.py:137
  37.8 6.4 %all-to-all-start.2 = ((bf16[8,32,640]{2,1,0:T(8,128)(2,1)}), bf16[8,32,640]{2,1,0:T(8,128)(2,1)S(1)}, u32[]{:S(2)}, u32[]{:S(2)}) async-start(bf16[8,32,640]{2,1,0:T(8,128)(2,1)} %pad_maximum_fusion.3), calls=%async_computation.2 | async-start | bytes 655360 | tf_op jit(solution)/shard_map/all_to_all | solution.py:140
  44.2 1.1 collective-permute-done.own_ref
  45.6 2.4 %collective-permute-start.5 = (bf16[4,512,128]{2,1,0:T(8,128)(2,1)S(1)}, bf16[4,512,128]{2,1,0:T(8,128)(2,1)S(1)}, u32[]{:S(2)}, u32[]{:S(2)}) collective-permute-start(bf16[4,512,128]{2,1,0:T(8,128)(2,1)S(1)} %collective-permute-done.4.own_ref), channel_id=1, source_target_pairs={{0,14},{2,0},{4,2},{6,4},{8,6},{10,8},{12,10},{14,12},{1,15},{3,1}... | collective-permute-start | bytes 1572872 | tf_op jit(solution)/shard_map/ppermute | solution.py:34
  48.2 3.9 %collective-permute-start.15 = (bf16[4,512,128]{2,1,0:T(8,128)(2,1)S(1)}, bf16[4,512,128]{2,1,0:T(8,128)(2,1)}, u32[]{:S(2)}, u32[]{:S(2)}) collective-permute-start(bf16[4,512,128]{2,1,0:T(8,128)(2,1)S(1)} %all-to-all-done.own_ref), channel_id=1, source_target_pairs={{0,1},{1,0},{2,3},{3,2},{4,5},{5,4},{6,7},{7,6},{8,9},{9,8},{10,11... | collective-permute-start | bytes 1572872 | tf_op jit(solution)/shard_map/ppermute | solution.py:34
  52.3 2.4 %all-to-all-done.2 = bf16[8,32,640]{2,1,0:T(8,128)(2,1)S(1)} async-done(((bf16[8,32,640]{2,1,0:T(8,128)(2,1)}), bf16[8,32,640]{2,1,0:T(8,128)(2,1)S(1)}, u32[]{:S(2)}, u32[]{:S(2)}) %all-to-all-start.2) | async-done | bytes 327712 | tf_op jit(solution)/shard_map/all_to_all | solution.py:140
  54.7 10.2 %collective-permute-done.1.own_ref = bf16[4,512,128]{2,1,0:T(8,128)(2,1)} collective-permute-done((bf16[4,512,128]{2,1,0:T(8,128)(2,1)}, bf16[4,512,128]{2,1,0:T(8,128)(2,1)}, u32[]{:S(2)}, u32[]{:S(2)}) %collective-permute-start.1) | collective-permute-done | bytes 524320 | tf_op jit(solution)/shard_map/ppermute | solution.py:34
  64.8 2.7 %collective-permute-start.6 = (bf16[4,512,128]{2,1,0:T(8,128)(2,1)S(1)}, bf16[4,512,128]{2,1,0:T(8,128)(2,1)S(1)}, u32[]{:S(2)}, u32[]{:S(2)}) collective-permute-start(bf16[4,512,128]{2,1,0:T(8,128)(2,1)S(1)} %collective-permute-done.5.own_ref), channel_id=1, source_target_pairs={{0,14},{2,0},{4,2},{6,4},{8,6},{10,8},{12,10},{14,12},{1,15},{3,1}... | collective-permute-start | bytes 1572872 | tf_op jit(solution)/shard_map/ppermute | solution.py:34
  68.3 4.2 %all-to-all-start.3 = ((f32[4,32,128]{2,1,0:T(8,128)}), f32[4,32,128]{2,1,0:T(8,128)S(1)}, u32[]{:S(2)}, u32[]{:S(2)}) async-start(f32[4,32,128]{2,1,0:T(8,128)} %broadcast_in_dim.24), calls=%async_computation.3 | async-start | bytes 131072 | tf_op jit(solution)/shard_map/all_to_all | solution.py:30
  72.5 3.1 %collective-permute-start.13 = (bf16[4,512,128]{2,1,0:T(8,128)(2,1)S(1)}, bf16[4,512,128]{2,1,0:T(8,128)(2,1)}, u32[]{:S(2)}, u32[]{:S(2)}) collective-permute-start(bf16[4,512,128]{2,1,0:T(8,128)(2,1)S(1)} %collective-permute-done.4.own_ref), channel_id=1, source_target_pairs={{0,1},{1,0},{2,3},{3,2},{4,5},{5,4},{6,7},{7,6},{8,9},{9,8},{10,11... | collective-permute-start | bytes 1572872 | tf_op jit(solution)/shard_map/ppermute | solution.py:34
  75.6 1.3 all-to-all-done.3
  77.7 6.1 %all-to-all-start.4 = ((bf16[32,32,128]{2,1,0:T(8,128)(2,1)}), bf16[32,32,128]{2,1,0:T(8,128)(2,1)}, u32[]{:S(2)}, u32[]{:S(2)}) async-start(bf16[32,32,128]{2,1,0:T(8,128)(2,1)} %broadcast_in_dim.25), calls=%async_computation.4 | async-start | bytes 524288 | tf_op jit(solution)/shard_map/all_to_all | solution.py:145
  84.0 5.0 %collective-permute-start.12 = (bf16[4,512,128]{2,1,0:T(8,128)(2,1)}, bf16[4,512,128]{2,1,0:T(8,128)(2,1)}, u32[]{:S(2)}, u32[]{:S(2)}) collective-permute-start(bf16[4,512,128]{2,1,0:T(8,128)(2,1)} %collective-permute-done.1.own_ref), channel_id=1, source_target_pairs={{0,1},{1,0},{2,3},{3,2},{4,5},{5,4},{6,7},{7,6},{8,9},{9,8},{10,11... | collective-permute-start | bytes 1572872 | tf_op jit(solution)/shard_map/ppermute | solution.py:34
  89.7 1.4 collective-permute-start.3
  92.2 1.2 collective-permute-start.7
  94.4 1.2 copy-done.6
  95.6 1.1 copy-done.9
  96.7 3.6 %shard_map.93 = (f32[224,8192]{1,0:T(8,128)S(1)}, f32[224,512]{1,0:T(8,128)S(1)}) custom-call(s32[2]{0:T(128)S(1)} %pad_add_fusion.7.at_ref, bf16[4,512,128]{2,1,0:T(8,128)(2,1)S(1)} %all-to-all-done.own_ref, bf16[4,512,128]{2,1,0:T(8,128)(2,1)} %collective-permute-done.15.other_ref, ...), custom_call_target="tpu_custom_call", output_to_operand_aliasing={{0}: (6, {}), {1}: (7, {})} | custom-call | flops 469762048 | bytes 6291456 | tf_op jit(solution)/shard_map/pallas_call | solution.py:60
  100.4 3.8 %shard_map.94 = (f32[224,8192]{1,0:T(8,128)S(1)}, f32[224,512]{1,0:T(8,128)S(1)}) custom-call(s32[2]{0:T(128)S(1)} %pad_add_fusion.6.at_ref, bf16[4,512,128]{2,1,0:T(8,128)(2,1)} %collective-permute-done.own_ref, bf16[4,512,128]{2,1,0:T(8,128)(2,1)} %collective-permute-done.14.other_ref, ...), custom_call_target="tpu_custom_call", output_to_operand_aliasing={{0}: (6, {}), {1}: (7, {})} | custom-call | flops 469762048 | bytes 6291456 | tf_op jit(solution)/shard_map/pallas_call | solution.py:60
  104.2 3.6 %shard_map.95 = (f32[224,8192]{1,0:T(8,128)S(1)}, f32[224,512]{1,0:T(8,128)S(1)}) custom-call(s32[2]{0:T(128)S(1)} %pad_add_fusion.5.at_ref, bf16[4,512,128]{2,1,0:T(8,128)(2,1)S(1)} %collective-permute-done.4.own_ref, bf16[4,512,128]{2,1,0:T(8,128)(2,1)} %collective-permute-done.13.other_ref, ...), custom_call_target="tpu_custom_call", output_to_operand_aliasing={{0}: (6, {}), {1}: (7, {})} | custom-call | flops 469762048 | bytes 6291456 | tf_op jit(solution)/shard_map/pallas_call | solution.py:60
  107.8 2.9 %copy-done = f32[224,8192]{1,0:T(8,128)} copy-done((f32[224,8192]{1,0:T(8,128)}, f32[224,8192]{1,0:T(8,128)S(1)}, u32[]{:S(2)}) %copy-start) | copy-done | bytes 7340056
  114.2 3.1 %copy-done.1 = f32[224,8192]{1,0:T(8,128)S(1)} copy-done((f32[224,8192]{1,0:T(8,128)S(1)}, f32[224,8192]{1,0:T(8,128)}, u32[]{:S(2)}) %copy-start.1) | copy-done | bytes 7340056
  117.3 2.0 %copy-done.7 = bf16[1,224,8192]{2,1,0:T(8,128)(2,1)S(1)} copy-done((bf16[1,224,8192]{2,1,0:T(8,128)(2,1)S(1)}, bf16[1,224,8192]{2,1,0:T(8,128)(2,1)}, u32[]{:S(2)}) %copy-start.7) | copy-done | bytes 3670040
  119.3 2.0 %copy-done.10 = bf16[224,8192]{1,0:T(8,128)(2,1)S(1)} copy-done((bf16[224,8192]{1,0:T(8,128)(2,1)S(1)}, bf16[224,8192]{1,0:T(8,128)(2,1)}, u32[]{:S(2)}) %copy-start.10) | copy-done | bytes 3670040
  121.3 3.8 %shard_map.96 = (f32[224,8192]{1,0:T(8,128)S(1)}, f32[224,512]{1,0:T(8,128)S(1)}) custom-call(s32[2]{0:T(128)S(1)} %pad_add_fusion.4.at_ref, bf16[4,512,128]{2,1,0:T(8,128)(2,1)} %collective-permute-done.1.own_ref, bf16[4,512,128]{2,1,0:T(8,128)(2,1)} %collective-permute-done.12.other_ref, ...), custom_call_target="tpu_custom_call", output_to_operand_aliasing={{0}: (6, {}), {1}: (7, {})} | custom-call | flops 469762048 | bytes 6291456 | tf_op jit(solution)/shard_map/pallas_call | solution.py:60
  125.1 3.6 %shard_map.97 = (f32[224,8192]{1,0:T(8,128)S(1)}, f32[224,512]{1,0:T(8,128)S(1)}) custom-call(s32[2]{0:T(128)S(1)} %pad_add_fusion.3.at_ref, bf16[4,512,128]{2,1,0:T(8,128)(2,1)S(1)} %collective-permute-done.5.own_ref, bf16[4,512,128]{2,1,0:T(8,128)(2,1)} %collective-permute-done.11.other_ref, ...), custom_call_target="tpu_custom_call", output_to_operand_aliasing={{0}: (6, {}), {1}: (7, {})} | custom-call | flops 469762048 | bytes 6291456 | tf_op jit(solution)/shard_map/pallas_call | solution.py:60
  128.8 2.9 %copy-done.2 = f32[224,8192]{1,0:T(8,128)} copy-done((f32[224,8192]{1,0:T(8,128)}, f32[224,8192]{1,0:T(8,128)S(1)}, u32[]{:S(2)}) %copy-start.2) | copy-done | bytes 7340056
  133.7 3.1 %copy-done.3 = f32[224,8192]{1,0:T(8,128)S(1)} copy-done((f32[224,8192]{1,0:T(8,128)S(1)}, f32[224,8192]{1,0:T(8,128)}, u32[]{:S(2)}) %copy-start.3) | copy-done | bytes 7340056
  136.8 2.0 %copy-done.8 = bf16[1,224,8192]{2,1,0:T(8,128)(2,1)S(1)} copy-done((bf16[1,224,8192]{2,1,0:T(8,128)(2,1)S(1)}, bf16[1,224,8192]{2,1,0:T(8,128)(2,1)}, u32[]{:S(2)}) %copy-start.8) | copy-done | bytes 3670040
  138.8 2.0 %copy-done.11 = bf16[224,8192]{1,0:T(8,128)(2,1)S(1)} copy-done((bf16[224,8192]{1,0:T(8,128)(2,1)S(1)}, bf16[224,8192]{1,0:T(8,128)(2,1)}, u32[]{:S(2)}) %copy-start.11) | copy-done | bytes 3670040
  140.9 3.6 %shard_map.98 = (f32[224,8192]{1,0:T(8,128)S(1)}, f32[224,512]{1,0:T(8,128)S(1)}) custom-call(s32[2]{0:T(128)S(1)} %pad_add_fusion.2.at_ref, bf16[4,512,128]{2,1,0:T(8,128)(2,1)S(1)} %collective-permute-done.2.own_ref, bf16[4,512,128]{2,1,0:T(8,128)(2,1)} %collective-permute-done.10.other_ref, ...), custom_call_target="tpu_custom_call", output_to_operand_aliasing={{0}: (6, {}), {1}: (7, {})} | custom-call | flops 469762048 | bytes 6291456 | tf_op jit(solution)/shard_map/pallas_call | solution.py:60
  144.5 3.6 %shard_map.99 = (f32[224,8192]{1,0:T(8,128)S(1)}, f32[224,512]{1,0:T(8,128)S(1)}) custom-call(s32[2]{0:T(128)S(1)} %pad_add_fusion.1.at_ref, bf16[4,512,128]{2,1,0:T(8,128)(2,1)S(1)} %collective-permute-done.6.own_ref, bf16[4,512,128]{2,1,0:T(8,128)(2,1)} %collective-permute-done.9.other_ref, ...), custom_call_target="tpu_custom_call", output_to_operand_aliasing={{0}: (6, {}), {1}: (7, {})} | custom-call | flops 469762048 | bytes 6291456 | tf_op jit(solution)/shard_map/pallas_call | solution.py:60
  148.1 3.6 %shard_map.100 = (f32[224,8192]{1,0:T(8,128)S(1)}, f32[224,512]{1,0:T(8,128)S(1)}) custom-call(s32[2]{0:T(128)S(1)} %pad_add_fusion.at_ref, bf16[4,512,128]{2,1,0:T(8,128)(2,1)S(1)} %constant_dynamic-update-slice_fusion.own_ref, bf16[4,512,128]{2,1,0:T(8,128)(2,1)} %collective-permute-done.8.other_ref, ...), custom_call_target="tpu_custom_call", output_to_operand_aliasing={{0}: (6, {}), {1}: (7, {})} | custom-call | flops 469762048 | bytes 6291456 | tf_op jit(solution)/shard_map/pallas_call | solution.py:60
  151.8 1.2 fusion
  153.0 2.9 %copy-done.4 = f32[224,8192]{1,0:T(8,128)} copy-done((f32[224,8192]{1,0:T(8,128)}, f32[224,8192]{1,0:T(8,128)S(1)}, u32[]{:S(2)}) %copy-start.4) | copy-done | bytes 7340056
  156.6 3.3 %all-to-all-start.5 = ((f32[4,32,224]{2,1,0:T(8,128)}), f32[4,32,224]{2,1,0:T(8,128)S(1)}, u32[]{:S(2)}, u32[]{:S(2)}) async-start(f32[4,32,224]{2,1,0:T(8,128)} %broadcast_in_dim.26), calls=%async_computation.5 | async-start | bytes 262144 | tf_op jit(solution)/shard_map/all_to_all | solution.py:30
  160.3 2.9 %cholesky.17 = f32[32,32]{1,0:T(8,128)S(1)} custom-call(f32[32,32]{1,0:T(8,128)S(1)} %fusion.23), custom_call_target="Cholesky" | custom-call | tf_op jit(solution)/shard_map/jit(cholesky)/cholesky | solution.py:173
  164.6 2.4 %custom-call.6 = f32[1,32,32]{1,2,0:T(8,128)S(1)} custom-call(f32[1,32,32]{2,1,0:T(8,128)S(1)} %fusion.20), custom_call_target="InvertDiagBlocksLowerTriangular" | custom-call | tf_op jit(solution)/shard_map/triangular_solve | solution.py:174
  167.0 1.0 fusion.12
  168.7 3.1 %copy-done.5 = f32[224,8192]{1,0:T(8,128)S(1)} copy-done((f32[224,8192]{1,0:T(8,128)S(1)}, f32[224,8192]{1,0:T(8,128)}, u32[]{:S(2)}) %copy-start.5) | copy-done | bytes 7340056
  171.8 4.9 %shard_map.101 = bf16[224,8192]{1,0:T(8,128)(2,1)} custom-call(f32[224,8192]{1,0:T(8,128)S(1)} %copy-done.5, bf16[64,224]{1,0:T(8,128)(2,1)S(1)} %pad_maximum_fusion.5.factor_ref, bf16[32,8192]{1,0:T(8,128)(2,1)S(1)} %reshape.50.basis_ref), custom_call_target="tpu_custom_call" | custom-call | flops 234881024 | bytes 12582912 | tf_op jit(solution)/shard_map/pallas_call | solution.py:96
  (110 shorter events, 19.1 us)
Async XLA Ops:
  0.6 8.1 %copy-start.14 = (bf16[512,224]{0,1:T(8,128)(2,1)S(1)}, bf16[512,224]{0,1:T(8,128)(2,1)}, u32[]{:S(2)}) copy-start(bf16[512,224]{0,1:T(8,128)(2,1)} %param.6) | copy-start | bytes 688132
  0.6 8.1 %copy-start.12 = (bf16[512,224]{0,1:T(8,128)(2,1)S(1)}, bf16[512,224]{0,1:T(8,128)(2,1)}, u32[]{:S(2)}) copy-start(bf16[512,224]{0,1:T(8,128)(2,1)} %param.7) | copy-start | bytes 688132
  0.7 11.8 %copy-start.16 = (bf16[512,128]{1,0:T(8,128)(2,1)S(1)}, bf16[512,128]{1,0:T(8,128)(2,1)}, u32[]{:S(2)}) copy-start(bf16[512,128]{1,0:T(8,128)(2,1)} %param.8) | copy-start | bytes 393220
  9.2 7.8 %collective-permute-start.16 = (bf16[32,4608]{1,0:T(8,128)(2,1)S(1)}, bf16[32,4608]{1,0:T(8,128)(2,1)S(1)}, u32[]{:S(2)}, u32[]{:S(2)}) collective-permute-start(bf16[32,4608]{1,0:T(8,128)(2,1)S(1)} %pad_maximum_fusion.1), channel_id=1, source_target_pairs={{0,1},{1,0},{2,3},{3,2},{4,5},{5,4},{6,7},{7,6},{8,9},{9,8},{10,11... | collective-permute-start | bytes 884744 | tf_op jit(solution)/shard_map/ppermute | solution.py:34
  13.3 13.1 %all-to-all-start = ((bf16[4,512,128]{2,1,0:T(8,128)(2,1)}), bf16[4,512,128]{2,1,0:T(8,128)(2,1)S(1)}, u32[]{:S(2)}, u32[]{:S(2)}) async-start(bf16[4,512,128]{2,1,0:T(8,128)(2,1)} %broadcast_in_dim.19), calls=%async_computation | async-start | bytes 1048576 | tf_op jit(solution)/shard_map/all_to_all | solution.py:115
  26.4 10.5 %all-to-all-start.1 = ((bf16[4,32,1536]{2,1,0:T(8,128)(2,1)}), bf16[4,32,1536]{2,1,0:T(8,128)(2,1)S(1)}, u32[]{:S(2)}, u32[]{:S(2)}) async-start(bf16[4,32,1536]{2,1,0:T(8,128)(2,1)} %pad_maximum_fusion), calls=%async_computation.1 | async-start | bytes 786432 | tf_op jit(solution)/shard_map/all_to_all | solution.py:137
  29.9 15.4 %collective-permute-start = (bf16[4,512,128]{2,1,0:T(8,128)(2,1)S(1)}, bf16[4,512,128]{2,1,0:T(8,128)(2,1)}, u32[]{:S(2)}, u32[]{:S(2)}) collective-permute-start(bf16[4,512,128]{2,1,0:T(8,128)(2,1)S(1)} %all-to-all-done.own_ref), channel_id=1, source_target_pairs={{0,2},{2,4},{4,6},{6,8},{8,10},{10,12},{12,14},{14,0},{1,3},{3,5},... | collective-permute-start | bytes 1572872 | tf_op jit(solution)/shard_map/ppermute | solution.py:34
  30.1 15.5 %collective-permute-start.4 = (bf16[4,512,128]{2,1,0:T(8,128)(2,1)S(1)}, bf16[4,512,128]{2,1,0:T(8,128)(2,1)S(1)}, u32[]{:S(2)}, u32[]{:S(2)}) collective-permute-start(bf16[4,512,128]{2,1,0:T(8,128)(2,1)S(1)} %all-to-all-done.own_ref), channel_id=1, source_target_pairs={{0,14},{2,0},{4,2},{6,4},{8,6},{10,8},{12,10},{14,12},{1,15},{3,1}... | collective-permute-start | bytes 1572872 | tf_op jit(solution)/shard_map/ppermute | solution.py:34
  37.8 16.8 %all-to-all-start.2 = ((bf16[8,32,640]{2,1,0:T(8,128)(2,1)}), bf16[8,32,640]{2,1,0:T(8,128)(2,1)S(1)}, u32[]{:S(2)}, u32[]{:S(2)}) async-start(bf16[8,32,640]{2,1,0:T(8,128)(2,1)} %pad_maximum_fusion.3), calls=%async_computation.2 | async-start | bytes 655360 | tf_op jit(solution)/shard_map/all_to_all | solution.py:140
  45.3 19.5 %collective-permute-start.1 = (bf16[4,512,128]{2,1,0:T(8,128)(2,1)}, bf16[4,512,128]{2,1,0:T(8,128)(2,1)}, u32[]{:S(2)}, u32[]{:S(2)}) collective-permute-start(bf16[4,512,128]{2,1,0:T(8,128)(2,1)} %collective-permute-done.own_ref), channel_id=1, source_target_pairs={{0,2},{2,4},{4,6},{6,8},{8,10},{10,12},{12,14},{14,0},{1,3},{3,5},... | collective-permute-start | bytes 1572872 | tf_op jit(solution)/shard_map/ppermute | solution.py:34
  45.6 19.2 %collective-permute-start.5 = (bf16[4,512,128]{2,1,0:T(8,128)(2,1)S(1)}, bf16[4,512,128]{2,1,0:T(8,128)(2,1)S(1)}, u32[]{:S(2)}, u32[]{:S(2)}) collective-permute-start(bf16[4,512,128]{2,1,0:T(8,128)(2,1)S(1)} %collective-permute-done.4.own_ref), channel_id=1, source_target_pairs={{0,14},{2,0},{4,2},{6,4},{8,6},{10,8},{12,10},{14,12},{1,15},{3,1}... | collective-permute-start | bytes 1572872 | tf_op jit(solution)/shard_map/ppermute | solution.py:34
  48.2 43.7 %collective-permute-start.15 = (bf16[4,512,128]{2,1,0:T(8,128)(2,1)S(1)}, bf16[4,512,128]{2,1,0:T(8,128)(2,1)}, u32[]{:S(2)}, u32[]{:S(2)}) collective-permute-start(bf16[4,512,128]{2,1,0:T(8,128)(2,1)S(1)} %all-to-all-done.own_ref), channel_id=1, source_target_pairs={{0,1},{1,0},{2,3},{3,2},{4,5},{5,4},{6,7},{7,6},{8,9},{9,8},{10,11... | collective-permute-start | bytes 1572872 | tf_op jit(solution)/shard_map/ppermute | solution.py:34
  52.2 40.1 %collective-permute-start.14 = (bf16[4,512,128]{2,1,0:T(8,128)(2,1)}, bf16[4,512,128]{2,1,0:T(8,128)(2,1)}, u32[]{:S(2)}, u32[]{:S(2)}) collective-permute-start(bf16[4,512,128]{2,1,0:T(8,128)(2,1)} %collective-permute-done.own_ref), channel_id=1, source_target_pairs={{0,1},{1,0},{2,3},{3,2},{4,5},{5,4},{6,7},{7,6},{8,9},{9,8},{10,11... | collective-permute-start | bytes 1572872 | tf_op jit(solution)/shard_map/ppermute | solution.py:34
  64.8 19.1 %collective-permute-start.2 = (bf16[4,512,128]{2,1,0:T(8,128)(2,1)}, bf16[4,512,128]{2,1,0:T(8,128)(2,1)S(1)}, u32[]{:S(2)}, u32[]{:S(2)}) collective-permute-start(bf16[4,512,128]{2,1,0:T(8,128)(2,1)} %collective-permute-done.1.own_ref), channel_id=1, source_target_pairs={{0,2},{2,4},{4,6},{6,8},{8,10},{10,12},{12,14},{14,0},{1,3},{3,5},... | collective-permute-start | bytes 1572872 | tf_op jit(solution)/shard_map/ppermute | solution.py:34
  64.8 24.9 %collective-permute-start.6 = (bf16[4,512,128]{2,1,0:T(8,128)(2,1)S(1)}, bf16[4,512,128]{2,1,0:T(8,128)(2,1)S(1)}, u32[]{:S(2)}, u32[]{:S(2)}) collective-permute-start(bf16[4,512,128]{2,1,0:T(8,128)(2,1)S(1)} %collective-permute-done.5.own_ref), channel_id=1, source_target_pairs={{0,14},{2,0},{4,2},{6,4},{8,6},{10,8},{12,10},{14,12},{1,15},{3,1}... | collective-permute-start | bytes 1572872 | tf_op jit(solution)/shard_map/ppermute | solution.py:34
  68.3 8.7 %all-to-all-start.3 = ((f32[4,32,128]{2,1,0:T(8,128)}), f32[4,32,128]{2,1,0:T(8,128)S(1)}, u32[]{:S(2)}, u32[]{:S(2)}) async-start(f32[4,32,128]{2,1,0:T(8,128)} %broadcast_in_dim.24), calls=%async_computation.3 | async-start | bytes 131072 | tf_op jit(solution)/shard_map/all_to_all | solution.py:30
  72.5 31.6 %collective-permute-start.13 = (bf16[4,512,128]{2,1,0:T(8,128)(2,1)S(1)}, bf16[4,512,128]{2,1,0:T(8,128)(2,1)}, u32[]{:S(2)}, u32[]{:S(2)}) collective-permute-start(bf16[4,512,128]{2,1,0:T(8,128)(2,1)S(1)} %collective-permute-done.4.own_ref), channel_id=1, source_target_pairs={{0,1},{1,0},{2,3},{3,2},{4,5},{5,4},{6,7},{7,6},{8,9},{9,8},{10,11... | collective-permute-start | bytes 1572872 | tf_op jit(solution)/shard_map/ppermute | solution.py:34
  77.7 33.0 %all-to-all-start.4 = ((bf16[32,32,128]{2,1,0:T(8,128)(2,1)}), bf16[32,32,128]{2,1,0:T(8,128)(2,1)}, u32[]{:S(2)}, u32[]{:S(2)}) async-start(bf16[32,32,128]{2,1,0:T(8,128)(2,1)} %broadcast_in_dim.25), calls=%async_computation.4 | async-start | bytes 524288 | tf_op jit(solution)/shard_map/all_to_all | solution.py:145
  84.0 29.8 %collective-permute-start.12 = (bf16[4,512,128]{2,1,0:T(8,128)(2,1)}, bf16[4,512,128]{2,1,0:T(8,128)(2,1)}, u32[]{:S(2)}, u32[]{:S(2)}) collective-permute-start(bf16[4,512,128]{2,1,0:T(8,128)(2,1)} %collective-permute-done.1.own_ref), channel_id=1, source_target_pairs={{0,1},{1,0},{2,3},{3,2},{4,5},{5,4},{6,7},{7,6},{8,9},{9,8},{10,11... | collective-permute-start | bytes 1572872 | tf_op jit(solution)/shard_map/ppermute | solution.py:34
  89.7 21.5 %collective-permute-start.3 = (bf16[4,256,128]{2,1,0:T(8,128)(2,1)}, bf16[4,256,128]{2,1,0:T(8,128)(2,1)}, u32[]{:S(2)}, u32[]{:S(2)}) collective-permute-start(bf16[4,256,128]{2,1,0:T(8,128)(2,1)} %slice.59), channel_id=1, source_target_pairs={{0,2},{2,4},{4,6},{6,8},{8,10},{10,12},{12,14},{14,0},{1,3},{3,5},... | collective-permute-start | bytes 786440 | tf_op jit(solution)/shard_map/ppermute | solution.py:34
  91.9 33.2 %collective-permute-start.11 = (bf16[4,512,128]{2,1,0:T(8,128)(2,1)S(1)}, bf16[4,512,128]{2,1,0:T(8,128)(2,1)}, u32[]{:S(2)}, u32[]{:S(2)}) collective-permute-start(bf16[4,512,128]{2,1,0:T(8,128)(2,1)S(1)} %collective-permute-done.5.own_ref), channel_id=1, source_target_pairs={{0,1},{1,0},{2,3},{3,2},{4,5},{5,4},{6,7},{7,6},{8,9},{9,8},{10,11... | collective-permute-start | bytes 1572872 | tf_op jit(solution)/shard_map/ppermute | solution.py:34
  92.2 20.0 %collective-permute-start.7 = (bf16[4,256,128]{2,1,0:T(8,128)(2,1)}, bf16[4,256,128]{2,1,0:T(8,128)(2,1)}, u32[]{:S(2)}, u32[]{:S(2)}) collective-permute-start(bf16[4,256,128]{2,1,0:T(8,128)(2,1)} %slice.60), channel_id=1, source_target_pairs={{0,14},{2,0},{4,2},{6,4},{8,6},{10,8},{12,10},{14,12},{1,15},{3,1}... | collective-permute-start | bytes 786440 | tf_op jit(solution)/shard_map/ppermute | solution.py:34
  93.6 2.0 %copy-start.6 = (bf16[1,224,8192]{2,1,0:T(8,128)(2,1)S(1)}, bf16[1,224,8192]{2,1,0:T(8,128)(2,1)}, u32[]{:S(2)}) copy-start(bf16[1,224,8192]{2,1,0:T(8,128)(2,1)} %param.10) | copy-start | bytes 11010052
  93.6 3.2 %copy-start.9 = (bf16[224,8192]{1,0:T(8,128)(2,1)S(1)}, bf16[224,8192]{1,0:T(8,128)(2,1)}, u32[]{:S(2)}) copy-start(bf16[224,8192]{1,0:T(8,128)(2,1)} %weight_ref.15) | copy-start | bytes 11010052
  107.8 2.9 %copy-start = (f32[224,8192]{1,0:T(8,128)}, f32[224,8192]{1,0:T(8,128)S(1)}, u32[]{:S(2)}) copy-start(f32[224,8192]{1,0:T(8,128)S(1)} %get-tuple-element.26.matrix_in) | copy-start | bytes 22020100
  110.7 21.0 %collective-permute-start.17 = (bf16[32,32,128]{2,1,0:T(8,128)(2,1)}, bf16[32,32,128]{2,1,0:T(8,128)(2,1)S(1)}, u32[]{:S(2)}, u32[]{:S(2)}) collective-permute-start(bf16[32,32,128]{2,1,0:T(8,128)(2,1)} %all-to-all-done.4), channel_id=1, source_target_pairs={{0,1},{1,0},{2,3},{3,2},{4,5},{5,4},{6,7},{7,6},{8,9},{9,8},{10,11... | collective-permute-start | bytes 786440 | tf_op jit(solution)/shard_map/ppermute | solution.py:34
  111.2 22.5 %collective-permute-start.10 = (bf16[4,512,128]{2,1,0:T(8,128)(2,1)S(1)}, bf16[4,512,128]{2,1,0:T(8,128)(2,1)}, u32[]{:S(2)}, u32[]{:S(2)}) collective-permute-start(bf16[4,512,128]{2,1,0:T(8,128)(2,1)S(1)} %collective-permute-done.2.own_ref), channel_id=1, source_target_pairs={{0,1},{1,0},{2,3},{3,2},{4,5},{5,4},{6,7},{7,6},{8,9},{9,8},{10,11... | collective-permute-start | bytes 1572872 | tf_op jit(solution)/shard_map/ppermute | solution.py:34
  112.3 32.2 %collective-permute-start.9 = (bf16[4,512,128]{2,1,0:T(8,128)(2,1)S(1)}, bf16[4,512,128]{2,1,0:T(8,128)(2,1)}, u32[]{:S(2)}, u32[]{:S(2)}) collective-permute-start(bf16[4,512,128]{2,1,0:T(8,128)(2,1)S(1)} %collective-permute-done.6.own_ref), channel_id=1, source_target_pairs={{0,1},{1,0},{2,3},{3,2},{4,5},{5,4},{6,7},{7,6},{8,9},{9,8},{10,11... | collective-permute-start | bytes 1572872 | tf_op jit(solution)/shard_map/ppermute | solution.py:34
  113.8 34.4 %collective-permute-start.8 = (bf16[4,512,128]{2,1,0:T(8,128)(2,1)S(1)}, bf16[4,512,128]{2,1,0:T(8,128)(2,1)}, u32[]{:S(2)}, u32[]{:S(2)}) collective-permute-start(bf16[4,512,128]{2,1,0:T(8,128)(2,1)S(1)} %constant_dynamic-update-slice_fusion.own_ref), channel_id=1, source_target_pairs={{0,1},{1,0},{2,3},{3,2},{4,5},{5,4},{6,7},{7,6},{8,9},{9,8},{10,11... | collective-permute-start | bytes 1572872 | tf_op jit(solution)/shard_map/ppermute | solution.py:34
  114.2 3.1 %copy-start.1 = (f32[224,8192]{1,0:T(8,128)S(1)}, f32[224,8192]{1,0:T(8,128)}, u32[]{:S(2)}) copy-start(f32[224,8192]{1,0:T(8,128)} %copy-done) | copy-start | bytes 22020100
  117.3 2.0 %copy-start.7 = (bf16[1,224,8192]{2,1,0:T(8,128)(2,1)S(1)}, bf16[1,224,8192]{2,1,0:T(8,128)(2,1)}, u32[]{:S(2)}) copy-start(bf16[1,224,8192]{2,1,0:T(8,128)(2,1)} %param.10) | copy-start | bytes 11010052
  119.3 2.0 %copy-start.10 = (bf16[224,8192]{1,0:T(8,128)(2,1)S(1)}, bf16[224,8192]{1,0:T(8,128)(2,1)}, u32[]{:S(2)}) copy-start(bf16[224,8192]{1,0:T(8,128)(2,1)} %weight_ref.15) | copy-start | bytes 11010052
  128.8 2.9 %copy-start.2 = (f32[224,8192]{1,0:T(8,128)}, f32[224,8192]{1,0:T(8,128)S(1)}, u32[]{:S(2)}) copy-start(f32[224,8192]{1,0:T(8,128)S(1)} %get-tuple-element.30.matrix_in) | copy-start | bytes 22020100
  133.7 3.1 %copy-start.3 = (f32[224,8192]{1,0:T(8,128)S(1)}, f32[224,8192]{1,0:T(8,128)}, u32[]{:S(2)}) copy-start(f32[224,8192]{1,0:T(8,128)} %copy-done.2) | copy-start | bytes 22020100
  136.8 2.0 %copy-start.8 = (bf16[1,224,8192]{2,1,0:T(8,128)(2,1)S(1)}, bf16[1,224,8192]{2,1,0:T(8,128)(2,1)}, u32[]{:S(2)}) copy-start(bf16[1,224,8192]{2,1,0:T(8,128)(2,1)} %param.10) | copy-start | bytes 11010052
  138.8 2.0 %copy-start.11 = (bf16[224,8192]{1,0:T(8,128)(2,1)S(1)}, bf16[224,8192]{1,0:T(8,128)(2,1)}, u32[]{:S(2)}) copy-start(bf16[224,8192]{1,0:T(8,128)(2,1)} %weight_ref.15) | copy-start | bytes 11010052
  151.8 15.2 %copy-start.13 = (bf16[512,224]{0,1:T(8,128)(2,1)S(1)}, bf16[512,224]{0,1:T(8,128)(2,1)}, u32[]{:S(2)}) copy-start(bf16[512,224]{0,1:T(8,128)(2,1)} %param.7) | copy-start | bytes 688132
  151.8 15.2 %copy-start.15 = (bf16[512,224]{0,1:T(8,128)(2,1)S(1)}, bf16[512,224]{0,1:T(8,128)(2,1)}, u32[]{:S(2)}) copy-start(bf16[512,224]{0,1:T(8,128)(2,1)} %param.6) | copy-start | bytes 688132
  153.0 2.9 %copy-start.4 = (f32[224,8192]{1,0:T(8,128)}, f32[224,8192]{1,0:T(8,128)S(1)}, u32[]{:S(2)}) copy-start(f32[224,8192]{1,0:T(8,128)S(1)} %get-tuple-element.37.matrix_ref) | copy-start | bytes 22020100
  156.6 11.6 %all-to-all-start.5 = ((f32[4,32,224]{2,1,0:T(8,128)}), f32[4,32,224]{2,1,0:T(8,128)S(1)}, u32[]{:S(2)}, u32[]{:S(2)}) async-start(f32[4,32,224]{2,1,0:T(8,128)} %broadcast_in_dim.26), calls=%async_computation.5 | async-start | bytes 262144 | tf_op jit(solution)/shard_map/all_to_all | solution.py:30
  168.4 8.3 %copy-start.17 = (f32[32,224]{1,0:T(8,128)}, f32[32,224]{1,0:T(8,128)S(1)}, u32[]{:S(2)}) copy-start(f32[32,224]{1,0:T(8,128)S(1)} %fusion.16) | copy-start | bytes 86020
  168.7 3.1 %copy-start.5 = (f32[224,8192]{1,0:T(8,128)S(1)}, f32[224,8192]{1,0:T(8,128)}, u32[]{:S(2)}) copy-start(f32[224,8192]{1,0:T(8,128)} %copy-done.4) | copy-start | bytes 22020100

commit v3 on v1

v3 whole, which is shorter than its diff:
```python
import functools

import jax
import jax.numpy as jnp
from jax import lax
from jax.experimental import pallas as pl
from jax.experimental.pallas import tpu as pltpu
from jax.sharding import Mesh, PartitionSpec as P

BF = jnp.bfloat16
F32 = jnp.float32
X, Z, CORES = 4, 8, 2
PLANE = ("x", "z", "core")
LANES = 128
NT = (((1,), (1,)), ((), ()))
TN = (((0,), (0,)), ((), ()))
VMEM = pl.BlockSpec(memory_space=pltpu.VMEM)
ANY = pl.BlockSpec(memory_space=pl.ANY)
HIGHEST = lax.Precision.HIGHEST


def dot(a, b):
    return jnp.dot(a, b, preferred_element_type=F32)


def split(a):
    high = a.astype(BF)
    return high, (a - high.astype(F32)).astype(BF)


def shift(a, axis, step, n):
    return lax.ppermute(a, axis, [(i, (i + step) % n) for i in range(n)])


def exchange(a, axis):
    return lax.all_to_all(a, axis, 0, 0)


def call(kernel, out, scratch=(), ins=None, outs=None, flops=0, moved=0, vmem=24):
    shapes = [jax.ShapeDtypeStruct(s, t) for s, t in out]
    return pl.pallas_call(
        kernel,
        in_specs=ins,
        out_specs=outs if outs is not None else [VMEM] * len(out),
        out_shape=shapes,
        scratch_shapes=list(scratch),
        cost_estimate=pl.CostEstimate(flops=flops, bytes_accessed=moved, transcendentals=0),
        compiler_params=pltpu.CompilerParams(vmem_limit_bytes=vmem << 20),
    )


def column(z, x, wide):
    return pl.multiple_of((x * Z + z) * (CORES * wide), CORES * wide)


def start_kernel(gate_ref, up_ref, q_ref, error_ref, hidden_ref, send_ref, mine_ref, error_buf, sems):
    rank = q_ref.shape[0]
    columns = error_ref.shape[1] // X
    copies = []
    for x in range(X):
        copies.append(pltpu.make_async_copy(error_ref.at[:, pl.ds(x * columns, columns)], error_buf.at[x], sems.at[x]))
        copies[x].start()
    gate = gate_ref[...].astype(F32)
    hidden = (gate * jax.nn.sigmoid(gate) * up_ref[...].astype(F32)).astype(BF)
    hidden_ref[...] = hidden
    high, low = split(q_ref[...])
    both = jnp.concatenate([high, low], axis=0)
    left = dot(both, hidden)
    left = (left[:rank] + left[rank:]).astype(BF)
    blocks = left.shape[1] // LANES
    for b in range(blocks):
        send_ref[b * rank:(b + 1) * rank, :] = left[:, b * LANES:(b + 1) * LANES]
    first = lax.axis_index("core") == 0
    for x in range(X):
        copies[x].wait()
        term = dot(both, error_buf[x])
        term = (term[:rank] + term[rank:]).astype(BF)
        for z in range(Z):
            at = (x * Z + z) * rank
            zero = term[:, (2 * z) * LANES:(2 * z + 1) * LANES]
            one = term[:, (2 * z + 1) * LANES:(2 * z + 2) * LANES]
            mine_ref[at:at + rank, :] = jnp.where(first, zero, one)
            at += blocks * rank
            send_ref[at:at + rank, :] = jnp.where(first, one, zero)


def slice_kernel(groups, terms_ref, cotangent_ref, out_ref):
    rank = out_ref.shape[1]
    terms = terms_ref[0].astype(F32)
    for i in range(1, Z):
        terms = terms + terms_ref[i].astype(F32)
    blocks = cotangent_ref.shape[0] // LANES
    total = terms[blocks * rank:]
    for b in range(blocks):
        total = total + dot(terms[b * rank:(b + 1) * rank].astype(BF), cotangent_ref[b * LANES:(b + 1) * LANES, :])
    total = total / groups
    for g in range(groups):
        out_ref[g] = total


def spread_kernel(terms_ref, out_ref):
    total = terms_ref[0]
    for g in range(1, terms_ref.shape[0]):
        total = total + terms_ref[g]
    total = total.astype(BF)
    for i in range(out_ref.shape[0]):
        out_ref[i] = total


def piece_kernel(steps, *refs):
    n = len(steps)
    own, other = refs[:n], refs[n:2 * n]
    hidden_ref, error_ref, weight_ref, d_in, matrix_ref, d_ref, error_buf, weight_buf, sems = refs[2 * n:]
    tokens, wide = own[0].shape[1:]
    width = CORES * wide
    me = lax.axis_index("z")
    first = lax.axis_index("core") == 0
    copies = []
    for i, step in enumerate(steps):
        for x in range(X):
            at = column(lax.rem(me + (Z - step), Z), x, wide)
            b = i * X + x
            pair = []
            for k, (source, target) in enumerate(((error_ref, error_buf), (weight_ref, weight_buf))):
                pair.append(pltpu.make_async_copy(source.at[:, pl.ds(at, width)], target.at[:, pl.ds(b * width, width)], sems.at[k, b]))
                pair[k].start()
            copies.append(pair)
    hidden = hidden_ref[...]
    total = d_in[...]
    for i in range(n):
        blocks = []
        for x in range(X):
            a, b = own[i][x], other[i][x]
            blocks += [jnp.where(first, a, b), jnp.where(first, b, a)]
            for copy in copies[i * X + x]:
                copy.wait()
        block = jnp.concatenate(blocks, axis=1)
        span = slice(i * X * width, (i + 1) * X * width)
        matrix_ref[:, span] = error_buf[:, span].astype(F32) + dot(hidden, block)
        total = total + lax.dot_general(block, weight_buf[:, span], NT, preferred_element_type=F32)
    d_ref[...] = total


def add_pieces(steps, own, other, hidden, error, weight, d_hidden):
    n = len(steps)
    tokens, wide = own[0].shape[1:]
    rows = hidden.shape[0]
    columns = n * X * CORES * wide
    return call(
        functools.partial(piece_kernel, steps),
        [((rows, columns), F32), ((tokens, rows), F32)],
        [pltpu.VMEM((rows, columns), BF), pltpu.VMEM((rows, columns), BF), pltpu.SemaphoreType.DMA((2, n * X))],
        [VMEM] * (2 * n + 1) + [ANY, ANY, VMEM],
        flops=4 * rows * tokens * columns,
        moved=4 * rows * columns,
    )(*own, *other, hidden, error, weight, d_hidden)


def basis_block(first, me, step, x, mine_ref, theirs_ref):
    at = x * Z + lax.rem(me + (Z - step), Z)
    a, b = mine_ref[at], theirs_ref[at]
    return jnp.concatenate([jnp.where(first, a, b), jnp.where(first, b, a)], axis=1)


def turn_kernel(layout, groups, *refs):
    n = len(layout)
    mine_ref, theirs_ref, out_ref, gram_ref = refs[n:]
    me = lax.axis_index("z")
    first = lax.axis_index("core") == 0
    total, gram = 0.0, 0.0
    for matrix_ref, steps in zip(refs[:n], layout):
        for i, step in enumerate(steps):
            basis = jnp.concatenate([basis_block(first, me, step, x, mine_ref, theirs_ref) for x in range(X)], axis=1)
            span = slice(i * basis.shape[1], (i + 1) * basis.shape[1])
            total = total + lax.dot_general(matrix_ref[:, span].astype(BF), basis, NT, preferred_element_type=F32)
            gram = gram + lax.dot_general(basis, basis, NT, preferred_element_type=F32)
    gram_ref[...] = gram
    total = total.T
    for g in range(groups):
        out_ref[g] = total


def final_kernel(layout, groups, *refs):
    n = len(layout)
    mine_ref, theirs_ref, terms_ref, inverse_ref, out_ref, q_ref, buf, sems = refs[n:]
    wide = mine_ref.shape[2]
    width = CORES * wide
    me = lax.axis_index("z")
    first = lax.axis_index("core") == 0
    total = terms_ref[0]
    for g in range(1, groups):
        total = total + terms_ref[g]
    inverse = inverse_ref[...]
    next_q = jnp.dot(inverse, total / groups, precision=HIGHEST, preferred_element_type=F32)
    q_ref[...] = next_q
    factor = lax.dot_general(inverse, next_q, TN, precision=HIGHEST, preferred_element_type=F32)
    high, low = split(factor.T)
    factor = jnp.concatenate([high, low], axis=1)
    copies = []
    for matrix_ref, steps in zip(refs[:n], layout):
        for i, step in enumerate(steps):
            basis = jnp.concatenate([basis_block(first, me, step, x, mine_ref, theirs_ref) for x in range(X)], axis=1)
            basis = jnp.concatenate([basis, basis], axis=0)
            span = slice(i * X * width, (i + 1) * X * width)
            buf[step] = (matrix_ref[:, span] - dot(factor, basis)).astype(BF)
            for x in range(X):
                at = column(lax.rem(me + (Z - step), Z), x, wide)
                copy = pltpu.make_async_copy(buf.at[step, :, pl.ds(x * width, width)], out_ref.at[:, pl.ds(at, width)], sems.at[step, x])
                copy.start()
                copies.append(copy)
    for copy in copies:
        copy.wait()


def local(gate, upward, cotangent, down_weight, error_buffer, start_q):
    groups = lax.axis_size("dp")
    rank = start_q.shape[1]
    tokens, wide = cotangent.shape
    error = error_buffer[0]
    rows, columns = error.shape
    tiles = tokens // LANES * rank

    hidden, send, mine = call(
        start_kernel,
        [((rows, tokens), BF), ((tiles + X * Z * rank, wide), BF), ((X * Z * rank, wide), BF)],
        [pltpu.VMEM((X, rows, columns // X), BF), pltpu.SemaphoreType.DMA((X,))],
        [VMEM, VMEM, VMEM, ANY],
        flops=4 * rows * rank * columns,
        moved=2 * rows * columns,
    )(gate.T, upward.T, start_q.T, error)
    theirs = shift(send, "core", 1, CORES)
    left = (send[:tiles].astype(F32) + theirs[:tiles].astype(F32)).astype(BF)
    part = (mine.astype(F32) + theirs[tiles:].astype(F32)).astype(BF).reshape(X, Z * rank, wide)

    spread = lambda a, n: jnp.broadcast_to(a[None], (n,) + a.shape)
    got = exchange(jnp.concatenate([spread(cotangent, X), spread(left, X), part], axis=1), "x")
    pieces, others = {0: got[:, :tokens]}, {}
    sums = got[:, tokens:].astype(F32).sum(0).astype(BF)
    terms = jnp.concatenate([spread(sums[:tiles], Z), sums[tiles:].reshape(Z, rank, wide)], axis=1)

    def ring(step):
        pieces[step] = shift(pieces[step - 1], "z", 1, Z)
        pieces[Z - step] = shift(pieces[(Z - step + 1) % Z], "z", Z - 1, Z)

    def swap(*steps):
        for step in steps:
            others[step] = shift(pieces[step], "core", 1, CORES)

    matrices, layout = [], []

    def use(steps, d_hidden):
        matrix, d_hidden = add_pieces(steps, [pieces[s] for s in steps], [others[s] for s in steps], hidden, error, down_weight, d_hidden)
        matrices.append(matrix)
        layout.append(steps)
        return d_hidden

    d_hidden = jnp.zeros((tokens, rows), F32)
    ring(1)
    swap(0)
    terms = exchange(terms, "z")
    d_hidden = use((0,), d_hidden)
    terms, pieces[1], pieces[7], d_hidden = lax.optimization_barrier((terms, pieces[1], pieces[7], d_hidden))
    ring(2)
    swap(1, 7)
    terms, = call(functools.partial(slice_kernel, groups), [((groups, rank, wide), F32)], ins=[VMEM, VMEM])(terms, cotangent)
    terms = exchange(terms, "dp")
    d_hidden = use((1, 7), d_hidden)
    terms, pieces[2], pieces[6], d_hidden = lax.optimization_barrier((terms, pieces[2], pieces[6], d_hidden))
    ring(3)
    swap(2, 6)
    mine, = call(spread_kernel, [((X * Z, rank, wide), BF)], ins=[VMEM])(terms)
    mine = exchange(mine, ("x", "z"))
    d_hidden = use((2, 6), d_hidden)
    pieces[3], pieces[5], d_hidden = lax.optimization_barrier((pieces[3], pieces[5], d_hidden))
    half = tokens // 2
    up = shift(pieces[3][:, :half], "z", 1, Z)
    down = shift(pieces[5][:, half:], "z", Z - 1, Z)
    swap(3, 5)
    d_hidden = use((3, 5), d_hidden)
    pieces[4] = jnp.concatenate([up, down], axis=1)
    swap(4)
    d_hidden = use((4,), d_hidden)
    theirs = shift(mine, "core", 1, CORES)

    terms, gram = call(
        functools.partial(turn_kernel, tuple(layout), groups),
        [((groups, rank, rows), F32), ((rank, rank), F32)],
        ins=[VMEM] * (len(layout) + 2),
        flops=2 * rows * rank * columns,
        moved=4 * rows * columns,
    )(*matrices, mine, theirs)
    terms = exchange(terms, "dp")
    lower = jnp.linalg.cholesky(gram)
    inverse = lax.linalg.triangular_solve(lower, jnp.eye(rank, dtype=F32), left_side=True, lower=True)

    d_hidden = d_hidden.T
    gate_f = gate.T.astype(F32)
    up_f = upward.T.astype(F32)
    sigma = jax.nn.sigmoid(gate_f)
    d_gate = (d_hidden * up_f * sigma * (1.0 + gate_f * (1.0 - sigma))).astype(BF).T
    d_up = (d_hidden * (gate_f * sigma)).astype(BF).T

    new_error, next_q = call(
        functools.partial(final_kernel, tuple(layout), groups),
        [((rows, columns), BF), ((rank, rows), F32)],
        [pltpu.VMEM((Z, rows, columns // Z), BF), pltpu.SemaphoreType.DMA((Z, X))],
        [VMEM] * (len(layout) + 4),
        [ANY, VMEM],
        flops=4 * rows * rank * columns,
        moved=6 * rows * columns,
    )(*matrices, mine, theirs, terms, inverse)
    return (d_gate, d_up, new_error[None], next_q.T)


def solution(mesh):
    mesh = Mesh(mesh.devices.reshape(mesh.shape["dp"], X, Z, CORES), ("dp",) + PLANE)
    in_specs = (
        P("dp", PLANE),
        P("dp", PLANE),
        P("dp", PLANE),
        P(PLANE, None),
        P("dp", PLANE, None),
        P(PLANE, None),
    )
    out_specs = (P("dp", PLANE), P("dp", PLANE), P("dp", PLANE, None), P(PLANE, None))
    return jax.shard_map(local, mesh=mesh, in_specs=in_specs, out_specs=out_specs, check_vma=False)
```

time: 152 us -> 167 us (1.099)
  local copies, waits for them, and re-layouts: 3.39 us -> 51.4 us
  blocking collectives: 44.9 us -> 15.9 us
  matrix products: 25.7 us -> 0.19 us
  starting transfers between devices: 22.6 us -> 46.9 us
  Pallas kernels: 0 us -> 23.2 us
  waiting for transfers between devices: 29.9 us -> 16.3 us
  between operations: 14.2 us -> 1.14 us
    unnamed x10 -> x79, local copies, waits for them, and re-layouts: 1.78 us -> 47.9 us
    all_to_all x3 -> x1, blocking collectives: 44.9 us -> 15.9 us  [exchange(): return lax.all_to_all(a, axis, 0, 0)]
    dot_general x10 -> x0, matrix products: 25.5 us -> none  [the longest x4 9.63 us: dot(): return jnp.dot(a, b, preferred_element_type=F32)]
    pallas_call x0 -> x10, Pallas kernels: none -> 23.2 us  [the longest x5 14.2 us: add_pieces(): call(functools.partial(piece_kernel, steps), [((rows, columns), F32), ((t...]
    ppermute x1 -> x18, starting transfers between devices: 3.33 us -> 25.6 us  [shift(): return lax.ppermute(a, axis, [(i, (i + step) % n) for i in range(n)])]
    all_to_all x3 -> x4, waiting for transfers between devices: 25 us -> 4.54 us  [exchange(): return lax.all_to_all(a, axis, 0, 0)]
    ppermute x1 -> x18, waiting for transfers between devices: 0.86 us -> 11.8 us  [shift(): return lax.ppermute(a, axis, [(i, (i + step) % n) for i in range(n)])]
    all_gather x1 -> x0, waiting for transfers between devices: 3.38 us -> none  [local(): piece = lax.all_gather(cotangent, PLANE, axis=1, tiled=True)]
  transfers between devices with their start and end apart: 5 -> 22, of which waited for: 4 -> 4; matrix products, arithmetic and copies ran while one was open for 15% -> 13% of each run, Pallas kernels for 0% -> 10%
where the time goes in v3:
time: 167 us; the launch traced here: 165 us
  local copies, waits for them, and re-layouts  51.4 us (31%)
  starting transfers between devices  46.9 us (28%)
  Pallas kernels  23.2 us (14%)
  waiting for transfers between devices  16.3 us (10%)
  blocking collectives  15.9 us (10%)
  other arithmetic  10.1 us (6%)
    unnamed x79, local copies, waits for them, and re-layouts  47.9 us
    ppermute x18, starting transfers between devices, shift(): return lax.ppermute(a, axis, [(i, (i + step) % n) for i in range(n)])  25.6 us
    all_to_all x4, starting transfers between devices, exchange(): return lax.all_to_all(a, axis, 0, 0)  21.3 us
    all_to_all x1, blocking collectives, exchange(): return lax.all_to_all(a, axis, 0, 0)  15.9 us
    pallas_call x5, Pallas kernels, add_pieces(): call(functools.partial(piece_kernel, steps), [((rows, columns), F32), ((t...  14.2 us
    ppermute x18, waiting for transfers between devices, shift(): return lax.ppermute(a, axis, [(i, (i + step) % n) for i in range(n)])  11.8 us
    all_to_all x4, waiting for transfers between devices, exchange(): return lax.all_to_all(a, axis, 0, 0)  4.54 us
    another operation x3, other arithmetic, local(): lower = jnp.linalg.cholesky(gram)  3.59 us
  transfers between devices with their start and end apart: 22, of which 4 were waited for; matrix products, arithmetic and copies ran while one was open for 13% of the time, Pallas kernels for 10%

profile of v3, /device:TPU:1, one launch (start us, length us, event | category | flops | bytes accessed | tf_op | source)
XLA Modules:
  0.0 165.2 jit_solution(3655536711158744315)
XLA Ops:
  0.6 2.0 %copy-done = bf16[1,224,8192]{2,1,0:T(8,128)(2,1)S(1)} copy-done((bf16[1,224,8192]{2,1,0:T(8,128)(2,1)S(1)}, bf16[1,224,8192]{2,1,0:T(8,128)(2,1)}, u32[]{:S(2)}) %copy-start) | copy-done | bytes 3670040
  5.3 1.9 %shard_map.93 = (bf16[224,512]{1,0:T(8,128)(2,1)S(1)}, bf16[1152,128]{1,0:T(8,128)(2,1)S(1)}, bf16[1024,128]{1,0:T(8,128)(2,1)S(1)}) custom-call(bf16[224,512]{1,0:T(8,128)(2,1)S(1)} %bitcast.23, bf16[224,512]{1,0:T(8,128)(2,1)S(1)} %bitcast.24, f32[32,224]{1,0:T(8,128)S(1)} %bitcast.25, bf16[224,8192]{1,0:T(8,128)(2,1)S(1)} %bitcast.17), custom_call_target="tpu_custom_call" | custom-call | flops 234881024 | bytes 3670016 | tf_op jit(solution)/shard_map/pallas_call | solution.py:223
  7.2 3.3 %collective-permute-start = (bf16[1152,128]{1,0:T(8,128)(2,1)S(1)}, bf16[1152,128]{1,0:T(8,128)(2,1)S(1)}, u32[]{:S(2)}, u32[]{:S(2)}) collective-permute-start(bf16[1152,128]{1,0:T(8,128)(2,1)S(1)} %get-tuple-element.32), channel_id=1, source_target_pairs={{0,1},{1,0},{2,3},{3,2},{4,5},{5,4},{6,7},{7,6},{8,9},{9,8},{10,11... | collective-permute-start | bytes 884744 | tf_op jit(solution)/shard_map/ppermute | solution.py:32
  10.5 1.2 collective-permute-done
  12.0 15.9 %all_to_all.25 = bf16[4,896,128]{2,1,0:T(8,128)(2,1)S(1)} all-to-all(bf16[4,896,128]{2,1,0:T(8,128)(2,1)S(1)} %pad_maximum_fusion), channel_id=1, replica_groups=mesh['dp'=4,'x'=4,'z'=8,'core'=2] {'x'}, dimensions={0} | all-to-all | bytes 1835008 | tf_op jit(solution)/shard_map/all_to_all | solution.py:36
  28.9 7.2 %all-to-all-start.1 = ((bf16[8,160,128]{2,1,0:T(8,128)(2,1)}), bf16[8,160,128]{2,1,0:T(8,128)(2,1)S(1)}, u32[]{:S(2)}, u32[]{:S(2)}) async-start(bf16[8,160,128]{2,1,0:T(8,128)(2,1)} %pad_maximum_fusion.1), calls=%async_computation.1 | async-start | bytes 655360 | tf_op jit(solution)/shard_map/all_to_all | solution.py:36
  37.3 2.2 %collective-permute-start.3 = (bf16[4,512,128]{2,1,0:T(8,128)(2,1)S(1)}, bf16[4,512,128]{2,1,0:T(8,128)(2,1)S(1)}, u32[]{:S(2)}, u32[]{:S(2)}) collective-permute-start(bf16[4,512,128]{2,1,0:T(8,128)(2,1)S(1)} %slice.51.refs_0_), channel_id=1, source_target_pairs={{0,1},{1,0},{2,3},{3,2},{4,5},{5,4},{6,7},{7,6},{8,9},{9,8},{10,11... | collective-permute-start | bytes 1572872 | tf_op jit(solution)/shard_map/ppermute | solution.py:32
  39.4 1.8 %collective-permute-start.1 = (bf16[4,512,128]{2,1,0:T(8,128)(2,1)S(1)}, bf16[4,512,128]{2,1,0:T(8,128)(2,1)S(1)}, u32[]{:S(2)}, u32[]{:S(2)}) collective-permute-start(bf16[4,512,128]{2,1,0:T(8,128)(2,1)S(1)} %slice.51.refs_0_), channel_id=1, source_target_pairs={{0,2},{2,4},{4,6},{6,8},{8,10},{10,12},{12,14},{14,0},{1,3},{3,5},... | collective-permute-start | bytes 1572872 | tf_op jit(solution)/shard_map/ppermute | solution.py:32
  41.2 1.2 collective-permute-start.2
  42.5 2.0 %copy-done.1 = bf16[1,224,8192]{2,1,0:T(8,128)(2,1)S(1)} copy-done((bf16[1,224,8192]{2,1,0:T(8,128)(2,1)S(1)}, bf16[1,224,8192]{2,1,0:T(8,128)(2,1)}, u32[]{:S(2)}) %copy-start.1) | copy-done | bytes 3670040
  44.5 2.0 %copy-done.5 = bf16[224,8192]{1,0:T(8,128)(2,1)S(1)} copy-done((bf16[224,8192]{1,0:T(8,128)(2,1)S(1)}, bf16[224,8192]{1,0:T(8,128)(2,1)}, u32[]{:S(2)}) %copy-start.5) | copy-done | bytes 3670040
  48.5 9.3 %collective-permute-done.1.refs_0_ = bf16[4,512,128]{2,1,0:T(8,128)(2,1)S(1)} collective-permute-done((bf16[4,512,128]{2,1,0:T(8,128)(2,1)S(1)}, bf16[4,512,128]{2,1,0:T(8,128)(2,1)S(1)}, u32[]{:S(2)}, u32[]{:S(2)}) %collective-permute-start.1) | collective-permute-done | bytes 524320 | tf_op jit(solution)/shard_map/ppermute | solution.py:32
  57.7 1.2 collective-permute-start.6
  59.9 1.8 %collective-permute-start.5 = (bf16[4,512,128]{2,1,0:T(8,128)(2,1)}, bf16[4,512,128]{2,1,0:T(8,128)(2,1)}, u32[]{:S(2)}, u32[]{:S(2)}) collective-permute-start(bf16[4,512,128]{2,1,0:T(8,128)(2,1)} %collective-permute-done.2.refs_1_), channel_id=1, source_target_pairs={{0,14},{2,0},{4,2},{6,4},{8,6},{10,8},{12,10},{14,12},{1,15},{3,1}... | collective-permute-start | bytes 1572872 | tf_op jit(solution)/shard_map/ppermute | solution.py:32
  62.5 4.2 %all-to-all-start.2 = ((f32[4,32,128]{2,1,0:T(8,128)}), f32[4,32,128]{2,1,0:T(8,128)}, u32[]{:S(2)}, u32[]{:S(2)}) async-start(f32[4,32,128]{2,1,0:T(8,128)} %shard_map.95), calls=%async_computation.2 | async-start | bytes 131072 | tf_op jit(solution)/shard_map/all_to_all | solution.py:36
  68.3 2.0 %copy-done.2 = bf16[1,224,8192]{2,1,0:T(8,128)(2,1)S(1)} copy-done((bf16[1,224,8192]{2,1,0:T(8,128)(2,1)S(1)}, bf16[1,224,8192]{2,1,0:T(8,128)(2,1)}, u32[]{:S(2)}) %copy-start.2) | copy-done | bytes 3670040
  70.3 2.0 %copy-done.6 = bf16[224,8192]{1,0:T(8,128)(2,1)S(1)} copy-done((bf16[224,8192]{1,0:T(8,128)(2,1)S(1)}, bf16[224,8192]{1,0:T(8,128)(2,1)}, u32[]{:S(2)}) %copy-start.6) | copy-done | bytes 3670040
  75.5 3.2 %shard_map.96 = (f32[224,2048]{1,0:T(8,128)S(1)}, f32[512,224]{1,0:T(8,128)S(1)}) custom-call(bf16[4,512,128]{2,1,0:T(8,128)(2,1)S(1)} %collective-permute-done.1.refs_0_, bf16[4,512,128]{2,1,0:T(8,128)(2,1)} %collective-permute-done.2.refs_1_, bf16[4,512,128]{2,1,0:T(8,128)(2,1)S(1)} %copy-done.30, bf16[4,512,128]{2,1,0:T(8,128)(2,1)S(1)} %copy-done.32, ...), custom_call_target="tpu_custom_call" | custom-call | flops 939524096 | bytes 1835008 | tf_op jit(solution)/shard_map/pallas_call | solution.py:149
  79.6 1.3 collective-permute-start.10
  81.0 2.7 %collective-permute-start.9 = (bf16[4,512,128]{2,1,0:T(8,128)(2,1)}, bf16[4,512,128]{2,1,0:T(8,128)(2,1)S(1)}, u32[]{:S(2)}, u32[]{:S(2)}) collective-permute-start(bf16[4,512,128]{2,1,0:T(8,128)(2,1)} %collective-permute-done.5.refs_1_), channel_id=1, source_target_pairs={{0,14},{2,0},{4,2},{6,4},{8,6},{10,8},{12,10},{14,12},{1,15},{3,1}... | collective-permute-start | bytes 1572872 | tf_op jit(solution)/shard_map/ppermute | solution.py:32
  83.7 2.0 %copy-done.3 = bf16[1,224,8192]{2,1,0:T(8,128)(2,1)S(1)} copy-done((bf16[1,224,8192]{2,1,0:T(8,128)(2,1)S(1)}, bf16[1,224,8192]{2,1,0:T(8,128)(2,1)}, u32[]{:S(2)}) %copy-start.3) | copy-done | bytes 3670040
  85.7 2.0 %copy-done.7 = bf16[224,8192]{1,0:T(8,128)(2,1)S(1)} copy-done((bf16[224,8192]{1,0:T(8,128)(2,1)S(1)}, bf16[224,8192]{1,0:T(8,128)(2,1)}, u32[]{:S(2)}) %copy-start.7) | copy-done | bytes 3670040
  88.8 3.4 %shard_map.97 = (f32[224,2048]{1,0:T(8,128)S(1)}, f32[512,224]{1,0:T(8,128)S(1)}) custom-call(bf16[4,512,128]{2,1,0:T(8,128)(2,1)} %collective-permute-done.4.refs_0_, bf16[4,512,128]{2,1,0:T(8,128)(2,1)} %collective-permute-done.5.refs_1_, bf16[4,512,128]{2,1,0:T(8,128)(2,1)S(1)} %collective-permute-done.10.refs_2_, ...), custom_call_target="tpu_custom_call" | custom-call | flops 939524096 | bytes 1835008 | tf_op jit(solution)/shard_map/pallas_call | solution.py:149
  92.2 1.2 copy-done.9
  94.3 1.3 collective-permute-done.8.refs_0_
  97.8 2.7 %collective-permute-start.13 = (bf16[4,256,128]{2,1,0:T(8,128)(2,1)}, bf16[4,256,128]{2,1,0:T(8,128)(2,1)S(1)}, u32[]{:S(2)}, u32[]{:S(2)}) collective-permute-start(bf16[4,256,128]{2,1,0:T(8,128)(2,1)} %slice.45), channel_id=1, source_target_pairs={{0,14},{2,0},{4,2},{6,4},{8,6},{10,8},{12,10},{14,12},{1,15},{3,1}... | collective-permute-start | bytes 786440 | tf_op jit(solution)/shard_map/ppermute | solution.py:32
  100.4 1.6 shard_map.100
  102.0 5.4 %all-to-all-start.3 = ((bf16[32,32,128]{2,1,0:T(8,128)(2,1)}), bf16[32,32,128]{2,1,0:T(8,128)(2,1)S(1)}, u32[]{:S(2)}, u32[]{:S(2)}) async-start(bf16[32,32,128]{2,1,0:T(8,128)(2,1)} %shard_map.100), calls=%async_computation.3 | async-start | bytes 524288 | tf_op jit(solution)/shard_map/all_to_all | solution.py:36
  107.4 2.2 %collective-permute-start.15 = (bf16[4,512,128]{2,1,0:T(8,128)(2,1)}, bf16[4,512,128]{2,1,0:T(8,128)(2,1)}, u32[]{:S(2)}, u32[]{:S(2)}) collective-permute-start(bf16[4,512,128]{2,1,0:T(8,128)(2,1)} %copy-done.16), channel_id=1, source_target_pairs={{0,1},{1,0},{2,3},{3,2},{4,5},{5,4},{6,7},{7,6},{8,9},{9,8},{10,11... | collective-permute-start | bytes 1572872 | tf_op jit(solution)/shard_map/ppermute | solution.py:32
  109.7 1.7 %constant_dynamic-update-slice_fusion.1 = bf16[4,512,128]{2,1,0:T(8,128)(2,1)} fusion(bf16[4,256,128]{2,1,0:T(8,128)(2,1)} %collective-permute-done.12), kind=kLoop, calls=%fused_computation.26 | loop fusion | bytes 524288
  112.5 4.5 %all-to-all-done.3.refs_5_ = bf16[32,32,128]{2,1,0:T(8,128)(2,1)S(1)} async-done(((bf16[32,32,128]{2,1,0:T(8,128)(2,1)}), bf16[32,32,128]{2,1,0:T(8,128)(2,1)S(1)}, u32[]{:S(2)}, u32[]{:S(2)}) %all-to-all-start.3) | async-done | bytes 262176 | tf_op jit(solution)/shard_map/all_to_all | solution.py:36
  117.1 3.7 %collective-permute-start.17 = (bf16[32,32,128]{2,1,0:T(8,128)(2,1)S(1)}, bf16[32,32,128]{2,1,0:T(8,128)(2,1)S(1)}, u32[]{:S(2)}, u32[]{:S(2)}) collective-permute-start(bf16[32,32,128]{2,1,0:T(8,128)(2,1)S(1)} %all-to-all-done.3.refs_5_), channel_id=1, source_target_pairs={{0,1},{1,0},{2,3},{3,2},{4,5},{5,4},{6,7},{7,6},{8,9},{9,8},{10,11... | collective-permute-start | bytes 786440 | tf_op jit(solution)/shard_map/ppermute | solution.py:32
  120.8 1.8 %copy.11 = bf16[512,224]{1,0:T(8,128)(2,1)} copy(bf16[512,224]{0,1:T(8,128)(2,1)} %param.6) | data formatting | bytes 458752 | tf_op args[0]
  122.6 1.8 %copy.10 = bf16[512,224]{1,0:T(8,128)(2,1)} copy(bf16[512,224]{0,1:T(8,128)(2,1)} %param.7) | data formatting | bytes 458752 | tf_op args[1]
  124.3 2.0 %copy-done.4 = bf16[1,224,8192]{2,1,0:T(8,128)(2,1)S(1)} copy-done((bf16[1,224,8192]{2,1,0:T(8,128)(2,1)S(1)}, bf16[1,224,8192]{2,1,0:T(8,128)(2,1)}, u32[]{:S(2)}) %copy-start.4) | copy-done | bytes 3670040
  126.4 2.0 %copy-done.8 = bf16[224,8192]{1,0:T(8,128)(2,1)S(1)} copy-done((bf16[224,8192]{1,0:T(8,128)(2,1)S(1)}, bf16[224,8192]{1,0:T(8,128)(2,1)}, u32[]{:S(2)}) %copy-start.8) | copy-done | bytes 3670040
  131.6 3.4 %shard_map.98 = (f32[224,2048]{1,0:T(8,128)S(1)}, f32[512,224]{1,0:T(8,128)S(1)}) custom-call(bf16[4,512,128]{2,1,0:T(8,128)(2,1)S(1)} %copy-done.17, bf16[4,512,128]{2,1,0:T(8,128)(2,1)S(1)} %copy-done.19, bf16[4,512,128]{2,1,0:T(8,128)(2,1)} %collective-permute-done.15.refs_2_, bf16[4,512,128]{2,1,0:T(8,128)(2,1)} %collective-permute-done.16.refs_3_, ...), custom_call_target="tpu_custom_call" | custom-call | flops 939524096 | bytes 1835008 | tf_op jit(solution)/shard_map/pallas_call | solution.py:149
  135.0 3.0 %shard_map.99 = (f32[224,1024]{1,0:T(8,128)S(1)}, f32[512,224]{1,0:T(8,128)S(1)}) custom-call(bf16[4,512,128]{2,1,0:T(8,128)(2,1)} %constant_dynamic-update-slice_fusion.refs_0_, bf16[4,512,128]{2,1,0:T(8,128)(2,1)} %collective-permute-done.14.refs_1_, bf16[224,512]{1,0:T(8,128)(2,1)S(1)} %get-tuple-element.34.refs_2_.refs_4_, ...), custom_call_target="tpu_custom_call" | custom-call | flops 469762048 | bytes 917504 | tf_op jit(solution)/shard_map/pallas_call | solution.py:149
  138.1 1.3 shard_map.101
  140.0 4.5 %all-to-all-start.4 = ((f32[4,32,224]{2,1,0:T(8,128)}), f32[4,32,224]{2,1,0:T(8,128)S(1)}, u32[]{:S(2)}, u32[]{:S(2)}) async-start(f32[4,32,224]{2,1,0:T(8,128)} %copy-done.34), calls=%async_computation.4 | async-start | bytes 262144 | tf_op jit(solution)/shard_map/all_to_all | solution.py:36
  144.6 2.9 %cholesky.17 = f32[32,32]{1,0:T(8,128)S(1)} custom-call(f32[32,32]{1,0:T(8,128)S(1)} %fusion.11), custom_call_target="Cholesky" | custom-call | tf_op jit(solution)/shard_map/jit(cholesky)/cholesky | solution.py:293
  148.9 2.4 %custom-call.6 = f32[1,32,32]{1,2,0:T(8,128)S(1)} custom-call(f32[1,32,32]{2,1,0:T(8,128)S(1)} %fusion.8), custom_call_target="InvertDiagBlocksLowerTriangular" | custom-call | tf_op jit(solution)/shard_map/triangular_solve | solution.py:294
  151.3 2.3 %fusion.7 = (bf16[512,224]{1,0:T(8,128)(2,1)}, bf16[512,224]{1,0:T(8,128)(2,1)}) fusion(f32[512,224]{1,0:T(8,128)} %copy-done.28, bf16[512,224]{1,0:T(8,128)(2,1)} %copy.11, bf16[512,224]{1,0:T(8,128)(2,1)} %copy.10), kind=kLoop, calls=%fused_computation.11 | loop fusion | flops 1720320 | bytes 1376256 | tf_op jit(solution)/shard_map/convert_element_type | solution.py:301
  153.8 1.8 %copy.13 = bf16[512,224]{0,1:T(8,128)(2,1)} copy(bf16[512,224]{1,0:T(8,128)(2,1)} %get-tuple-element.65) | data formatting | bytes 458752
  155.6 1.8 %copy.14 = bf16[512,224]{0,1:T(8,128)(2,1)} copy(bf16[512,224]{1,0:T(8,128)(2,1)} %get-tuple-element.64) | data formatting | bytes 458752
  157.3 1.5 copy-done.11
  158.8 1.5 copy-done.13
  161.5 3.5 %shard_map.102 = (bf16[224,8192]{1,0:T(8,128)(2,1)}, f32[32,224]{1,0:T(8,128)}) custom-call(f32[224,1024]{1,0:T(8,128)S(1)} %get-tuple-element.50.refs_0_, f32[224,2048]{1,0:T(8,128)S(1)} %get-tuple-element.51.refs_1_, f32[224,2048]{1,0:T(8,128)S(1)} %copy-done.11, f32[224,2048]{1,0:T(8,128)S(1)} %copy-done.13, f32[224,1024]{1,0:T(8,128)S(1)} %copy-done.15, ...), custom_call_target="tpu_custom_call" | custom-call | flops 234881024 | bytes 11010048 | tf_op jit(solution)/shard_map/pallas_call | solution.py:303
  (110 shorter events, 26.2 us)
Async XLA Ops:
  0.6 2.0 %copy-start = (bf16[1,224,8192]{2,1,0:T(8,128)(2,1)S(1)}, bf16[1,224,8192]{2,1,0:T(8,128)(2,1)}, u32[]{:S(2)}) copy-start(bf16[1,224,8192]{2,1,0:T(8,128)(2,1)} %param.10) | copy-start | bytes 11010052
  5.3 6.6 %copy-start.33 = (bf16[512,128]{1,0:T(8,128)(2,1)S(1)}, bf16[512,128]{1,0:T(8,128)(2,1)}, u32[]{:S(2)}) copy-start(bf16[512,128]{1,0:T(8,128)(2,1)} %cotangent_ref.1) | copy-start | bytes 393220
  7.2 4.5 %collective-permute-start = (bf16[1152,128]{1,0:T(8,128)(2,1)S(1)}, bf16[1152,128]{1,0:T(8,128)(2,1)S(1)}, u32[]{:S(2)}, u32[]{:S(2)}) collective-permute-start(bf16[1152,128]{1,0:T(8,128)(2,1)S(1)} %get-tuple-element.32), channel_id=1, source_target_pairs={{0,1},{1,0},{2,3},{3,2},{4,5},{5,4},{6,7},{7,6},{8,9},{9,8},{10,11... | collective-permute-start | bytes 884744 | tf_op jit(solution)/shard_map/ppermute | solution.py:32
  27.9 1.1 copy-start.36
  28.9 28.8 %all-to-all-start.1 = ((bf16[8,160,128]{2,1,0:T(8,128)(2,1)}), bf16[8,160,128]{2,1,0:T(8,128)(2,1)S(1)}, u32[]{:S(2)}, u32[]{:S(2)}) async-start(bf16[8,160,128]{2,1,0:T(8,128)(2,1)} %pad_maximum_fusion.1), calls=%async_computation.1 | async-start | bytes 655360 | tf_op jit(solution)/shard_map/all_to_all | solution.py:36
  37.3 5.1 %collective-permute-start.3 = (bf16[4,512,128]{2,1,0:T(8,128)(2,1)S(1)}, bf16[4,512,128]{2,1,0:T(8,128)(2,1)S(1)}, u32[]{:S(2)}, u32[]{:S(2)}) collective-permute-start(bf16[4,512,128]{2,1,0:T(8,128)(2,1)S(1)} %slice.51.refs_0_), channel_id=1, source_target_pairs={{0,1},{1,0},{2,3},{3,2},{4,5},{5,4},{6,7},{7,6},{8,9},{9,8},{10,11... | collective-permute-start | bytes 1572872 | tf_op jit(solution)/shard_map/ppermute | solution.py:32
  39.4 18.3 %collective-permute-start.1 = (bf16[4,512,128]{2,1,0:T(8,128)(2,1)S(1)}, bf16[4,512,128]{2,1,0:T(8,128)(2,1)S(1)}, u32[]{:S(2)}, u32[]{:S(2)}) collective-permute-start(bf16[4,512,128]{2,1,0:T(8,128)(2,1)S(1)} %slice.51.refs_0_), channel_id=1, source_target_pairs={{0,2},{2,4},{4,6},{6,8},{8,10},{10,12},{12,14},{14,0},{1,3},{3,5},... | collective-permute-start | bytes 1572872 | tf_op jit(solution)/shard_map/ppermute | solution.py:32
  41.2 16.5 %collective-permute-start.2 = (bf16[4,512,128]{2,1,0:T(8,128)(2,1)S(1)}, bf16[4,512,128]{2,1,0:T(8,128)(2,1)}, u32[]{:S(2)}, u32[]{:S(2)}) collective-permute-start(bf16[4,512,128]{2,1,0:T(8,128)(2,1)S(1)} %slice.51.refs_0_), channel_id=1, source_target_pairs={{0,14},{2,0},{4,2},{6,4},{8,6},{10,8},{12,10},{14,12},{1,15},{3,1}... | collective-permute-start | bytes 1572872 | tf_op jit(solution)/shard_map/ppermute | solution.py:32
  42.4 2.0 %copy-start.1 = (bf16[1,224,8192]{2,1,0:T(8,128)(2,1)S(1)}, bf16[1,224,8192]{2,1,0:T(8,128)(2,1)}, u32[]{:S(2)}) copy-start(bf16[1,224,8192]{2,1,0:T(8,128)(2,1)} %param.10) | copy-start | bytes 11010052
  44.5 2.0 %copy-start.5 = (bf16[224,8192]{1,0:T(8,128)(2,1)S(1)}, bf16[224,8192]{1,0:T(8,128)(2,1)}, u32[]{:S(2)}) copy-start(bf16[224,8192]{1,0:T(8,128)(2,1)} %refs_4_.3) | copy-start | bytes 11010052
  57.7 9.0 %collective-permute-start.6 = (bf16[4,512,128]{2,1,0:T(8,128)(2,1)S(1)}, bf16[4,512,128]{2,1,0:T(8,128)(2,1)S(1)}, u32[]{:S(2)}, u32[]{:S(2)}) collective-permute-start(bf16[4,512,128]{2,1,0:T(8,128)(2,1)S(1)} %collective-permute-done.1.refs_0_), channel_id=1, source_target_pairs={{0,1},{1,0},{2,3},{3,2},{4,5},{5,4},{6,7},{7,6},{8,9},{9,8},{10,11... | collective-permute-start | bytes 1572872 | tf_op jit(solution)/shard_map/ppermute | solution.py:32
  59.0 8.5 %collective-permute-start.7 = (bf16[4,512,128]{2,1,0:T(8,128)(2,1)}, bf16[4,512,128]{2,1,0:T(8,128)(2,1)S(1)}, u32[]{:S(2)}, u32[]{:S(2)}) collective-permute-start(bf16[4,512,128]{2,1,0:T(8,128)(2,1)} %collective-permute-done.2.refs_1_), channel_id=1, source_target_pairs={{0,1},{1,0},{2,3},{3,2},{4,5},{5,4},{6,7},{7,6},{8,9},{9,8},{10,11... | collective-permute-start | bytes 1572872 | tf_op jit(solution)/shard_map/ppermute | solution.py:32
  59.1 20.5 %collective-permute-start.4 = (bf16[4,512,128]{2,1,0:T(8,128)(2,1)S(1)}, bf16[4,512,128]{2,1,0:T(8,128)(2,1)}, u32[]{:S(2)}, u32[]{:S(2)}) collective-permute-start(bf16[4,512,128]{2,1,0:T(8,128)(2,1)S(1)} %collective-permute-done.1.refs_0_), channel_id=1, source_target_pairs={{0,2},{2,4},{4,6},{6,8},{8,10},{10,12},{12,14},{14,0},{1,3},{3,5},... | collective-permute-start | bytes 1572872 | tf_op jit(solution)/shard_map/ppermute | solution.py:32
  59.9 19.7 %collective-permute-start.5 = (bf16[4,512,128]{2,1,0:T(8,128)(2,1)}, bf16[4,512,128]{2,1,0:T(8,128)(2,1)}, u32[]{:S(2)}, u32[]{:S(2)}) collective-permute-start(bf16[4,512,128]{2,1,0:T(8,128)(2,1)} %collective-permute-done.2.refs_1_), channel_id=1, source_target_pairs={{0,14},{2,0},{4,2},{6,4},{8,6},{10,8},{12,10},{14,12},{1,15},{3,1}... | collective-permute-start | bytes 1572872 | tf_op jit(solution)/shard_map/ppermute | solution.py:32
  62.5 17.0 %all-to-all-start.2 = ((f32[4,32,128]{2,1,0:T(8,128)}), f32[4,32,128]{2,1,0:T(8,128)}, u32[]{:S(2)}, u32[]{:S(2)}) async-start(f32[4,32,128]{2,1,0:T(8,128)} %shard_map.95), calls=%async_computation.2 | async-start | bytes 131072 | tf_op jit(solution)/shard_map/all_to_all | solution.py:36
  68.3 2.0 %copy-start.2 = (bf16[1,224,8192]{2,1,0:T(8,128)(2,1)S(1)}, bf16[1,224,8192]{2,1,0:T(8,128)(2,1)}, u32[]{:S(2)}) copy-start(bf16[1,224,8192]{2,1,0:T(8,128)(2,1)} %param.10) | copy-start | bytes 11010052
  70.3 2.0 %copy-start.6 = (bf16[224,8192]{1,0:T(8,128)(2,1)S(1)}, bf16[224,8192]{1,0:T(8,128)(2,1)}, u32[]{:S(2)}) copy-start(bf16[224,8192]{1,0:T(8,128)(2,1)} %refs_4_.3) | copy-start | bytes 11010052
  72.4 1.0 copy-start.25
  73.4 1.0 copy-start.30
  74.5 1.0 copy-start.32
  79.6 4.1 %collective-permute-start.10 = (bf16[4,512,128]{2,1,0:T(8,128)(2,1)}, bf16[4,512,128]{2,1,0:T(8,128)(2,1)S(1)}, u32[]{:S(2)}, u32[]{:S(2)}) collective-permute-start(bf16[4,512,128]{2,1,0:T(8,128)(2,1)} %collective-permute-done.4.refs_0_), channel_id=1, source_target_pairs={{0,1},{1,0},{2,3},{3,2},{4,5},{5,4},{6,7},{7,6},{8,9},{9,8},{10,11... | collective-permute-start | bytes 1572872 | tf_op jit(solution)/shard_map/ppermute | solution.py:32
  80.9 2.8 %collective-permute-start.11 = (bf16[4,512,128]{2,1,0:T(8,128)(2,1)}, bf16[4,512,128]{2,1,0:T(8,128)(2,1)S(1)}, u32[]{:S(2)}, u32[]{:S(2)}) collective-permute-start(bf16[4,512,128]{2,1,0:T(8,128)(2,1)} %collective-permute-done.5.refs_1_), channel_id=1, source_target_pairs={{0,1},{1,0},{2,3},{3,2},{4,5},{5,4},{6,7},{7,6},{8,9},{9,8},{10,11... | collective-permute-start | bytes 1572872 | tf_op jit(solution)/shard_map/ppermute | solution.py:32
  81.0 14.5 %collective-permute-start.8 = (bf16[4,512,128]{2,1,0:T(8,128)(2,1)}, bf16[4,512,128]{2,1,0:T(8,128)(2,1)S(1)}, u32[]{:S(2)}, u32[]{:S(2)}) collective-permute-start(bf16[4,512,128]{2,1,0:T(8,128)(2,1)} %collective-permute-done.4.refs_0_), channel_id=1, source_target_pairs={{0,2},{2,4},{4,6},{6,8},{8,10},{10,12},{12,14},{14,0},{1,3},{3,5},... | collective-permute-start | bytes 1572872 | tf_op jit(solution)/shard_map/ppermute | solution.py:32
  81.0 14.5 %collective-permute-start.9 = (bf16[4,512,128]{2,1,0:T(8,128)(2,1)}, bf16[4,512,128]{2,1,0:T(8,128)(2,1)S(1)}, u32[]{:S(2)}, u32[]{:S(2)}) collective-permute-start(bf16[4,512,128]{2,1,0:T(8,128)(2,1)} %collective-permute-done.5.refs_1_), channel_id=1, source_target_pairs={{0,14},{2,0},{4,2},{6,4},{8,6},{10,8},{12,10},{14,12},{1,15},{3,1}... | collective-permute-start | bytes 1572872 | tf_op jit(solution)/shard_map/ppermute | solution.py:32
  83.7 2.0 %copy-start.3 = (bf16[1,224,8192]{2,1,0:T(8,128)(2,1)S(1)}, bf16[1,224,8192]{2,1,0:T(8,128)(2,1)}, u32[]{:S(2)}) copy-start(bf16[1,224,8192]{2,1,0:T(8,128)(2,1)} %param.10) | copy-start | bytes 11010052
  85.7 2.0 %copy-start.7 = (bf16[224,8192]{1,0:T(8,128)(2,1)S(1)}, bf16[224,8192]{1,0:T(8,128)(2,1)}, u32[]{:S(2)}) copy-start(bf16[224,8192]{1,0:T(8,128)(2,1)} %refs_4_.3) | copy-start | bytes 11010052
  87.8 1.0 copy-start.27
  92.2 1.2 copy-start.9
  95.5 1.5 copy-start.18
  97.0 12.6 %collective-permute-start.12 = (bf16[4,256,128]{2,1,0:T(8,128)(2,1)}, bf16[4,256,128]{2,1,0:T(8,128)(2,1)}, u32[]{:S(2)}, u32[]{:S(2)}) collective-permute-start(bf16[4,256,128]{2,1,0:T(8,128)(2,1)} %slice.44), channel_id=1, source_target_pairs={{0,2},{2,4},{4,6},{6,8},{8,10},{10,12},{12,14},{14,0},{1,3},{3,5},... | collective-permute-start | bytes 786440 | tf_op jit(solution)/shard_map/ppermute | solution.py:32
  97.8 13.6 %collective-permute-start.13 = (bf16[4,256,128]{2,1,0:T(8,128)(2,1)}, bf16[4,256,128]{2,1,0:T(8,128)(2,1)S(1)}, u32[]{:S(2)}, u32[]{:S(2)}) collective-permute-start(bf16[4,256,128]{2,1,0:T(8,128)(2,1)} %slice.45), channel_id=1, source_target_pairs={{0,14},{2,0},{4,2},{6,4},{8,6},{10,8},{12,10},{14,12},{1,15},{3,1}... | collective-permute-start | bytes 786440 | tf_op jit(solution)/shard_map/ppermute | solution.py:32
  102.0 15.1 %all-to-all-start.3 = ((bf16[32,32,128]{2,1,0:T(8,128)(2,1)}), bf16[32,32,128]{2,1,0:T(8,128)(2,1)S(1)}, u32[]{:S(2)}, u32[]{:S(2)}) async-start(bf16[32,32,128]{2,1,0:T(8,128)(2,1)} %shard_map.100), calls=%async_computation.3 | async-start | bytes 524288 | tf_op jit(solution)/shard_map/all_to_all | solution.py:36
  107.4 16.9 %collective-permute-start.15 = (bf16[4,512,128]{2,1,0:T(8,128)(2,1)}, bf16[4,512,128]{2,1,0:T(8,128)(2,1)}, u32[]{:S(2)}, u32[]{:S(2)}) collective-permute-start(bf16[4,512,128]{2,1,0:T(8,128)(2,1)} %copy-done.16), channel_id=1, source_target_pairs={{0,1},{1,0},{2,3},{3,2},{4,5},{5,4},{6,7},{7,6},{8,9},{9,8},{10,11... | collective-permute-start | bytes 1572872 | tf_op jit(solution)/shard_map/ppermute | solution.py:32
  109.6 14.8 %collective-permute-start.16 = (bf16[4,512,128]{2,1,0:T(8,128)(2,1)}, bf16[4,512,128]{2,1,0:T(8,128)(2,1)}, u32[]{:S(2)}, u32[]{:S(2)}) collective-permute-start(bf16[4,512,128]{2,1,0:T(8,128)(2,1)} %copy-done.18), channel_id=1, source_target_pairs={{0,1},{1,0},{2,3},{3,2},{4,5},{5,4},{6,7},{7,6},{8,9},{9,8},{10,11... | collective-permute-start | bytes 1572872 | tf_op jit(solution)/shard_map/ppermute | solution.py:32
  112.1 22.8 %collective-permute-start.14 = (bf16[4,512,128]{2,1,0:T(8,128)(2,1)}, bf16[4,512,128]{2,1,0:T(8,128)(2,1)}, u32[]{:S(2)}, u32[]{:S(2)}) collective-permute-start(bf16[4,512,128]{2,1,0:T(8,128)(2,1)} %constant_dynamic-update-slice_fusion.refs_0_), channel_id=1, source_target_pairs={{0,1},{1,0},{2,3},{3,2},{4,5},{5,4},{6,7},{7,6},{8,9},{9,8},{10,11... | collective-permute-start | bytes 1572872 | tf_op jit(solution)/shard_map/ppermute | solution.py:32
  117.1 20.9 %collective-permute-start.17 = (bf16[32,32,128]{2,1,0:T(8,128)(2,1)S(1)}, bf16[32,32,128]{2,1,0:T(8,128)(2,1)S(1)}, u32[]{:S(2)}, u32[]{:S(2)}) collective-permute-start(bf16[32,32,128]{2,1,0:T(8,128)(2,1)S(1)} %all-to-all-done.3.refs_5_), channel_id=1, source_target_pairs={{0,1},{1,0},{2,3},{3,2},{4,5},{5,4},{6,7},{7,6},{8,9},{9,8},{10,11... | collective-permute-start | bytes 786440 | tf_op jit(solution)/shard_map/ppermute | solution.py:32
  124.3 2.0 %copy-start.4 = (bf16[1,224,8192]{2,1,0:T(8,128)(2,1)S(1)}, bf16[1,224,8192]{2,1,0:T(8,128)(2,1)}, u32[]{:S(2)}) copy-start(bf16[1,224,8192]{2,1,0:T(8,128)(2,1)} %param.10) | copy-start | bytes 11010052
  126.4 2.0 %copy-start.8 = (bf16[224,8192]{1,0:T(8,128)(2,1)S(1)}, bf16[224,8192]{1,0:T(8,128)(2,1)}, u32[]{:S(2)}) copy-start(bf16[224,8192]{1,0:T(8,128)(2,1)} %refs_4_.3) | copy-start | bytes 11010052
  128.4 1.0 copy-start.17
  129.5 1.0 copy-start.19
  135.0 3.1 %copy-start.12 = (f32[224,2048]{1,0:T(8,128)}, f32[224,2048]{1,0:T(8,128)S(1)}, u32[]{:S(2)}) copy-start(f32[224,2048]{1,0:T(8,128)S(1)} %get-tuple-element.53.refs_3_) | copy-start | bytes 5505028
  135.0 3.1 %copy-start.10 = (f32[224,2048]{1,0:T(8,128)S(1)}, f32[224,2048]{1,0:T(8,128)}, u32[]{:S(2)}) copy-start(f32[224,2048]{1,0:T(8,128)} %copy-done.9) | copy-start | bytes 5505028
  138.0 1.4 copy-start.14
  138.0 1.4 copy-start.28
  140.0 17.3 %all-to-all-start.4 = ((f32[4,32,224]{2,1,0:T(8,128)}), f32[4,32,224]{2,1,0:T(8,128)S(1)}, u32[]{:S(2)}, u32[]{:S(2)}) async-start(f32[4,32,224]{2,1,0:T(8,128)} %copy-done.34), calls=%async_computation.4 | async-start | bytes 262144 | tf_op jit(solution)/shard_map/all_to_all | solution.py:36
  157.3 1.5 copy-start.11
  158.8 1.5 copy-start.13
  160.3 1.2 copy-start.15
  (11 other events, 9.1 us)

commit v4 on v3

v4 whole, which is shorter than its diff:
```python
import functools

import jax
import jax.numpy as jnp
from jax import lax
from jax.experimental import pallas as pl
from jax.experimental.pallas import tpu as pltpu
from jax.sharding import Mesh, PartitionSpec as P

BF = jnp.bfloat16
F32 = jnp.float32
X, Z, CORES = 4, 8, 2
PLANE = ("x", "z", "core")
LANES = 128
NT = (((1,), (1,)), ((), ()))
TN = (((0,), (0,)), ((), ()))
VMEM = pl.BlockSpec(memory_space=pltpu.VMEM)
HBM = pl.BlockSpec(memory_space=pltpu.HBM)
HIGHEST = lax.Precision.HIGHEST


def dot(a, b):
    return jnp.dot(a, b, preferred_element_type=F32)


def split(a):
    high = a.astype(BF)
    return high, (a - high.astype(F32)).astype(BF)


def shift(a, axis, step, n):
    return lax.ppermute(a, axis, [(i, (i + step) % n) for i in range(n)])


def exchange(a, axis):
    return lax.all_to_all(a, axis, 0, 0)


def call(kernel, out, scratch=(), ins=None, outs=None, flops=0, moved=0, vmem=16):
    outs = outs if outs is not None else [VMEM] * len(out)
    run = pl.pallas_call(
        kernel,
        in_specs=[VMEM if spec is None else spec for spec in ins],
        out_specs=[VMEM if spec is None else spec for spec in outs],
        out_shape=[jax.ShapeDtypeStruct(s, t) if spec is None else spec.memory_space(s, t) for spec, (s, t) in zip(outs, out)],
        scratch_shapes=list(scratch),
        cost_estimate=pl.CostEstimate(flops=flops, bytes_accessed=moved, transcendentals=0),
        compiler_params=pltpu.CompilerParams(vmem_limit_bytes=vmem << 20),
    )

    def placed(a, spec):
        return a if spec is None else pltpu.with_memory_space_constraint(a, spec.memory_space)

    return lambda *args: run(*(placed(a, spec) for a, spec in zip(args, ins)))


def back(axis, step, n):
    return lax.rem(lax.axis_index(axis) + (n - step), n)


def column(step, hop, wide):
    chip = back("x", hop, X) * Z + back("z", step, Z)
    return pl.multiple_of(chip * (CORES * wide), CORES * wide)


def fetch(source, target, sem):
    copy = pltpu.make_async_copy(source, target, sem)
    copy.start()
    return copy


def start_kernel(gate_hbm, up_hbm, q_hbm, error_ref, hidden_ref, send_ref, mine_ref, gate_ref, up_ref, q_ref, error_buf, sems):
    rank = q_ref.shape[0]
    columns = error_ref.shape[1] // X
    small = [fetch(a, b, sems.at[X + i]) for i, (a, b) in enumerate(((gate_hbm, gate_ref), (up_hbm, up_ref), (q_hbm, q_ref)))]
    copies = [fetch(error_ref.at[:, pl.ds(x * columns, columns)], error_buf.at[x], sems.at[x]) for x in range(X)]
    for copy in small:
        copy.wait()
    gate = gate_ref[...].astype(F32)
    hidden = (gate * jax.nn.sigmoid(gate) * up_ref[...].astype(F32)).astype(BF)
    hidden_ref[...] = hidden
    high, low = split(q_ref[...])
    both = jnp.concatenate([high, low], axis=0)
    left = dot(both, hidden)
    left = (left[:rank] + left[rank:]).astype(BF)
    blocks = left.shape[1] // LANES
    for b in range(blocks):
        send_ref[b * rank:(b + 1) * rank, :] = left[:, b * LANES:(b + 1) * LANES]
    first = lax.axis_index("core") == 0
    for x in range(X):
        copies[x].wait()
        term = dot(both, error_buf[x])
        term = (term[:rank] + term[rank:]).astype(BF)
        for z in range(Z):
            at = (x * Z + z) * rank
            zero = term[:, (2 * z) * LANES:(2 * z + 1) * LANES]
            one = term[:, (2 * z + 1) * LANES:(2 * z + 2) * LANES]
            mine_ref[at:at + rank, :] = jnp.where(first, zero, one)
            at += blocks * rank
            send_ref[at:at + rank, :] = jnp.where(first, one, zero)


def pack_kernel(send_ref, theirs_ref, mine_ref, out_ref):
    tiles = send_ref.shape[0] - mine_ref.shape[0]
    left = (send_ref[:tiles, :].astype(F32) + theirs_ref[:tiles, :].astype(F32)).astype(BF)
    part = (mine_ref[...].astype(F32) + theirs_ref[tiles:, :].astype(F32)).astype(BF)
    size = part.shape[0] // X
    for x in range(X):
        out_ref[x, :tiles, :] = left
        out_ref[x, tiles:, :] = part[x * size:(x + 1) * size]


def repack_kernel(terms_ref, out_ref):
    total = terms_ref[0].astype(F32)
    for x in range(1, X):
        total = total + terms_ref[x].astype(F32)
    total = total.astype(BF)
    rank = (terms_ref.shape[1] - out_ref.shape[1]) // (Z - 1)
    tiles = out_ref.shape[1] - rank
    for z in range(Z):
        out_ref[z, :tiles, :] = total[:tiles]
        out_ref[z, tiles:, :] = total[tiles + z * rank:tiles + (z + 1) * rank]


def slice_kernel(groups, terms_ref, cotangent_ref, out_ref):
    rank = out_ref.shape[1]
    terms = terms_ref[0].astype(F32)
    for i in range(1, Z):
        terms = terms + terms_ref[i].astype(F32)
    blocks = cotangent_ref.shape[0] // LANES
    total = terms[blocks * rank:]
    for b in range(blocks):
        total = total + dot(terms[b * rank:(b + 1) * rank].astype(BF), cotangent_ref[b * LANES:(b + 1) * LANES, :])
    total = total / groups
    for g in range(groups):
        out_ref[g] = total


def spread_kernel(terms_ref, out_ref):
    total = terms_ref[0]
    for g in range(1, terms_ref.shape[0]):
        total = total + terms_ref[g]
    total = total.astype(BF)
    for i in range(out_ref.shape[0]):
        out_ref[i] = total


def piece_kernel(steps, last, *refs):
    n = len(steps)
    own, other = refs[:n], refs[n:2 * n]
    refs = refs[2 * n:]
    hidden_ref, error_ref, weight_ref, d_in = refs[:4]
    refs = refs[4:]
    if last:
        gate_hbm, up_hbm, matrix_ref, d_gate_ref, d_up_ref, error_buf, weight_buf, sems, gate_ref, up_ref, pair_sems = refs
        pair = [fetch(gate_hbm, gate_ref, pair_sems.at[0]), fetch(up_hbm, up_ref, pair_sems.at[1])]
    else:
        matrix_ref, d_ref, error_buf, weight_buf, sems = refs
    wide = own[0].shape[2]
    width = CORES * wide
    first = lax.axis_index("core") == 0
    copies = []
    for i, step in enumerate(steps):
        for hop in range(X):
            at = column(step, hop, wide)
            b = i * X + hop
            for k, (source, target) in enumerate(((error_ref, error_buf), (weight_ref, weight_buf))):
                copies.append(fetch(source.at[:, pl.ds(at, width)], target.at[:, pl.ds(b * width, width)], sems.at[k, b]))
    hidden = hidden_ref[...]
    total = d_in[...]
    for i in range(n):
        blocks = []
        for hop in range(X):
            a, b = own[i][hop], other[i][hop]
            blocks += [jnp.where(first, a, b), jnp.where(first, b, a)]
        for copy in copies[2 * X * i:2 * X * (i + 1)]:
            copy.wait()
        block = jnp.concatenate(blocks, axis=1)
        span = slice(i * X * width, (i + 1) * X * width)
        matrix_ref[:, span] = error_buf[:, span].astype(F32) + dot(hidden, block)
        total = total + lax.dot_general(block, weight_buf[:, span], NT, preferred_element_type=F32)
    if not last:
        d_ref[...] = total
        return
    for copy in pair:
        copy.wait()
    total = total.T
    gate = gate_ref[...].astype(F32)
    sigma = jax.nn.sigmoid(gate)
    d_gate_ref[...] = (total * up_ref[...].astype(F32) * sigma * (1.0 + gate * (1.0 - sigma))).astype(BF)
    d_up_ref[...] = (total * (gate * sigma)).astype(BF)


def add_pieces(steps, own, other, hidden, error, weight, d_hidden, gate=None, upward=None):
    n = len(steps)
    tokens, wide = own[0].shape[1:]
    rows = hidden.shape[0]
    columns = n * X * CORES * wide
    last = gate is not None
    scratch = [pltpu.VMEM((rows, columns), BF), pltpu.VMEM((rows, columns), BF), pltpu.SemaphoreType.DMA((2, n * X))]
    if last:
        scratch += [pltpu.VMEM((rows, tokens), BF), pltpu.VMEM((rows, tokens), BF), pltpu.SemaphoreType.DMA((2,))]
    return call(
        functools.partial(piece_kernel, steps, last),
        [((rows, columns), F32)] + ([((rows, tokens), BF)] * 2 if last else [((tokens, rows), F32)]),
        scratch,
        [VMEM] * (2 * n + 1) + [HBM, HBM, VMEM] + [HBM, HBM] * last,
        [VMEM, None, None] if last else None,
        flops=4 * rows * tokens * columns,
        moved=4 * rows * columns,
    )(*own, *other, hidden, error, weight, d_hidden, *([gate, upward] if last else []))


def basis_block(first, step, hop, mine_ref, theirs_ref):
    at = back("x", hop, X) * Z + back("z", step, Z)
    a, b = mine_ref[at], theirs_ref[at]
    return jnp.concatenate([jnp.where(first, a, b), jnp.where(first, b, a)], axis=1)


def turn_kernel(layout, groups, *refs):
    n = len(layout)
    mine_ref, theirs_ref, out_ref, gram_ref = refs[n:]
    first = lax.axis_index("core") == 0
    total, gram = 0.0, 0.0
    for matrix_ref, steps in zip(refs[:n], layout):
        for i, step in enumerate(steps):
            basis = jnp.concatenate([basis_block(first, step, hop, mine_ref, theirs_ref) for hop in range(X)], axis=1)
            span = slice(i * basis.shape[1], (i + 1) * basis.shape[1])
            total = total + lax.dot_general(matrix_ref[:, span].astype(BF), basis, NT, preferred_element_type=F32)
            gram = gram + lax.dot_general(basis, basis, NT, preferred_element_type=F32)
    gram_ref[...] = gram
    total = total.T
    for g in range(groups):
        out_ref[g] = total


def inverse_kernel(gram_ref, out_ref):
    n = gram_ref.shape[0]
    row = lax.broadcasted_iota(jnp.int32, (n, 2 * n), 0)
    col = lax.broadcasted_iota(jnp.int32, (n, 2 * n), 1)
    both = jnp.concatenate([gram_ref[...], jnp.zeros((n, n), F32)], axis=1) + jnp.where(col == row + n, 1.0, 0.0)
    for k in range(n):
        pivot = both[k:k + 1, k:k + 1]
        scaled = both[k:k + 1, :] * lax.rsqrt(pivot)
        column_k = both[:, k:k + 1] * lax.rsqrt(pivot)
        both = jnp.where(row > k, both - column_k * scaled, jnp.where(row == k, scaled, both))
    out_ref[...] = both[:, n:]


def final_kernel(layout, groups, *refs):
    n = len(layout)
    mine_ref, theirs_ref, terms_ref, inverse_ref, out_ref, q_ref, buf, sems = refs[n:]
    wide = mine_ref.shape[2]
    width = CORES * wide
    first = lax.axis_index("core") == 0
    total = terms_ref[0]
    for g in range(1, groups):
        total = total + terms_ref[g]
    inverse = inverse_ref[...]
    next_q = jnp.dot(inverse, total / groups, precision=HIGHEST, preferred_element_type=F32)
    q_ref[...] = next_q
    factor = lax.dot_general(inverse, next_q, TN, precision=HIGHEST, preferred_element_type=F32)
    high, low = split(factor.T)
    factor = jnp.concatenate([high, low], axis=1)
    copies = []
    for matrix_ref, steps in zip(refs[:n], layout):
        for i, step in enumerate(steps):
            basis = jnp.concatenate([basis_block(first, step, hop, mine_ref, theirs_ref) for hop in range(X)], axis=1)
            basis = jnp.concatenate([basis, basis], axis=0)
            span = slice(i * X * width, (i + 1) * X * width)
            buf[step] = (matrix_ref[:, span] - dot(factor, basis)).astype(BF)
            for x in range(X):
                at = column(step, x, wide)
                copies.append(fetch(buf.at[step, :, pl.ds(x * width, width)], out_ref.at[:, pl.ds(at, width)], sems.at[step, x]))
    for copy in copies:
        copy.wait()


def local(gate, upward, cotangent, down_weight, error_buffer, start_q):
    groups = lax.axis_size("dp")
    rank = start_q.shape[1]
    tokens, wide = cotangent.shape
    error = error_buffer[0]
    rows, columns = error.shape
    tiles = tokens // LANES * rank

    blocks = [cotangent] + [shift(cotangent, "x", hop, X) for hop in range(1, X)]
    pieces, others = {0: jnp.stack(blocks)}, {}

    hidden, send, mine = call(
        start_kernel,
        [((rows, tokens), BF), ((tiles + X * Z * rank, wide), BF), ((X * Z * rank, wide), BF)],
        [
            pltpu.VMEM((rows, tokens), BF),
            pltpu.VMEM((rows, tokens), BF),
            pltpu.VMEM((rank, rows), F32),
            pltpu.VMEM((X, rows, columns // X), BF),
            pltpu.SemaphoreType.DMA((X + 3,)),
        ],
        [HBM, HBM, HBM, HBM],
        flops=4 * rows * rank * columns,
        moved=2 * rows * columns,
    )(gate.T, upward.T, start_q.T, error)
    theirs = shift(send, "core", 1, CORES)
    terms, = call(pack_kernel, [((X, tiles + Z * rank, wide), BF)], ins=[VMEM] * 3)(send, theirs, mine)

    def ring(step):
        pieces[step] = shift(pieces[step - 1], "z", 1, Z)
        pieces[Z - step] = shift(pieces[(Z - step + 1) % Z], "z", Z - 1, Z)

    def swap(*steps):
        for step in steps:
            others[step] = shift(pieces[step], "core", 1, CORES)

    matrices, layout = [], []

    def use(steps, d_hidden, *more):
        matrix, *rest = add_pieces(steps, [pieces[s] for s in steps], [others[s] for s in steps], hidden, error, down_weight, d_hidden, *more)
        matrices.append(matrix)
        layout.append(steps)
        return rest if more else rest[0]

    d_hidden = jnp.zeros((tokens, rows), F32)
    ring(1)
    swap(0)
    terms = exchange(terms, "x")
    terms, pieces[1], pieces[7] = lax.optimization_barrier((terms, pieces[1], pieces[7]))
    ring(2)
    swap(1, 7)
    terms, = call(repack_kernel, [((Z, tiles + rank, wide), BF)], ins=[VMEM])(terms)
    terms = exchange(terms, "z")
    d_hidden = use((0,), d_hidden)
    terms, pieces[2], pieces[6], d_hidden = lax.optimization_barrier((terms, pieces[2], pieces[6], d_hidden))
    ring(3)
    swap(2, 6)
    terms, = call(functools.partial(slice_kernel, groups), [((groups, rank, wide), F32)], ins=[VMEM, None])(terms, cotangent)
    terms = exchange(terms, "dp")
    d_hidden = use((1, 7), d_hidden)
    terms, pieces[3], pieces[5], d_hidden = lax.optimization_barrier((terms, pieces[3], pieces[5], d_hidden))
    half = tokens // 2
    up = shift(pieces[3][:, :half], "z", 1, Z)
    down = shift(pieces[5][:, half:], "z", Z - 1, Z)
    swap(3, 5)
    mine, = call(spread_kernel, [((X * Z, rank, wide), BF)], ins=[VMEM])(terms)
    mine = exchange(mine, ("x", "z"))
    d_hidden = use((2, 6), d_hidden)
    pieces[4] = jnp.concatenate([up, down], axis=1)
    swap(4)
    mine, d_hidden = lax.optimization_barrier((mine, d_hidden))
    theirs = shift(mine, "core", 1, CORES)
    d_hidden = use((3, 5), d_hidden)
    d_gate, d_up = use((4,), d_hidden, gate.T, upward.T)

    terms, gram = call(
        functools.partial(turn_kernel, tuple(layout), groups),
        [((groups, rank, rows), F32), ((rank, rank), F32)],
        ins=[VMEM] * (len(layout) + 2),
        flops=2 * rows * rank * columns,
        moved=4 * rows * columns,
    )(*matrices, mine, theirs)
    terms = exchange(terms, "dp")
    inverse, = call(inverse_kernel, [((rank, rank), F32)], ins=[VMEM])(gram)

    new_error, next_q = call(
        functools.partial(final_kernel, tuple(layout), groups),
        [((rows, columns), BF), ((rank, rows), F32)],
        [pltpu.VMEM((Z, rows, columns // Z), BF), pltpu.SemaphoreType.DMA((Z, X))],
        [VMEM] * (len(layout) + 4),
        [HBM, None],
        flops=4 * rows * rank * columns,
        moved=6 * rows * columns,
    )(*matrices, mine, theirs, terms, inverse)
    return (d_gate.T, d_up.T, new_error[None], next_q.T)


def solution(mesh):
    mesh = Mesh(mesh.devices.reshape(mesh.shape["dp"], X, Z, CORES), ("dp",) + PLANE)
    in_specs = (
        P("dp", PLANE),
        P("dp", PLANE),
        P("dp", PLANE),
        P(PLANE, None),
        P("dp", PLANE, None),
        P(PLANE, None),
    )
    out_specs = (P("dp", PLANE), P("dp", PLANE), P("dp", PLANE, None), P(PLANE, None))
    return jax.shard_map(local, mesh=mesh, in_specs=in_specs, out_specs=out_specs, check_vma=False)
```

time: 167 us -> 134 us (0.80)
  local copies, waits for them, and re-layouts: 51.4 us -> 21.9 us
  Pallas kernels: 23.2 us -> 33.5 us
  other arithmetic: 10.1 us -> 0.07 us
  blocking collectives: 15.9 us -> 9.46 us
  waiting for transfers between devices: 16.3 us -> 19 us
    unnamed x79 -> x45, local copies, waits for them, and re-layouts: 47.9 us -> 17.6 us
    pallas_call x10 -> x13, Pallas kernels: 23.2 us -> 33.5 us  [call(): return lambda *args: run(*(placed(a, spec) for a, spec in zip(args, ins)))]
    another operation x5 -> x1, other arithmetic: 6.68 us -> 0.07 us  [local(): pieces, others = ({0: jnp.stack(blocks)}, {})]
    all_to_all x1, blocking collectives: 15.9 us -> 9.46 us  [exchange(): return lax.all_to_all(a, axis, 0, 0)]
    ppermute x18 -> x21, waiting for transfers between devices: 11.8 us -> 16.7 us  [shift(): return lax.ppermute(a, axis, [(i, (i + step) % n) for i in range(n)])]
    ppermute x18 -> x21, starting transfers between devices: 25.6 us -> 29.4 us  [shift(): return lax.ppermute(a, axis, [(i, (i + step) % n) for i in range(n)])]
    all_to_all x4, starting transfers between devices: 21.3 us -> 18.4 us  [exchange(): return lax.all_to_all(a, axis, 0, 0)]
    convert_element_type x3 -> x0, other arithmetic: 2.37 us -> none  [the longest x1 2.29 us: local(): d_up = (d_hidden * (gate_f * sigma)).astype(BF).T]
  transfers between devices with their start and end apart: 22 -> 25, of which waited for: 4 -> 5; matrix products, arithmetic and copies ran while one was open for 13% -> 3% of each run, Pallas kernels for 10% -> 21%
where the time goes in v4:
time: 134 us; the launch traced here: 133 us
  starting transfers between devices  47.8 us (36%)
  Pallas kernels  33.5 us (25%)
  local copies, waits for them, and re-layouts  21.9 us (16%)
  waiting for transfers between devices  19 us (14%)
  blocking collectives  9.46 us (7%)
    pallas_call x13, Pallas kernels, call(): return lambda *args: run(*(placed(a, spec) for a, spec in zip(args, ins)))  33.5 us
    ppermute x21, starting transfers between devices, shift(): return lax.ppermute(a, axis, [(i, (i + step) % n) for i in range(n)])  29.4 us
    all_to_all x4, starting transfers between devices, exchange(): return lax.all_to_all(a, axis, 0, 0)  18.4 us
    unnamed x45, local copies, waits for them, and re-layouts  17.6 us
    ppermute x21, waiting for transfers between devices, shift(): return lax.ppermute(a, axis, [(i, (i + step) % n) for i in range(n)])  16.7 us
    all_to_all x1, blocking collectives, exchange(): return lax.all_to_all(a, axis, 0, 0)  9.46 us
  transfers between devices with their start and end apart: 25, of which 5 were waited for; matrix products, arithmetic and copies ran while one was open for 3% of the time, Pallas kernels for 21%

profile of v4, /device:TPU:1, one launch (start us, length us, event | category | flops | bytes accessed | tf_op | source)
XLA Modules:
  0.0 132.8 jit_solution(15519392308262983145)
XLA Ops:
  0.6 3.7 %collective-permute-start.2 = (bf16[512,128]{1,0:T(8,128)(2,1)}, bf16[512,128]{1,0:T(8,128)(2,1)S(1)}, u32[]{:S(2)}, u32[]{:S(2)}) collective-permute-start(bf16[512,128]{1,0:T(8,128)(2,1)} %cotangent_ref.1), channel_id=1, source_target_pairs={{0,32},{16,48},{32,0},{48,16},{1,33},{17,49},{33,1},{49,17},{2,34}... | collective-permute-start | bytes 393224 | tf_op jit(solution)/shard_map/ppermute | solution.py:32
  4.6 2.4 %collective-permute-start.3 = (bf16[512,128]{1,0:T(8,128)(2,1)}, bf16[512,128]{1,0:T(8,128)(2,1)S(1)}, u32[]{:S(2)}, u32[]{:S(2)}) collective-permute-start(bf16[512,128]{1,0:T(8,128)(2,1)} %cotangent_ref.1), channel_id=1, source_target_pairs={{0,48},{16,0},{32,16},{48,32},{1,49},{17,1},{33,17},{49,33},{2,50}... | collective-permute-start | bytes 393224 | tf_op jit(solution)/shard_map/ppermute | solution.py:32
  7.0 2.7 %shard_map.93 = (bf16[224,512]{1,0:T(8,128)(2,1)S(1)}, bf16[1152,128]{1,0:T(8,128)(2,1)S(1)}, bf16[1024,128]{1,0:T(8,128)(2,1)S(1)}) custom-call(bf16[224,512]{1,0:T(8,128)(2,1)} %bitcast.19, bf16[224,512]{1,0:T(8,128)(2,1)} %bitcast.21, f32[32,224]{1,0:T(8,128)} %bitcast.26, bf16[224,8192]{1,0:T(8,128)(2,1)} %bitcast.13), custom_call_target="tpu_custom_call" | custom-call | flops 234881024 | bytes 3670016 | tf_op jit(solution)/shard_map/pallas_call | solution.py:54
  9.7 1.6 %collective-permute-start = (bf16[1152,128]{1,0:T(8,128)(2,1)S(1)}, bf16[1152,128]{1,0:T(8,128)(2,1)S(1)}, u32[]{:S(2)}, u32[]{:S(2)}) collective-permute-start(bf16[1152,128]{1,0:T(8,128)(2,1)S(1)} %get-tuple-element.35.send_ref), channel_id=1, source_target_pairs={{0,1},{1,0},{2,3},{3,2},{4,5},{5,4},{6,7},{7,6},{8,9},{9,8},{10,11... | collective-permute-start | bytes 884744 | tf_op jit(solution)/shard_map/ppermute | solution.py:32
  11.8 5.2 %collective-permute-start.5 = (bf16[4,512,128]{2,1,0:T(8,128)(2,1)S(1)}, bf16[4,512,128]{2,1,0:T(8,128)(2,1)S(1)}, u32[]{:S(2)}, u32[]{:S(2)}) collective-permute-start(bf16[4,512,128]{2,1,0:T(8,128)(2,1)S(1)} %pad_maximum_fusion.refs_0_), channel_id=1, source_target_pairs={{0,14},{2,0},{4,2},{6,4},{8,6},{10,8},{12,10},{14,12},{1,15},{3,1}... | collective-permute-start | bytes 1572872 | tf_op jit(solution)/shard_map/ppermute | solution.py:32
  17.1 9.5 %all_to_all.25.terms_ref = bf16[4,384,128]{2,1,0:T(8,128)(2,1)S(1)} all-to-all(bf16[4,384,128]{2,1,0:T(8,128)(2,1)S(1)} %shard_map.94), channel_id=1, replica_groups=mesh['dp'=4,'x'=4,'z'=8,'core'=2] {'x'}, dimensions={0} | all-to-all | bytes 786432 | tf_op jit(solution)/shard_map/all_to_all | solution.py:36
  27.2 3.2 %collective-permute-done.4.refs_0_ = bf16[4,512,128]{2,1,0:T(8,128)(2,1)} collective-permute-done((bf16[4,512,128]{2,1,0:T(8,128)(2,1)S(1)}, bf16[4,512,128]{2,1,0:T(8,128)(2,1)}, u32[]{:S(2)}, u32[]{:S(2)}) %collective-permute-start.4) | collective-permute-done | bytes 524320 | tf_op jit(solution)/shard_map/ppermute | solution.py:32
  30.4 0.8 shard_map.95
  31.2 3.4 %all-to-all-start.1 = ((bf16[8,160,128]{2,1,0:T(8,128)(2,1)}), bf16[8,160,128]{2,1,0:T(8,128)(2,1)S(1)}, u32[]{:S(2)}, u32[]{:S(2)}) async-start(bf16[8,160,128]{2,1,0:T(8,128)(2,1)} %shard_map.95), calls=%async_computation.1 | async-start | bytes 655360 | tf_op jit(solution)/shard_map/all_to_all | solution.py:36
  34.7 2.3 %collective-permute-start.8 = (bf16[4,512,128]{2,1,0:T(8,128)(2,1)S(1)}, bf16[4,512,128]{2,1,0:T(8,128)(2,1)S(1)}, u32[]{:S(2)}, u32[]{:S(2)}) collective-permute-start(bf16[4,512,128]{2,1,0:T(8,128)(2,1)S(1)} %pad_maximum_fusion.refs_0_), channel_id=1, source_target_pairs={{0,1},{1,0},{2,3},{3,2},{4,5},{5,4},{6,7},{7,6},{8,9},{9,8},{10,11... | collective-permute-start | bytes 1572872 | tf_op jit(solution)/shard_map/ppermute | solution.py:32
  37.0 1.6 %collective-permute-start.6 = (bf16[4,512,128]{2,1,0:T(8,128)(2,1)}, bf16[4,512,128]{2,1,0:T(8,128)(2,1)}, u32[]{:S(2)}, u32[]{:S(2)}) collective-permute-start(bf16[4,512,128]{2,1,0:T(8,128)(2,1)} %collective-permute-done.4.refs_0_), channel_id=1, source_target_pairs={{0,2},{2,4},{4,6},{6,8},{8,10},{10,12},{12,14},{14,0},{1,3},{3,5},... | collective-permute-start | bytes 1572872 | tf_op jit(solution)/shard_map/ppermute | solution.py:32
  38.6 1.3 collective-permute-start.7
  40.4 2.1 %shard_map.96 = (f32[224,1024]{1,0:T(8,128)S(1)}, f32[512,224]{1,0:T(8,128)S(1)}) custom-call(bf16[4,512,128]{2,1,0:T(8,128)(2,1)S(1)} %pad_maximum_fusion.refs_0_, bf16[4,512,128]{2,1,0:T(8,128)(2,1)S(1)} %collective-permute-done.8.refs_1_, bf16[224,512]{1,0:T(8,128)(2,1)S(1)} %get-tuple-element.40.refs_2_.refs_4_, bf16[224,8192]{1,0:T(8,128)(2,1)} %bitcast.14, ...), custom_call_target="tpu_custom_call" | custom-call | flops 469762048 | bytes 917504 | tf_op jit(solution)/shard_map/pallas_call | solution.py:54
  43.3 12.3 %collective-permute-done.6.refs_0_ = bf16[4,512,128]{2,1,0:T(8,128)(2,1)} collective-permute-done((bf16[4,512,128]{2,1,0:T(8,128)(2,1)}, bf16[4,512,128]{2,1,0:T(8,128)(2,1)}, u32[]{:S(2)}, u32[]{:S(2)}) %collective-permute-start.6) | collective-permute-done | bytes 524320 | tf_op jit(solution)/shard_map/ppermute | solution.py:32
  55.7 1.0 collective-permute-start.9
  56.6 1.7 %collective-permute-start.10 = (bf16[4,512,128]{2,1,0:T(8,128)(2,1)}, bf16[4,512,128]{2,1,0:T(8,128)(2,1)S(1)}, u32[]{:S(2)}, u32[]{:S(2)}) collective-permute-start(bf16[4,512,128]{2,1,0:T(8,128)(2,1)} %collective-permute-done.7.refs_1_), channel_id=1, source_target_pairs={{0,14},{2,0},{4,2},{6,4},{8,6},{10,8},{12,10},{14,12},{1,15},{3,1}... | collective-permute-start | bytes 1572872 | tf_op jit(solution)/shard_map/ppermute | solution.py:32
  58.3 0.8 shard_map.97
  59.1 4.2 %all-to-all-start.2 = ((f32[4,32,128]{2,1,0:T(8,128)}), f32[4,32,128]{2,1,0:T(8,128)}, u32[]{:S(2)}, u32[]{:S(2)}) async-start(f32[4,32,128]{2,1,0:T(8,128)} %shard_map.97), calls=%async_computation.2 | async-start | bytes 131072 | tf_op jit(solution)/shard_map/all_to_all | solution.py:36
  63.3 1.0 copy-done.13
  64.4 1.0 copy-done.17
  65.4 4.5 %shard_map.98 = (f32[224,2048]{1,0:T(8,128)S(1)}, f32[512,224]{1,0:T(8,128)S(1)}) custom-call(bf16[4,512,128]{2,1,0:T(8,128)(2,1)} %collective-permute-done.4.refs_0_, bf16[4,512,128]{2,1,0:T(8,128)(2,1)S(1)} %copy-done.13, bf16[4,512,128]{2,1,0:T(8,128)(2,1)} %collective-permute-done.11.refs_2_, bf16[4,512,128]{2,1,0:T(8,128)(2,1)} %collective-permute-done.12.refs_3_, ...), custom_call_target="tpu_custom_call" | custom-call | flops 939524096 | bytes 1835008 | tf_op jit(solution)/shard_map/pallas_call | solution.py:54
  69.9 0.8 copy-done.14
  70.7 1.9 %slice.6 = bf16[4,256,128]{2,1,0:T(8,128)(2,1)} slice(bf16[4,512,128]{2,1,0:T(8,128)(2,1)} %collective-permute-done.9.refs_0_), slice={[0:4], [0:256], [0:128]} | slice | bytes 524288 | tf_op jit(solution)/shard_map/slice | solution.py:341
  72.6 1.1 collective-permute-start.13
  74.4 1.6 %collective-permute-start.14 = (bf16[4,256,128]{2,1,0:T(8,128)(2,1)}, bf16[4,256,128]{2,1,0:T(8,128)(2,1)}, u32[]{:S(2)}, u32[]{:S(2)}) collective-permute-start(bf16[4,256,128]{2,1,0:T(8,128)(2,1)} %slice.7), channel_id=1, source_target_pairs={{0,14},{2,0},{4,2},{6,4},{8,6},{10,8},{12,10},{14,12},{1,15},{3,1}... | collective-permute-start | bytes 786440 | tf_op jit(solution)/shard_map/ppermute | solution.py:32
  76.0 3.2 %collective-permute-start.18 = (bf16[4,512,128]{2,1,0:T(8,128)(2,1)}, bf16[4,512,128]{2,1,0:T(8,128)(2,1)}, u32[]{:S(2)}, u32[]{:S(2)}) collective-permute-start(bf16[4,512,128]{2,1,0:T(8,128)(2,1)} %collective-permute-done.6.refs_0_), channel_id=1, source_target_pairs={{0,1},{1,0},{2,3},{3,2},{4,5},{5,4},{6,7},{7,6},{8,9},{9,8},{10,11... | collective-permute-start | bytes 1572872 | tf_op jit(solution)/shard_map/ppermute | solution.py:32
  79.7 0.9 shard_map.99
  81.3 6.2 %all-to-all-start.3 = ((bf16[32,32,128]{2,1,0:T(8,128)(2,1)}), bf16[32,32,128]{2,1,0:T(8,128)(2,1)S(1)}, u32[]{:S(2)}, u32[]{:S(2)}) async-start(bf16[32,32,128]{2,1,0:T(8,128)(2,1)} %copy-done.9), calls=%async_computation.3 | async-start | bytes 524288 | tf_op jit(solution)/shard_map/all_to_all | solution.py:36
  87.9 1.7 %constant_dynamic-update-slice_fusion.1 = bf16[4,512,128]{2,1,0:T(8,128)(2,1)} fusion(bf16[4,256,128]{2,1,0:T(8,128)(2,1)} %collective-permute-done.13), kind=kLoop, calls=%fused_computation.2 | loop fusion | bytes 524288
  89.6 1.7 %constant_dynamic-update-slice_fusion.refs_0_ = bf16[4,512,128]{2,1,0:T(8,128)(2,1)} fusion(bf16[4,512,128]{2,1,0:T(8,128)(2,1)} %constant_dynamic-update-slice_fusion.1, bf16[4,256,128]{2,1,0:T(8,128)(2,1)} %collective-permute-done.14), kind=kLoop, calls=%fused_computation.1 | loop fusion | bytes 524288 | tf_op jit(solution)/shard_map/concatenate | solution.py:347
  91.6 1.0 copy-done.15
  92.6 4.6 %shard_map.100 = (f32[224,2048]{1,0:T(8,128)S(1)}, f32[512,224]{1,0:T(8,128)S(1)}) custom-call(bf16[4,512,128]{2,1,0:T(8,128)(2,1)} %collective-permute-done.6.refs_0_, bf16[4,512,128]{2,1,0:T(8,128)(2,1)} %collective-permute-done.7.refs_1_, bf16[4,512,128]{2,1,0:T(8,128)(2,1)} %collective-permute-done.18.refs_2_, ...), custom_call_target="tpu_custom_call" | custom-call | flops 939524096 | bytes 1835008 | tf_op jit(solution)/shard_map/pallas_call | solution.py:54
  97.3 1.2 copy-done
  98.5 0.8 copy-done.18
  99.3 0.9 collective-permute-start.20
  100.2 1.0 copy-done.8
  101.2 1.0 copy-done.19
  102.3 4.5 %shard_map.101 = (f32[224,2048]{1,0:T(8,128)S(1)}, f32[512,224]{1,0:T(8,128)S(1)}) custom-call(bf16[4,512,128]{2,1,0:T(8,128)(2,1)} %collective-permute-done.9.refs_0_, bf16[4,512,128]{2,1,0:T(8,128)(2,1)S(1)} %copy-done.8, bf16[4,512,128]{2,1,0:T(8,128)(2,1)} %collective-permute-done.16.refs_2_, bf16[4,512,128]{2,1,0:T(8,128)(2,1)} %collective-permute-done.17.refs_3_, ...), custom_call_target="tpu_custom_call" | custom-call | flops 939524096 | bytes 1835008 | tf_op jit(solution)/shard_map/pallas_call | solution.py:54
  106.8 5.2 %shard_map.102 = (f32[224,1024]{1,0:T(8,128)S(1)}, bf16[224,512]{1,0:T(8,128)(2,1)}, bf16[224,512]{1,0:T(8,128)(2,1)}) custom-call(bf16[4,512,128]{2,1,0:T(8,128)(2,1)} %constant_dynamic-update-slice_fusion.refs_0_, bf16[4,512,128]{2,1,0:T(8,128)(2,1)} %collective-permute-done.15.refs_1_, bf16[224,512]{1,0:T(8,128)(2,1)S(1)} %get-tuple-element.40.refs_2_.refs_4_, ...), custom_call_target="tpu_custom_call" | custom-call | flops 469762048 | bytes 917504 | tf_op jit(solution)/shard_map/pallas_call | solution.py:54
  112.0 1.3 shard_map.103
  114.0 4.5 %all-to-all-start.4 = ((f32[4,32,224]{2,1,0:T(8,128)}), f32[4,32,224]{2,1,0:T(8,128)S(1)}, u32[]{:S(2)}, u32[]{:S(2)}) async-start(f32[4,32,224]{2,1,0:T(8,128)} %copy-done.21), calls=%async_computation.4 | async-start | bytes 262144 | tf_op jit(solution)/shard_map/all_to_all | solution.py:36
  118.5 2.6 %shard_map.104.refs_8_ = f32[32,32]{1,0:T(8,128)S(1)} custom-call(f32[32,32]{1,0:T(8,128)S(1)} %get-tuple-element.63.gram_ref), custom_call_target="tpu_custom_call" | custom-call | tf_op jit(solution)/shard_map/pallas_call | solution.py:54
  121.1 2.3 %all-to-all-done.4.refs_7_ = f32[4,32,224]{2,1,0:T(8,128)S(1)} async-done(((f32[4,32,224]{2,1,0:T(8,128)}), f32[4,32,224]{2,1,0:T(8,128)S(1)}, u32[]{:S(2)}, u32[]{:S(2)}) %all-to-all-start.4) | async-done | bytes 114720 | tf_op jit(solution)/shard_map/all_to_all | solution.py:36
  124.0 1.5 %copy-done.2 = f32[224,2048]{1,0:T(8,128)S(1)} copy-done((f32[224,2048]{1,0:T(8,128)S(1)}, f32[224,2048]{1,0:T(8,128)}, u32[]{:S(2)}) %copy-start.2) | copy-done | bytes 1835032
  125.5 1.5 %copy-done.4 = f32[224,2048]{1,0:T(8,128)S(1)} copy-done((f32[224,2048]{1,0:T(8,128)S(1)}, f32[224,2048]{1,0:T(8,128)}, u32[]{:S(2)}) %copy-start.4) | copy-done | bytes 1835032
  127.0 1.2 copy-done.6
  128.2 0.9 copy-done.11
  129.1 3.5 %shard_map.105 = (bf16[224,8192]{1,0:T(8,128)(2,1)}, f32[32,224]{1,0:T(8,128)}) custom-call(f32[224,1024]{1,0:T(8,128)S(1)} %get-tuple-element.56.refs_0_, f32[224,2048]{1,0:T(8,128)S(1)} %get-tuple-element.57.refs_1_, f32[224,2048]{1,0:T(8,128)S(1)} %copy-done.2, f32[224,2048]{1,0:T(8,128)S(1)} %copy-done.4, f32[224,1024]{1,0:T(8,128)S(1)} %copy-done.6, ...), custom_call_target="tpu_custom_call" | custom-call | flops 234881024 | bytes 11010048 | tf_op jit(solution)/shard_map/pallas_call | solution.py:54
  (66 shorter events, 6.8 us)
Async XLA Ops:
  0.6 11.1 %copy-start.20 = (bf16[512,128]{1,0:T(8,128)(2,1)S(1)}, bf16[512,128]{1,0:T(8,128)(2,1)}, u32[]{:S(2)}) copy-start(bf16[512,128]{1,0:T(8,128)(2,1)} %cotangent_ref.1) | copy-start | bytes 393220
  0.6 10.6 %collective-permute-start.2 = (bf16[512,128]{1,0:T(8,128)(2,1)}, bf16[512,128]{1,0:T(8,128)(2,1)S(1)}, u32[]{:S(2)}, u32[]{:S(2)}) collective-permute-start(bf16[512,128]{1,0:T(8,128)(2,1)} %cotangent_ref.1), channel_id=1, source_target_pairs={{0,32},{16,48},{32,0},{48,16},{1,33},{17,49},{33,1},{49,17},{2,34}... | collective-permute-start | bytes 393224 | tf_op jit(solution)/shard_map/ppermute | solution.py:32
  4.3 7.4 %collective-permute-start.1 = (bf16[512,128]{1,0:T(8,128)(2,1)}, bf16[512,128]{1,0:T(8,128)(2,1)S(1)}, u32[]{:S(2)}, u32[]{:S(2)}) collective-permute-start(bf16[512,128]{1,0:T(8,128)(2,1)} %cotangent_ref.1), channel_id=1, source_target_pairs={{0,16},{16,32},{32,48},{48,0},{1,17},{17,33},{33,49},{49,1},{2,18}... | collective-permute-start | bytes 393224 | tf_op jit(solution)/shard_map/ppermute | solution.py:32
  4.6 7.1 %collective-permute-start.3 = (bf16[512,128]{1,0:T(8,128)(2,1)}, bf16[512,128]{1,0:T(8,128)(2,1)S(1)}, u32[]{:S(2)}, u32[]{:S(2)}) collective-permute-start(bf16[512,128]{1,0:T(8,128)(2,1)} %cotangent_ref.1), channel_id=1, source_target_pairs={{0,48},{16,0},{32,16},{48,32},{1,49},{17,1},{33,17},{49,33},{2,50}... | collective-permute-start | bytes 393224 | tf_op jit(solution)/shard_map/ppermute | solution.py:32
  9.7 7.4 %collective-permute-start = (bf16[1152,128]{1,0:T(8,128)(2,1)S(1)}, bf16[1152,128]{1,0:T(8,128)(2,1)S(1)}, u32[]{:S(2)}, u32[]{:S(2)}) collective-permute-start(bf16[1152,128]{1,0:T(8,128)(2,1)S(1)} %get-tuple-element.35.send_ref), channel_id=1, source_target_pairs={{0,1},{1,0},{2,3},{3,2},{4,5},{5,4},{6,7},{7,6},{8,9},{9,8},{10,11... | collective-permute-start | bytes 884744 | tf_op jit(solution)/shard_map/ppermute | solution.py:32
  11.8 15.4 %collective-permute-start.5 = (bf16[4,512,128]{2,1,0:T(8,128)(2,1)S(1)}, bf16[4,512,128]{2,1,0:T(8,128)(2,1)S(1)}, u32[]{:S(2)}, u32[]{:S(2)}) collective-permute-start(bf16[4,512,128]{2,1,0:T(8,128)(2,1)S(1)} %pad_maximum_fusion.refs_0_), channel_id=1, source_target_pairs={{0,14},{2,0},{4,2},{6,4},{8,6},{10,8},{12,10},{14,12},{1,15},{3,1}... | collective-permute-start | bytes 1572872 | tf_op jit(solution)/shard_map/ppermute | solution.py:32
  17.0 13.4 %collective-permute-start.4 = (bf16[4,512,128]{2,1,0:T(8,128)(2,1)S(1)}, bf16[4,512,128]{2,1,0:T(8,128)(2,1)}, u32[]{:S(2)}, u32[]{:S(2)}) collective-permute-start(bf16[4,512,128]{2,1,0:T(8,128)(2,1)S(1)} %pad_maximum_fusion.refs_0_), channel_id=1, source_target_pairs={{0,2},{2,4},{4,6},{6,8},{8,10},{10,12},{12,14},{14,0},{1,3},{3,5},... | collective-permute-start | bytes 1572872 | tf_op jit(solution)/shard_map/ppermute | solution.py:32
  27.2 15.3 %copy-start.12 = (bf16[4,512,128]{2,1,0:T(8,128)(2,1)}, bf16[4,512,128]{2,1,0:T(8,128)(2,1)S(1)}, u32[]{:S(2)}) copy-start(bf16[4,512,128]{2,1,0:T(8,128)(2,1)S(1)} %collective-permute-done.5.refs_1_) | copy-start | bytes 1572868
  31.2 24.4 %all-to-all-start.1 = ((bf16[8,160,128]{2,1,0:T(8,128)(2,1)}), bf16[8,160,128]{2,1,0:T(8,128)(2,1)S(1)}, u32[]{:S(2)}, u32[]{:S(2)}) async-start(bf16[8,160,128]{2,1,0:T(8,128)(2,1)} %shard_map.95), calls=%async_computation.1 | async-start | bytes 655360 | tf_op jit(solution)/shard_map/all_to_all | solution.py:36
  34.7 5.7 %collective-permute-start.8 = (bf16[4,512,128]{2,1,0:T(8,128)(2,1)S(1)}, bf16[4,512,128]{2,1,0:T(8,128)(2,1)S(1)}, u32[]{:S(2)}, u32[]{:S(2)}) collective-permute-start(bf16[4,512,128]{2,1,0:T(8,128)(2,1)S(1)} %pad_maximum_fusion.refs_0_), channel_id=1, source_target_pairs={{0,1},{1,0},{2,3},{3,2},{4,5},{5,4},{6,7},{7,6},{8,9},{9,8},{10,11... | collective-permute-start | bytes 1572872 | tf_op jit(solution)/shard_map/ppermute | solution.py:32
  37.0 18.7 %collective-permute-start.6 = (bf16[4,512,128]{2,1,0:T(8,128)(2,1)}, bf16[4,512,128]{2,1,0:T(8,128)(2,1)}, u32[]{:S(2)}, u32[]{:S(2)}) collective-permute-start(bf16[4,512,128]{2,1,0:T(8,128)(2,1)} %collective-permute-done.4.refs_0_), channel_id=1, source_target_pairs={{0,2},{2,4},{4,6},{6,8},{8,10},{10,12},{12,14},{14,0},{1,3},{3,5},... | collective-permute-start | bytes 1572872 | tf_op jit(solution)/shard_map/ppermute | solution.py:32
  38.6 17.1 %collective-permute-start.7 = (bf16[4,512,128]{2,1,0:T(8,128)(2,1)S(1)}, bf16[4,512,128]{2,1,0:T(8,128)(2,1)}, u32[]{:S(2)}, u32[]{:S(2)}) collective-permute-start(bf16[4,512,128]{2,1,0:T(8,128)(2,1)S(1)} %collective-permute-done.5.refs_1_), channel_id=1, source_target_pairs={{0,14},{2,0},{4,2},{6,4},{8,6},{10,8},{12,10},{14,12},{1,15},{3,1}... | collective-permute-start | bytes 1572872 | tf_op jit(solution)/shard_map/ppermute | solution.py:32
  39.8 23.5 %collective-permute-start.11 = (bf16[4,512,128]{2,1,0:T(8,128)(2,1)}, bf16[4,512,128]{2,1,0:T(8,128)(2,1)}, u32[]{:S(2)}, u32[]{:S(2)}) collective-permute-start(bf16[4,512,128]{2,1,0:T(8,128)(2,1)} %collective-permute-done.4.refs_0_), channel_id=1, source_target_pairs={{0,1},{1,0},{2,3},{3,2},{4,5},{5,4},{6,7},{7,6},{8,9},{9,8},{10,11... | collective-permute-start | bytes 1572872 | tf_op jit(solution)/shard_map/ppermute | solution.py:32
  40.3 23.0 %collective-permute-start.12 = (bf16[4,512,128]{2,1,0:T(8,128)(2,1)S(1)}, bf16[4,512,128]{2,1,0:T(8,128)(2,1)}, u32[]{:S(2)}, u32[]{:S(2)}) collective-permute-start(bf16[4,512,128]{2,1,0:T(8,128)(2,1)S(1)} %collective-permute-done.5.refs_1_), channel_id=1, source_target_pairs={{0,1},{1,0},{2,3},{3,2},{4,5},{5,4},{6,7},{7,6},{8,9},{9,8},{10,11... | collective-permute-start | bytes 1572872 | tf_op jit(solution)/shard_map/ppermute | solution.py:32
  42.5 0.8 copy-start.16
  55.7 15.0 %collective-permute-start.9 = (bf16[4,512,128]{2,1,0:T(8,128)(2,1)}, bf16[4,512,128]{2,1,0:T(8,128)(2,1)}, u32[]{:S(2)}, u32[]{:S(2)}) collective-permute-start(bf16[4,512,128]{2,1,0:T(8,128)(2,1)} %collective-permute-done.6.refs_0_), channel_id=1, source_target_pairs={{0,2},{2,4},{4,6},{6,8},{8,10},{10,12},{12,14},{14,0},{1,3},{3,5},... | collective-permute-start | bytes 1572872 | tf_op jit(solution)/shard_map/ppermute | solution.py:32
  56.6 14.0 %collective-permute-start.10 = (bf16[4,512,128]{2,1,0:T(8,128)(2,1)}, bf16[4,512,128]{2,1,0:T(8,128)(2,1)S(1)}, u32[]{:S(2)}, u32[]{:S(2)}) collective-permute-start(bf16[4,512,128]{2,1,0:T(8,128)(2,1)} %collective-permute-done.7.refs_1_), channel_id=1, source_target_pairs={{0,14},{2,0},{4,2},{6,4},{8,6},{10,8},{12,10},{14,12},{1,15},{3,1}... | collective-permute-start | bytes 1572872 | tf_op jit(solution)/shard_map/ppermute | solution.py:32
  59.1 11.6 %all-to-all-start.2 = ((f32[4,32,128]{2,1,0:T(8,128)}), f32[4,32,128]{2,1,0:T(8,128)}, u32[]{:S(2)}, u32[]{:S(2)}) async-start(f32[4,32,128]{2,1,0:T(8,128)} %shard_map.97), calls=%async_computation.2 | async-start | bytes 131072 | tf_op jit(solution)/shard_map/all_to_all | solution.py:36
  63.3 1.0 copy-start.13
  64.4 1.0 copy-start.17
  69.9 0.8 copy-start.14
  70.7 10.6 %copy-start.7 = (bf16[4,512,128]{2,1,0:T(8,128)(2,1)}, bf16[4,512,128]{2,1,0:T(8,128)(2,1)S(1)}, u32[]{:S(2)}) copy-start(bf16[4,512,128]{2,1,0:T(8,128)(2,1)S(1)} %collective-permute-done.10.refs_1_) | copy-start | bytes 1572868
  72.6 15.0 %collective-permute-start.13 = (bf16[4,256,128]{2,1,0:T(8,128)(2,1)}, bf16[4,256,128]{2,1,0:T(8,128)(2,1)}, u32[]{:S(2)}, u32[]{:S(2)}) collective-permute-start(bf16[4,256,128]{2,1,0:T(8,128)(2,1)} %slice.6), channel_id=1, source_target_pairs={{0,2},{2,4},{4,6},{6,8},{8,10},{10,12},{12,14},{14,0},{1,3},{3,5},... | collective-permute-start | bytes 786440 | tf_op jit(solution)/shard_map/ppermute | solution.py:32
  74.4 15.3 %collective-permute-start.14 = (bf16[4,256,128]{2,1,0:T(8,128)(2,1)}, bf16[4,256,128]{2,1,0:T(8,128)(2,1)}, u32[]{:S(2)}, u32[]{:S(2)}) collective-permute-start(bf16[4,256,128]{2,1,0:T(8,128)(2,1)} %slice.7), channel_id=1, source_target_pairs={{0,14},{2,0},{4,2},{6,4},{8,6},{10,8},{12,10},{14,12},{1,15},{3,1}... | collective-permute-start | bytes 786440 | tf_op jit(solution)/shard_map/ppermute | solution.py:32
  76.0 15.6 %collective-permute-start.18 = (bf16[4,512,128]{2,1,0:T(8,128)(2,1)}, bf16[4,512,128]{2,1,0:T(8,128)(2,1)}, u32[]{:S(2)}, u32[]{:S(2)}) collective-permute-start(bf16[4,512,128]{2,1,0:T(8,128)(2,1)} %collective-permute-done.6.refs_0_), channel_id=1, source_target_pairs={{0,1},{1,0},{2,3},{3,2},{4,5},{5,4},{6,7},{7,6},{8,9},{9,8},{10,11... | collective-permute-start | bytes 1572872 | tf_op jit(solution)/shard_map/ppermute | solution.py:32
  79.2 12.4 %collective-permute-start.19 = (bf16[4,512,128]{2,1,0:T(8,128)(2,1)}, bf16[4,512,128]{2,1,0:T(8,128)(2,1)}, u32[]{:S(2)}, u32[]{:S(2)}) collective-permute-start(bf16[4,512,128]{2,1,0:T(8,128)(2,1)} %collective-permute-done.7.refs_1_), channel_id=1, source_target_pairs={{0,1},{1,0},{2,3},{3,2},{4,5},{5,4},{6,7},{7,6},{8,9},{9,8},{10,11... | collective-permute-start | bytes 1572872 | tf_op jit(solution)/shard_map/ppermute | solution.py:32
  79.2 21.0 %collective-permute-start.16 = (bf16[4,512,128]{2,1,0:T(8,128)(2,1)}, bf16[4,512,128]{2,1,0:T(8,128)(2,1)}, u32[]{:S(2)}, u32[]{:S(2)}) collective-permute-start(bf16[4,512,128]{2,1,0:T(8,128)(2,1)} %collective-permute-done.9.refs_0_), channel_id=1, source_target_pairs={{0,1},{1,0},{2,3},{3,2},{4,5},{5,4},{6,7},{7,6},{8,9},{9,8},{10,11... | collective-permute-start | bytes 1572872 | tf_op jit(solution)/shard_map/ppermute | solution.py:32
  80.6 0.7 copy-start.9
  81.3 18.0 %all-to-all-start.3 = ((bf16[32,32,128]{2,1,0:T(8,128)(2,1)}), bf16[32,32,128]{2,1,0:T(8,128)(2,1)S(1)}, u32[]{:S(2)}, u32[]{:S(2)}) async-start(bf16[32,32,128]{2,1,0:T(8,128)(2,1)} %copy-done.9), calls=%async_computation.3 | async-start | bytes 524288 | tf_op jit(solution)/shard_map/all_to_all | solution.py:36
  87.5 12.6 %collective-permute-start.17 = (bf16[4,512,128]{2,1,0:T(8,128)(2,1)}, bf16[4,512,128]{2,1,0:T(8,128)(2,1)}, u32[]{:S(2)}, u32[]{:S(2)}) collective-permute-start(bf16[4,512,128]{2,1,0:T(8,128)(2,1)} %copy-done.7), channel_id=1, source_target_pairs={{0,1},{1,0},{2,3},{3,2},{4,5},{5,4},{6,7},{7,6},{8,9},{9,8},{10,11... | collective-permute-start | bytes 1572872 | tf_op jit(solution)/shard_map/ppermute | solution.py:32
  91.3 15.4 %collective-permute-start.15 = (bf16[4,512,128]{2,1,0:T(8,128)(2,1)}, bf16[4,512,128]{2,1,0:T(8,128)(2,1)}, u32[]{:S(2)}, u32[]{:S(2)}) collective-permute-start(bf16[4,512,128]{2,1,0:T(8,128)(2,1)} %constant_dynamic-update-slice_fusion.refs_0_), channel_id=1, source_target_pairs={{0,1},{1,0},{2,3},{3,2},{4,5},{5,4},{6,7},{7,6},{8,9},{9,8},{10,11... | collective-permute-start | bytes 1572872 | tf_op jit(solution)/shard_map/ppermute | solution.py:32
  91.6 1.0 copy-start.15
  97.2 1.2 copy-start
  98.5 0.8 copy-start.18
  99.3 12.7 %collective-permute-start.20 = (bf16[32,32,128]{2,1,0:T(8,128)(2,1)S(1)}, bf16[32,32,128]{2,1,0:T(8,128)(2,1)S(1)}, u32[]{:S(2)}, u32[]{:S(2)}) collective-permute-start(bf16[32,32,128]{2,1,0:T(8,128)(2,1)S(1)} %all-to-all-done.3.refs_5_), channel_id=1, source_target_pairs={{0,1},{1,0},{2,3},{3,2},{4,5},{5,4},{6,7},{7,6},{8,9},{9,8},{10,11... | collective-permute-start | bytes 786440 | tf_op jit(solution)/shard_map/ppermute | solution.py:32
  100.2 1.0 copy-start.8
  101.2 1.0 copy-start.19
  106.7 5.3 %copy-start.3 = (f32[224,2048]{1,0:T(8,128)}, f32[224,2048]{1,0:T(8,128)S(1)}, u32[]{:S(2)}) copy-start(f32[224,2048]{1,0:T(8,128)S(1)} %get-tuple-element.59.refs_3_) | copy-start | bytes 5505028
  106.7 5.3 %copy-start.1 = (f32[224,2048]{1,0:T(8,128)S(1)}, f32[224,2048]{1,0:T(8,128)}, u32[]{:S(2)}) copy-start(f32[224,2048]{1,0:T(8,128)} %copy-done) | copy-start | bytes 5505028
  112.0 1.3 %copy-start.5 = (f32[224,1024]{1,0:T(8,128)}, f32[224,1024]{1,0:T(8,128)S(1)}, u32[]{:S(2)}) copy-start(f32[224,1024]{1,0:T(8,128)S(1)} %get-tuple-element.60.refs_4_) | copy-start | bytes 2752516
  113.3 0.7 copy-start.21
  114.0 9.4 %all-to-all-start.4 = ((f32[4,32,224]{2,1,0:T(8,128)}), f32[4,32,224]{2,1,0:T(8,128)S(1)}, u32[]{:S(2)}, u32[]{:S(2)}) async-start(f32[4,32,224]{2,1,0:T(8,128)} %copy-done.21), calls=%async_computation.4 | async-start | bytes 262144 | tf_op jit(solution)/shard_map/all_to_all | solution.py:36
  123.4 0.7 copy-start.10
  124.0 1.5 %copy-start.2 = (f32[224,2048]{1,0:T(8,128)S(1)}, f32[224,2048]{1,0:T(8,128)}, u32[]{:S(2)}) copy-start(f32[224,2048]{1,0:T(8,128)} %copy-done) | copy-start | bytes 5505028
  125.5 1.5 %copy-start.4 = (f32[224,2048]{1,0:T(8,128)S(1)}, f32[224,2048]{1,0:T(8,128)}, u32[]{:S(2)}) copy-start(f32[224,2048]{1,0:T(8,128)} %copy-done.3) | copy-start | bytes 5505028
  127.0 1.2 copy-start.6
  128.2 0.9 copy-start.11

commit v5 on v4

--- a/solution.py
+++ b/solution.py
@@ -58,9 +58,14 @@
     return lax.rem(lax.axis_index(axis) + (n - step), n)
 
 
-def column(step, hop, wide):
+def columns_of(step, hop, wide):
     chip = back("x", hop, X) * Z + back("z", step, Z)
-    return pl.multiple_of(chip * (CORES * wide), CORES * wide)
+    core = lax.axis_index("core")
+    return [pl.multiple_of((chip * CORES + c) * wide, wide) for c in (core, 1 - core)]
+
+
+def slabs(ref, step, wide):
+    return jnp.concatenate([ref[:, pl.ds(at, wide)] for hop in range(X) for at in columns_of(step, hop, wide)], axis=1)
 
 
 def fetch(source, target, sem):
@@ -69,11 +74,12 @@
     return copy
 
 
-def start_kernel(gate_hbm, up_hbm, q_hbm, error_ref, hidden_ref, send_ref, mine_ref, gate_ref, up_ref, q_ref, error_buf, sems):
+def start_kernel(gate_hbm, up_hbm, q_hbm, error_ref, hidden_ref, send_ref, mine_ref, error_buf, gate_ref, up_ref, q_ref, sems):
     rank = q_ref.shape[0]
     columns = error_ref.shape[1] // X
     small = [fetch(a, b, sems.at[X + i]) for i, (a, b) in enumerate(((gate_hbm, gate_ref), (up_hbm, up_ref), (q_hbm, q_ref)))]
-    copies = [fetch(error_ref.at[:, pl.ds(x * columns, columns)], error_buf.at[x], sems.at[x]) for x in range(X)]
+    spans = [slice(x * columns, (x + 1) * columns) for x in range(X)]
+    copies = [fetch(error_ref.at[:, spans[x]], error_buf.at[:, spans[x]], sems.at[x]) for x in range(X)]
     for copy in small:
         copy.wait()
     gate = gate_ref[...].astype(F32)
@@ -89,7 +95,7 @@
     first = lax.axis_index("core") == 0
     for x in range(X):
         copies[x].wait()
-        term = dot(both, error_buf[x])
+        term = dot(both, error_buf[:, spans[x]])
         term = (term[:rank] + term[rank:]).astype(BF)
         for z in range(Z):
             at = (x * Z + z) * rank
@@ -98,6 +104,11 @@
             mine_ref[at:at + rank, :] = jnp.where(first, zero, one)
             at += blocks * rank
             send_ref[at:at + rank, :] = jnp.where(first, one, zero)
+
+
+def stack_kernel(*refs):
+    for i, ref in enumerate(refs[:-1]):
+        refs[-1][i] = ref[...]
 
 
 def pack_kernel(send_ref, theirs_ref, mine_ref, out_ref):
@@ -145,40 +156,30 @@
         out_ref[i] = total
 
 
-def piece_kernel(steps, last, *refs):
+def piece_kernel(steps, first, last, *refs):
     n = len(steps)
     own, other = refs[:n], refs[n:2 * n]
     refs = refs[2 * n:]
-    hidden_ref, error_ref, weight_ref, d_in = refs[:4]
-    refs = refs[4:]
-    if last:
-        gate_hbm, up_hbm, matrix_ref, d_gate_ref, d_up_ref, error_buf, weight_buf, sems, gate_ref, up_ref, pair_sems = refs
-        pair = [fetch(gate_hbm, gate_ref, pair_sems.at[0]), fetch(up_hbm, up_ref, pair_sems.at[1])]
+    if first:
+        hidden_ref, error_ref, weight_hbm, matrix_ref, d_ref, weight_ref, sem = refs
+        copy = fetch(weight_hbm, weight_ref, sem.at[0])
+    elif last:
+        hidden_ref, error_ref, weight_ref, d_in, gate_hbm, up_hbm, matrix_ref, d_gate_ref, d_up_ref, gate_ref, up_ref, sem = refs
+        pair = [fetch(gate_hbm, gate_ref, sem.at[0]), fetch(up_hbm, up_ref, sem.at[1])]
     else:
-        matrix_ref, d_ref, error_buf, weight_buf, sems = refs
+        hidden_ref, error_ref, weight_ref, d_in, matrix_ref, d_ref = refs
     wide = own[0].shape[2]
-    width = CORES * wide
-    first = lax.axis_index("core") == 0
-    copies = []
+    blocks = [jnp.concatenate([ref[hop] for hop in range(X) for ref in (own[i], other[i])], axis=1) for i in range(n)]
+    width = blocks[0].shape[1]
     for i, step in enumerate(steps):
-        for hop in range(X):
-            at = column(step, hop, wide)
-            b = i * X + hop
-            for k, (source, target) in enumerate(((error_ref, error_buf), (weight_ref, weight_buf))):
-                copies.append(fetch(source.at[:, pl.ds(at, width)], target.at[:, pl.ds(b * width, width)], sems.at[k, b]))
-    hidden = hidden_ref[...]
-    total = d_in[...]
-    for i in range(n):
-        blocks = []
-        for hop in range(X):
-            a, b = own[i][hop], other[i][hop]
-            blocks += [jnp.where(first, a, b), jnp.where(first, b, a)]
-        for copy in copies[2 * X * i:2 * X * (i + 1)]:
-            copy.wait()
-        block = jnp.concatenate(blocks, axis=1)
-        span = slice(i * X * width, (i + 1) * X * width)
-        matrix_ref[:, span] = error_buf[:, span].astype(F32) + dot(hidden, block)
-        total = total + lax.dot_general(block, weight_buf[:, span], NT, preferred_element_type=F32)
+        matrix_ref[:, i * width:(i + 1) * width] = slabs(error_ref, step, wide).astype(F32) + dot(hidden_ref[...], blocks[i])
+    if first:
+        copy.wait()
+    block = jnp.concatenate(blocks, axis=1)
+    weight = jnp.concatenate([slabs(weight_ref, step, wide) for step in steps], axis=1)
+    total = lax.dot_general(block, weight, NT, preferred_element_type=F32)
+    if not first:
+        total = total + d_in[...]
     if not last:
         d_ref[...] = total
         return
@@ -196,38 +197,48 @@
     tokens, wide = own[0].shape[1:]
     rows = hidden.shape[0]
     columns = n * X * CORES * wide
-    last = gate is not None
-    scratch = [pltpu.VMEM((rows, columns), BF), pltpu.VMEM((rows, columns), BF), pltpu.SemaphoreType.DMA((2, n * X))]
+    first, last = d_hidden is None, gate is not None
+    out = [((rows, columns), F32)]
+    scratch, outs, ins = [], None, [VMEM] * (2 * n + 2)
     if last:
-        scratch += [pltpu.VMEM((rows, tokens), BF), pltpu.VMEM((rows, tokens), BF), pltpu.SemaphoreType.DMA((2,))]
+        out += [((rows, tokens), BF)] * 2
+        outs = [VMEM, None, None]
+        ins += [VMEM, VMEM, HBM, HBM]
+        scratch = [pltpu.VMEM((rows, tokens), BF), pltpu.VMEM((rows, tokens), BF), pltpu.SemaphoreType.DMA((2,))]
+        more = [d_hidden, gate, upward]
+    elif first:
+        out += [((tokens, rows), F32), (weight.shape, BF)]
+        ins += [HBM]
+        scratch = [pltpu.SemaphoreType.DMA((1,))]
+        more = []
+    else:
+        out += [((tokens, rows), F32)]
+        ins += [VMEM, VMEM]
+        more = [d_hidden]
     return call(
-        functools.partial(piece_kernel, steps, last),
-        [((rows, columns), F32)] + ([((rows, tokens), BF)] * 2 if last else [((tokens, rows), F32)]),
+        functools.partial(piece_kernel, steps, first, last),
+        out,
         scratch,
-        [VMEM] * (2 * n + 1) + [HBM, HBM, VMEM] + [HBM, HBM] * last,
-        [VMEM, None, None] if last else None,
+        ins,
+        outs,
         flops=4 * rows * tokens * columns,
         moved=4 * rows * columns,
-    )(*own, *other, hidden, error, weight, d_hidden, *([gate, upward] if last else []))
-
-
-def basis_block(first, step, hop, mine_ref, theirs_ref):
-    at = back("x", hop, X) * Z + back("z", step, Z)
-    a, b = mine_ref[at], theirs_ref[at]
-    return jnp.concatenate([jnp.where(first, a, b), jnp.where(first, b, a)], axis=1)
+    )(*own, *other, hidden, error, weight, *more)
+
+
+def basis_slab(step, mine_ref, theirs_ref):
+    chips = [back("x", hop, X) * Z + back("z", step, Z) for hop in range(X)]
+    return jnp.concatenate([ref[chip] for chip in chips for ref in (mine_ref, theirs_ref)], axis=1)
 
 
 def turn_kernel(layout, groups, *refs):
     n = len(layout)
     mine_ref, theirs_ref, out_ref, gram_ref = refs[n:]
-    first = lax.axis_index("core") == 0
     total, gram = 0.0, 0.0
     for matrix_ref, steps in zip(refs[:n], layout):
-        for i, step in enumerate(steps):
-            basis = jnp.concatenate([basis_block(first, step, hop, mine_ref, theirs_ref) for hop in range(X)], axis=1)
-            span = slice(i * basis.shape[1], (i + 1) * basis.shape[1])
-            total = total + lax.dot_general(matrix_ref[:, span].astype(BF), basis, NT, preferred_element_type=F32)
-            gram = gram + lax.dot_general(basis, basis, NT, preferred_element_type=F32)
+        basis = jnp.concatenate([basis_slab(step, mine_ref, theirs_ref) for step in steps], axis=1)
+        total = total + lax.dot_general(matrix_ref[...].astype(BF), basis, NT, preferred_element_type=F32)
+        gram = gram + lax.dot_general(basis, basis, NT, preferred_element_type=F32)
     gram_ref[...] = gram
     total = total.T
     for g in range(groups):
@@ -251,8 +262,8 @@
     n = len(layout)
     mine_ref, theirs_ref, terms_ref, inverse_ref, out_ref, q_ref, buf, sems = refs[n:]
     wide = mine_ref.shape[2]
-    width = CORES * wide
-    first = lax.axis_index("core") == 0
+    width = X * CORES * wide
+    span = buf.shape[1] // X
     total = terms_ref[0]
     for g in range(1, groups):
         total = total + terms_ref[g]
@@ -263,15 +274,19 @@
     high, low = split(factor.T)
     factor = jnp.concatenate([high, low], axis=1)
     copies = []
-    for matrix_ref, steps in zip(refs[:n], layout):
-        for i, step in enumerate(steps):
-            basis = jnp.concatenate([basis_block(first, step, hop, mine_ref, theirs_ref) for hop in range(X)], axis=1)
-            basis = jnp.concatenate([basis, basis], axis=0)
-            span = slice(i * X * width, (i + 1) * X * width)
-            buf[step] = (matrix_ref[:, span] - dot(factor, basis)).astype(BF)
-            for x in range(X):
-                at = column(step, x, wide)
-                copies.append(fetch(buf.at[step, :, pl.ds(x * width, width)], out_ref.at[:, pl.ds(at, width)], sems.at[step, x]))
+    for hop in range(X):
+        chip = back("x", hop, X)
+        for matrix_ref, steps in zip(refs[:n], layout):
+            for i, step in enumerate(steps):
+                at = chip * Z + back("z", step, Z)
+                basis = jnp.concatenate([mine_ref[at], theirs_ref[at]], axis=1)
+                basis = jnp.concatenate([basis, basis], axis=0)
+                start = i * width + hop * CORES * wide
+                result = (matrix_ref[:, start:start + CORES * wide] - dot(factor, basis)).astype(BF)
+                for c, place in enumerate(columns_of(step, hop, wide)):
+                    buf[:, pl.ds(place, wide)] = result[:, c * wide:(c + 1) * wide]
+        part = pl.ds(pl.multiple_of(chip * span, span), span)
+        copies.append(fetch(buf.at[:, part], out_ref.at[:, part], sems.at[hop]))
     for copy in copies:
         copy.wait()
 
@@ -285,16 +300,16 @@
     tiles = tokens // LANES * rank
 
     blocks = [cotangent] + [shift(cotangent, "x", hop, X) for hop in range(1, X)]
-    pieces, others = {0: jnp.stack(blocks)}, {}
-
-    hidden, send, mine = call(
+    stacked, = call(stack_kernel, [((X, tokens, wide), BF)], ins=[None] + [VMEM] * (X - 1))(*blocks)
+    pieces, others = {0: stacked}, {}
+
+    hidden, send, mine, error = call(
         start_kernel,
-        [((rows, tokens), BF), ((tiles + X * Z * rank, wide), BF), ((X * Z * rank, wide), BF)],
+        [((rows, tokens), BF), ((tiles + X * Z * rank, wide), BF), ((X * Z * rank, wide), BF), ((rows, columns), BF)],
         [
             pltpu.VMEM((rows, tokens), BF),
             pltpu.VMEM((rows, tokens), BF),
             pltpu.VMEM((rank, rows), F32),
-            pltpu.VMEM((X, rows, columns // X), BF),
             pltpu.SemaphoreType.DMA((X + 3,)),
         ],
         [HBM, HBM, HBM, HBM],
@@ -315,12 +330,12 @@
     matrices, layout = [], []
 
     def use(steps, d_hidden, *more):
-        matrix, *rest = add_pieces(steps, [pieces[s] for s in steps], [others[s] for s in steps], hidden, error, down_weight, d_hidden, *more)
+        matrix, *rest = add_pieces(steps, [pieces[s] for s in steps], [others[s] for s in steps], hidden, error, weight, d_hidden, *more)
         matrices.append(matrix)
         layout.append(steps)
-        return rest if more else rest[0]
-
-    d_hidden = jnp.zeros((tokens, rows), F32)
+        return rest if len(rest) > 1 else rest[0]
+
+    weight = down_weight
     ring(1)
     swap(0)
     terms = exchange(terms, "x")
@@ -329,7 +344,7 @@
     swap(1, 7)
     terms, = call(repack_kernel, [((Z, tiles + rank, wide), BF)], ins=[VMEM])(terms)
     terms = exchange(terms, "z")
-    d_hidden = use((0,), d_hidden)
+    d_hidden, weight = use((0,), None)
     terms, pieces[2], pieces[6], d_hidden = lax.optimization_barrier((terms, pieces[2], pieces[6], d_hidden))
     ring(3)
     swap(2, 6)
@@ -337,18 +352,15 @@
     terms = exchange(terms, "dp")
     d_hidden = use((1, 7), d_hidden)
     terms, pieces[3], pieces[5], d_hidden = lax.optimization_barrier((terms, pieces[3], pieces[5], d_hidden))
-    half = tokens // 2
-    up = shift(pieces[3][:, :half], "z", 1, Z)
-    down = shift(pieces[5][:, half:], "z", Z - 1, Z)
+    pieces[4] = shift(pieces[3], "z", 1, Z)
     swap(3, 5)
     mine, = call(spread_kernel, [((X * Z, rank, wide), BF)], ins=[VMEM])(terms)
     mine = exchange(mine, ("x", "z"))
     d_hidden = use((2, 6), d_hidden)
-    pieces[4] = jnp.concatenate([up, down], axis=1)
     swap(4)
+    d_hidden = use((3, 5), d_hidden)
     mine, d_hidden = lax.optimization_barrier((mine, d_hidden))
     theirs = shift(mine, "core", 1, CORES)
-    d_hidden = use((3, 5), d_hidden)
     d_gate, d_up = use((4,), d_hidden, gate.T, upward.T)
 
     terms, gram = call(
@@ -364,7 +376,7 @@
     new_error, next_q = call(
         functools.partial(final_kernel, tuple(layout), groups),
         [((rows, columns), BF), ((rank, rows), F32)],
-        [pltpu.VMEM((Z, rows, columns // Z), BF), pltpu.SemaphoreType.DMA((Z, X))],
+        [pltpu.VMEM((rows, columns), BF), pltpu.SemaphoreType.DMA((X,))],
         [VMEM] * (len(layout) + 4),
         [HBM, None],
         flops=4 * rows * rank * columns,

time: 134 us -> 137 us (1.022)
  the two profiles are of different devices: /device:TPU:1 before, /device:TPU:96 now
where the time goes in v5:
time: 137 us; the launch traced here: 136 us
  starting transfers between devices  37 us (27%)
  local copies, waits for them, and re-layouts  31.8 us (23%)
  Pallas kernels  28.6 us (21%)
  waiting for transfers between devices  26.4 us (19%)
  blocking collectives  11.1 us (8%)
    unnamed x54, local copies, waits for them, and re-layouts  31.8 us
    pallas_call x14, Pallas kernels, call(): return lambda *args: run(*(placed(a, spec) for a, spec in zip(args, ins)))  28.6 us
    ppermute x20, waiting for transfers between devices, shift(): return lax.ppermute(a, axis, [(i, (i + step) % n) for i in range(n)])  23 us
    all_to_all x4, starting transfers between devices, exchange(): return lax.all_to_all(a, axis, 0, 0)  19.8 us
    ppermute x20, starting transfers between devices, shift(): return lax.ppermute(a, axis, [(i, (i + step) % n) for i in range(n)])  17.2 us
    all_to_all x1, blocking collectives, exchange(): return lax.all_to_all(a, axis, 0, 0)  11.1 us
    all_to_all x4, waiting for transfers between devices, exchange(): return lax.all_to_all(a, axis, 0, 0)  3.4 us
  transfers between devices with their start and end apart: 24, of which 7 were waited for; matrix products, arithmetic and copies ran while one was open for 0% of the time, Pallas kernels for 17%

profile of v5, /device:TPU:96, one launch (start us, length us, event | category | flops | bytes accessed | tf_op | source)
XLA Modules:
  0.0 136.0 jit_solution(10081793659475807454)
XLA Ops:
  0.6 1.6 %collective-permute-start.1 = (bf16[512,128]{1,0:T(8,128)(2,1)}, bf16[512,128]{1,0:T(8,128)(2,1)S(1)}, u32[]{:S(2)}, u32[]{:S(2)}) collective-permute-start(bf16[512,128]{1,0:T(8,128)(2,1)} %cotangent_ref.1), channel_id=1, source_target_pairs={{0,16},{16,32},{32,48},{48,0},{1,17},{17,33},{33,49},{49,1},{2,18}... | collective-permute-start | bytes 393224 | tf_op jit(solution)/shard_map/ppermute | solution.py:32
  2.2 2.7 %collective-permute-start.2 = (bf16[512,128]{1,0:T(8,128)(2,1)}, bf16[512,128]{1,0:T(8,128)(2,1)S(1)}, u32[]{:S(2)}, u32[]{:S(2)}) collective-permute-start(bf16[512,128]{1,0:T(8,128)(2,1)} %cotangent_ref.1), channel_id=1, source_target_pairs={{0,32},{16,48},{32,0},{48,16},{1,33},{17,49},{33,1},{49,17},{2,34}... | collective-permute-start | bytes 393224 | tf_op jit(solution)/shard_map/ppermute | solution.py:32
  4.9 1.4 %collective-permute-start.3 = (bf16[512,128]{1,0:T(8,128)(2,1)}, bf16[512,128]{1,0:T(8,128)(2,1)S(1)}, u32[]{:S(2)}, u32[]{:S(2)}) collective-permute-start(bf16[512,128]{1,0:T(8,128)(2,1)} %cotangent_ref.1), channel_id=1, source_target_pairs={{0,48},{16,0},{32,16},{48,32},{1,49},{17,1},{33,17},{49,33},{2,50}... | collective-permute-start | bytes 393224 | tf_op jit(solution)/shard_map/ppermute | solution.py:32
  6.4 2.7 %shard_map.93 = (bf16[224,512]{1,0:T(8,128)(2,1)S(1)}, bf16[1152,128]{1,0:T(8,128)(2,1)S(1)}, bf16[1024,128]{1,0:T(8,128)(2,1)S(1)}, bf16[224,8192]{1,0:T(8,128)(2,1)S(1)}) custom-call(bf16[224,512]{1,0:T(8,128)(2,1)} %bitcast.9, bf16[224,512]{1,0:T(8,128)(2,1)} %bitcast.11, f32[32,224]{1,0:T(8,128)} %bitcast.13, bf16[224,8192]{1,0:T(8,128)(2,1)} %bitcast.8), custom_call_target="tpu_custom_call" | custom-call | flops 234881024 | bytes 3670016 | tf_op jit(solution)/shard_map/pallas_call | solution.py:54
  9.1 1.8 %copy-done = bf16[224,8192]{1,0:T(8,128)(2,1)} copy-done((bf16[224,8192]{1,0:T(8,128)(2,1)}, bf16[224,8192]{1,0:T(8,128)(2,1)S(1)}, u32[]{:S(2)}) %copy-start) | copy-done | bytes 3670040
  11.2 3.2 %collective-permute-start.4 = (bf16[4,512,128]{2,1,0:T(8,128)(2,1)S(1)}, bf16[4,512,128]{2,1,0:T(8,128)(2,1)S(1)}, u32[]{:S(2)}, u32[]{:S(2)}) collective-permute-start(bf16[4,512,128]{2,1,0:T(8,128)(2,1)S(1)} %shard_map.95.refs_0_), channel_id=1, source_target_pairs={{0,2},{2,4},{4,6},{6,8},{8,10},{10,12},{12,14},{14,0},{1,3},{3,5},... | collective-permute-start | bytes 1572872 | tf_op jit(solution)/shard_map/ppermute | solution.py:32
  14.5 11.1 %all_to_all.25.terms_ref = bf16[4,384,128]{2,1,0:T(8,128)(2,1)S(1)} all-to-all(bf16[4,384,128]{2,1,0:T(8,128)(2,1)S(1)} %shard_map.94), channel_id=1, replica_groups=mesh['dp'=4,'x'=4,'z'=8,'core'=2] {'x'}, dimensions={0} | all-to-all | bytes 786432 | tf_op jit(solution)/shard_map/all_to_all | solution.py:36
  26.0 3.4 %collective-permute-done.5.refs_1_ = bf16[4,512,128]{2,1,0:T(8,128)(2,1)S(1)} collective-permute-done((bf16[4,512,128]{2,1,0:T(8,128)(2,1)S(1)}, bf16[4,512,128]{2,1,0:T(8,128)(2,1)S(1)}, u32[]{:S(2)}, u32[]{:S(2)}) %collective-permute-start.5) | collective-permute-done | bytes 524320 | tf_op jit(solution)/shard_map/ppermute | solution.py:32
  29.5 0.9 shard_map.96
  30.3 5.1 %all-to-all-start.1 = ((bf16[8,160,128]{2,1,0:T(8,128)(2,1)}), bf16[8,160,128]{2,1,0:T(8,128)(2,1)S(1)}, u32[]{:S(2)}, u32[]{:S(2)}) async-start(bf16[8,160,128]{2,1,0:T(8,128)(2,1)} %shard_map.96), calls=%async_computation.1 | async-start | bytes 655360 | tf_op jit(solution)/shard_map/all_to_all | solution.py:36
  35.4 2.7 %collective-permute-start.6 = (bf16[4,512,128]{2,1,0:T(8,128)(2,1)S(1)}, bf16[4,512,128]{2,1,0:T(8,128)(2,1)}, u32[]{:S(2)}, u32[]{:S(2)}) collective-permute-start(bf16[4,512,128]{2,1,0:T(8,128)(2,1)S(1)} %collective-permute-done.4.refs_0_), channel_id=1, source_target_pairs={{0,2},{2,4},{4,6},{6,8},{8,10},{10,12},{12,14},{14,0},{1,3},{3,5},... | collective-permute-start | bytes 1572872 | tf_op jit(solution)/shard_map/ppermute | solution.py:32
  38.6 2.0 %copy-done.1 = bf16[224,8192]{1,0:T(8,128)(2,1)S(1)} copy-done((bf16[224,8192]{1,0:T(8,128)(2,1)S(1)}, bf16[224,8192]{1,0:T(8,128)(2,1)}, u32[]{:S(2)}) %copy-start.1) | copy-done | bytes 3670040
  40.7 2.8 %shard_map.97 = (f32[224,1024]{1,0:T(8,128)S(1)}, f32[512,224]{1,0:T(8,128)S(1)}, bf16[224,8192]{1,0:T(8,128)(2,1)S(1)}) custom-call(bf16[4,512,128]{2,1,0:T(8,128)(2,1)S(1)} %shard_map.95.refs_0_, bf16[4,512,128]{2,1,0:T(8,128)(2,1)S(1)} %collective-permute-done.8.refs_1_, bf16[224,512]{1,0:T(8,128)(2,1)S(1)} %get-tuple-element.42.refs_2_.refs_4_, ...), custom_call_target="tpu_custom_call" | custom-call | flops 469762048 | bytes 917504 | tf_op jit(solution)/shard_map/pallas_call | solution.py:54
  43.5 1.8 %copy-done.5 = bf16[224,8192]{1,0:T(8,128)(2,1)} copy-done((bf16[224,8192]{1,0:T(8,128)(2,1)}, bf16[224,8192]{1,0:T(8,128)(2,1)S(1)}, u32[]{:S(2)}) %copy-start.5) | copy-done | bytes 3670040
  45.3 0.8 copy-done.21
  46.1 7.6 %collective-permute-done.6.refs_0_ = bf16[4,512,128]{2,1,0:T(8,128)(2,1)} collective-permute-done((bf16[4,512,128]{2,1,0:T(8,128)(2,1)S(1)}, bf16[4,512,128]{2,1,0:T(8,128)(2,1)}, u32[]{:S(2)}, u32[]{:S(2)}) %collective-permute-start.6) | collective-permute-done | bytes 524320 | tf_op jit(solution)/shard_map/ppermute | solution.py:32
  53.7 2.4 %collective-permute-done.7.refs_1_ = bf16[4,512,128]{2,1,0:T(8,128)(2,1)} collective-permute-done((bf16[4,512,128]{2,1,0:T(8,128)(2,1)S(1)}, bf16[4,512,128]{2,1,0:T(8,128)(2,1)}, u32[]{:S(2)}, u32[]{:S(2)}) %collective-permute-start.7) | collective-permute-done | bytes 524320 | tf_op jit(solution)/shard_map/ppermute | solution.py:32
  56.1 3.2 %collective-permute-start.9 = (bf16[4,512,128]{2,1,0:T(8,128)(2,1)}, bf16[4,512,128]{2,1,0:T(8,128)(2,1)}, u32[]{:S(2)}, u32[]{:S(2)}) collective-permute-start(bf16[4,512,128]{2,1,0:T(8,128)(2,1)} %collective-permute-done.6.refs_0_), channel_id=1, source_target_pairs={{0,2},{2,4},{4,6},{6,8},{8,10},{10,12},{12,14},{14,0},{1,3},{3,5},... | collective-permute-start | bytes 1572872 | tf_op jit(solution)/shard_map/ppermute | solution.py:32
  60.2 4.5 %all-to-all-start.2 = ((f32[4,32,128]{2,1,0:T(8,128)}), f32[4,32,128]{2,1,0:T(8,128)}, u32[]{:S(2)}, u32[]{:S(2)}) async-start(f32[4,32,128]{2,1,0:T(8,128)} %shard_map.98), calls=%async_computation.2 | async-start | bytes 131072 | tf_op jit(solution)/shard_map/all_to_all | solution.py:36
  64.7 2.0 %copy-done.2 = bf16[224,8192]{1,0:T(8,128)(2,1)S(1)} copy-done((bf16[224,8192]{1,0:T(8,128)(2,1)S(1)}, bf16[224,8192]{1,0:T(8,128)(2,1)}, u32[]{:S(2)}) %copy-start.2) | copy-done | bytes 3670040
  66.7 2.0 %copy-done.6 = bf16[224,8192]{1,0:T(8,128)(2,1)S(1)} copy-done((bf16[224,8192]{1,0:T(8,128)(2,1)S(1)}, bf16[224,8192]{1,0:T(8,128)(2,1)}, u32[]{:S(2)}) %copy-start.6) | copy-done | bytes 3670040
  68.7 1.0 copy-done.18
  69.8 1.0 copy-done.22
  70.8 2.5 %shard_map.99 = (f32[224,2048]{1,0:T(8,128)S(1)}, f32[512,224]{1,0:T(8,128)S(1)}) custom-call(bf16[4,512,128]{2,1,0:T(8,128)(2,1)S(1)} %collective-permute-done.4.refs_0_, bf16[4,512,128]{2,1,0:T(8,128)(2,1)S(1)} %copy-done.18, bf16[4,512,128]{2,1,0:T(8,128)(2,1)} %collective-permute-done.11.refs_2_, bf16[4,512,128]{2,1,0:T(8,128)(2,1)} %collective-permute-done.12.refs_3_, ...), custom_call_target="tpu_custom_call" | custom-call | flops 939524096 | bytes 1835008 | tf_op jit(solution)/shard_map/pallas_call | solution.py:54
  73.3 0.8 copy-done.19
  75.5 1.6 %shard_map.100 = bf16[32,32,128]{2,1,0:T(8,128)(2,1)} custom-call(f32[4,32,128]{2,1,0:T(8,128)} %all-to-all-done.2.terms_ref), custom_call_target="tpu_custom_call" | custom-call | tf_op jit(solution)/shard_map/pallas_call | solution.py:54
  77.1 5.7 %all-to-all-start.3 = ((bf16[32,32,128]{2,1,0:T(8,128)(2,1)}), bf16[32,32,128]{2,1,0:T(8,128)(2,1)S(1)}, u32[]{:S(2)}, u32[]{:S(2)}) async-start(bf16[32,32,128]{2,1,0:T(8,128)(2,1)} %shard_map.100), calls=%async_computation.3 | async-start | bytes 524288 | tf_op jit(solution)/shard_map/all_to_all | solution.py:36
  82.8 8.8 %collective-permute-done.13.refs_0_ = bf16[4,512,128]{2,1,0:T(8,128)(2,1)} collective-permute-done((bf16[4,512,128]{2,1,0:T(8,128)(2,1)}, bf16[4,512,128]{2,1,0:T(8,128)(2,1)}, u32[]{:S(2)}, u32[]{:S(2)}) %collective-permute-start.13) | collective-permute-done | bytes 524320 | tf_op jit(solution)/shard_map/ppermute | solution.py:32
  91.6 2.0 %copy-done.3 = bf16[224,8192]{1,0:T(8,128)(2,1)S(1)} copy-done((bf16[224,8192]{1,0:T(8,128)(2,1)S(1)}, bf16[224,8192]{1,0:T(8,128)(2,1)}, u32[]{:S(2)}) %copy-start.3) | copy-done | bytes 3670040
  93.7 2.0 %copy-done.7 = bf16[224,8192]{1,0:T(8,128)(2,1)S(1)} copy-done((bf16[224,8192]{1,0:T(8,128)(2,1)S(1)}, bf16[224,8192]{1,0:T(8,128)(2,1)}, u32[]{:S(2)}) %copy-start.7) | copy-done | bytes 3670040
  95.7 1.0 copy-done.20
  96.8 2.9 %shard_map.101 = (f32[224,2048]{1,0:T(8,128)S(1)}, f32[512,224]{1,0:T(8,128)S(1)}) custom-call(bf16[4,512,128]{2,1,0:T(8,128)(2,1)} %collective-permute-done.6.refs_0_, bf16[4,512,128]{2,1,0:T(8,128)(2,1)} %collective-permute-done.7.refs_1_, bf16[4,512,128]{2,1,0:T(8,128)(2,1)} %collective-permute-done.17.refs_2_, ...), custom_call_target="tpu_custom_call" | custom-call | flops 939524096 | bytes 1835008 | tf_op jit(solution)/shard_map/pallas_call | solution.py:54
  99.6 1.2 copy-done.9
  100.9 2.8 %shard_map.102 = (f32[224,2048]{1,0:T(8,128)S(1)}, f32[512,224]{1,0:T(8,128)S(1)}) custom-call(bf16[4,512,128]{2,1,0:T(8,128)(2,1)} %collective-permute-done.9.refs_0_, bf16[4,512,128]{2,1,0:T(8,128)(2,1)} %collective-permute-done.10.refs_1_, bf16[4,512,128]{2,1,0:T(8,128)(2,1)} %collective-permute-done.15.refs_2_, ...), custom_call_target="tpu_custom_call" | custom-call | flops 939524096 | bytes 1835008 | tf_op jit(solution)/shard_map/pallas_call | solution.py:54
  103.7 1.3 copy-done.12
  105.0 0.8 copy-done.23
  106.3 2.0 %copy-done.4 = bf16[224,8192]{1,0:T(8,128)(2,1)S(1)} copy-done((bf16[224,8192]{1,0:T(8,128)(2,1)S(1)}, bf16[224,8192]{1,0:T(8,128)(2,1)}, u32[]{:S(2)}) %copy-start.4) | copy-done | bytes 3670040
  108.3 2.0 %copy-done.8 = bf16[224,8192]{1,0:T(8,128)(2,1)S(1)} copy-done((bf16[224,8192]{1,0:T(8,128)(2,1)S(1)}, bf16[224,8192]{1,0:T(8,128)(2,1)}, u32[]{:S(2)}) %copy-start.8) | copy-done | bytes 3670040
  110.3 1.0 copy-done.24
  111.4 3.8 %shard_map.103 = (f32[224,1024]{1,0:T(8,128)S(1)}, bf16[224,512]{1,0:T(8,128)(2,1)}, bf16[224,512]{1,0:T(8,128)(2,1)}) custom-call(bf16[4,512,128]{2,1,0:T(8,128)(2,1)} %collective-permute-done.13.refs_0_, bf16[4,512,128]{2,1,0:T(8,128)(2,1)} %collective-permute-done.14.refs_1_, bf16[224,512]{1,0:T(8,128)(2,1)S(1)} %get-tuple-element.42.refs_2_.refs_4_, ...), custom_call_target="tpu_custom_call" | custom-call | flops 469762048 | bytes 917504 | tf_op jit(solution)/shard_map/pallas_call | solution.py:54
  115.2 1.3 shard_map.104
  117.1 4.5 %all-to-all-start.4 = ((f32[4,32,224]{2,1,0:T(8,128)}), f32[4,32,224]{2,1,0:T(8,128)S(1)}, u32[]{:S(2)}, u32[]{:S(2)}) async-start(f32[4,32,224]{2,1,0:T(8,128)} %copy-done.26), calls=%async_computation.4 | async-start | bytes 262144 | tf_op jit(solution)/shard_map/all_to_all | solution.py:36
  121.7 2.6 %shard_map.105.refs_8_ = f32[32,32]{1,0:T(8,128)S(1)} custom-call(f32[32,32]{1,0:T(8,128)S(1)} %get-tuple-element.67.gram_ref), custom_call_target="tpu_custom_call" | custom-call | tf_op jit(solution)/shard_map/pallas_call | solution.py:54
  124.2 3.4 %all-to-all-done.4.refs_7_ = f32[4,32,224]{2,1,0:T(8,128)S(1)} async-done(((f32[4,32,224]{2,1,0:T(8,128)}), f32[4,32,224]{2,1,0:T(8,128)S(1)}, u32[]{:S(2)}, u32[]{:S(2)}) %all-to-all-start.4) | async-done | bytes 114720 | tf_op jit(solution)/shard_map/all_to_all | solution.py:36
  127.6 1.5 %copy-done.11 = f32[224,2048]{1,0:T(8,128)S(1)} copy-done((f32[224,2048]{1,0:T(8,128)S(1)}, f32[224,2048]{1,0:T(8,128)}, u32[]{:S(2)}) %copy-start.11) | copy-done | bytes 1835032
  129.1 1.5 %copy-done.14 = f32[224,2048]{1,0:T(8,128)S(1)} copy-done((f32[224,2048]{1,0:T(8,128)S(1)}, f32[224,2048]{1,0:T(8,128)}, u32[]{:S(2)}) %copy-start.14) | copy-done | bytes 1835032
  130.6 1.2 copy-done.16
  131.8 4.0 %shard_map.106 = (bf16[224,8192]{1,0:T(8,128)(2,1)}, f32[32,224]{1,0:T(8,128)}) custom-call(f32[224,1024]{1,0:T(8,128)S(1)} %get-tuple-element.60.refs_0_, f32[224,2048]{1,0:T(8,128)S(1)} %get-tuple-element.61.refs_1_, f32[224,2048]{1,0:T(8,128)S(1)} %copy-done.11, f32[224,2048]{1,0:T(8,128)S(1)} %copy-done.14, f32[224,1024]{1,0:T(8,128)S(1)} %copy-done.16, ...), custom_call_target="tpu_custom_call" | custom-call | flops 234881024 | bytes 11010048 | tf_op jit(solution)/shard_map/pallas_call | solution.py:54
  (69 shorter events, 4.7 us)
Async XLA Ops:
  0.6 10.5 %copy-start.25 = (bf16[512,128]{1,0:T(8,128)(2,1)S(1)}, bf16[512,128]{1,0:T(8,128)(2,1)}, u32[]{:S(2)}) copy-start(bf16[512,128]{1,0:T(8,128)(2,1)} %cotangent_ref.1) | copy-start | bytes 393220
  0.6 10.3 %collective-permute-start.1 = (bf16[512,128]{1,0:T(8,128)(2,1)}, bf16[512,128]{1,0:T(8,128)(2,1)S(1)}, u32[]{:S(2)}, u32[]{:S(2)}) collective-permute-start(bf16[512,128]{1,0:T(8,128)(2,1)} %cotangent_ref.1), channel_id=1, source_target_pairs={{0,16},{16,32},{32,48},{48,0},{1,17},{17,33},{33,49},{49,1},{2,18}... | collective-permute-start | bytes 393224 | tf_op jit(solution)/shard_map/ppermute | solution.py:32
  2.2 9.0 %collective-permute-start.2 = (bf16[512,128]{1,0:T(8,128)(2,1)}, bf16[512,128]{1,0:T(8,128)(2,1)S(1)}, u32[]{:S(2)}, u32[]{:S(2)}) collective-permute-start(bf16[512,128]{1,0:T(8,128)(2,1)} %cotangent_ref.1), channel_id=1, source_target_pairs={{0,32},{16,48},{32,0},{48,16},{1,33},{17,49},{33,1},{49,17},{2,34}... | collective-permute-start | bytes 393224 | tf_op jit(solution)/shard_map/ppermute | solution.py:32
  4.9 6.2 %collective-permute-start.3 = (bf16[512,128]{1,0:T(8,128)(2,1)}, bf16[512,128]{1,0:T(8,128)(2,1)S(1)}, u32[]{:S(2)}, u32[]{:S(2)}) collective-permute-start(bf16[512,128]{1,0:T(8,128)(2,1)} %cotangent_ref.1), channel_id=1, source_target_pairs={{0,48},{16,0},{32,16},{48,32},{1,49},{17,1},{33,17},{49,33},{2,50}... | collective-permute-start | bytes 393224 | tf_op jit(solution)/shard_map/ppermute | solution.py:32
  9.1 1.8 %copy-start = (bf16[224,8192]{1,0:T(8,128)(2,1)}, bf16[224,8192]{1,0:T(8,128)(2,1)S(1)}, u32[]{:S(2)}) copy-start(bf16[224,8192]{1,0:T(8,128)(2,1)S(1)} %get-tuple-element.43.refs_3_.refs_5_) | copy-start | bytes 11010052
  10.9 3.5 %collective-permute-start = (bf16[1152,128]{1,0:T(8,128)(2,1)S(1)}, bf16[1152,128]{1,0:T(8,128)(2,1)S(1)}, u32[]{:S(2)}, u32[]{:S(2)}) collective-permute-start(bf16[1152,128]{1,0:T(8,128)(2,1)S(1)} %get-tuple-element.37.send_ref), channel_id=1, source_target_pairs={{0,1},{1,0},{2,3},{3,2},{4,5},{5,4},{6,7},{7,6},{8,9},{9,8},{10,11... | collective-permute-start | bytes 884744 | tf_op jit(solution)/shard_map/ppermute | solution.py:32
  11.2 14.8 %collective-permute-start.4 = (bf16[4,512,128]{2,1,0:T(8,128)(2,1)S(1)}, bf16[4,512,128]{2,1,0:T(8,128)(2,1)S(1)}, u32[]{:S(2)}, u32[]{:S(2)}) collective-permute-start(bf16[4,512,128]{2,1,0:T(8,128)(2,1)S(1)} %shard_map.95.refs_0_), channel_id=1, source_target_pairs={{0,2},{2,4},{4,6},{6,8},{8,10},{10,12},{12,14},{14,0},{1,3},{3,5},... | collective-permute-start | bytes 1572872 | tf_op jit(solution)/shard_map/ppermute | solution.py:32
  14.4 15.0 %collective-permute-start.5 = (bf16[4,512,128]{2,1,0:T(8,128)(2,1)S(1)}, bf16[4,512,128]{2,1,0:T(8,128)(2,1)S(1)}, u32[]{:S(2)}, u32[]{:S(2)}) collective-permute-start(bf16[4,512,128]{2,1,0:T(8,128)(2,1)S(1)} %shard_map.95.refs_0_), channel_id=1, source_target_pairs={{0,14},{2,0},{4,2},{6,4},{8,6},{10,8},{12,10},{14,12},{1,15},{3,1}... | collective-permute-start | bytes 1572872 | tf_op jit(solution)/shard_map/ppermute | solution.py:32
  29.5 14.0 %copy-start.17 = (bf16[4,512,128]{2,1,0:T(8,128)(2,1)}, bf16[4,512,128]{2,1,0:T(8,128)(2,1)S(1)}, u32[]{:S(2)}) copy-start(bf16[4,512,128]{2,1,0:T(8,128)(2,1)S(1)} %collective-permute-done.5.refs_1_) | copy-start | bytes 1572868
  30.3 25.8 %all-to-all-start.1 = ((bf16[8,160,128]{2,1,0:T(8,128)(2,1)}), bf16[8,160,128]{2,1,0:T(8,128)(2,1)S(1)}, u32[]{:S(2)}, u32[]{:S(2)}) async-start(bf16[8,160,128]{2,1,0:T(8,128)(2,1)} %shard_map.96), calls=%async_computation.1 | async-start | bytes 655360 | tf_op jit(solution)/shard_map/all_to_all | solution.py:36
  35.4 3.2 %collective-permute-start.8 = (bf16[4,512,128]{2,1,0:T(8,128)(2,1)S(1)}, bf16[4,512,128]{2,1,0:T(8,128)(2,1)S(1)}, u32[]{:S(2)}, u32[]{:S(2)}) collective-permute-start(bf16[4,512,128]{2,1,0:T(8,128)(2,1)S(1)} %shard_map.95.refs_0_), channel_id=1, source_target_pairs={{0,1},{1,0},{2,3},{3,2},{4,5},{5,4},{6,7},{7,6},{8,9},{9,8},{10,11... | collective-permute-start | bytes 1572872 | tf_op jit(solution)/shard_map/ppermute | solution.py:32
  35.4 18.3 %collective-permute-start.6 = (bf16[4,512,128]{2,1,0:T(8,128)(2,1)S(1)}, bf16[4,512,128]{2,1,0:T(8,128)(2,1)}, u32[]{:S(2)}, u32[]{:S(2)}) collective-permute-start(bf16[4,512,128]{2,1,0:T(8,128)(2,1)S(1)} %collective-permute-done.4.refs_0_), channel_id=1, source_target_pairs={{0,2},{2,4},{4,6},{6,8},{8,10},{10,12},{12,14},{14,0},{1,3},{3,5},... | collective-permute-start | bytes 1572872 | tf_op jit(solution)/shard_map/ppermute | solution.py:32
  38.1 18.0 %collective-permute-start.7 = (bf16[4,512,128]{2,1,0:T(8,128)(2,1)S(1)}, bf16[4,512,128]{2,1,0:T(8,128)(2,1)}, u32[]{:S(2)}, u32[]{:S(2)}) collective-permute-start(bf16[4,512,128]{2,1,0:T(8,128)(2,1)S(1)} %collective-permute-done.5.refs_1_), channel_id=1, source_target_pairs={{0,14},{2,0},{4,2},{6,4},{8,6},{10,8},{12,10},{14,12},{1,15},{3,1}... | collective-permute-start | bytes 1572872 | tf_op jit(solution)/shard_map/ppermute | solution.py:32
  38.1 26.5 %collective-permute-start.11 = (bf16[4,512,128]{2,1,0:T(8,128)(2,1)S(1)}, bf16[4,512,128]{2,1,0:T(8,128)(2,1)}, u32[]{:S(2)}, u32[]{:S(2)}) collective-permute-start(bf16[4,512,128]{2,1,0:T(8,128)(2,1)S(1)} %collective-permute-done.4.refs_0_), channel_id=1, source_target_pairs={{0,1},{1,0},{2,3},{3,2},{4,5},{5,4},{6,7},{7,6},{8,9},{9,8},{10,11... | collective-permute-start | bytes 1572872 | tf_op jit(solution)/shard_map/ppermute | solution.py:32
  38.3 26.3 %collective-permute-start.12 = (bf16[4,512,128]{2,1,0:T(8,128)(2,1)S(1)}, bf16[4,512,128]{2,1,0:T(8,128)(2,1)}, u32[]{:S(2)}, u32[]{:S(2)}) collective-permute-start(bf16[4,512,128]{2,1,0:T(8,128)(2,1)S(1)} %collective-permute-done.5.refs_1_), channel_id=1, source_target_pairs={{0,1},{1,0},{2,3},{3,2},{4,5},{5,4},{6,7},{7,6},{8,9},{9,8},{10,11... | collective-permute-start | bytes 1572872 | tf_op jit(solution)/shard_map/ppermute | solution.py:32
  38.6 2.0 %copy-start.1 = (bf16[224,8192]{1,0:T(8,128)(2,1)S(1)}, bf16[224,8192]{1,0:T(8,128)(2,1)}, u32[]{:S(2)}) copy-start(bf16[224,8192]{1,0:T(8,128)(2,1)} %copy-done) | copy-start | bytes 11010052
  43.5 1.8 %copy-start.5 = (bf16[224,8192]{1,0:T(8,128)(2,1)}, bf16[224,8192]{1,0:T(8,128)(2,1)S(1)}, u32[]{:S(2)}) copy-start(bf16[224,8192]{1,0:T(8,128)(2,1)S(1)} %get-tuple-element.48.refs_6_.refs_4_) | copy-start | bytes 11010052
  56.1 18.0 %collective-permute-start.10 = (bf16[4,512,128]{2,1,0:T(8,128)(2,1)}, bf16[4,512,128]{2,1,0:T(8,128)(2,1)}, u32[]{:S(2)}, u32[]{:S(2)}) collective-permute-start(bf16[4,512,128]{2,1,0:T(8,128)(2,1)} %collective-permute-done.7.refs_1_), channel_id=1, source_target_pairs={{0,14},{2,0},{4,2},{6,4},{8,6},{10,8},{12,10},{14,12},{1,15},{3,1}... | collective-permute-start | bytes 1572872 | tf_op jit(solution)/shard_map/ppermute | solution.py:32
  56.1 18.0 %collective-permute-start.9 = (bf16[4,512,128]{2,1,0:T(8,128)(2,1)}, bf16[4,512,128]{2,1,0:T(8,128)(2,1)}, u32[]{:S(2)}, u32[]{:S(2)}) collective-permute-start(bf16[4,512,128]{2,1,0:T(8,128)(2,1)} %collective-permute-done.6.refs_0_), channel_id=1, source_target_pairs={{0,2},{2,4},{4,6},{6,8},{8,10},{10,12},{12,14},{14,0},{1,3},{3,5},... | collective-permute-start | bytes 1572872 | tf_op jit(solution)/shard_map/ppermute | solution.py:32
  60.2 14.0 %all-to-all-start.2 = ((f32[4,32,128]{2,1,0:T(8,128)}), f32[4,32,128]{2,1,0:T(8,128)}, u32[]{:S(2)}, u32[]{:S(2)}) async-start(f32[4,32,128]{2,1,0:T(8,128)} %shard_map.98), calls=%async_computation.2 | async-start | bytes 131072 | tf_op jit(solution)/shard_map/all_to_all | solution.py:36
  64.6 2.0 %copy-start.2 = (bf16[224,8192]{1,0:T(8,128)(2,1)S(1)}, bf16[224,8192]{1,0:T(8,128)(2,1)}, u32[]{:S(2)}) copy-start(bf16[224,8192]{1,0:T(8,128)(2,1)} %copy-done) | copy-start | bytes 11010052
  66.7 2.0 %copy-start.6 = (bf16[224,8192]{1,0:T(8,128)(2,1)S(1)}, bf16[224,8192]{1,0:T(8,128)(2,1)}, u32[]{:S(2)}) copy-start(bf16[224,8192]{1,0:T(8,128)(2,1)} %copy-done.5) | copy-start | bytes 11010052
  68.7 1.0 copy-start.18
  69.8 1.0 copy-start.22
  73.3 0.8 copy-start.19
  74.1 17.5 %collective-permute-start.13 = (bf16[4,512,128]{2,1,0:T(8,128)(2,1)}, bf16[4,512,128]{2,1,0:T(8,128)(2,1)}, u32[]{:S(2)}, u32[]{:S(2)}) collective-permute-start(bf16[4,512,128]{2,1,0:T(8,128)(2,1)} %collective-permute-done.9.refs_0_), channel_id=1, source_target_pairs={{0,2},{2,4},{4,6},{6,8},{8,10},{10,12},{12,14},{14,0},{1,3},{3,5},... | collective-permute-start | bytes 1572872 | tf_op jit(solution)/shard_map/ppermute | solution.py:32
  74.5 17.2 %collective-permute-start.17 = (bf16[4,512,128]{2,1,0:T(8,128)(2,1)}, bf16[4,512,128]{2,1,0:T(8,128)(2,1)}, u32[]{:S(2)}, u32[]{:S(2)}) collective-permute-start(bf16[4,512,128]{2,1,0:T(8,128)(2,1)} %collective-permute-done.6.refs_0_), channel_id=1, source_target_pairs={{0,1},{1,0},{2,3},{3,2},{4,5},{5,4},{6,7},{7,6},{8,9},{9,8},{10,11... | collective-permute-start | bytes 1572872 | tf_op jit(solution)/shard_map/ppermute | solution.py:32
  74.5 17.1 %collective-permute-start.18 = (bf16[4,512,128]{2,1,0:T(8,128)(2,1)}, bf16[4,512,128]{2,1,0:T(8,128)(2,1)}, u32[]{:S(2)}, u32[]{:S(2)}) collective-permute-start(bf16[4,512,128]{2,1,0:T(8,128)(2,1)} %collective-permute-done.7.refs_1_), channel_id=1, source_target_pairs={{0,1},{1,0},{2,3},{3,2},{4,5},{5,4},{6,7},{7,6},{8,9},{9,8},{10,11... | collective-permute-start | bytes 1572872 | tf_op jit(solution)/shard_map/ppermute | solution.py:32
  75.0 25.9 %collective-permute-start.15 = (bf16[4,512,128]{2,1,0:T(8,128)(2,1)}, bf16[4,512,128]{2,1,0:T(8,128)(2,1)}, u32[]{:S(2)}, u32[]{:S(2)}) collective-permute-start(bf16[4,512,128]{2,1,0:T(8,128)(2,1)} %collective-permute-done.9.refs_0_), channel_id=1, source_target_pairs={{0,1},{1,0},{2,3},{3,2},{4,5},{5,4},{6,7},{7,6},{8,9},{9,8},{10,11... | collective-permute-start | bytes 1572872 | tf_op jit(solution)/shard_map/ppermute | solution.py:32
  75.1 25.8 %collective-permute-start.16 = (bf16[4,512,128]{2,1,0:T(8,128)(2,1)}, bf16[4,512,128]{2,1,0:T(8,128)(2,1)}, u32[]{:S(2)}, u32[]{:S(2)}) collective-permute-start(bf16[4,512,128]{2,1,0:T(8,128)(2,1)} %collective-permute-done.10.refs_1_), channel_id=1, source_target_pairs={{0,1},{1,0},{2,3},{3,2},{4,5},{5,4},{6,7},{7,6},{8,9},{9,8},{10,11... | collective-permute-start | bytes 1572872 | tf_op jit(solution)/shard_map/ppermute | solution.py:32
  77.1 28.7 %all-to-all-start.3 = ((bf16[32,32,128]{2,1,0:T(8,128)(2,1)}), bf16[32,32,128]{2,1,0:T(8,128)(2,1)S(1)}, u32[]{:S(2)}, u32[]{:S(2)}) async-start(bf16[32,32,128]{2,1,0:T(8,128)(2,1)} %shard_map.100), calls=%async_computation.3 | async-start | bytes 524288 | tf_op jit(solution)/shard_map/all_to_all | solution.py:36
  91.6 14.6 %collective-permute-start.14 = (bf16[4,512,128]{2,1,0:T(8,128)(2,1)}, bf16[4,512,128]{2,1,0:T(8,128)(2,1)}, u32[]{:S(2)}, u32[]{:S(2)}) collective-permute-start(bf16[4,512,128]{2,1,0:T(8,128)(2,1)} %collective-permute-done.13.refs_0_), channel_id=1, source_target_pairs={{0,1},{1,0},{2,3},{3,2},{4,5},{5,4},{6,7},{7,6},{8,9},{9,8},{10,11... | collective-permute-start | bytes 1572872 | tf_op jit(solution)/shard_map/ppermute | solution.py:32
  91.6 2.0 %copy-start.3 = (bf16[224,8192]{1,0:T(8,128)(2,1)S(1)}, bf16[224,8192]{1,0:T(8,128)(2,1)}, u32[]{:S(2)}) copy-start(bf16[224,8192]{1,0:T(8,128)(2,1)} %copy-done) | copy-start | bytes 11010052
  93.7 2.0 %copy-start.7 = (bf16[224,8192]{1,0:T(8,128)(2,1)S(1)}, bf16[224,8192]{1,0:T(8,128)(2,1)}, u32[]{:S(2)}) copy-start(bf16[224,8192]{1,0:T(8,128)(2,1)} %copy-done.5) | copy-start | bytes 11010052
  95.7 1.0 copy-start.20
  99.6 1.3 copy-start.9
  103.7 1.3 copy-start.12
  105.8 9.4 %collective-permute-start.19 = (bf16[32,32,128]{2,1,0:T(8,128)(2,1)S(1)}, bf16[32,32,128]{2,1,0:T(8,128)(2,1)S(1)}, u32[]{:S(2)}, u32[]{:S(2)}) collective-permute-start(bf16[32,32,128]{2,1,0:T(8,128)(2,1)S(1)} %all-to-all-done.3.refs_5_), channel_id=1, source_target_pairs={{0,1},{1,0},{2,3},{3,2},{4,5},{5,4},{6,7},{7,6},{8,9},{9,8},{10,11... | collective-permute-start | bytes 786440 | tf_op jit(solution)/shard_map/ppermute | solution.py:32
  106.3 2.0 %copy-start.4 = (bf16[224,8192]{1,0:T(8,128)(2,1)S(1)}, bf16[224,8192]{1,0:T(8,128)(2,1)}, u32[]{:S(2)}) copy-start(bf16[224,8192]{1,0:T(8,128)(2,1)} %copy-done) | copy-start | bytes 11010052
  108.3 2.0 %copy-start.8 = (bf16[224,8192]{1,0:T(8,128)(2,1)S(1)}, bf16[224,8192]{1,0:T(8,128)(2,1)}, u32[]{:S(2)}) copy-start(bf16[224,8192]{1,0:T(8,128)(2,1)} %copy-done.5) | copy-start | bytes 11010052
  110.3 1.0 copy-start.24
  111.4 3.8 %copy-start.10 = (f32[224,2048]{1,0:T(8,128)S(1)}, f32[224,2048]{1,0:T(8,128)}, u32[]{:S(2)}) copy-start(f32[224,2048]{1,0:T(8,128)} %copy-done.9) | copy-start | bytes 5505028
  111.4 3.8 %copy-start.13 = (f32[224,2048]{1,0:T(8,128)S(1)}, f32[224,2048]{1,0:T(8,128)}, u32[]{:S(2)}) copy-start(f32[224,2048]{1,0:T(8,128)} %copy-done.12) | copy-start | bytes 5505028
  115.2 1.3 copy-start.15
  117.1 10.5 %all-to-all-start.4 = ((f32[4,32,224]{2,1,0:T(8,128)}), f32[4,32,224]{2,1,0:T(8,128)S(1)}, u32[]{:S(2)}, u32[]{:S(2)}) async-start(f32[4,32,224]{2,1,0:T(8,128)} %copy-done.26), calls=%async_computation.4 | async-start | bytes 262144 | tf_op jit(solution)/shard_map/all_to_all | solution.py:36
  127.6 1.5 %copy-start.11 = (f32[224,2048]{1,0:T(8,128)S(1)}, f32[224,2048]{1,0:T(8,128)}, u32[]{:S(2)}) copy-start(f32[224,2048]{1,0:T(8,128)} %copy-done.9) | copy-start | bytes 5505028
  129.1 1.5 %copy-start.14 = (f32[224,2048]{1,0:T(8,128)S(1)}, f32[224,2048]{1,0:T(8,128)}, u32[]{:S(2)}) copy-start(f32[224,2048]{1,0:T(8,128)} %copy-done.12) | copy-start | bytes 5505028
  130.6 1.2 copy-start.16
  (3 other events, 2.3 us)

commit v6 on v5

--- a/solution.py
+++ b/solution.py
@@ -134,7 +134,7 @@
 
 
 def slice_kernel(groups, terms_ref, cotangent_ref, out_ref):
-    rank = out_ref.shape[1]
+    rank = out_ref.shape[0]
     terms = terms_ref[0].astype(F32)
     for i in range(1, Z):
         terms = terms + terms_ref[i].astype(F32)
@@ -142,16 +142,22 @@
     total = terms[blocks * rank:]
     for b in range(blocks):
         total = total + dot(terms[b * rank:(b + 1) * rank].astype(BF), cotangent_ref[b * LANES:(b + 1) * LANES, :])
-    total = total / groups
-    for g in range(groups):
-        out_ref[g] = total
-
-
-def spread_kernel(terms_ref, out_ref):
-    total = terms_ref[0]
-    for g in range(1, terms_ref.shape[0]):
-        total = total + terms_ref[g]
-    total = total.astype(BF)
+    out_ref[...] = total / groups
+
+
+def ordered_sum(refs, buf):
+    n = len(refs)
+    for k, ref in enumerate(refs):
+        buf[back("dp", k, n)] = ref[...]
+    total = buf[0]
+    for g in range(1, n):
+        total = total + buf[g]
+    return total
+
+
+def spread_kernel(*refs):
+    out_ref, buf = refs[-2:]
+    total = ordered_sum(refs[:-2], buf).astype(BF)
     for i in range(out_ref.shape[0]):
         out_ref[i] = total
 
@@ -231,7 +237,7 @@
     return jnp.concatenate([ref[chip] for chip in chips for ref in (mine_ref, theirs_ref)], axis=1)
 
 
-def turn_kernel(layout, groups, *refs):
+def turn_kernel(layout, *refs):
     n = len(layout)
     mine_ref, theirs_ref, out_ref, gram_ref = refs[n:]
     total, gram = 0.0, 0.0
@@ -240,9 +246,7 @@
         total = total + lax.dot_general(matrix_ref[...].astype(BF), basis, NT, preferred_element_type=F32)
         gram = gram + lax.dot_general(basis, basis, NT, preferred_element_type=F32)
     gram_ref[...] = gram
-    total = total.T
-    for g in range(groups):
-        out_ref[g] = total
+    out_ref[...] = total.T
 
 
 def inverse_kernel(gram_ref, out_ref):
@@ -260,13 +264,12 @@
 
 def final_kernel(layout, groups, *refs):
     n = len(layout)
-    mine_ref, theirs_ref, terms_ref, inverse_ref, out_ref, q_ref, buf, sems = refs[n:]
+    mine_ref, theirs_ref, inverse_ref = refs[n:n + 3]
+    out_ref, q_ref, buf, terms_buf, sems = refs[n + 3 + groups:]
     wide = mine_ref.shape[2]
     width = X * CORES * wide
     span = buf.shape[1] // X
-    total = terms_ref[0]
-    for g in range(1, groups):
-        total = total + terms_ref[g]
+    total = ordered_sum(refs[n + 3:n + 3 + groups], terms_buf)
     inverse = inverse_ref[...]
     next_q = jnp.dot(inverse, total / groups, precision=HIGHEST, preferred_element_type=F32)
     q_ref[...] = next_q
@@ -300,7 +303,7 @@
     tiles = tokens // LANES * rank
 
     blocks = [cotangent] + [shift(cotangent, "x", hop, X) for hop in range(1, X)]
-    stacked, = call(stack_kernel, [((X, tokens, wide), BF)], ins=[None] + [VMEM] * (X - 1))(*blocks)
+    stacked, = call(stack_kernel, [((X, tokens, wide), BF)], ins=[VMEM] * X)(*blocks)
     pieces, others = {0: stacked}, {}
 
     hidden, send, mine, error = call(
@@ -335,53 +338,58 @@
         layout.append(steps)
         return rest if len(rest) > 1 else rest[0]
 
+    def around(a):
+        return [a] + [shift(a, "dp", k, groups) for k in range(1, groups)]
+
+    tie = lax.optimization_barrier
     weight = down_weight
     ring(1)
     swap(0)
     terms = exchange(terms, "x")
-    terms, pieces[1], pieces[7] = lax.optimization_barrier((terms, pieces[1], pieces[7]))
+    terms, pieces[1], pieces[7] = tie((terms, pieces[1], pieces[7]))
     ring(2)
     swap(1, 7)
+    terms, others[1], others[7] = tie((terms, others[1], others[7]))
     terms, = call(repack_kernel, [((Z, tiles + rank, wide), BF)], ins=[VMEM])(terms)
     terms = exchange(terms, "z")
-    d_hidden, weight = use((0,), None)
-    terms, pieces[2], pieces[6], d_hidden = lax.optimization_barrier((terms, pieces[2], pieces[6], d_hidden))
+    terms, pieces[2], pieces[6] = tie((terms, pieces[2], pieces[6]))
     ring(3)
     swap(2, 6)
-    terms, = call(functools.partial(slice_kernel, groups), [((groups, rank, wide), F32)], ins=[VMEM, None])(terms, cotangent)
-    terms = exchange(terms, "dp")
-    d_hidden = use((1, 7), d_hidden)
-    terms, pieces[3], pieces[5], d_hidden = lax.optimization_barrier((terms, pieces[3], pieces[5], d_hidden))
+    terms, = call(functools.partial(slice_kernel, groups), [((rank, wide), F32)], ins=[VMEM, VMEM])(terms, cotangent)
+    terms = around(terms)
+    d_hidden, weight = use((0, 1, 7), None)
+    d_hidden = use((2, 6), d_hidden)
+    mine, = call(spread_kernel, [((X * Z, rank, wide), BF)], [pltpu.VMEM((groups, rank, wide), F32)], [VMEM] * groups)(*terms)
+    mine, pieces[3], pieces[5], d_hidden = tie((mine, pieces[3], pieces[5], d_hidden))
     pieces[4] = shift(pieces[3], "z", 1, Z)
     swap(3, 5)
-    mine, = call(spread_kernel, [((X * Z, rank, wide), BF)], ins=[VMEM])(terms)
+    mine, others[3], others[5] = tie((mine, others[3], others[5]))
     mine = exchange(mine, ("x", "z"))
-    d_hidden = use((2, 6), d_hidden)
+    mine, pieces[4], d_hidden = tie((mine, pieces[4], d_hidden))
+    theirs = shift(mine, "core", 1, CORES)
     swap(4)
     d_hidden = use((3, 5), d_hidden)
-    mine, d_hidden = lax.optimization_barrier((mine, d_hidden))
-    theirs = shift(mine, "core", 1, CORES)
     d_gate, d_up = use((4,), d_hidden, gate.T, upward.T)
 
     terms, gram = call(
-        functools.partial(turn_kernel, tuple(layout), groups),
-        [((groups, rank, rows), F32), ((rank, rank), F32)],
+        functools.partial(turn_kernel, tuple(layout)),
+        [((rank, rows), F32), ((rank, rank), F32)],
         ins=[VMEM] * (len(layout) + 2),
         flops=2 * rows * rank * columns,
         moved=4 * rows * columns,
     )(*matrices, mine, theirs)
-    terms = exchange(terms, "dp")
+    terms = around(terms)
     inverse, = call(inverse_kernel, [((rank, rank), F32)], ins=[VMEM])(gram)
 
     new_error, next_q = call(
         functools.partial(final_kernel, tuple(layout), groups),
         [((rows, columns), BF), ((rank, rows), F32)],
-        [pltpu.VMEM((rows, columns), BF), pltpu.SemaphoreType.DMA((X,))],
-        [VMEM] * (len(layout) + 4),
+        [pltpu.VMEM((rows, columns), BF), pltpu.VMEM((groups, rank, rows), F32), pltpu.SemaphoreType.DMA((X,))],
+        [VMEM] * (len(layout) + 3 + groups),
         [HBM, None],
         flops=4 * rows * rank * columns,
         moved=6 * rows * columns,
-    )(*matrices, mine, theirs, terms, inverse)
+    )(*matrices, mine, theirs, inverse, *terms)
     return (d_gate.T, d_up.T, new_error[None], next_q.T)
 
 

time: 137 us -> 149 us (1.088)
  the two profiles are of different devices: /device:TPU:96 before, /device:TPU:1 now
where the time goes in v6:
time: 149 us; the launch traced here: 148 us
  starting transfers between devices  45.5 us (31%)
  waiting for transfers between devices  42.5 us (29%)
  Pallas kernels  25.8 us (17%)
  local copies, waits for them, and re-layouts  23.5 us (16%)
  blocking collectives  9.54 us (6%)
    ppermute x26, waiting for transfers between devices, shift(): return lax.ppermute(a, axis, [(i, (i + step) % n) for i in range(n)])  39.5 us
    ppermute x26, starting transfers between devices, shift(): return lax.ppermute(a, axis, [(i, (i + step) % n) for i in range(n)])  37.5 us
    pallas_call x13, Pallas kernels, call(): return lambda *args: run(*(placed(a, spec) for a, spec in zip(args, ins)))  25.8 us
    unnamed x54, local copies, waits for them, and re-layouts  23.5 us
    all_to_all x1, blocking collectives, exchange(): return lax.all_to_all(a, axis, 0, 0)  9.54 us
    all_to_all x2, starting transfers between devices, exchange(): return lax.all_to_all(a, axis, 0, 0)  8.06 us
    all_to_all x2, waiting for transfers between devices, exchange(): return lax.all_to_all(a, axis, 0, 0)  3.03 us
  transfers between devices with their start and end apart: 28, of which 13 were waited for; matrix products, arithmetic and copies ran while one was open for 0% of the time, Pallas kernels for 13%

profile of v6, /device:TPU:1, one launch (start us, length us, event | category | flops | bytes accessed | tf_op | source)
XLA Modules:
  0.0 147.8 jit_solution(11525820723918603796)
XLA Ops:
  0.6 3.4 %collective-permute-start.3 = (bf16[512,128]{1,0:T(8,128)(2,1)}, bf16[512,128]{1,0:T(8,128)(2,1)S(1)}, u32[]{:S(2)}, u32[]{:S(2)}) collective-permute-start(bf16[512,128]{1,0:T(8,128)(2,1)} %cotangent_ref.1), channel_id=1, source_target_pairs={{0,48},{16,0},{32,16},{48,32},{1,49},{17,1},{33,17},{49,33},{2,50}... | collective-permute-start | bytes 393224 | tf_op jit(solution)/shard_map/ppermute | solution.py:32
  5.2 2.7 %shard_map.93 = (bf16[224,512]{1,0:T(8,128)(2,1)S(1)}, bf16[1152,128]{1,0:T(8,128)(2,1)S(1)}, bf16[1024,128]{1,0:T(8,128)(2,1)S(1)}, bf16[224,8192]{1,0:T(8,128)(2,1)S(1)}) custom-call(bf16[224,512]{1,0:T(8,128)(2,1)} %bitcast.9, bf16[224,512]{1,0:T(8,128)(2,1)} %bitcast.11, f32[32,224]{1,0:T(8,128)} %bitcast.13, bf16[224,8192]{1,0:T(8,128)(2,1)} %bitcast.8), custom_call_target="tpu_custom_call" | custom-call | flops 234881024 | bytes 3670016 | tf_op jit(solution)/shard_map/pallas_call | solution.py:54
  7.9 1.8 %copy-done = bf16[224,8192]{1,0:T(8,128)(2,1)} copy-done((bf16[224,8192]{1,0:T(8,128)(2,1)}, bf16[224,8192]{1,0:T(8,128)(2,1)S(1)}, u32[]{:S(2)}) %copy-start) | copy-done | bytes 3670040
  9.7 1.5 %collective-permute-start = (bf16[1152,128]{1,0:T(8,128)(2,1)S(1)}, bf16[1152,128]{1,0:T(8,128)(2,1)S(1)}, u32[]{:S(2)}, u32[]{:S(2)}) collective-permute-start(bf16[1152,128]{1,0:T(8,128)(2,1)S(1)} %get-tuple-element.41.send_ref), channel_id=1, source_target_pairs={{0,1},{1,0},{2,3},{3,2},{4,5},{5,4},{6,7},{7,6},{8,9},{9,8},{10,11... | collective-permute-start | bytes 884744 | tf_op jit(solution)/shard_map/ppermute | solution.py:32
  11.2 2.6 %collective-permute-done.1.refs_1_ = bf16[512,128]{1,0:T(8,128)(2,1)S(1)} collective-permute-done((bf16[512,128]{1,0:T(8,128)(2,1)}, bf16[512,128]{1,0:T(8,128)(2,1)S(1)}, u32[]{:S(2)}, u32[]{:S(2)}) %collective-permute-start.1) | collective-permute-done | bytes 131104 | tf_op jit(solution)/shard_map/ppermute | solution.py:32
  13.8 5.7 %collective-permute-start.5 = (bf16[4,512,128]{2,1,0:T(8,128)(2,1)S(1)}, bf16[4,512,128]{2,1,0:T(8,128)(2,1)S(1)}, u32[]{:S(2)}, u32[]{:S(2)}) collective-permute-start(bf16[4,512,128]{2,1,0:T(8,128)(2,1)S(1)} %shard_map.95.refs_0_), channel_id=1, source_target_pairs={{0,14},{2,0},{4,2},{6,4},{8,6},{10,8},{12,10},{14,12},{1,15},{3,1}... | collective-permute-start | bytes 1572872 | tf_op jit(solution)/shard_map/ppermute | solution.py:32
  19.6 9.5 %all_to_all.15.terms_ref = bf16[4,384,128]{2,1,0:T(8,128)(2,1)S(1)} all-to-all(bf16[4,384,128]{2,1,0:T(8,128)(2,1)S(1)} %shard_map.94), channel_id=1, replica_groups=mesh['dp'=4,'x'=4,'z'=8,'core'=2] {'x'}, dimensions={0} | all-to-all | bytes 786432 | tf_op jit(solution)/shard_map/all_to_all | solution.py:36
  29.1 1.0 collective-permute-done.5.refs_2_
  30.1 3.1 %collective-permute-done.4.refs_1_ = bf16[4,512,128]{2,1,0:T(8,128)(2,1)S(1)} collective-permute-done((bf16[4,512,128]{2,1,0:T(8,128)(2,1)S(1)}, bf16[4,512,128]{2,1,0:T(8,128)(2,1)S(1)}, u32[]{:S(2)}, u32[]{:S(2)}) %collective-permute-start.4) | collective-permute-done | bytes 524320 | tf_op jit(solution)/shard_map/ppermute | solution.py:32
  33.1 1.9 %collective-permute-start.6 = (bf16[4,512,128]{2,1,0:T(8,128)(2,1)S(1)}, bf16[4,512,128]{2,1,0:T(8,128)(2,1)S(1)}, u32[]{:S(2)}, u32[]{:S(2)}) collective-permute-start(bf16[4,512,128]{2,1,0:T(8,128)(2,1)S(1)} %collective-permute-done.4.refs_1_), channel_id=1, source_target_pairs={{0,1},{1,0},{2,3},{3,2},{4,5},{5,4},{6,7},{7,6},{8,9},{9,8},{10,11... | collective-permute-start | bytes 1572872 | tf_op jit(solution)/shard_map/ppermute | solution.py:32
  35.0 1.5 %collective-permute-done.6.refs_4_ = bf16[4,512,128]{2,1,0:T(8,128)(2,1)S(1)} collective-permute-done((bf16[4,512,128]{2,1,0:T(8,128)(2,1)S(1)}, bf16[4,512,128]{2,1,0:T(8,128)(2,1)S(1)}, u32[]{:S(2)}, u32[]{:S(2)}) %collective-permute-start.6) | collective-permute-done | bytes 524320 | tf_op jit(solution)/shard_map/ppermute | solution.py:32
  38.9 3.4 %all-to-all-start.1 = ((bf16[8,160,128]{2,1,0:T(8,128)(2,1)}), bf16[8,160,128]{2,1,0:T(8,128)(2,1)S(1)}, u32[]{:S(2)}, u32[]{:S(2)}) async-start(bf16[8,160,128]{2,1,0:T(8,128)(2,1)} %shard_map.96), calls=%async_computation.1 | async-start | bytes 655360 | tf_op jit(solution)/shard_map/all_to_all | solution.py:36
  42.3 1.4 collective-permute-start.8
  43.7 1.4 collective-permute-start.9
  46.0 17.9 %collective-permute-done.8.refs_0_ = bf16[4,512,128]{2,1,0:T(8,128)(2,1)} collective-permute-done((bf16[4,512,128]{2,1,0:T(8,128)(2,1)S(1)}, bf16[4,512,128]{2,1,0:T(8,128)(2,1)}, u32[]{:S(2)}, u32[]{:S(2)}) %collective-permute-start.8) | collective-permute-done | bytes 524320 | tf_op jit(solution)/shard_map/ppermute | solution.py:32
  64.0 1.2 collective-permute-start.15
  65.3 2.7 %collective-permute-start.14 = (bf16[4,512,128]{2,1,0:T(8,128)(2,1)}, bf16[4,512,128]{2,1,0:T(8,128)(2,1)S(1)}, u32[]{:S(2)}, u32[]{:S(2)}) collective-permute-start(bf16[4,512,128]{2,1,0:T(8,128)(2,1)} %collective-permute-done.9.refs_1_), channel_id=1, source_target_pairs={{0,14},{2,0},{4,2},{6,4},{8,6},{10,8},{12,10},{14,12},{1,15},{3,1}... | collective-permute-start | bytes 1572872 | tf_op jit(solution)/shard_map/ppermute | solution.py:32
  68.9 2.7 %collective-permute-start.12 = (f32[32,128]{1,0:T(8,128)S(1)}, f32[32,128]{1,0:T(8,128)S(1)}, u32[]{:S(2)}, u32[]{:S(2)}) collective-permute-start(f32[32,128]{1,0:T(8,128)S(1)} %shard_map.97.refs_0_), channel_id=1, source_target_pairs={{0,192},{64,0},{128,64},{192,128},{1,193},{65,1},{129,65},{193,129... | collective-permute-start | bytes 49160 | tf_op jit(solution)/shard_map/ppermute | solution.py:32
  72.5 2.3 %collective-permute-start.11 = (f32[32,128]{1,0:T(8,128)S(1)}, f32[32,128]{1,0:T(8,128)S(1)}, u32[]{:S(2)}, u32[]{:S(2)}) collective-permute-start(f32[32,128]{1,0:T(8,128)S(1)} %shard_map.97.refs_0_), channel_id=1, source_target_pairs={{0,128},{64,192},{128,0},{192,64},{1,129},{65,193},{129,1},{193,65... | collective-permute-start | bytes 49160 | tf_op jit(solution)/shard_map/ppermute | solution.py:32
  74.8 1.8 %collective-permute-done.11.refs_2_ = f32[32,128]{1,0:T(8,128)S(1)} collective-permute-done((f32[32,128]{1,0:T(8,128)S(1)}, f32[32,128]{1,0:T(8,128)S(1)}, u32[]{:S(2)}, u32[]{:S(2)}) %collective-permute-start.11) | collective-permute-done | bytes 16416 | tf_op jit(solution)/shard_map/ppermute | solution.py:32
  76.6 1.3 collective-permute-start.10
  77.9 2.0 %copy-done.1 = bf16[224,8192]{1,0:T(8,128)(2,1)S(1)} copy-done((bf16[224,8192]{1,0:T(8,128)(2,1)S(1)}, bf16[224,8192]{1,0:T(8,128)(2,1)}, u32[]{:S(2)}) %copy-start.1) | copy-done | bytes 3670040
  80.0 1.0 copy-done.18
  81.0 1.0 copy-done.20
  82.1 1.0 copy-done.22
  83.1 1.0 copy-done.24
  84.2 1.0 copy-done.26
  85.2 4.2 %shard_map.99 = (f32[224,3072]{1,0:T(8,128)S(1)}, f32[512,224]{1,0:T(8,128)S(1)}, bf16[224,8192]{1,0:T(8,128)(2,1)S(1)}) custom-call(bf16[4,512,128]{2,1,0:T(8,128)(2,1)S(1)} %shard_map.95.refs_0_, bf16[4,512,128]{2,1,0:T(8,128)(2,1)S(1)} %copy-done.20, bf16[4,512,128]{2,1,0:T(8,128)(2,1)S(1)} %copy-done.18, bf16[4,512,128]{2,1,0:T(8,128)(2,1)S(1)} %copy-done.26, ...), custom_call_target="tpu_custom_call" | custom-call | flops 1409286144 | bytes 2752512 | tf_op jit(solution)/shard_map/pallas_call | solution.py:54
  90.2 3.0 %shard_map.100 = (f32[224,2048]{1,0:T(8,128)S(1)}, f32[512,224]{1,0:T(8,128)S(1)}) custom-call(bf16[4,512,128]{2,1,0:T(8,128)(2,1)} %collective-permute-done.8.refs_0_, bf16[4,512,128]{2,1,0:T(8,128)(2,1)} %collective-permute-done.9.refs_1_, bf16[4,512,128]{2,1,0:T(8,128)(2,1)S(1)} %collective-permute-done.15.refs_2_, ...), custom_call_target="tpu_custom_call" | custom-call | flops 939524096 | bytes 1835008 | tf_op jit(solution)/shard_map/pallas_call | solution.py:54
  93.3 1.3 copy-done.6
  95.4 2.5 %collective-permute-start.19 = (bf16[4,512,128]{2,1,0:T(8,128)(2,1)S(1)}, bf16[4,512,128]{2,1,0:T(8,128)(2,1)S(1)}, u32[]{:S(2)}, u32[]{:S(2)}) collective-permute-start(bf16[4,512,128]{2,1,0:T(8,128)(2,1)S(1)} %collective-permute-done.14.refs_1_), channel_id=1, source_target_pairs={{0,1},{1,0},{2,3},{3,2},{4,5},{5,4},{6,7},{7,6},{8,9},{9,8},{10,11... | collective-permute-start | bytes 1572872 | tf_op jit(solution)/shard_map/ppermute | solution.py:32
  101.6 4.6 %all-to-all-start.2 = ((bf16[32,32,128]{2,1,0:T(8,128)(2,1)}), bf16[32,32,128]{2,1,0:T(8,128)(2,1)S(1)}, u32[]{:S(2)}, u32[]{:S(2)}) async-start(bf16[32,32,128]{2,1,0:T(8,128)(2,1)} %shard_map.98), calls=%async_computation.2 | async-start | bytes 524288 | tf_op jit(solution)/shard_map/all_to_all | solution.py:36
  106.3 7.7 %collective-permute-done.20.refs_0_ = bf16[4,512,128]{2,1,0:T(8,128)(2,1)} collective-permute-done((bf16[4,512,128]{2,1,0:T(8,128)(2,1)}, bf16[4,512,128]{2,1,0:T(8,128)(2,1)}, u32[]{:S(2)}, u32[]{:S(2)}) %collective-permute-start.20) | collective-permute-done | bytes 524320 | tf_op jit(solution)/shard_map/ppermute | solution.py:32
  114.0 3.0 %all-to-all-done.2.refs_4_ = bf16[32,32,128]{2,1,0:T(8,128)(2,1)S(1)} async-done(((bf16[32,32,128]{2,1,0:T(8,128)(2,1)}), bf16[32,32,128]{2,1,0:T(8,128)(2,1)S(1)}, u32[]{:S(2)}, u32[]{:S(2)}) %all-to-all-start.2) | async-done | bytes 262176 | tf_op jit(solution)/shard_map/all_to_all | solution.py:36
  117.0 2.6 %collective-permute-start.21 = (bf16[4,512,128]{2,1,0:T(8,128)(2,1)}, bf16[4,512,128]{2,1,0:T(8,128)(2,1)S(1)}, u32[]{:S(2)}, u32[]{:S(2)}) collective-permute-start(bf16[4,512,128]{2,1,0:T(8,128)(2,1)} %collective-permute-done.20.refs_0_), channel_id=1, source_target_pairs={{0,1},{1,0},{2,3},{3,2},{4,5},{5,4},{6,7},{7,6},{8,9},{9,8},{10,11... | collective-permute-start | bytes 1572872 | tf_op jit(solution)/shard_map/ppermute | solution.py:32
  119.6 2.0 %copy-done.3 = bf16[224,8192]{1,0:T(8,128)(2,1)S(1)} copy-done((bf16[224,8192]{1,0:T(8,128)(2,1)S(1)}, bf16[224,8192]{1,0:T(8,128)(2,1)}, u32[]{:S(2)}) %copy-start.3) | copy-done | bytes 3670040
  121.7 2.0 %copy-done.5 = bf16[224,8192]{1,0:T(8,128)(2,1)S(1)} copy-done((bf16[224,8192]{1,0:T(8,128)(2,1)S(1)}, bf16[224,8192]{1,0:T(8,128)(2,1)}, u32[]{:S(2)}) %copy-start.5) | copy-done | bytes 3670040
  123.7 1.0 copy-done.9
  124.7 1.0 copy-done.11
  125.8 1.0 copy-done.13
  126.8 1.0 copy-done.15
  127.9 2.4 %shard_map.101 = (f32[224,2048]{1,0:T(8,128)S(1)}, f32[512,224]{1,0:T(8,128)S(1)}) custom-call(bf16[4,512,128]{2,1,0:T(8,128)(2,1)} %collective-permute-done.13.refs_0_, bf16[4,512,128]{2,1,0:T(8,128)(2,1)S(1)} %copy-done.9, bf16[4,512,128]{2,1,0:T(8,128)(2,1)S(1)} %copy-done.15, bf16[4,512,128]{2,1,0:T(8,128)(2,1)S(1)} %copy-done.13, ...), custom_call_target="tpu_custom_call" | custom-call | flops 939524096 | bytes 1835008 | tf_op jit(solution)/shard_map/pallas_call | solution.py:54
  130.3 3.8 %shard_map.102 = (f32[224,1024]{1,0:T(8,128)S(1)}, bf16[224,512]{1,0:T(8,128)(2,1)}, bf16[224,512]{1,0:T(8,128)(2,1)}) custom-call(bf16[4,512,128]{2,1,0:T(8,128)(2,1)} %collective-permute-done.20.refs_0_, bf16[4,512,128]{2,1,0:T(8,128)(2,1)S(1)} %collective-permute-done.21.refs_1_, bf16[224,512]{1,0:T(8,128)(2,1)S(1)} %get-tuple-element.50.refs_6_.refs_4_.refs_2_, ...), custom_call_target="tpu_custom_call" | custom-call | flops 469762048 | bytes 917504 | tf_op jit(solution)/shard_map/pallas_call | solution.py:54
  134.1 1.3 shard_map.103
  135.4 2.4 %collective-permute-start.25 = (f32[32,224]{1,0:T(8,128)S(1)}, f32[32,224]{1,0:T(8,128)S(1)}, u32[]{:S(2)}, u32[]{:S(2)}) collective-permute-start(f32[32,224]{1,0:T(8,128)S(1)} %get-tuple-element.75.refs_7_), channel_id=1, source_target_pairs={{0,192},{64,0},{128,64},{192,128},{1,193},{65,1},{129,65},{193,129... | collective-permute-start | bytes 86024 | tf_op jit(solution)/shard_map/ppermute | solution.py:32
  137.8 1.6 %collective-permute-start.24 = (f32[32,224]{1,0:T(8,128)S(1)}, f32[32,224]{1,0:T(8,128)S(1)}, u32[]{:S(2)}, u32[]{:S(2)}) collective-permute-start(f32[32,224]{1,0:T(8,128)S(1)} %get-tuple-element.75.refs_7_), channel_id=1, source_target_pairs={{0,128},{64,192},{128,0},{192,64},{1,129},{65,193},{129,1},{193,65... | collective-permute-start | bytes 86024 | tf_op jit(solution)/shard_map/ppermute | solution.py:32
  140.1 2.6 %shard_map.104.refs_6_ = f32[32,32]{1,0:T(8,128)S(1)} custom-call(f32[32,32]{1,0:T(8,128)S(1)} %get-tuple-element.74.gram_ref), custom_call_target="tpu_custom_call" | custom-call | tf_op jit(solution)/shard_map/pallas_call | solution.py:54
  143.7 4.0 %shard_map.105 = (bf16[224,8192]{1,0:T(8,128)(2,1)}, f32[32,224]{1,0:T(8,128)}) custom-call(f32[224,3072]{1,0:T(8,128)S(1)} %get-tuple-element.69.refs_0_, f32[224,2048]{1,0:T(8,128)S(1)} %copy-done.7, f32[224,2048]{1,0:T(8,128)S(1)} %get-tuple-element.71.refs_2_, f32[224,1024]{1,0:T(8,128)S(1)} %get-tuple-element.72.refs_3_, ...), custom_call_target="tpu_custom_call" | custom-call | flops 234881024 | bytes 11010048 | tf_op jit(solution)/shard_map/pallas_call | solution.py:54
  (76 shorter events, 13.6 us)
Async XLA Ops:
  0.6 13.1 %copy-start.16 = (bf16[512,128]{1,0:T(8,128)(2,1)S(1)}, bf16[512,128]{1,0:T(8,128)(2,1)}, u32[]{:S(2)}) copy-start(bf16[512,128]{1,0:T(8,128)(2,1)} %cotangent_ref.1) | copy-start | bytes 393220
  0.6 10.6 %collective-permute-start.3 = (bf16[512,128]{1,0:T(8,128)(2,1)}, bf16[512,128]{1,0:T(8,128)(2,1)S(1)}, u32[]{:S(2)}, u32[]{:S(2)}) collective-permute-start(bf16[512,128]{1,0:T(8,128)(2,1)} %cotangent_ref.1), channel_id=1, source_target_pairs={{0,48},{16,0},{32,16},{48,32},{1,49},{17,1},{33,17},{49,33},{2,50}... | collective-permute-start | bytes 393224 | tf_op jit(solution)/shard_map/ppermute | solution.py:32
  4.0 7.2 %collective-permute-start.2 = (bf16[512,128]{1,0:T(8,128)(2,1)}, bf16[512,128]{1,0:T(8,128)(2,1)S(1)}, u32[]{:S(2)}, u32[]{:S(2)}) collective-permute-start(bf16[512,128]{1,0:T(8,128)(2,1)} %cotangent_ref.1), channel_id=1, source_target_pairs={{0,32},{16,48},{32,0},{48,16},{1,33},{17,49},{33,1},{49,17},{2,34}... | collective-permute-start | bytes 393224 | tf_op jit(solution)/shard_map/ppermute | solution.py:32
  4.5 9.2 %collective-permute-start.1 = (bf16[512,128]{1,0:T(8,128)(2,1)}, bf16[512,128]{1,0:T(8,128)(2,1)S(1)}, u32[]{:S(2)}, u32[]{:S(2)}) collective-permute-start(bf16[512,128]{1,0:T(8,128)(2,1)} %cotangent_ref.1), channel_id=1, source_target_pairs={{0,16},{16,32},{32,48},{48,0},{1,17},{17,33},{33,49},{49,1},{2,18}... | collective-permute-start | bytes 393224 | tf_op jit(solution)/shard_map/ppermute | solution.py:32
  7.8 1.8 %copy-start = (bf16[224,8192]{1,0:T(8,128)(2,1)}, bf16[224,8192]{1,0:T(8,128)(2,1)S(1)}, u32[]{:S(2)}) copy-start(bf16[224,8192]{1,0:T(8,128)(2,1)S(1)} %get-tuple-element.51.refs_7_.refs_5_.refs_3_) | copy-start | bytes 11010052
  9.7 9.8 %collective-permute-start = (bf16[1152,128]{1,0:T(8,128)(2,1)S(1)}, bf16[1152,128]{1,0:T(8,128)(2,1)S(1)}, u32[]{:S(2)}, u32[]{:S(2)}) collective-permute-start(bf16[1152,128]{1,0:T(8,128)(2,1)S(1)} %get-tuple-element.41.send_ref), channel_id=1, source_target_pairs={{0,1},{1,0},{2,3},{3,2},{4,5},{5,4},{6,7},{7,6},{8,9},{9,8},{10,11... | collective-permute-start | bytes 884744 | tf_op jit(solution)/shard_map/ppermute | solution.py:32
  13.8 16.2 %collective-permute-start.5 = (bf16[4,512,128]{2,1,0:T(8,128)(2,1)S(1)}, bf16[4,512,128]{2,1,0:T(8,128)(2,1)S(1)}, u32[]{:S(2)}, u32[]{:S(2)}) collective-permute-start(bf16[4,512,128]{2,1,0:T(8,128)(2,1)S(1)} %shard_map.95.refs_0_), channel_id=1, source_target_pairs={{0,14},{2,0},{4,2},{6,4},{8,6},{10,8},{12,10},{14,12},{1,15},{3,1}... | collective-permute-start | bytes 1572872 | tf_op jit(solution)/shard_map/ppermute | solution.py:32
  19.5 13.7 %collective-permute-start.4 = (bf16[4,512,128]{2,1,0:T(8,128)(2,1)S(1)}, bf16[4,512,128]{2,1,0:T(8,128)(2,1)S(1)}, u32[]{:S(2)}, u32[]{:S(2)}) collective-permute-start(bf16[4,512,128]{2,1,0:T(8,128)(2,1)S(1)} %shard_map.95.refs_0_), channel_id=1, source_target_pairs={{0,2},{2,4},{4,6},{6,8},{8,10},{10,12},{12,14},{14,0},{1,3},{3,5},... | collective-permute-start | bytes 1572872 | tf_op jit(solution)/shard_map/ppermute | solution.py:32
  30.1 47.9 %copy-start.17 = (bf16[4,512,128]{2,1,0:T(8,128)(2,1)}, bf16[4,512,128]{2,1,0:T(8,128)(2,1)S(1)}, u32[]{:S(2)}) copy-start(bf16[4,512,128]{2,1,0:T(8,128)(2,1)S(1)} %collective-permute-done.5.refs_2_) | copy-start | bytes 1572868
  33.1 44.8 %copy-start.19 = (bf16[4,512,128]{2,1,0:T(8,128)(2,1)}, bf16[4,512,128]{2,1,0:T(8,128)(2,1)S(1)}, u32[]{:S(2)}) copy-start(bf16[4,512,128]{2,1,0:T(8,128)(2,1)S(1)} %collective-permute-done.4.refs_1_) | copy-start | bytes 1572868
  33.1 3.4 %collective-permute-start.6 = (bf16[4,512,128]{2,1,0:T(8,128)(2,1)S(1)}, bf16[4,512,128]{2,1,0:T(8,128)(2,1)S(1)}, u32[]{:S(2)}, u32[]{:S(2)}) collective-permute-start(bf16[4,512,128]{2,1,0:T(8,128)(2,1)S(1)} %collective-permute-done.4.refs_1_), channel_id=1, source_target_pairs={{0,1},{1,0},{2,3},{3,2},{4,5},{5,4},{6,7},{7,6},{8,9},{9,8},{10,11... | collective-permute-start | bytes 1572872 | tf_op jit(solution)/shard_map/ppermute | solution.py:32
  35.0 2.3 %collective-permute-start.7 = (bf16[4,512,128]{2,1,0:T(8,128)(2,1)S(1)}, bf16[4,512,128]{2,1,0:T(8,128)(2,1)S(1)}, u32[]{:S(2)}, u32[]{:S(2)}) collective-permute-start(bf16[4,512,128]{2,1,0:T(8,128)(2,1)S(1)} %collective-permute-done.5.refs_2_), channel_id=1, source_target_pairs={{0,1},{1,0},{2,3},{3,2},{4,5},{5,4},{6,7},{7,6},{8,9},{9,8},{10,11... | collective-permute-start | bytes 1572872 | tf_op jit(solution)/shard_map/ppermute | solution.py:32
  36.6 41.4 %copy-start.21 = (bf16[4,512,128]{2,1,0:T(8,128)(2,1)}, bf16[4,512,128]{2,1,0:T(8,128)(2,1)S(1)}, u32[]{:S(2)}) copy-start(bf16[4,512,128]{2,1,0:T(8,128)(2,1)S(1)} %collective-permute-done.6.refs_4_) | copy-start | bytes 1572868
  38.9 25.1 %all-to-all-start.1 = ((bf16[8,160,128]{2,1,0:T(8,128)(2,1)}), bf16[8,160,128]{2,1,0:T(8,128)(2,1)S(1)}, u32[]{:S(2)}, u32[]{:S(2)}) async-start(bf16[8,160,128]{2,1,0:T(8,128)(2,1)} %shard_map.96), calls=%async_computation.1 | async-start | bytes 655360 | tf_op jit(solution)/shard_map/all_to_all | solution.py:36
  42.3 21.6 %collective-permute-start.8 = (bf16[4,512,128]{2,1,0:T(8,128)(2,1)S(1)}, bf16[4,512,128]{2,1,0:T(8,128)(2,1)}, u32[]{:S(2)}, u32[]{:S(2)}) collective-permute-start(bf16[4,512,128]{2,1,0:T(8,128)(2,1)S(1)} %collective-permute-done.4.refs_1_), channel_id=1, source_target_pairs={{0,2},{2,4},{4,6},{6,8},{8,10},{10,12},{12,14},{14,0},{1,3},{3,5},... | collective-permute-start | bytes 1572872 | tf_op jit(solution)/shard_map/ppermute | solution.py:32
  43.7 20.3 %collective-permute-start.9 = (bf16[4,512,128]{2,1,0:T(8,128)(2,1)S(1)}, bf16[4,512,128]{2,1,0:T(8,128)(2,1)}, u32[]{:S(2)}, u32[]{:S(2)}) collective-permute-start(bf16[4,512,128]{2,1,0:T(8,128)(2,1)S(1)} %collective-permute-done.5.refs_2_), channel_id=1, source_target_pairs={{0,14},{2,0},{4,2},{6,4},{8,6},{10,8},{12,10},{14,12},{1,15},{3,1}... | collective-permute-start | bytes 1572872 | tf_op jit(solution)/shard_map/ppermute | solution.py:32
  45.1 23.0 %collective-permute-start.17 = (bf16[4,512,128]{2,1,0:T(8,128)(2,1)S(1)}, bf16[4,512,128]{2,1,0:T(8,128)(2,1)S(1)}, u32[]{:S(2)}, u32[]{:S(2)}) collective-permute-start(bf16[4,512,128]{2,1,0:T(8,128)(2,1)S(1)} %shard_map.95.refs_0_), channel_id=1, source_target_pairs={{0,1},{1,0},{2,3},{3,2},{4,5},{5,4},{6,7},{7,6},{8,9},{9,8},{10,11... | collective-permute-start | bytes 1572872 | tf_op jit(solution)/shard_map/ppermute | solution.py:32
  64.0 26.3 %collective-permute-start.15 = (bf16[4,512,128]{2,1,0:T(8,128)(2,1)}, bf16[4,512,128]{2,1,0:T(8,128)(2,1)S(1)}, u32[]{:S(2)}, u32[]{:S(2)}) collective-permute-start(bf16[4,512,128]{2,1,0:T(8,128)(2,1)} %collective-permute-done.8.refs_0_), channel_id=1, source_target_pairs={{0,1},{1,0},{2,3},{3,2},{4,5},{5,4},{6,7},{7,6},{8,9},{9,8},{10,11... | collective-permute-start | bytes 1572872 | tf_op jit(solution)/shard_map/ppermute | solution.py:32
  65.2 25.1 %collective-permute-start.16 = (bf16[4,512,128]{2,1,0:T(8,128)(2,1)}, bf16[4,512,128]{2,1,0:T(8,128)(2,1)S(1)}, u32[]{:S(2)}, u32[]{:S(2)}) collective-permute-start(bf16[4,512,128]{2,1,0:T(8,128)(2,1)} %collective-permute-done.9.refs_1_), channel_id=1, source_target_pairs={{0,1},{1,0},{2,3},{3,2},{4,5},{5,4},{6,7},{7,6},{8,9},{9,8},{10,11... | collective-permute-start | bytes 1572872 | tf_op jit(solution)/shard_map/ppermute | solution.py:32
  65.3 30.1 %collective-permute-start.13 = (bf16[4,512,128]{2,1,0:T(8,128)(2,1)}, bf16[4,512,128]{2,1,0:T(8,128)(2,1)}, u32[]{:S(2)}, u32[]{:S(2)}) collective-permute-start(bf16[4,512,128]{2,1,0:T(8,128)(2,1)} %collective-permute-done.8.refs_0_), channel_id=1, source_target_pairs={{0,2},{2,4},{4,6},{6,8},{8,10},{10,12},{12,14},{14,0},{1,3},{3,5},... | collective-permute-start | bytes 1572872 | tf_op jit(solution)/shard_map/ppermute | solution.py:32
  65.3 30.1 %collective-permute-start.14 = (bf16[4,512,128]{2,1,0:T(8,128)(2,1)}, bf16[4,512,128]{2,1,0:T(8,128)(2,1)S(1)}, u32[]{:S(2)}, u32[]{:S(2)}) collective-permute-start(bf16[4,512,128]{2,1,0:T(8,128)(2,1)} %collective-permute-done.9.refs_1_), channel_id=1, source_target_pairs={{0,14},{2,0},{4,2},{6,4},{8,6},{10,8},{12,10},{14,12},{1,15},{3,1}... | collective-permute-start | bytes 1572872 | tf_op jit(solution)/shard_map/ppermute | solution.py:32
  68.9 3.6 %collective-permute-start.12 = (f32[32,128]{1,0:T(8,128)S(1)}, f32[32,128]{1,0:T(8,128)S(1)}, u32[]{:S(2)}, u32[]{:S(2)}) collective-permute-start(f32[32,128]{1,0:T(8,128)S(1)} %shard_map.97.refs_0_), channel_id=1, source_target_pairs={{0,192},{64,0},{128,64},{192,128},{1,193},{65,1},{129,65},{193,129... | collective-permute-start | bytes 49160 | tf_op jit(solution)/shard_map/ppermute | solution.py:32
  72.5 4.1 %collective-permute-start.11 = (f32[32,128]{1,0:T(8,128)S(1)}, f32[32,128]{1,0:T(8,128)S(1)}, u32[]{:S(2)}, u32[]{:S(2)}) collective-permute-start(f32[32,128]{1,0:T(8,128)S(1)} %shard_map.97.refs_0_), channel_id=1, source_target_pairs={{0,128},{64,192},{128,0},{192,64},{1,129},{65,193},{129,1},{193,65... | collective-permute-start | bytes 49160 | tf_op jit(solution)/shard_map/ppermute | solution.py:32
  76.6 12.8 %collective-permute-start.10 = (f32[32,128]{1,0:T(8,128)S(1)}, f32[32,128]{1,0:T(8,128)S(1)}, u32[]{:S(2)}, u32[]{:S(2)}) collective-permute-start(f32[32,128]{1,0:T(8,128)S(1)} %shard_map.97.refs_0_), channel_id=1, source_target_pairs={{0,64},{64,128},{128,192},{192,0},{1,65},{65,129},{129,193},{193,1... | collective-permute-start | bytes 49160 | tf_op jit(solution)/shard_map/ppermute | solution.py:32
  77.9 2.0 %copy-start.1 = (bf16[224,8192]{1,0:T(8,128)(2,1)S(1)}, bf16[224,8192]{1,0:T(8,128)(2,1)}, u32[]{:S(2)}) copy-start(bf16[224,8192]{1,0:T(8,128)(2,1)} %copy-done) | copy-start | bytes 11010052
  80.0 1.0 copy-start.18
  81.0 1.0 copy-start.20
  82.1 1.0 copy-start.22
  83.1 1.0 copy-start.24
  84.2 1.0 copy-start.26
  85.2 5.0 %copy-start.2 = (bf16[224,8192]{1,0:T(8,128)(2,1)S(1)}, bf16[224,8192]{1,0:T(8,128)(2,1)}, u32[]{:S(2)}) copy-start(bf16[224,8192]{1,0:T(8,128)(2,1)} %copy-done) | copy-start | bytes 11010052
  89.4 3.9 %copy-start.4 = (bf16[224,8192]{1,0:T(8,128)(2,1)}, bf16[224,8192]{1,0:T(8,128)(2,1)S(1)}, u32[]{:S(2)}) copy-start(bf16[224,8192]{1,0:T(8,128)(2,1)S(1)} %get-tuple-element.54.refs_6_.refs_4_) | copy-start | bytes 11010052
  93.3 1.3 copy-start.6
  95.4 4.0 %collective-permute-start.19 = (bf16[4,512,128]{2,1,0:T(8,128)(2,1)S(1)}, bf16[4,512,128]{2,1,0:T(8,128)(2,1)S(1)}, u32[]{:S(2)}, u32[]{:S(2)}) collective-permute-start(bf16[4,512,128]{2,1,0:T(8,128)(2,1)S(1)} %collective-permute-done.14.refs_1_), channel_id=1, source_target_pairs={{0,1},{1,0},{2,3},{3,2},{4,5},{5,4},{6,7},{7,6},{8,9},{9,8},{10,11... | collective-permute-start | bytes 1572872 | tf_op jit(solution)/shard_map/ppermute | solution.py:32
  98.7 2.1 %collective-permute-start.18 = (bf16[4,512,128]{2,1,0:T(8,128)(2,1)}, bf16[4,512,128]{2,1,0:T(8,128)(2,1)S(1)}, u32[]{:S(2)}, u32[]{:S(2)}) collective-permute-start(bf16[4,512,128]{2,1,0:T(8,128)(2,1)} %collective-permute-done.13.refs_0_), channel_id=1, source_target_pairs={{0,1},{1,0},{2,3},{3,2},{4,5},{5,4},{6,7},{7,6},{8,9},{9,8},{10,11... | collective-permute-start | bytes 1572872 | tf_op jit(solution)/shard_map/ppermute | solution.py:32
  98.7 15.3 %collective-permute-start.20 = (bf16[4,512,128]{2,1,0:T(8,128)(2,1)}, bf16[4,512,128]{2,1,0:T(8,128)(2,1)}, u32[]{:S(2)}, u32[]{:S(2)}) collective-permute-start(bf16[4,512,128]{2,1,0:T(8,128)(2,1)} %collective-permute-done.13.refs_0_), channel_id=1, source_target_pairs={{0,2},{2,4},{4,6},{6,8},{8,10},{10,12},{12,14},{14,0},{1,3},{3,5},... | collective-permute-start | bytes 1572872 | tf_op jit(solution)/shard_map/ppermute | solution.py:32
  101.6 15.4 %all-to-all-start.2 = ((bf16[32,32,128]{2,1,0:T(8,128)(2,1)}), bf16[32,32,128]{2,1,0:T(8,128)(2,1)S(1)}, u32[]{:S(2)}, u32[]{:S(2)}) async-start(bf16[32,32,128]{2,1,0:T(8,128)(2,1)} %shard_map.98), calls=%async_computation.2 | async-start | bytes 524288 | tf_op jit(solution)/shard_map/all_to_all | solution.py:36
  117.0 13.2 %collective-permute-start.21 = (bf16[4,512,128]{2,1,0:T(8,128)(2,1)}, bf16[4,512,128]{2,1,0:T(8,128)(2,1)S(1)}, u32[]{:S(2)}, u32[]{:S(2)}) collective-permute-start(bf16[4,512,128]{2,1,0:T(8,128)(2,1)} %collective-permute-done.20.refs_0_), channel_id=1, source_target_pairs={{0,1},{1,0},{2,3},{3,2},{4,5},{5,4},{6,7},{7,6},{8,9},{9,8},{10,11... | collective-permute-start | bytes 1572872 | tf_op jit(solution)/shard_map/ppermute | solution.py:32
  119.6 14.5 %collective-permute-start.22 = (bf16[32,32,128]{2,1,0:T(8,128)(2,1)S(1)}, bf16[32,32,128]{2,1,0:T(8,128)(2,1)S(1)}, u32[]{:S(2)}, u32[]{:S(2)}) collective-permute-start(bf16[32,32,128]{2,1,0:T(8,128)(2,1)S(1)} %all-to-all-done.2.refs_4_), channel_id=1, source_target_pairs={{0,1},{1,0},{2,3},{3,2},{4,5},{5,4},{6,7},{7,6},{8,9},{9,8},{10,11... | collective-permute-start | bytes 786440 | tf_op jit(solution)/shard_map/ppermute | solution.py:32
  119.6 2.0 %copy-start.3 = (bf16[224,8192]{1,0:T(8,128)(2,1)S(1)}, bf16[224,8192]{1,0:T(8,128)(2,1)}, u32[]{:S(2)}) copy-start(bf16[224,8192]{1,0:T(8,128)(2,1)} %copy-done) | copy-start | bytes 11010052
  121.7 2.0 %copy-start.5 = (bf16[224,8192]{1,0:T(8,128)(2,1)S(1)}, bf16[224,8192]{1,0:T(8,128)(2,1)}, u32[]{:S(2)}) copy-start(bf16[224,8192]{1,0:T(8,128)(2,1)} %copy-done.4) | copy-start | bytes 11010052
  123.7 1.0 copy-start.9
  124.7 1.0 copy-start.11
  125.8 1.0 copy-start.13
  130.2 3.8 %copy-start.7 = (f32[224,2048]{1,0:T(8,128)S(1)}, f32[224,2048]{1,0:T(8,128)}, u32[]{:S(2)}) copy-start(f32[224,2048]{1,0:T(8,128)} %copy-done.6) | copy-start | bytes 5505028
  135.4 7.4 %collective-permute-start.25 = (f32[32,224]{1,0:T(8,128)S(1)}, f32[32,224]{1,0:T(8,128)S(1)}, u32[]{:S(2)}, u32[]{:S(2)}) collective-permute-start(f32[32,224]{1,0:T(8,128)S(1)} %get-tuple-element.75.refs_7_), channel_id=1, source_target_pairs={{0,192},{64,0},{128,64},{192,128},{1,193},{65,1},{129,65},{193,129... | collective-permute-start | bytes 86024 | tf_op jit(solution)/shard_map/ppermute | solution.py:32
  137.8 4.9 %collective-permute-start.24 = (f32[32,224]{1,0:T(8,128)S(1)}, f32[32,224]{1,0:T(8,128)S(1)}, u32[]{:S(2)}, u32[]{:S(2)}) collective-permute-start(f32[32,224]{1,0:T(8,128)S(1)} %get-tuple-element.75.refs_7_), channel_id=1, source_target_pairs={{0,128},{64,192},{128,0},{192,64},{1,129},{65,193},{129,1},{193,65... | collective-permute-start | bytes 86024 | tf_op jit(solution)/shard_map/ppermute | solution.py:32
  139.4 4.3 %collective-permute-start.23 = (f32[32,224]{1,0:T(8,128)S(1)}, f32[32,224]{1,0:T(8,128)S(1)}, u32[]{:S(2)}, u32[]{:S(2)}) collective-permute-start(f32[32,224]{1,0:T(8,128)S(1)} %get-tuple-element.75.refs_7_), channel_id=1, source_target_pairs={{0,64},{64,128},{128,192},{192,0},{1,65},{65,129},{129,193},{193,1... | collective-permute-start | bytes 86024 | tf_op jit(solution)/shard_map/ppermute | solution.py:32
  (7 other events, 5.9 us)

commit v7 on v5

v7 whole, which is shorter than its diff:
```python
import functools

import jax
import jax.numpy as jnp
from jax import lax
from jax.experimental import pallas as pl
from jax.experimental.pallas import tpu as pltpu
from jax.sharding import Mesh, PartitionSpec as P

BF = jnp.bfloat16
F32 = jnp.float32
X, Z, CORES = 4, 8, 2
PLANE = ("x", "z", "core")
LANES = 128
NT = (((1,), (1,)), ((), ()))
TN = (((0,), (0,)), ((), ()))
VMEM = pl.BlockSpec(memory_space=pltpu.VMEM)
HBM = pl.BlockSpec(memory_space=pltpu.HBM)
HIGHEST = lax.Precision.HIGHEST


def dot(a, b):
    return jnp.dot(a, b, preferred_element_type=F32)


def split(a):
    high = a.astype(BF)
    return high, (a - high.astype(F32)).astype(BF)


def shift(a, axis, step, n):
    return lax.ppermute(a, axis, [(i, (i + step) % n) for i in range(n)])


def exchange(a, axis):
    return lax.all_to_all(a, axis, 0, 0)


def call(kernel, out, scratch=(), ins=None, outs=None, flops=0, moved=0, vmem=16):
    outs = outs if outs is not None else [VMEM] * len(out)
    run = pl.pallas_call(
        kernel,
        in_specs=[VMEM if spec is None else spec for spec in ins],
        out_specs=[VMEM if spec is None else spec for spec in outs],
        out_shape=[jax.ShapeDtypeStruct(s, t) if spec is None else spec.memory_space(s, t) for spec, (s, t) in zip(outs, out)],
        scratch_shapes=list(scratch),
        cost_estimate=pl.CostEstimate(flops=flops, bytes_accessed=moved, transcendentals=0),
        compiler_params=pltpu.CompilerParams(vmem_limit_bytes=vmem << 20),
    )

    def placed(a, spec):
        return a if spec is None else pltpu.with_memory_space_constraint(a, spec.memory_space)

    return lambda *args: run(*(placed(a, spec) for a, spec in zip(args, ins)))


def back(axis, step, n):
    return lax.rem(lax.axis_index(axis) + (n - step), n)


def chip_of(step, hop):
    return back("x", hop, X) * Z + back("z", step, Z)


def columns_of(step, hop, wide):
    core = lax.axis_index("core")
    return [pl.multiple_of((chip_of(step, hop) * CORES + c) * wide, wide) for c in (core, 1 - core)]


def fetch(source, target, sem):
    copy = pltpu.make_async_copy(source, target, sem)
    copy.start()
    return copy


def left_kernel(gate_hbm, up_hbm, q_hbm, hidden_hbm, left_ref, gate_ref, up_ref, q_ref, hidden_ref, sems):
    rank = q_ref.shape[0]
    for copy in [fetch(a, b, sems.at[i]) for i, (a, b) in enumerate(((gate_hbm, gate_ref), (up_hbm, up_ref), (q_hbm, q_ref)))]:
        copy.wait()
    gate = gate_ref[...].astype(F32)
    hidden = (gate * jax.nn.sigmoid(gate) * up_ref[...].astype(F32)).astype(BF)
    hidden_ref[...] = hidden
    copy = fetch(hidden_ref, hidden_hbm, sems.at[3])
    left = dot(jnp.concatenate(split(q_ref[...]), axis=0), hidden)
    left = (left[:rank] + left[rank:]).astype(BF)
    for b in range(left.shape[1] // LANES):
        left_ref[b * rank:(b + 1) * rank, :] = left[:, b * LANES:(b + 1) * LANES]
    copy.wait()


def chip_kernel(left_ref, theirs_ref, out_ref):
    left = (left_ref[...].astype(F32) + theirs_ref[...].astype(F32)).astype(BF)
    for z in range(Z):
        out_ref[z] = left


def error_kernel(q_hbm, error_ref, send_ref, mine_ref, q_ref, error_buf, sems):
    rank = q_ref.shape[0]
    columns = error_ref.shape[1] // X
    small = fetch(q_hbm, q_ref, sems.at[X])
    spans = [slice(x * columns, (x + 1) * columns) for x in range(X)]
    copies = [fetch(error_ref.at[:, spans[x]], error_buf.at[:, spans[x]], sems.at[x]) for x in range(X)]
    small.wait()
    both = jnp.concatenate(split(q_ref[...]), axis=0)
    first = lax.axis_index("core") == 0
    for x in range(X):
        copies[x].wait()
        term = dot(both, error_buf[:, spans[x]])
        term = (term[:rank] + term[rank:]).astype(BF)
        for z in range(Z):
            at = (x * Z + z) * rank
            zero = term[:, (2 * z) * LANES:(2 * z + 1) * LANES]
            one = term[:, (2 * z + 1) * LANES:(2 * z + 2) * LANES]
            mine_ref[at:at + rank, :] = jnp.where(first, zero, one)
            send_ref[at:at + rank, :] = jnp.where(first, one, zero)


def stack_kernel(*refs):
    for i, ref in enumerate(refs[:-1]):
        refs[-1][i] = ref[...]


def pack_kernel(left_ref, theirs_ref, mine_ref, out_ref):
    left = left_ref[0].astype(F32)
    for z in range(1, Z):
        left = left + left_ref[z].astype(F32)
    left = left.astype(BF)
    tiles = left.shape[0]
    part = (mine_ref[...].astype(F32) + theirs_ref[...].astype(F32)).astype(BF)
    size = part.shape[0] // X
    for x in range(X):
        out_ref[x, :tiles, :] = left
        out_ref[x, tiles:, :] = part[x * size:(x + 1) * size]


def repack_kernel(terms_ref, left_ref, part_ref):
    total = terms_ref[0].astype(F32)
    for x in range(1, X):
        total = total + terms_ref[x].astype(F32)
    total = total.astype(BF)
    tiles = left_ref.shape[0]
    rank = part_ref.shape[1]
    left_ref[...] = total[:tiles]
    for z in range(Z):
        part_ref[z] = total[tiles + z * rank:tiles + (z + 1) * rank]


def slice_kernel(groups, left_ref, part_ref, cotangent_ref, out_ref):
    rank = out_ref.shape[1]
    total = part_ref[0].astype(F32)
    for z in range(1, Z):
        total = total + part_ref[z].astype(F32)
    for b in range(cotangent_ref.shape[0] // LANES):
        total = total + dot(left_ref[b * rank:(b + 1) * rank, :], cotangent_ref[b * LANES:(b + 1) * LANES, :])
    total = total / groups
    for g in range(groups):
        out_ref[g] = total


def spread_kernel(terms_ref, out_ref):
    total = terms_ref[0]
    for g in range(1, terms_ref.shape[0]):
        total = total + terms_ref[g]
    total = total.astype(BF)
    for i in range(out_ref.shape[0]):
        out_ref[i] = total


def ordered_sum(refs, buf):
    n = len(refs)
    for k, ref in enumerate(refs):
        buf[back("dp", k, n)] = ref[...]
    total = buf[0]
    for g in range(1, n):
        total = total + buf[g]
    return total


def slab(ref, step, wide):
    return jnp.concatenate([ref[:, pl.ds(at, wide)] for hop in range(X) for at in columns_of(step, hop, wide)], axis=1)


def wait_all(copies):
    for copy in copies:
        copy.wait()


def piece_kernel(steps, *refs):
    n = len(steps)
    own, other = refs[:n], refs[n:2 * n]
    hidden_hbm, error_hbm, weight_hbm, gate_hbm, up_hbm, matrix_hbm, short_hbm, d_gate_ref, d_up_ref = refs[2 * n:2 * n + 9]
    own_buf, other_buf, hidden_ref, error_ref, weight_ref, gate_ref, up_ref, matrix_ref, short_ref, sems = refs[2 * n + 9:]
    wide = own_buf.shape[3]
    width = matrix_ref.shape[1] // n
    both = [fetch(hidden_hbm, hidden_ref, sems.at[0, n]), fetch(error_hbm, error_ref, sems.at[1, n])]
    copies = []
    for i in range(n):
        copies.append([fetch(own[i], own_buf.at[i], sems.at[0, i]), fetch(other[i], other_buf.at[i], sems.at[1, i])])
        if i == 0:
            late = [fetch(weight_hbm, weight_ref, sems.at[2, n])]
    pair = [fetch(gate_hbm, gate_ref, sems.at[0, n + 1]), fetch(up_hbm, up_ref, sems.at[1, n + 1])]
    wait_all(both)
    out = []
    total = None
    for i, step in enumerate(steps):
        wait_all(copies[i])
        block = jnp.concatenate([buf[i, hop] for hop in range(X) for buf in (own_buf, other_buf)], axis=1)
        span = pl.ds(i * width, width)
        matrix = slab(error_ref, step, wide).astype(F32) + dot(hidden_ref[...], block)
        matrix_ref[:, span] = matrix
        short_ref[:, span] = matrix.astype(BF)
        out.append(fetch(matrix_ref.at[:, span], matrix_hbm.at[:, span], sems.at[2, i]))
        out.append(fetch(short_ref.at[:, span], short_hbm.at[:, span], sems.at[3, i]))
        if i == 0:
            wait_all(late)
        term = lax.dot_general(block, slab(weight_ref, step, wide), NT, preferred_element_type=F32)
        total = term if total is None else total + term
    wait_all(pair)
    total = total.T
    gate = gate_ref[...].astype(F32)
    sigma = jax.nn.sigmoid(gate)
    d_gate_ref[...] = (total * up_ref[...].astype(F32) * sigma * (1.0 + gate * (1.0 - sigma))).astype(BF)
    d_up_ref[...] = (total * (gate * sigma)).astype(BF)
    wait_all(out)


def use_pieces(steps, own, other, hidden, error, weight, gate, upward):
    n = len(steps)
    tokens, wide = own[0].shape[1:]
    rows, columns = error.shape
    return call(
        functools.partial(piece_kernel, steps),
        [((rows, columns), F32), ((rows, columns), BF), ((rows, tokens), BF), ((rows, tokens), BF)],
        [
            pltpu.VMEM((n, X, tokens, wide), BF),
            pltpu.VMEM((n, X, tokens, wide), BF),
            pltpu.VMEM((rows, tokens), BF),
            pltpu.VMEM((rows, columns), BF),
            pltpu.VMEM((rows, columns), BF),
            pltpu.VMEM((rows, tokens), BF),
            pltpu.VMEM((rows, tokens), BF),
            pltpu.VMEM((rows, columns), F32),
            pltpu.VMEM((rows, columns), BF),
            pltpu.SemaphoreType.DMA((4, n + 2)),
        ],
        [HBM] * (2 * n + 5),
        [HBM, HBM, None, None],
        flops=4 * rows * tokens * columns,
        moved=30 << 20,
        vmem=52,
    )(*own, *other, hidden, error, weight, gate, upward)


def turn_kernel(steps, short_hbm, mine_ref, theirs_ref, out_ref, gram_ref, short_ref, sems):
    width = short_ref.shape[1] // len(steps)
    spans = [slice(i * width, (i + 1) * width) for i in range(len(steps))]
    copies = [fetch(short_hbm.at[:, span], short_ref.at[:, span], sems.at[i]) for i, span in enumerate(spans)]
    total, gram = 0.0, 0.0
    for i, step in enumerate(steps):
        basis = jnp.concatenate([ref[chip_of(step, hop)] for hop in range(X) for ref in (mine_ref, theirs_ref)], axis=1)
        gram = gram + lax.dot_general(basis, basis, NT, preferred_element_type=F32)
        copies[i].wait()
        total = total + lax.dot_general(short_ref[:, spans[i]], basis, NT, preferred_element_type=F32)
    gram_ref[...] = gram
    out_ref[...] = total.T


def inverse_kernel(gram_ref, out_ref):
    n = gram_ref.shape[0]
    row = lax.broadcasted_iota(jnp.int32, (n, 2 * n), 0)
    col = lax.broadcasted_iota(jnp.int32, (n, 2 * n), 1)
    both = jnp.concatenate([gram_ref[...], jnp.zeros((n, n), F32)], axis=1) + jnp.where(col == row + n, 1.0, 0.0)
    for k in range(n):
        pivot = both[k:k + 1, k:k + 1]
        scaled = both[k:k + 1, :] * lax.rsqrt(pivot)
        column_k = both[:, k:k + 1] * lax.rsqrt(pivot)
        both = jnp.where(row > k, both - column_k * scaled, jnp.where(row == k, scaled, both))
    out_ref[...] = both[:, n:]


def final_kernel(steps, groups, *refs):
    matrix_ref, mine_ref, theirs_ref, inverse_ref = refs[:4]
    out_ref, q_ref, buf, terms_buf, sems = refs[4 + groups:]
    wide = mine_ref.shape[2]
    width = CORES * wide
    span = buf.shape[1] // X
    total = ordered_sum(refs[4:4 + groups], terms_buf)
    inverse = inverse_ref[...]
    next_q = jnp.dot(inverse, total / groups, precision=HIGHEST, preferred_element_type=F32)
    q_ref[...] = next_q
    factor = lax.dot_general(inverse, next_q, TN, precision=HIGHEST, preferred_element_type=F32)
    high, low = split(factor.T)
    factor = jnp.concatenate([high, low], axis=1)
    copies = []
    for hop in range(X):
        for i, step in enumerate(steps):
            at = chip_of(step, hop)
            basis = jnp.concatenate([mine_ref[at], theirs_ref[at]], axis=1)
            basis = jnp.concatenate([basis, basis], axis=0)
            start = (i * X + hop) * width
            result = (matrix_ref[:, start:start + width] - dot(factor, basis)).astype(BF)
            for c, place in enumerate(columns_of(step, hop, wide)):
                buf[:, pl.ds(place, wide)] = result[:, c * wide:(c + 1) * wide]
        part = pl.ds(pl.multiple_of(back("x", hop, X) * span, span), span)
        copies.append(fetch(buf.at[:, part], out_ref.at[:, part], sems.at[hop]))
    wait_all(copies)


def local(gate, upward, cotangent, down_weight, error_buffer, start_q):
    groups = lax.axis_size("dp")
    rank = start_q.shape[1]
    tokens, wide = cotangent.shape
    error = error_buffer[0]
    rows, columns = error.shape
    tiles = tokens // LANES * rank
    tie = lax.optimization_barrier

    blocks = [cotangent] + [shift(cotangent, "x", hop, X) for hop in range(1, X)]
    hidden, left = call(
        left_kernel,
        [((rows, tokens), BF), ((tiles, LANES), BF)],
        [
            pltpu.VMEM((rows, tokens), BF),
            pltpu.VMEM((rows, tokens), BF),
            pltpu.VMEM((rank, rows), F32),
            pltpu.VMEM((rows, tokens), BF),
            pltpu.SemaphoreType.DMA((4,)),
        ],
        [HBM] * 3,
        [HBM, VMEM],
        moved=6 * rows * tokens,
    )(gate.T, upward.T, start_q.T)
    theirs = shift(left, "core", 1, CORES)
    send, mine = call(
        error_kernel,
        [((X * Z * rank, wide), BF), ((X * Z * rank, wide), BF)],
        [pltpu.VMEM((rank, rows), F32), pltpu.VMEM((rows, columns), BF), pltpu.SemaphoreType.DMA((X + 1,))],
        [HBM, HBM],
        flops=4 * rows * rank * columns,
        moved=2 * rows * columns,
    )(start_q.T, error)
    part = shift(send, "core", 1, CORES)
    tied = tie((left, theirs, *blocks[1:]))
    left, theirs, blocks[1:] = tied[0], tied[1], tied[2:]
    stacked, = call(stack_kernel, [((X, tokens, wide), BF)], ins=[None] * X, outs=[None])(*blocks)
    pieces, others = {0: stacked}, {}
    steps = (0, 1, 7, 2, 6, 3, 5, 4)

    def ring(step, payload=None):
        up, down = pieces[step - 1], pieces[(Z - step + 1) % Z]
        if payload is not None:
            payload, up, down = tie((payload, up, down))
        pieces[step] = shift(up, "z", 1, Z)
        if step < Z // 2:
            pieces[Z - step] = shift(down, "z", Z - 1, Z)
        return payload

    def swap(*steps):
        for step in steps:
            others[step] = shift(pieces[step], "core", 1, CORES)

    left, = call(chip_kernel, [((Z, tiles, LANES), BF)], ins=[VMEM, VMEM])(left, theirs)
    left = ring(1, left)
    swap(0)
    left = exchange(left, "z")
    left, pieces[1], pieces[7] = tie((left, pieces[1], pieces[7]))
    terms, = call(pack_kernel, [((X, tiles + Z * rank, wide), BF)], ins=[VMEM] * 3)(left, part, mine)
    terms = ring(2, terms)
    swap(1, 7)
    terms = exchange(terms, "x")
    terms, pieces[2], pieces[6] = tie((terms, pieces[2], pieces[6]))
    left, part = call(repack_kernel, [((tiles, LANES), BF), ((Z, rank, wide), BF)], ins=[VMEM])(terms)
    part = ring(3, part)
    swap(2, 6)
    part = exchange(part, "z")
    part, pieces[3], pieces[5] = tie((part, pieces[3], pieces[5]))
    terms, = call(functools.partial(slice_kernel, groups), [((groups, rank, wide), F32)], ins=[VMEM, VMEM, None])(left, part, cotangent)
    terms = ring(4, terms)
    swap(3, 5)
    terms = exchange(terms, "dp")
    terms, pieces[4] = tie((terms, pieces[4]))
    mine, = call(spread_kernel, [((X * Z, rank, wide), BF)], ins=[VMEM])(terms)
    mine = exchange(mine, ("x", "z"))
    swap(4)
    matrix, short, d_gate, d_up = use_pieces(
        steps, [pieces[s] for s in steps], [others[s] for s in steps], hidden, error, down_weight, gate.T, upward.T)
    mine, short = tie((mine, short))
    theirs = shift(mine, "core", 1, CORES)

    terms, gram = call(
        functools.partial(turn_kernel, steps),
        [((rank, rows), F32), ((rank, rank), F32)],
        [pltpu.VMEM((rows, columns), BF), pltpu.SemaphoreType.DMA((Z,))],
        [HBM, VMEM, VMEM],
        flops=2 * rows * rank * columns,
        moved=4 * rows * columns,
    )(short, mine, theirs)
    terms = [terms] + [shift(terms, "dp", k, groups) for k in range(1, groups)]
    inverse, = call(inverse_kernel, [((rank, rank), F32)], ins=[VMEM])(gram)

    new_error, next_q = call(
        functools.partial(final_kernel, steps, groups),
        [((rows, columns), BF), ((rank, rows), F32)],
        [pltpu.VMEM((rows, columns), BF), pltpu.VMEM((groups, rank, rows), F32), pltpu.SemaphoreType.DMA((X,))],
        [VMEM] * (4 + groups),
        [HBM, None],
        flops=4 * rows * rank * columns,
        moved=6 * rows * columns,
    )(matrix, mine, theirs, inverse, *terms)
    return (d_gate.T, d_up.T, new_error[None], next_q.T)


def solution(mesh):
    mesh = Mesh(mesh.devices.reshape(mesh.shape["dp"], X, Z, CORES), ("dp",) + PLANE)
    in_specs = (
        P("dp", PLANE),
        P("dp", PLANE),
        P("dp", PLANE),
        P(PLANE, None),
        P("dp", PLANE, None),
        P(PLANE, None),
    )
    out_specs = (P("dp", PLANE), P("dp", PLANE), P("dp", PLANE, None), P(PLANE, None))
    return jax.shard_map(local, mesh=mesh, in_specs=in_specs, out_specs=out_specs, check_vma=False)
```

time: 137 us -> 120 us (0.88)
  the two profiles are of different devices: /device:TPU:96 before, /device:TPU:1 now
where the time goes in v7:
time: 120 us
  starting transfers between devices  56.3 us (47%)
  Pallas kernels  27.9 us (23%)
  blocking collectives  22.5 us (19%)
  waiting for transfers between devices  7.84 us (7%)
  local copies, waits for them, and re-layouts  4.01 us (3%)
    ppermute x24, starting transfers between devices, shift(): return lax.ppermute(a, axis, [(i, (i + step) % n) for i in range(n)])  39.6 us
    pallas_call x12, Pallas kernels, call(): return lambda *args: run(*(placed(a, spec) for a, spec in zip(args, ins)))  27.9 us
    all_to_all x2, blocking collectives, exchange(): return lax.all_to_all(a, axis, 0, 0)  22.5 us
    all_to_all x3, starting transfers between devices, exchange(): return lax.all_to_all(a, axis, 0, 0)  16.7 us
    all_to_all x3, waiting for transfers between devices, exchange(): return lax.all_to_all(a, axis, 0, 0)  5.29 us
    unnamed x18, local copies, waits for them, and re-layouts  4.01 us
    ppermute x24, waiting for transfers between devices, shift(): return lax.ppermute(a, axis, [(i, (i + step) % n) for i in range(n)])  2.55 us
  transfers between devices with their start and end apart: 27, of which 5 were waited for; matrix products, arithmetic and copies ran while one was open for 0% of the time, Pallas kernels for 16%

profile of v7, /device:TPU:1, one launch (start us, length us, event | category | flops | bytes accessed | tf_op | source)
XLA Modules:
  0.0 119.5 jit_solution(8101879266909334066)
XLA Ops:
  0.6 2.1 %collective-permute-start.1 = (bf16[512,128]{1,0:T(8,128)(2,1)}, bf16[512,128]{1,0:T(8,128)(2,1)S(1)}, u32[]{:S(2)}, u32[]{:S(2)}) collective-permute-start(bf16[512,128]{1,0:T(8,128)(2,1)} %cotangent_ref.1), channel_id=1, source_target_pairs={{0,16},{16,32},{32,48},{48,0},{1,17},{17,33},{33,49},{49,1},{2,18}... | collective-permute-start | bytes 393224 | tf_op jit(solution)/shard_map/ppermute | solution.py:32
  2.7 2.5 %collective-permute-start.2 = (bf16[512,128]{1,0:T(8,128)(2,1)}, bf16[512,128]{1,0:T(8,128)(2,1)S(1)}, u32[]{:S(2)}, u32[]{:S(2)}) collective-permute-start(bf16[512,128]{1,0:T(8,128)(2,1)} %cotangent_ref.1), channel_id=1, source_target_pairs={{0,32},{16,48},{32,0},{48,16},{1,33},{17,49},{33,1},{49,17},{2,34}... | collective-permute-start | bytes 393224 | tf_op jit(solution)/shard_map/ppermute | solution.py:32
  5.2 1.2 collective-permute-start.3
  6.4 1.9 %shard_map.93 = (bf16[224,512]{1,0:T(8,128)(2,1)}, bf16[128,128]{1,0:T(8,128)(2,1)S(1)}) custom-call(bf16[224,512]{1,0:T(8,128)(2,1)} %bitcast.10, bf16[224,512]{1,0:T(8,128)(2,1)} %bitcast.12, f32[32,224]{1,0:T(8,128)} %bitcast.14), custom_call_target="tpu_custom_call" | custom-call | bytes 688128 | tf_op jit(solution)/shard_map/pallas_call | solution.py:54
  8.2 1.6 %collective-permute-start = (bf16[128,128]{1,0:T(8,128)(2,1)S(1)}, bf16[128,128]{1,0:T(8,128)(2,1)S(1)}, u32[]{:S(2)}, u32[]{:S(2)}) collective-permute-start(bf16[128,128]{1,0:T(8,128)(2,1)S(1)} %get-tuple-element.51.left_ref), channel_id=1, source_target_pairs={{0,1},{1,0},{2,3},{3,2},{4,5},{5,4},{6,7},{7,6},{8,9},{9,8},{10,11... | collective-permute-start | bytes 98312 | tf_op jit(solution)/shard_map/ppermute | solution.py:32
  9.8 0.9 collective-permute-done.theirs_ref
  10.7 0.0 collective-permute-done.1.refs_1_
  10.7 0.4 collective-permute-done.2.refs_2_
  11.1 0.7 shard_map.95
  11.8 0.9 copy-done.2
  12.8 1.7 %collective-permute-start.4 = (bf16[4,512,128]{2,1,0:T(8,128)(2,1)S(1)}, bf16[4,512,128]{2,1,0:T(8,128)(2,1)S(1)}, u32[]{:S(2)}, u32[]{:S(2)}) collective-permute-start(bf16[4,512,128]{2,1,0:T(8,128)(2,1)S(1)} %shard_map.94.refs_0_), channel_id=1, source_target_pairs={{0,2},{2,4},{4,6},{6,8},{8,10},{10,12},{12,14},{14,0},{1,3},{3,5},... | collective-permute-start | bytes 1572872 | tf_op jit(solution)/shard_map/ppermute | solution.py:32
  14.5 4.0 %collective-permute-start.5 = (bf16[4,512,128]{2,1,0:T(8,128)(2,1)S(1)}, bf16[4,512,128]{2,1,0:T(8,128)(2,1)S(1)}, u32[]{:S(2)}, u32[]{:S(2)}) collective-permute-start(bf16[4,512,128]{2,1,0:T(8,128)(2,1)S(1)} %shard_map.94.refs_0_), channel_id=1, source_target_pairs={{0,14},{2,0},{4,2},{6,4},{8,6},{10,8},{12,10},{14,12},{1,15},{3,1}... | collective-permute-start | bytes 1572872 | tf_op jit(solution)/shard_map/ppermute | solution.py:32
  18.5 5.2 %all-to-all-start = ((bf16[8,128,128]{2,1,0:T(8,128)(2,1)}), bf16[8,128,128]{2,1,0:T(8,128)(2,1)S(1)}, u32[]{:S(2)}, u32[]{:S(2)}) async-start(bf16[8,128,128]{2,1,0:T(8,128)(2,1)} %shard_map.95), calls=%async_computation | async-start | bytes 524288 | tf_op jit(solution)/shard_map/all_to_all | solution.py:36
  23.7 2.4 %shard_map.96 = (bf16[1024,128]{1,0:T(8,128)(2,1)S(1)}, bf16[1024,128]{1,0:T(8,128)(2,1)S(1)}) custom-call(f32[32,224]{1,0:T(8,128)} %bitcast.15, bf16[224,8192]{1,0:T(8,128)(2,1)} %bitcast.8), custom_call_target="tpu_custom_call" | custom-call | flops 234881024 | bytes 3670016 | tf_op jit(solution)/shard_map/pallas_call | solution.py:54
  26.2 2.5 %collective-permute-start.6 = (bf16[1024,128]{1,0:T(8,128)(2,1)S(1)}, bf16[1024,128]{1,0:T(8,128)(2,1)S(1)}, u32[]{:S(2)}, u32[]{:S(2)}) collective-permute-start(bf16[1024,128]{1,0:T(8,128)(2,1)S(1)} %get-tuple-element.59), channel_id=1, source_target_pairs={{0,1},{1,0},{2,3},{3,2},{4,5},{5,4},{6,7},{7,6},{8,9},{9,8},{10,11... | collective-permute-start | bytes 786440 | tf_op jit(solution)/shard_map/ppermute | solution.py:32
  28.7 5.3 %all-to-all-done.left_ref = bf16[8,128,128]{2,1,0:T(8,128)(2,1)S(1)} async-done(((bf16[8,128,128]{2,1,0:T(8,128)(2,1)}), bf16[8,128,128]{2,1,0:T(8,128)(2,1)S(1)}, u32[]{:S(2)}, u32[]{:S(2)}) %all-to-all-start) | async-done | bytes 262176 | tf_op jit(solution)/shard_map/all_to_all | solution.py:36
  34.0 0.1 shard_map.97
  34.1 2.6 %collective-permute-start.7 = (bf16[4,512,128]{2,1,0:T(8,128)(2,1)S(1)}, bf16[4,512,128]{2,1,0:T(8,128)(2,1)S(1)}, u32[]{:S(2)}, u32[]{:S(2)}) collective-permute-start(bf16[4,512,128]{2,1,0:T(8,128)(2,1)S(1)} %collective-permute-done.4.refs_1_), channel_id=1, source_target_pairs={{0,2},{2,4},{4,6},{6,8},{8,10},{10,12},{12,14},{14,0},{1,3},{3,5},... | collective-permute-start | bytes 1572872 | tf_op jit(solution)/shard_map/ppermute | solution.py:32
  36.7 0.1 collective-permute-start.8
  36.8 9.8 %all_to_all.25.terms_ref = bf16[4,384,128]{2,1,0:T(8,128)(2,1)S(1)} all-to-all(bf16[4,384,128]{2,1,0:T(8,128)(2,1)S(1)} %shard_map.97), channel_id=1, replica_groups=mesh['dp'=4,'x'=4,'z'=8,'core'=2] {'x'}, dimensions={0} | all-to-all | bytes 786432 | tf_op jit(solution)/shard_map/all_to_all | solution.py:36
  46.7 0.1 shard_map.98
  46.7 0.5 collective-permute-start.10
  47.3 1.1 collective-permute-start.9
  48.4 12.7 %all_to_all.26.part_ref = bf16[8,32,128]{2,1,0:T(8,128)(2,1)S(1)} all-to-all(bf16[8,32,128]{2,1,0:T(8,128)(2,1)S(1)} %get-tuple-element.68), channel_id=1, replica_groups=mesh['dp'=4,'x'=4,'z'=8,'core'=2] {'z'}, dimensions={0} | all-to-all | bytes 131072 | tf_op jit(solution)/shard_map/all_to_all | solution.py:36
  61.1 0.8 shard_map.99
  61.9 0.3 collective-permute-start.11
  62.2 6.4 %collective-permute-start.12 = (bf16[4,512,128]{2,1,0:T(8,128)(2,1)S(1)}, bf16[4,512,128]{2,1,0:T(8,128)(2,1)}, u32[]{:S(2)}, u32[]{:S(2)}) collective-permute-start(bf16[4,512,128]{2,1,0:T(8,128)(2,1)S(1)} %shard_map.94.refs_0_), channel_id=1, source_target_pairs={{0,1},{1,0},{2,3},{3,2},{4,5},{5,4},{6,7},{7,6},{8,9},{9,8},{10,11... | collective-permute-start | bytes 1572872 | tf_op jit(solution)/shard_map/ppermute | solution.py:32
  68.6 0.5 collective-permute-start.14
  69.1 4.2 %all-to-all-start.3 = ((f32[4,32,128]{2,1,0:T(8,128)}), f32[4,32,128]{2,1,0:T(8,128)S(1)}, u32[]{:S(2)}, u32[]{:S(2)}) async-start(f32[4,32,128]{2,1,0:T(8,128)} %shard_map.99), calls=%async_computation.3 | async-start | bytes 131072 | tf_op jit(solution)/shard_map/all_to_all | solution.py:36
  73.3 0.3 collective-permute-start.15
  73.6 5.5 %collective-permute-start.16 = (bf16[4,512,128]{2,1,0:T(8,128)(2,1)S(1)}, bf16[4,512,128]{2,1,0:T(8,128)(2,1)}, u32[]{:S(2)}, u32[]{:S(2)}) collective-permute-start(bf16[4,512,128]{2,1,0:T(8,128)(2,1)S(1)} %collective-permute-done.8.refs_4_), channel_id=1, source_target_pairs={{0,1},{1,0},{2,3},{3,2},{4,5},{5,4},{6,7},{7,6},{8,9},{9,8},{10,11... | collective-permute-start | bytes 1572872 | tf_op jit(solution)/shard_map/ppermute | solution.py:32
  79.2 0.1 collective-permute-start.17
  79.3 0.4 collective-permute-start.18
  79.7 0.1 collective-permute-start.19
  79.8 0.7 shard_map.101
  80.5 7.3 %all-to-all-start.4 = ((bf16[32,32,128]{2,1,0:T(8,128)(2,1)}), bf16[32,32,128]{2,1,0:T(8,128)(2,1)S(1)}, u32[]{:S(2)}, u32[]{:S(2)}) async-start(bf16[32,32,128]{2,1,0:T(8,128)(2,1)} %shard_map.101), calls=%async_computation.4 | async-start | bytes 524288 | tf_op jit(solution)/shard_map/all_to_all | solution.py:36
  88.0 11.1 %shard_map.100 = (f32[224,8192]{1,0:T(8,128)}, bf16[224,8192]{1,0:T(8,128)(2,1)}, bf16[224,512]{1,0:T(8,128)(2,1)}, bf16[224,512]{1,0:T(8,128)(2,1)}) custom-call(bf16[4,512,128]{2,1,0:T(8,128)(2,1)} %copy-done.1, bf16[4,512,128]{2,1,0:T(8,128)(2,1)} %copy-done.4, bf16[4,512,128]{2,1,0:T(8,128)(2,1)} %copy-done.5, bf16[4,512,128]{2,1,0:T(8,128)(2,1)} %copy-done.6, ...), custom_call_target="tpu_custom_call" | custom-call | flops 3758096384 | bytes 31457280 | tf_op jit(solution)/shard_map/pallas_call | solution.py:54
  99.1 1.7 %collective-permute-start.20 = (bf16[32,32,128]{2,1,0:T(8,128)(2,1)S(1)}, bf16[32,32,128]{2,1,0:T(8,128)(2,1)S(1)}, u32[]{:S(2)}, u32[]{:S(2)}) collective-permute-start(bf16[32,32,128]{2,1,0:T(8,128)(2,1)S(1)} %all-to-all-done.4.mine_ref.refs_1_), channel_id=1, source_target_pairs={{0,1},{1,0},{2,3},{3,2},{4,5},{5,4},{6,7},{7,6},{8,9},{9,8},{10,11... | collective-permute-start | bytes 786440 | tf_op jit(solution)/shard_map/ppermute | solution.py:32
  100.8 1.2 collective-permute-done.20.theirs_ref.refs_2_
  101.9 3.4 %shard_map.102 = (f32[32,224]{1,0:T(8,128)S(1)}, f32[32,32]{1,0:T(8,128)S(1)}) custom-call(bf16[224,8192]{1,0:T(8,128)(2,1)} %get-tuple-element.85.short_hbm, bf16[32,32,128]{2,1,0:T(8,128)(2,1)S(1)} %all-to-all-done.4.mine_ref.refs_1_, bf16[32,32,128]{2,1,0:T(8,128)(2,1)S(1)} %collective-permute-done.20.theirs_ref.refs_2_), custom_call_target="tpu_custom_call" | custom-call | flops 117440512 | bytes 7340032 | tf_op jit(solution)/shard_map/pallas_call | solution.py:54
  105.3 0.5 collective-permute-start.21
  105.9 2.7 %collective-permute-start.22 = (f32[32,224]{1,0:T(8,128)S(1)}, f32[32,224]{1,0:T(8,128)S(1)}, u32[]{:S(2)}, u32[]{:S(2)}) collective-permute-start(f32[32,224]{1,0:T(8,128)S(1)} %get-tuple-element.87.refs_4_), channel_id=1, source_target_pairs={{0,128},{64,192},{128,0},{192,64},{1,129},{65,193},{129,1},{193,65... | collective-permute-start | bytes 86024 | tf_op jit(solution)/shard_map/ppermute | solution.py:32
  108.5 1.1 collective-permute-start.23
  109.6 2.6 %shard_map.103.refs_3_ = f32[32,32]{1,0:T(8,128)S(1)} custom-call(f32[32,32]{1,0:T(8,128)S(1)} %get-tuple-element.86.gram_ref), custom_call_target="tpu_custom_call" | custom-call | tf_op jit(solution)/shard_map/pallas_call | solution.py:54
  112.2 0.0 collective-permute-done.22.refs_6_
  112.2 0.1 collective-permute-done.23.refs_7_
  112.3 3.1 %copy-done = f32[224,8192]{1,0:T(8,128)S(1)} copy-done((f32[224,8192]{1,0:T(8,128)S(1)}, f32[224,8192]{1,0:T(8,128)}, u32[]{:S(2)}) %copy-start) | copy-done | bytes 7340056
  115.4 4.0 %shard_map.104 = (bf16[224,8192]{1,0:T(8,128)(2,1)}, f32[32,224]{1,0:T(8,128)}) custom-call(f32[224,8192]{1,0:T(8,128)S(1)} %copy-done, bf16[32,32,128]{2,1,0:T(8,128)(2,1)S(1)} %all-to-all-done.4.mine_ref.refs_1_, bf16[32,32,128]{2,1,0:T(8,128)(2,1)S(1)} %collective-permute-done.20.theirs_ref.refs_2_, f32[32,32]{1,0:T(8,128)S(1)} %shard_map.103.refs_3_, ...), custom_call_target="tpu_custom_call" | custom-call | flops 234881024 | bytes 11010048 | tf_op jit(solution)/shard_map/pallas_call | solution.py:54
  (38 shorter events, 0.1 us)
Async XLA Ops:
  0.6 10.1 %collective-permute-start.1 = (bf16[512,128]{1,0:T(8,128)(2,1)}, bf16[512,128]{1,0:T(8,128)(2,1)S(1)}, u32[]{:S(2)}, u32[]{:S(2)}) collective-permute-start(bf16[512,128]{1,0:T(8,128)(2,1)} %cotangent_ref.1), channel_id=1, source_target_pairs={{0,16},{16,32},{32,48},{48,0},{1,17},{17,33},{33,49},{49,1},{2,18}... | collective-permute-start | bytes 393224 | tf_op jit(solution)/shard_map/ppermute | solution.py:32
  2.7 8.4 %collective-permute-start.2 = (bf16[512,128]{1,0:T(8,128)(2,1)}, bf16[512,128]{1,0:T(8,128)(2,1)S(1)}, u32[]{:S(2)}, u32[]{:S(2)}) collective-permute-start(bf16[512,128]{1,0:T(8,128)(2,1)} %cotangent_ref.1), channel_id=1, source_target_pairs={{0,32},{16,48},{32,0},{48,16},{1,33},{17,49},{33,1},{49,17},{2,34}... | collective-permute-start | bytes 393224 | tf_op jit(solution)/shard_map/ppermute | solution.py:32
  5.2 5.9 %collective-permute-start.3 = (bf16[512,128]{1,0:T(8,128)(2,1)}, bf16[512,128]{1,0:T(8,128)(2,1)S(1)}, u32[]{:S(2)}, u32[]{:S(2)}) collective-permute-start(bf16[512,128]{1,0:T(8,128)(2,1)} %cotangent_ref.1), channel_id=1, source_target_pairs={{0,48},{16,0},{32,16},{48,32},{1,49},{17,1},{33,17},{49,33},{2,50}... | collective-permute-start | bytes 393224 | tf_op jit(solution)/shard_map/ppermute | solution.py:32
  8.2 2.5 %collective-permute-start = (bf16[128,128]{1,0:T(8,128)(2,1)S(1)}, bf16[128,128]{1,0:T(8,128)(2,1)S(1)}, u32[]{:S(2)}, u32[]{:S(2)}) collective-permute-start(bf16[128,128]{1,0:T(8,128)(2,1)S(1)} %get-tuple-element.51.left_ref), channel_id=1, source_target_pairs={{0,1},{1,0},{2,3},{3,2},{4,5},{5,4},{6,7},{7,6},{8,9},{9,8},{10,11... | collective-permute-start | bytes 98312 | tf_op jit(solution)/shard_map/ppermute | solution.py:32
  11.8 0.9 copy-start.2
  12.7 48.3 %copy-start.3 = (bf16[512,128]{1,0:T(8,128)(2,1)S(1)}, bf16[512,128]{1,0:T(8,128)(2,1)}, u32[]{:S(2)}) copy-start(bf16[512,128]{1,0:T(8,128)(2,1)} %cotangent_ref.1) | copy-start | bytes 393220
  12.8 67.7 %copy-start.1 = (bf16[4,512,128]{2,1,0:T(8,128)(2,1)}, bf16[4,512,128]{2,1,0:T(8,128)(2,1)S(1)}, u32[]{:S(2)}) copy-start(bf16[4,512,128]{2,1,0:T(8,128)(2,1)S(1)} %shard_map.94.refs_0_) | copy-start | bytes 1572868
  12.8 21.1 %collective-permute-start.4 = (bf16[4,512,128]{2,1,0:T(8,128)(2,1)S(1)}, bf16[4,512,128]{2,1,0:T(8,128)(2,1)S(1)}, u32[]{:S(2)}, u32[]{:S(2)}) collective-permute-start(bf16[4,512,128]{2,1,0:T(8,128)(2,1)S(1)} %shard_map.94.refs_0_), channel_id=1, source_target_pairs={{0,2},{2,4},{4,6},{6,8},{8,10},{10,12},{12,14},{14,0},{1,3},{3,5},... | collective-permute-start | bytes 1572872 | tf_op jit(solution)/shard_map/ppermute | solution.py:32
  14.5 19.4 %collective-permute-start.5 = (bf16[4,512,128]{2,1,0:T(8,128)(2,1)S(1)}, bf16[4,512,128]{2,1,0:T(8,128)(2,1)S(1)}, u32[]{:S(2)}, u32[]{:S(2)}) collective-permute-start(bf16[4,512,128]{2,1,0:T(8,128)(2,1)S(1)} %shard_map.94.refs_0_), channel_id=1, source_target_pairs={{0,14},{2,0},{4,2},{6,4},{8,6},{10,8},{12,10},{14,12},{1,15},{3,1}... | collective-permute-start | bytes 1572872 | tf_op jit(solution)/shard_map/ppermute | solution.py:32
  18.5 15.4 %all-to-all-start = ((bf16[8,128,128]{2,1,0:T(8,128)(2,1)}), bf16[8,128,128]{2,1,0:T(8,128)(2,1)S(1)}, u32[]{:S(2)}, u32[]{:S(2)}) async-start(bf16[8,128,128]{2,1,0:T(8,128)(2,1)} %shard_map.95), calls=%async_computation | async-start | bytes 524288 | tf_op jit(solution)/shard_map/all_to_all | solution.py:36
  26.2 7.8 %collective-permute-start.6 = (bf16[1024,128]{1,0:T(8,128)(2,1)S(1)}, bf16[1024,128]{1,0:T(8,128)(2,1)S(1)}, u32[]{:S(2)}, u32[]{:S(2)}) collective-permute-start(bf16[1024,128]{1,0:T(8,128)(2,1)S(1)} %get-tuple-element.59), channel_id=1, source_target_pairs={{0,1},{1,0},{2,3},{3,2},{4,5},{5,4},{6,7},{7,6},{8,9},{9,8},{10,11... | collective-permute-start | bytes 786440 | tf_op jit(solution)/shard_map/ppermute | solution.py:32
  33.9 54.0 %copy-start.4 = (bf16[4,512,128]{2,1,0:T(8,128)(2,1)}, bf16[4,512,128]{2,1,0:T(8,128)(2,1)S(1)}, u32[]{:S(2)}) copy-start(bf16[4,512,128]{2,1,0:T(8,128)(2,1)S(1)} %collective-permute-done.4.refs_1_) | copy-start | bytes 1572868
  33.9 54.0 %copy-start.5 = (bf16[4,512,128]{2,1,0:T(8,128)(2,1)}, bf16[4,512,128]{2,1,0:T(8,128)(2,1)S(1)}, u32[]{:S(2)}) copy-start(bf16[4,512,128]{2,1,0:T(8,128)(2,1)S(1)} %collective-permute-done.5.refs_2_) | copy-start | bytes 1572868
  34.1 12.6 %collective-permute-start.7 = (bf16[4,512,128]{2,1,0:T(8,128)(2,1)S(1)}, bf16[4,512,128]{2,1,0:T(8,128)(2,1)S(1)}, u32[]{:S(2)}, u32[]{:S(2)}) collective-permute-start(bf16[4,512,128]{2,1,0:T(8,128)(2,1)S(1)} %collective-permute-done.4.refs_1_), channel_id=1, source_target_pairs={{0,2},{2,4},{4,6},{6,8},{8,10},{10,12},{12,14},{14,0},{1,3},{3,5},... | collective-permute-start | bytes 1572872 | tf_op jit(solution)/shard_map/ppermute | solution.py:32
  36.7 10.0 %collective-permute-start.8 = (bf16[4,512,128]{2,1,0:T(8,128)(2,1)S(1)}, bf16[4,512,128]{2,1,0:T(8,128)(2,1)S(1)}, u32[]{:S(2)}, u32[]{:S(2)}) collective-permute-start(bf16[4,512,128]{2,1,0:T(8,128)(2,1)S(1)} %collective-permute-done.5.refs_2_), channel_id=1, source_target_pairs={{0,14},{2,0},{4,2},{6,4},{8,6},{10,8},{12,10},{14,12},{1,15},{3,1}... | collective-permute-start | bytes 1572872 | tf_op jit(solution)/shard_map/ppermute | solution.py:32
  46.7 41.3 %copy-start.6 = (bf16[4,512,128]{2,1,0:T(8,128)(2,1)}, bf16[4,512,128]{2,1,0:T(8,128)(2,1)S(1)}, u32[]{:S(2)}) copy-start(bf16[4,512,128]{2,1,0:T(8,128)(2,1)S(1)} %collective-permute-done.7.refs_3_) | copy-start | bytes 1572868
  46.7 41.3 %copy-start.7 = (bf16[4,512,128]{2,1,0:T(8,128)(2,1)}, bf16[4,512,128]{2,1,0:T(8,128)(2,1)S(1)}, u32[]{:S(2)}) copy-start(bf16[4,512,128]{2,1,0:T(8,128)(2,1)S(1)} %collective-permute-done.8.refs_4_) | copy-start | bytes 1572868
  46.7 14.3 %collective-permute-start.10 = (bf16[4,512,128]{2,1,0:T(8,128)(2,1)S(1)}, bf16[4,512,128]{2,1,0:T(8,128)(2,1)S(1)}, u32[]{:S(2)}, u32[]{:S(2)}) collective-permute-start(bf16[4,512,128]{2,1,0:T(8,128)(2,1)S(1)} %collective-permute-done.8.refs_4_), channel_id=1, source_target_pairs={{0,14},{2,0},{4,2},{6,4},{8,6},{10,8},{12,10},{14,12},{1,15},{3,1}... | collective-permute-start | bytes 1572872 | tf_op jit(solution)/shard_map/ppermute | solution.py:32
  47.3 13.8 %collective-permute-start.9 = (bf16[4,512,128]{2,1,0:T(8,128)(2,1)S(1)}, bf16[4,512,128]{2,1,0:T(8,128)(2,1)}, u32[]{:S(2)}, u32[]{:S(2)}) collective-permute-start(bf16[4,512,128]{2,1,0:T(8,128)(2,1)S(1)} %collective-permute-done.7.refs_3_), channel_id=1, source_target_pairs={{0,2},{2,4},{4,6},{6,8},{8,10},{10,12},{12,14},{14,0},{1,3},{3,5},... | collective-permute-start | bytes 1572872 | tf_op jit(solution)/shard_map/ppermute | solution.py:32
  61.0 26.9 %copy-start.8 = (bf16[4,512,128]{2,1,0:T(8,128)(2,1)}, bf16[4,512,128]{2,1,0:T(8,128)(2,1)S(1)}, u32[]{:S(2)}) copy-start(bf16[4,512,128]{2,1,0:T(8,128)(2,1)S(1)} %collective-permute-done.10.refs_6_) | copy-start | bytes 1572868
  61.9 11.7 %collective-permute-start.11 = (bf16[4,512,128]{2,1,0:T(8,128)(2,1)}, bf16[4,512,128]{2,1,0:T(8,128)(2,1)}, u32[]{:S(2)}, u32[]{:S(2)}) collective-permute-start(bf16[4,512,128]{2,1,0:T(8,128)(2,1)} %collective-permute-done.9.refs_5_), channel_id=1, source_target_pairs={{0,2},{2,4},{4,6},{6,8},{8,10},{10,12},{12,14},{14,0},{1,3},{3,5},... | collective-permute-start | bytes 1572872 | tf_op jit(solution)/shard_map/ppermute | solution.py:32
  62.2 17.0 %collective-permute-start.12 = (bf16[4,512,128]{2,1,0:T(8,128)(2,1)S(1)}, bf16[4,512,128]{2,1,0:T(8,128)(2,1)}, u32[]{:S(2)}, u32[]{:S(2)}) collective-permute-start(bf16[4,512,128]{2,1,0:T(8,128)(2,1)S(1)} %shard_map.94.refs_0_), channel_id=1, source_target_pairs={{0,1},{1,0},{2,3},{3,2},{4,5},{5,4},{6,7},{7,6},{8,9},{9,8},{10,11... | collective-permute-start | bytes 1572872 | tf_op jit(solution)/shard_map/ppermute | solution.py:32
  68.6 10.6 %collective-permute-start.13 = (bf16[4,512,128]{2,1,0:T(8,128)(2,1)S(1)}, bf16[4,512,128]{2,1,0:T(8,128)(2,1)}, u32[]{:S(2)}, u32[]{:S(2)}) collective-permute-start(bf16[4,512,128]{2,1,0:T(8,128)(2,1)S(1)} %collective-permute-done.4.refs_1_), channel_id=1, source_target_pairs={{0,1},{1,0},{2,3},{3,2},{4,5},{5,4},{6,7},{7,6},{8,9},{9,8},{10,11... | collective-permute-start | bytes 1572872 | tf_op jit(solution)/shard_map/ppermute | solution.py:32
  68.6 11.0 %collective-permute-start.14 = (bf16[4,512,128]{2,1,0:T(8,128)(2,1)S(1)}, bf16[4,512,128]{2,1,0:T(8,128)(2,1)}, u32[]{:S(2)}, u32[]{:S(2)}) collective-permute-start(bf16[4,512,128]{2,1,0:T(8,128)(2,1)S(1)} %collective-permute-done.5.refs_2_), channel_id=1, source_target_pairs={{0,1},{1,0},{2,3},{3,2},{4,5},{5,4},{6,7},{7,6},{8,9},{9,8},{10,11... | collective-permute-start | bytes 1572872 | tf_op jit(solution)/shard_map/ppermute | solution.py:32
  69.1 10.0 %all-to-all-start.3 = ((f32[4,32,128]{2,1,0:T(8,128)}), f32[4,32,128]{2,1,0:T(8,128)S(1)}, u32[]{:S(2)}, u32[]{:S(2)}) async-start(f32[4,32,128]{2,1,0:T(8,128)} %shard_map.99), calls=%async_computation.3 | async-start | bytes 131072 | tf_op jit(solution)/shard_map/all_to_all | solution.py:36
  73.3 14.5 %collective-permute-start.15 = (bf16[4,512,128]{2,1,0:T(8,128)(2,1)S(1)}, bf16[4,512,128]{2,1,0:T(8,128)(2,1)}, u32[]{:S(2)}, u32[]{:S(2)}) collective-permute-start(bf16[4,512,128]{2,1,0:T(8,128)(2,1)S(1)} %collective-permute-done.7.refs_3_), channel_id=1, source_target_pairs={{0,1},{1,0},{2,3},{3,2},{4,5},{5,4},{6,7},{7,6},{8,9},{9,8},{10,11... | collective-permute-start | bytes 1572872 | tf_op jit(solution)/shard_map/ppermute | solution.py:32
  73.6 14.3 %collective-permute-start.16 = (bf16[4,512,128]{2,1,0:T(8,128)(2,1)S(1)}, bf16[4,512,128]{2,1,0:T(8,128)(2,1)}, u32[]{:S(2)}, u32[]{:S(2)}) collective-permute-start(bf16[4,512,128]{2,1,0:T(8,128)(2,1)S(1)} %collective-permute-done.8.refs_4_), channel_id=1, source_target_pairs={{0,1},{1,0},{2,3},{3,2},{4,5},{5,4},{6,7},{7,6},{8,9},{9,8},{10,11... | collective-permute-start | bytes 1572872 | tf_op jit(solution)/shard_map/ppermute | solution.py:32
  79.2 8.7 %collective-permute-start.17 = (bf16[4,512,128]{2,1,0:T(8,128)(2,1)}, bf16[4,512,128]{2,1,0:T(8,128)(2,1)}, u32[]{:S(2)}, u32[]{:S(2)}) collective-permute-start(bf16[4,512,128]{2,1,0:T(8,128)(2,1)} %collective-permute-done.9.refs_5_), channel_id=1, source_target_pairs={{0,1},{1,0},{2,3},{3,2},{4,5},{5,4},{6,7},{7,6},{8,9},{9,8},{10,11... | collective-permute-start | bytes 1572872 | tf_op jit(solution)/shard_map/ppermute | solution.py:32
  79.3 8.6 %collective-permute-start.18 = (bf16[4,512,128]{2,1,0:T(8,128)(2,1)S(1)}, bf16[4,512,128]{2,1,0:T(8,128)(2,1)}, u32[]{:S(2)}, u32[]{:S(2)}) collective-permute-start(bf16[4,512,128]{2,1,0:T(8,128)(2,1)S(1)} %collective-permute-done.10.refs_6_), channel_id=1, source_target_pairs={{0,1},{1,0},{2,3},{3,2},{4,5},{5,4},{6,7},{7,6},{8,9},{9,8},{10,11... | collective-permute-start | bytes 1572872 | tf_op jit(solution)/shard_map/ppermute | solution.py:32
  79.7 8.2 %collective-permute-start.19 = (bf16[4,512,128]{2,1,0:T(8,128)(2,1)}, bf16[4,512,128]{2,1,0:T(8,128)(2,1)}, u32[]{:S(2)}, u32[]{:S(2)}) collective-permute-start(bf16[4,512,128]{2,1,0:T(8,128)(2,1)} %collective-permute-done.11.refs_7_), channel_id=1, source_target_pairs={{0,1},{1,0},{2,3},{3,2},{4,5},{5,4},{6,7},{7,6},{8,9},{9,8},{10,11... | collective-permute-start | bytes 1572872 | tf_op jit(solution)/shard_map/ppermute | solution.py:32
  80.5 18.6 %all-to-all-start.4 = ((bf16[32,32,128]{2,1,0:T(8,128)(2,1)}), bf16[32,32,128]{2,1,0:T(8,128)(2,1)S(1)}, u32[]{:S(2)}, u32[]{:S(2)}) async-start(bf16[32,32,128]{2,1,0:T(8,128)(2,1)} %shard_map.101), calls=%async_computation.4 | async-start | bytes 524288 | tf_op jit(solution)/shard_map/all_to_all | solution.py:36
  99.1 2.8 %collective-permute-start.20 = (bf16[32,32,128]{2,1,0:T(8,128)(2,1)S(1)}, bf16[32,32,128]{2,1,0:T(8,128)(2,1)S(1)}, u32[]{:S(2)}, u32[]{:S(2)}) collective-permute-start(bf16[32,32,128]{2,1,0:T(8,128)(2,1)S(1)} %all-to-all-done.4.mine_ref.refs_1_), channel_id=1, source_target_pairs={{0,1},{1,0},{2,3},{3,2},{4,5},{5,4},{6,7},{7,6},{8,9},{9,8},{10,11... | collective-permute-start | bytes 786440 | tf_op jit(solution)/shard_map/ppermute | solution.py:32
  105.3 6.8 %collective-permute-start.21 = (f32[32,224]{1,0:T(8,128)S(1)}, f32[32,224]{1,0:T(8,128)S(1)}, u32[]{:S(2)}, u32[]{:S(2)}) collective-permute-start(f32[32,224]{1,0:T(8,128)S(1)} %get-tuple-element.87.refs_4_), channel_id=1, source_target_pairs={{0,64},{64,128},{128,192},{192,0},{1,65},{65,129},{129,193},{193,1... | collective-permute-start | bytes 86024 | tf_op jit(solution)/shard_map/ppermute | solution.py:32
  105.9 6.3 %collective-permute-start.22 = (f32[32,224]{1,0:T(8,128)S(1)}, f32[32,224]{1,0:T(8,128)S(1)}, u32[]{:S(2)}, u32[]{:S(2)}) collective-permute-start(f32[32,224]{1,0:T(8,128)S(1)} %get-tuple-element.87.refs_4_), channel_id=1, source_target_pairs={{0,128},{64,192},{128,0},{192,64},{1,129},{65,193},{129,1},{193,65... | collective-permute-start | bytes 86024 | tf_op jit(solution)/shard_map/ppermute | solution.py:32
  108.5 3.7 %collective-permute-start.23 = (f32[32,224]{1,0:T(8,128)S(1)}, f32[32,224]{1,0:T(8,128)S(1)}, u32[]{:S(2)}, u32[]{:S(2)}) collective-permute-start(f32[32,224]{1,0:T(8,128)S(1)} %get-tuple-element.87.refs_4_), channel_id=1, source_target_pairs={{0,192},{64,0},{128,64},{192,128},{1,193},{65,1},{129,65},{193,129... | collective-permute-start | bytes 86024 | tf_op jit(solution)/shard_map/ppermute | solution.py:32
  112.3 3.1 %copy-start = (f32[224,8192]{1,0:T(8,128)S(1)}, f32[224,8192]{1,0:T(8,128)}, u32[]{:S(2)}) copy-start(f32[224,8192]{1,0:T(8,128)} %get-tuple-element.81.refs_0_) | copy-start | bytes 22020100

commit v8 on v7

--- a/solution.py
+++ b/solution.py
@@ -188,8 +188,8 @@
 def piece_kernel(steps, *refs):
     n = len(steps)
     own, other = refs[:n], refs[n:2 * n]
-    hidden_hbm, error_hbm, weight_hbm, gate_hbm, up_hbm, matrix_hbm, short_hbm, d_gate_ref, d_up_ref = refs[2 * n:2 * n + 9]
-    own_buf, other_buf, hidden_ref, error_ref, weight_ref, gate_ref, up_ref, matrix_ref, short_ref, sems = refs[2 * n + 9:]
+    hidden_hbm, error_hbm, weight_hbm, gate_hbm, up_hbm, matrix_hbm, d_gate_ref, d_up_ref = refs[2 * n:2 * n + 8]
+    own_buf, other_buf, hidden_ref, error_ref, weight_ref, gate_ref, up_ref, matrix_ref, sems = refs[2 * n + 8:]
     wide = own_buf.shape[3]
     width = matrix_ref.shape[1] // n
     both = [fetch(hidden_hbm, hidden_ref, sems.at[0, n]), fetch(error_hbm, error_ref, sems.at[1, n])]
@@ -206,11 +206,8 @@
         wait_all(copies[i])
         block = jnp.concatenate([buf[i, hop] for hop in range(X) for buf in (own_buf, other_buf)], axis=1)
         span = pl.ds(i * width, width)
-        matrix = slab(error_ref, step, wide).astype(F32) + dot(hidden_ref[...], block)
-        matrix_ref[:, span] = matrix
-        short_ref[:, span] = matrix.astype(BF)
+        matrix_ref[:, span] = slab(error_ref, step, wide).astype(F32) + dot(hidden_ref[...], block)
         out.append(fetch(matrix_ref.at[:, span], matrix_hbm.at[:, span], sems.at[2, i]))
-        out.append(fetch(short_ref.at[:, span], short_hbm.at[:, span], sems.at[3, i]))
         if i == 0:
             wait_all(late)
         term = lax.dot_general(block, slab(weight_ref, step, wide), NT, preferred_element_type=F32)
@@ -230,7 +227,7 @@
     rows, columns = error.shape
     return call(
         functools.partial(piece_kernel, steps),
-        [((rows, columns), F32), ((rows, columns), BF), ((rows, tokens), BF), ((rows, tokens), BF)],
+        [((rows, columns), F32), ((rows, tokens), BF), ((rows, tokens), BF)],
         [
             pltpu.VMEM((n, X, tokens, wide), BF),
             pltpu.VMEM((n, X, tokens, wide), BF),
@@ -240,29 +237,27 @@
             pltpu.VMEM((rows, tokens), BF),
             pltpu.VMEM((rows, tokens), BF),
             pltpu.VMEM((rows, columns), F32),
-            pltpu.VMEM((rows, columns), BF),
-            pltpu.SemaphoreType.DMA((4, n + 2)),
+            pltpu.SemaphoreType.DMA((3, n + 2)),
         ],
         [HBM] * (2 * n + 5),
-        [HBM, HBM, None, None],
+        [HBM, None, None],
         flops=4 * rows * tokens * columns,
         moved=30 << 20,
         vmem=52,
     )(*own, *other, hidden, error, weight, gate, upward)
 
 
-def turn_kernel(steps, short_hbm, mine_ref, theirs_ref, out_ref, gram_ref, short_ref, sems):
-    width = short_ref.shape[1] // len(steps)
-    spans = [slice(i * width, (i + 1) * width) for i in range(len(steps))]
-    copies = [fetch(short_hbm.at[:, span], short_ref.at[:, span], sems.at[i]) for i, span in enumerate(spans)]
-    total, gram = 0.0, 0.0
-    for i, step in enumerate(steps):
-        basis = jnp.concatenate([ref[chip_of(step, hop)] for hop in range(X) for ref in (mine_ref, theirs_ref)], axis=1)
-        gram = gram + lax.dot_general(basis, basis, NT, preferred_element_type=F32)
-        copies[i].wait()
-        total = total + lax.dot_general(short_ref[:, spans[i]], basis, NT, preferred_element_type=F32)
-    gram_ref[...] = gram
-    out_ref[...] = total.T
+def load_kernel(source_hbm, out_ref, sems):
+    part = source_hbm.shape[1] // X
+    spans = [pl.ds(i * part, part) for i in range(X)]
+    wait_all([fetch(source_hbm.at[:, span], out_ref.at[:, span], sems.at[i]) for i, span in enumerate(spans)])
+
+
+def turn_kernel(steps, matrix_ref, mine_ref, theirs_ref, out_ref, gram_ref):
+    chips = [chip_of(step, hop) for step in steps for hop in range(X)]
+    basis = jnp.concatenate([ref[chip] for chip in chips for ref in (mine_ref, theirs_ref)], axis=1)
+    gram_ref[...] = lax.dot_general(basis, basis, NT, preferred_element_type=F32)
+    out_ref[...] = lax.dot_general(matrix_ref[...].astype(BF), basis, NT, preferred_element_type=F32).T
 
 
 def inverse_kernel(gram_ref, out_ref):
@@ -348,8 +343,6 @@
 
     def ring(step, payload=None):
         up, down = pieces[step - 1], pieces[(Z - step + 1) % Z]
-        if payload is not None:
-            payload, up, down = tie((payload, up, down))
         pieces[step] = shift(up, "z", 1, Z)
         if step < Z // 2:
             pieces[Z - step] = shift(down, "z", Z - 1, Z)
@@ -382,19 +375,19 @@
     mine, = call(spread_kernel, [((X * Z, rank, wide), BF)], ins=[VMEM])(terms)
     mine = exchange(mine, ("x", "z"))
     swap(4)
-    matrix, short, d_gate, d_up = use_pieces(
+    matrix, d_gate, d_up = use_pieces(
         steps, [pieces[s] for s in steps], [others[s] for s in steps], hidden, error, down_weight, gate.T, upward.T)
-    mine, short = tie((mine, short))
+    mine, matrix = tie((mine, matrix))
     theirs = shift(mine, "core", 1, CORES)
+    matrix, = call(load_kernel, [((rows, columns), F32)], [pltpu.SemaphoreType.DMA((X,))], [HBM])(matrix)
 
     terms, gram = call(
         functools.partial(turn_kernel, steps),
         [((rank, rows), F32), ((rank, rank), F32)],
-        [pltpu.VMEM((rows, columns), BF), pltpu.SemaphoreType.DMA((Z,))],
-        [HBM, VMEM, VMEM],
+        ins=[VMEM] * 3,
         flops=2 * rows * rank * columns,
         moved=4 * rows * columns,
-    )(short, mine, theirs)
+    )(matrix, mine, theirs)
     terms = [terms] + [shift(terms, "dp", k, groups) for k in range(1, groups)]
     inverse, = call(inverse_kernel, [((rank, rank), F32)], ins=[VMEM])(gram)
 

time: 120 us -> 116 us (0.967)
  local copies, waits for them, and re-layouts: 4.01 us -> 0.94 us
    unnamed x18, local copies, waits for them, and re-layouts: 4.01 us -> 0.94 us
    pallas_call x12 -> x13, Pallas kernels: 27.9 us -> 28.8 us  [call(): return lambda *args: run(*(placed(a, spec) for a, spec in zip(args, ins)))]
  transfers between devices with their start and end apart: 27 -> 27, of which waited for: 5 -> 4; matrix products, arithmetic and copies ran while one was open for 0% -> 0% of each run, Pallas kernels for 16% -> 20%
where the time goes in v8:
time: 116 us; the launch traced here: 115 us
  starting transfers between devices  56 us (48%)
  Pallas kernels  28.8 us (25%)
  blocking collectives  21.9 us (19%)
  waiting for transfers between devices  6.72 us (6%)
    ppermute x24, starting transfers between devices, shift(): return lax.ppermute(a, axis, [(i, (i + step) % n) for i in range(n)])  39.3 us
    pallas_call x13, Pallas kernels, call(): return lambda *args: run(*(placed(a, spec) for a, spec in zip(args, ins)))  28.8 us
    all_to_all x2, blocking collectives, exchange(): return lax.all_to_all(a, axis, 0, 0)  21.9 us
    all_to_all x3, starting transfers between devices, exchange(): return lax.all_to_all(a, axis, 0, 0)  16.7 us
    all_to_all x3, waiting for transfers between devices, exchange(): return lax.all_to_all(a, axis, 0, 0)  5.34 us
  transfers between devices with their start and end apart: 27, of which 4 were waited for; matrix products, arithmetic and copies ran while one was open for 0% of the time, Pallas kernels for 20%

profile of v8, /device:TPU:1, one launch (start us, length us, event | category | flops | bytes accessed | tf_op | source)
XLA Modules:
  0.0 115.3 jit_solution(3666447996495878584)
XLA Ops:
  0.6 2.1 %collective-permute-start.1 = (bf16[512,128]{1,0:T(8,128)(2,1)}, bf16[512,128]{1,0:T(8,128)(2,1)S(1)}, u32[]{:S(2)}, u32[]{:S(2)}) collective-permute-start(bf16[512,128]{1,0:T(8,128)(2,1)} %cotangent_ref.1), channel_id=1, source_target_pairs={{0,16},{16,32},{32,48},{48,0},{1,17},{17,33},{33,49},{49,1},{2,18}... | collective-permute-start | bytes 393224 | tf_op jit(solution)/shard_map/ppermute | solution.py:32
  2.7 2.5 %collective-permute-start.2 = (bf16[512,128]{1,0:T(8,128)(2,1)}, bf16[512,128]{1,0:T(8,128)(2,1)S(1)}, u32[]{:S(2)}, u32[]{:S(2)}) collective-permute-start(bf16[512,128]{1,0:T(8,128)(2,1)} %cotangent_ref.1), channel_id=1, source_target_pairs={{0,32},{16,48},{32,0},{48,16},{1,33},{17,49},{33,1},{49,17},{2,34}... | collective-permute-start | bytes 393224 | tf_op jit(solution)/shard_map/ppermute | solution.py:32
  5.2 1.2 %collective-permute-start.3 = (bf16[512,128]{1,0:T(8,128)(2,1)}, bf16[512,128]{1,0:T(8,128)(2,1)S(1)}, u32[]{:S(2)}, u32[]{:S(2)}) collective-permute-start(bf16[512,128]{1,0:T(8,128)(2,1)} %cotangent_ref.1), channel_id=1, source_target_pairs={{0,48},{16,0},{32,16},{48,32},{1,49},{17,1},{33,17},{49,33},{2,50}... | collective-permute-start | bytes 393224 | tf_op jit(solution)/shard_map/ppermute | solution.py:32
  6.4 1.9 %shard_map.93 = (bf16[224,512]{1,0:T(8,128)(2,1)}, bf16[128,128]{1,0:T(8,128)(2,1)S(1)}) custom-call(bf16[224,512]{1,0:T(8,128)(2,1)} %bitcast.10, bf16[224,512]{1,0:T(8,128)(2,1)} %bitcast.12, f32[32,224]{1,0:T(8,128)} %bitcast.14), custom_call_target="tpu_custom_call" | custom-call | bytes 688128 | tf_op jit(solution)/shard_map/pallas_call | solution.py:54
  8.3 1.6 %collective-permute-start = (bf16[128,128]{1,0:T(8,128)(2,1)S(1)}, bf16[128,128]{1,0:T(8,128)(2,1)S(1)}, u32[]{:S(2)}, u32[]{:S(2)}) collective-permute-start(bf16[128,128]{1,0:T(8,128)(2,1)S(1)} %get-tuple-element.39.left_ref), channel_id=1, source_target_pairs={{0,1},{1,0},{2,3},{3,2},{4,5},{5,4},{6,7},{7,6},{8,9},{9,8},{10,11... | collective-permute-start | bytes 98312 | tf_op jit(solution)/shard_map/ppermute | solution.py:32
  9.9 0.9 collective-permute-done.theirs_ref
  10.7 0.4 collective-permute-done.2.refs_2_
  11.1 0.9 copy-done.1
  12.1 0.0 copy-start
  12.1 1.7 %collective-permute-start.4 = (bf16[4,512,128]{2,1,0:T(8,128)(2,1)S(1)}, bf16[4,512,128]{2,1,0:T(8,128)(2,1)S(1)}, u32[]{:S(2)}, u32[]{:S(2)}) collective-permute-start(bf16[4,512,128]{2,1,0:T(8,128)(2,1)S(1)} %shard_map.94.refs_0_), channel_id=1, source_target_pairs={{0,2},{2,4},{4,6},{6,8},{8,10},{10,12},{12,14},{14,0},{1,3},{3,5},... | collective-permute-start | bytes 1572872 | tf_op jit(solution)/shard_map/ppermute | solution.py:32
  13.8 4.0 %collective-permute-start.5 = (bf16[4,512,128]{2,1,0:T(8,128)(2,1)S(1)}, bf16[4,512,128]{2,1,0:T(8,128)(2,1)S(1)}, u32[]{:S(2)}, u32[]{:S(2)}) collective-permute-start(bf16[4,512,128]{2,1,0:T(8,128)(2,1)S(1)} %shard_map.94.refs_0_), channel_id=1, source_target_pairs={{0,14},{2,0},{4,2},{6,4},{8,6},{10,8},{12,10},{14,12},{1,15},{3,1}... | collective-permute-start | bytes 1572872 | tf_op jit(solution)/shard_map/ppermute | solution.py:32
  17.8 0.7 shard_map.95
  18.5 5.2 %all-to-all-start = ((bf16[8,128,128]{2,1,0:T(8,128)(2,1)}), bf16[8,128,128]{2,1,0:T(8,128)(2,1)S(1)}, u32[]{:S(2)}, u32[]{:S(2)}) async-start(bf16[8,128,128]{2,1,0:T(8,128)(2,1)} %shard_map.95), calls=%async_computation | async-start | bytes 524288 | tf_op jit(solution)/shard_map/all_to_all | solution.py:36
  23.7 2.4 %shard_map.96 = (bf16[1024,128]{1,0:T(8,128)(2,1)S(1)}, bf16[1024,128]{1,0:T(8,128)(2,1)S(1)}) custom-call(f32[32,224]{1,0:T(8,128)} %bitcast.15, bf16[224,8192]{1,0:T(8,128)(2,1)} %bitcast.8), custom_call_target="tpu_custom_call" | custom-call | flops 234881024 | bytes 3670016 | tf_op jit(solution)/shard_map/pallas_call | solution.py:54
  26.2 2.5 %collective-permute-start.6 = (bf16[1024,128]{1,0:T(8,128)(2,1)S(1)}, bf16[1024,128]{1,0:T(8,128)(2,1)S(1)}, u32[]{:S(2)}, u32[]{:S(2)}) collective-permute-start(bf16[1024,128]{1,0:T(8,128)(2,1)S(1)} %get-tuple-element.44), channel_id=1, source_target_pairs={{0,1},{1,0},{2,3},{3,2},{4,5},{5,4},{6,7},{7,6},{8,9},{9,8},{10,11... | collective-permute-start | bytes 786440 | tf_op jit(solution)/shard_map/ppermute | solution.py:32
  28.7 5.3 %all-to-all-done.left_ref = bf16[8,128,128]{2,1,0:T(8,128)(2,1)S(1)} async-done(((bf16[8,128,128]{2,1,0:T(8,128)(2,1)}), bf16[8,128,128]{2,1,0:T(8,128)(2,1)S(1)}, u32[]{:S(2)}, u32[]{:S(2)}) %all-to-all-start) | async-done | bytes 262176 | tf_op jit(solution)/shard_map/all_to_all | solution.py:36
  34.0 2.1 %collective-permute-start.7 = (bf16[4,512,128]{2,1,0:T(8,128)(2,1)S(1)}, bf16[4,512,128]{2,1,0:T(8,128)(2,1)S(1)}, u32[]{:S(2)}, u32[]{:S(2)}) collective-permute-start(bf16[4,512,128]{2,1,0:T(8,128)(2,1)S(1)} %collective-permute-done.4.refs_1_), channel_id=1, source_target_pairs={{0,2},{2,4},{4,6},{6,8},{8,10},{10,12},{12,14},{14,0},{1,3},{3,5},... | collective-permute-start | bytes 1572872 | tf_op jit(solution)/shard_map/ppermute | solution.py:32
  36.1 0.6 collective-permute-start.8
  36.8 0.1 shard_map.97
  36.9 9.4 %all_to_all.25.terms_ref = bf16[4,384,128]{2,1,0:T(8,128)(2,1)S(1)} all-to-all(bf16[4,384,128]{2,1,0:T(8,128)(2,1)S(1)} %shard_map.97), channel_id=1, replica_groups=mesh['dp'=4,'x'=4,'z'=8,'core'=2] {'x'}, dimensions={0} | all-to-all | bytes 786432 | tf_op jit(solution)/shard_map/all_to_all | solution.py:36
  46.3 1.1 collective-permute-start.10
  47.4 0.4 collective-permute-start.9
  47.9 0.1 shard_map.98
  47.9 12.4 %all_to_all.26.part_ref = bf16[8,32,128]{2,1,0:T(8,128)(2,1)S(1)} all-to-all(bf16[8,32,128]{2,1,0:T(8,128)(2,1)S(1)} %get-tuple-element.49), channel_id=1, replica_groups=mesh['dp'=4,'x'=4,'z'=8,'core'=2] {'z'}, dimensions={0} | all-to-all | bytes 131072 | tf_op jit(solution)/shard_map/all_to_all | solution.py:36
  60.4 0.4 collective-permute-start.11
  60.7 6.8 %collective-permute-start.12 = (bf16[4,512,128]{2,1,0:T(8,128)(2,1)S(1)}, bf16[4,512,128]{2,1,0:T(8,128)(2,1)}, u32[]{:S(2)}, u32[]{:S(2)}) collective-permute-start(bf16[4,512,128]{2,1,0:T(8,128)(2,1)S(1)} %shard_map.94.refs_0_), channel_id=1, source_target_pairs={{0,1},{1,0},{2,3},{3,2},{4,5},{5,4},{6,7},{7,6},{8,9},{9,8},{10,11... | collective-permute-start | bytes 1572872 | tf_op jit(solution)/shard_map/ppermute | solution.py:32
  67.6 0.1 collective-permute-start.13
  67.7 0.4 collective-permute-start.14
  68.1 0.8 shard_map.99
  68.9 4.2 %all-to-all-start.3 = ((f32[4,32,128]{2,1,0:T(8,128)}), f32[4,32,128]{2,1,0:T(8,128)S(1)}, u32[]{:S(2)}, u32[]{:S(2)}) async-start(f32[4,32,128]{2,1,0:T(8,128)} %shard_map.99), calls=%async_computation.3 | async-start | bytes 131072 | tf_op jit(solution)/shard_map/all_to_all | solution.py:36
  73.1 0.4 collective-permute-start.15
  73.5 4.5 %collective-permute-start.16 = (bf16[4,512,128]{2,1,0:T(8,128)(2,1)}, bf16[4,512,128]{2,1,0:T(8,128)(2,1)}, u32[]{:S(2)}, u32[]{:S(2)}) collective-permute-start(bf16[4,512,128]{2,1,0:T(8,128)(2,1)} %copy-done.6), channel_id=1, source_target_pairs={{0,1},{1,0},{2,3},{3,2},{4,5},{5,4},{6,7},{7,6},{8,9},{9,8},{10,11... | collective-permute-start | bytes 1572872 | tf_op jit(solution)/shard_map/ppermute | solution.py:32
  78.0 1.1 collective-permute-start.17
  79.1 0.1 collective-permute-start.18
  79.2 0.4 collective-permute-start.19
  79.6 0.7 shard_map.101
  80.3 7.3 %all-to-all-start.4 = ((bf16[32,32,128]{2,1,0:T(8,128)(2,1)}), bf16[32,32,128]{2,1,0:T(8,128)(2,1)S(1)}, u32[]{:S(2)}, u32[]{:S(2)}) async-start(bf16[32,32,128]{2,1,0:T(8,128)(2,1)} %shard_map.101), calls=%async_computation.4 | async-start | bytes 524288 | tf_op jit(solution)/shard_map/all_to_all | solution.py:36
  87.7 11.0 %shard_map.100 = (f32[224,8192]{1,0:T(8,128)}, bf16[224,512]{1,0:T(8,128)(2,1)}, bf16[224,512]{1,0:T(8,128)(2,1)}) custom-call(bf16[4,512,128]{2,1,0:T(8,128)(2,1)} %copy-done, bf16[4,512,128]{2,1,0:T(8,128)(2,1)} %copy-done.3, bf16[4,512,128]{2,1,0:T(8,128)(2,1)} %copy-done.4, bf16[4,512,128]{2,1,0:T(8,128)(2,1)} %copy-done.5, ...), custom_call_target="tpu_custom_call" | custom-call | flops 3758096384 | bytes 31457280 | tf_op jit(solution)/shard_map/pallas_call | solution.py:54
  98.7 1.8 %collective-permute-start.20 = (bf16[32,32,128]{2,1,0:T(8,128)(2,1)S(1)}, bf16[32,32,128]{2,1,0:T(8,128)(2,1)S(1)}, u32[]{:S(2)}, u32[]{:S(2)}) collective-permute-start(bf16[32,32,128]{2,1,0:T(8,128)(2,1)S(1)} %all-to-all-done.4.mine_ref.refs_1_), channel_id=1, source_target_pairs={{0,1},{1,0},{2,3},{3,2},{4,5},{5,4},{6,7},{7,6},{8,9},{9,8},{10,11... | collective-permute-start | bytes 786440 | tf_op jit(solution)/shard_map/ppermute | solution.py:32
  100.6 3.2 %shard_map.102.matrix_ref.refs_0_ = f32[224,8192]{1,0:T(8,128)S(1)} custom-call(f32[224,8192]{1,0:T(8,128)} %get-tuple-element.60.source_hbm), custom_call_target="tpu_custom_call" | custom-call | tf_op jit(solution)/shard_map/pallas_call | solution.py:54
  103.8 1.3 %shard_map.103 = (f32[32,224]{1,0:T(8,128)S(1)}, f32[32,32]{1,0:T(8,128)S(1)}) custom-call(f32[224,8192]{1,0:T(8,128)S(1)} %shard_map.102.matrix_ref.refs_0_, bf16[32,32,128]{2,1,0:T(8,128)(2,1)S(1)} %all-to-all-done.4.mine_ref.refs_1_, bf16[32,32,128]{2,1,0:T(8,128)(2,1)S(1)} %collective-permute-done.20.theirs_ref.refs_2_), custom_call_target="tpu_custom_call" | custom-call | flops 117440512 | bytes 7340032 | tf_op jit(solution)/shard_map/pallas_call | solution.py:54
  105.1 0.3 collective-permute-start.21
  105.4 2.0 %collective-permute-start.22 = (f32[32,224]{1,0:T(8,128)S(1)}, f32[32,224]{1,0:T(8,128)S(1)}, u32[]{:S(2)}, u32[]{:S(2)}) collective-permute-start(f32[32,224]{1,0:T(8,128)S(1)} %get-tuple-element.63.refs_4_), channel_id=1, source_target_pairs={{0,128},{64,192},{128,0},{192,64},{1,129},{65,193},{129,1},{193,65... | collective-permute-start | bytes 86024 | tf_op jit(solution)/shard_map/ppermute | solution.py:32
  107.4 1.1 collective-permute-start.23
  108.5 2.6 %shard_map.104.refs_3_ = f32[32,32]{1,0:T(8,128)S(1)} custom-call(f32[32,32]{1,0:T(8,128)S(1)} %get-tuple-element.62.gram_ref), custom_call_target="tpu_custom_call" | custom-call | tf_op jit(solution)/shard_map/pallas_call | solution.py:54
  111.1 0.0 collective-permute-done.22.refs_6_
  111.1 0.1 collective-permute-done.23.refs_7_
  111.1 4.0 %shard_map.105 = (bf16[224,8192]{1,0:T(8,128)(2,1)}, f32[32,224]{1,0:T(8,128)}) custom-call(f32[224,8192]{1,0:T(8,128)S(1)} %shard_map.102.matrix_ref.refs_0_, bf16[32,32,128]{2,1,0:T(8,128)(2,1)S(1)} %all-to-all-done.4.mine_ref.refs_1_, bf16[32,32,128]{2,1,0:T(8,128)(2,1)S(1)} %collective-permute-done.20.theirs_ref.refs_2_, ...), custom_call_target="tpu_custom_call" | custom-call | flops 234881024 | bytes 11010048 | tf_op jit(solution)/shard_map/pallas_call | solution.py:54
  (39 shorter events, 0.1 us)
Async XLA Ops:
  0.6 10.1 %collective-permute-start.1 = (bf16[512,128]{1,0:T(8,128)(2,1)}, bf16[512,128]{1,0:T(8,128)(2,1)S(1)}, u32[]{:S(2)}, u32[]{:S(2)}) collective-permute-start(bf16[512,128]{1,0:T(8,128)(2,1)} %cotangent_ref.1), channel_id=1, source_target_pairs={{0,16},{16,32},{32,48},{48,0},{1,17},{17,33},{33,49},{49,1},{2,18}... | collective-permute-start | bytes 393224 | tf_op jit(solution)/shard_map/ppermute | solution.py:32
  2.7 8.4 %collective-permute-start.2 = (bf16[512,128]{1,0:T(8,128)(2,1)}, bf16[512,128]{1,0:T(8,128)(2,1)S(1)}, u32[]{:S(2)}, u32[]{:S(2)}) collective-permute-start(bf16[512,128]{1,0:T(8,128)(2,1)} %cotangent_ref.1), channel_id=1, source_target_pairs={{0,32},{16,48},{32,0},{48,16},{1,33},{17,49},{33,1},{49,17},{2,34}... | collective-permute-start | bytes 393224 | tf_op jit(solution)/shard_map/ppermute | solution.py:32
  5.2 5.9 %collective-permute-start.3 = (bf16[512,128]{1,0:T(8,128)(2,1)}, bf16[512,128]{1,0:T(8,128)(2,1)S(1)}, u32[]{:S(2)}, u32[]{:S(2)}) collective-permute-start(bf16[512,128]{1,0:T(8,128)(2,1)} %cotangent_ref.1), channel_id=1, source_target_pairs={{0,48},{16,0},{32,16},{48,32},{1,49},{17,1},{33,17},{49,33},{2,50}... | collective-permute-start | bytes 393224 | tf_op jit(solution)/shard_map/ppermute | solution.py:32
  8.3 2.5 %collective-permute-start = (bf16[128,128]{1,0:T(8,128)(2,1)S(1)}, bf16[128,128]{1,0:T(8,128)(2,1)S(1)}, u32[]{:S(2)}, u32[]{:S(2)}) collective-permute-start(bf16[128,128]{1,0:T(8,128)(2,1)S(1)} %get-tuple-element.39.left_ref), channel_id=1, source_target_pairs={{0,1},{1,0},{2,3},{3,2},{4,5},{5,4},{6,7},{7,6},{8,9},{9,8},{10,11... | collective-permute-start | bytes 98312 | tf_op jit(solution)/shard_map/ppermute | solution.py:32
  11.1 0.9 copy-start.1
  12.1 56.8 %copy-start = (bf16[4,512,128]{2,1,0:T(8,128)(2,1)}, bf16[4,512,128]{2,1,0:T(8,128)(2,1)S(1)}, u32[]{:S(2)}) copy-start(bf16[4,512,128]{2,1,0:T(8,128)(2,1)S(1)} %shard_map.94.refs_0_) | copy-start | bytes 1572868
  12.1 56.0 %copy-start.2 = (bf16[512,128]{1,0:T(8,128)(2,1)S(1)}, bf16[512,128]{1,0:T(8,128)(2,1)}, u32[]{:S(2)}) copy-start(bf16[512,128]{1,0:T(8,128)(2,1)} %cotangent_ref.1) | copy-start | bytes 393220
  12.1 21.9 %collective-permute-start.4 = (bf16[4,512,128]{2,1,0:T(8,128)(2,1)S(1)}, bf16[4,512,128]{2,1,0:T(8,128)(2,1)S(1)}, u32[]{:S(2)}, u32[]{:S(2)}) collective-permute-start(bf16[4,512,128]{2,1,0:T(8,128)(2,1)S(1)} %shard_map.94.refs_0_), channel_id=1, source_target_pairs={{0,2},{2,4},{4,6},{6,8},{8,10},{10,12},{12,14},{14,0},{1,3},{3,5},... | collective-permute-start | bytes 1572872 | tf_op jit(solution)/shard_map/ppermute | solution.py:32
  13.8 20.2 %collective-permute-start.5 = (bf16[4,512,128]{2,1,0:T(8,128)(2,1)S(1)}, bf16[4,512,128]{2,1,0:T(8,128)(2,1)S(1)}, u32[]{:S(2)}, u32[]{:S(2)}) collective-permute-start(bf16[4,512,128]{2,1,0:T(8,128)(2,1)S(1)} %shard_map.94.refs_0_), channel_id=1, source_target_pairs={{0,14},{2,0},{4,2},{6,4},{8,6},{10,8},{12,10},{14,12},{1,15},{3,1}... | collective-permute-start | bytes 1572872 | tf_op jit(solution)/shard_map/ppermute | solution.py:32
  18.5 15.4 %all-to-all-start = ((bf16[8,128,128]{2,1,0:T(8,128)(2,1)}), bf16[8,128,128]{2,1,0:T(8,128)(2,1)S(1)}, u32[]{:S(2)}, u32[]{:S(2)}) async-start(bf16[8,128,128]{2,1,0:T(8,128)(2,1)} %shard_map.95), calls=%async_computation | async-start | bytes 524288 | tf_op jit(solution)/shard_map/all_to_all | solution.py:36
  26.2 10.6 %collective-permute-start.6 = (bf16[1024,128]{1,0:T(8,128)(2,1)S(1)}, bf16[1024,128]{1,0:T(8,128)(2,1)S(1)}, u32[]{:S(2)}, u32[]{:S(2)}) collective-permute-start(bf16[1024,128]{1,0:T(8,128)(2,1)S(1)} %get-tuple-element.44), channel_id=1, source_target_pairs={{0,1},{1,0},{2,3},{3,2},{4,5},{5,4},{6,7},{7,6},{8,9},{9,8},{10,11... | collective-permute-start | bytes 786440 | tf_op jit(solution)/shard_map/ppermute | solution.py:32
  34.0 53.7 %copy-start.3 = (bf16[4,512,128]{2,1,0:T(8,128)(2,1)}, bf16[4,512,128]{2,1,0:T(8,128)(2,1)S(1)}, u32[]{:S(2)}) copy-start(bf16[4,512,128]{2,1,0:T(8,128)(2,1)S(1)} %collective-permute-done.4.refs_1_) | copy-start | bytes 1572868
  34.0 53.7 %copy-start.4 = (bf16[4,512,128]{2,1,0:T(8,128)(2,1)}, bf16[4,512,128]{2,1,0:T(8,128)(2,1)S(1)}, u32[]{:S(2)}) copy-start(bf16[4,512,128]{2,1,0:T(8,128)(2,1)S(1)} %collective-permute-done.5.refs_2_) | copy-start | bytes 1572868
  34.0 12.3 %collective-permute-start.7 = (bf16[4,512,128]{2,1,0:T(8,128)(2,1)S(1)}, bf16[4,512,128]{2,1,0:T(8,128)(2,1)S(1)}, u32[]{:S(2)}, u32[]{:S(2)}) collective-permute-start(bf16[4,512,128]{2,1,0:T(8,128)(2,1)S(1)} %collective-permute-done.4.refs_1_), channel_id=1, source_target_pairs={{0,2},{2,4},{4,6},{6,8},{8,10},{10,12},{12,14},{14,0},{1,3},{3,5},... | collective-permute-start | bytes 1572872 | tf_op jit(solution)/shard_map/ppermute | solution.py:32
  36.1 10.2 %collective-permute-start.8 = (bf16[4,512,128]{2,1,0:T(8,128)(2,1)S(1)}, bf16[4,512,128]{2,1,0:T(8,128)(2,1)S(1)}, u32[]{:S(2)}, u32[]{:S(2)}) collective-permute-start(bf16[4,512,128]{2,1,0:T(8,128)(2,1)S(1)} %collective-permute-done.5.refs_2_), channel_id=1, source_target_pairs={{0,14},{2,0},{4,2},{6,4},{8,6},{10,8},{12,10},{14,12},{1,15},{3,1}... | collective-permute-start | bytes 1572872 | tf_op jit(solution)/shard_map/ppermute | solution.py:32
  46.3 41.4 %copy-start.5 = (bf16[4,512,128]{2,1,0:T(8,128)(2,1)}, bf16[4,512,128]{2,1,0:T(8,128)(2,1)S(1)}, u32[]{:S(2)}) copy-start(bf16[4,512,128]{2,1,0:T(8,128)(2,1)S(1)} %collective-permute-done.7.refs_3_) | copy-start | bytes 1572868
  46.3 21.3 %copy-start.6 = (bf16[4,512,128]{2,1,0:T(8,128)(2,1)}, bf16[4,512,128]{2,1,0:T(8,128)(2,1)S(1)}, u32[]{:S(2)}) copy-start(bf16[4,512,128]{2,1,0:T(8,128)(2,1)S(1)} %collective-permute-done.8.refs_4_) | copy-start | bytes 1572868
  46.3 14.0 %collective-permute-start.10 = (bf16[4,512,128]{2,1,0:T(8,128)(2,1)S(1)}, bf16[4,512,128]{2,1,0:T(8,128)(2,1)S(1)}, u32[]{:S(2)}, u32[]{:S(2)}) collective-permute-start(bf16[4,512,128]{2,1,0:T(8,128)(2,1)S(1)} %collective-permute-done.8.refs_4_), channel_id=1, source_target_pairs={{0,14},{2,0},{4,2},{6,4},{8,6},{10,8},{12,10},{14,12},{1,15},{3,1}... | collective-permute-start | bytes 1572872 | tf_op jit(solution)/shard_map/ppermute | solution.py:32
  47.4 12.9 %collective-permute-start.9 = (bf16[4,512,128]{2,1,0:T(8,128)(2,1)S(1)}, bf16[4,512,128]{2,1,0:T(8,128)(2,1)S(1)}, u32[]{:S(2)}, u32[]{:S(2)}) collective-permute-start(bf16[4,512,128]{2,1,0:T(8,128)(2,1)S(1)} %collective-permute-done.7.refs_3_), channel_id=1, source_target_pairs={{0,2},{2,4},{4,6},{6,8},{8,10},{10,12},{12,14},{14,0},{1,3},{3,5},... | collective-permute-start | bytes 1572872 | tf_op jit(solution)/shard_map/ppermute | solution.py:32
  60.4 27.4 %copy-start.7 = (bf16[4,512,128]{2,1,0:T(8,128)(2,1)}, bf16[4,512,128]{2,1,0:T(8,128)(2,1)S(1)}, u32[]{:S(2)}) copy-start(bf16[4,512,128]{2,1,0:T(8,128)(2,1)S(1)} %collective-permute-done.10.refs_6_) | copy-start | bytes 1572868
  60.4 27.4 %copy-start.8 = (bf16[4,512,128]{2,1,0:T(8,128)(2,1)}, bf16[4,512,128]{2,1,0:T(8,128)(2,1)S(1)}, u32[]{:S(2)}) copy-start(bf16[4,512,128]{2,1,0:T(8,128)(2,1)S(1)} %collective-permute-done.9.refs_5_) | copy-start | bytes 1572868
  60.4 13.1 %collective-permute-start.11 = (bf16[4,512,128]{2,1,0:T(8,128)(2,1)S(1)}, bf16[4,512,128]{2,1,0:T(8,128)(2,1)}, u32[]{:S(2)}, u32[]{:S(2)}) collective-permute-start(bf16[4,512,128]{2,1,0:T(8,128)(2,1)S(1)} %collective-permute-done.9.refs_5_), channel_id=1, source_target_pairs={{0,2},{2,4},{4,6},{6,8},{8,10},{10,12},{12,14},{14,0},{1,3},{3,5},... | collective-permute-start | bytes 1572872 | tf_op jit(solution)/shard_map/ppermute | solution.py:32
  60.7 17.2 %collective-permute-start.12 = (bf16[4,512,128]{2,1,0:T(8,128)(2,1)S(1)}, bf16[4,512,128]{2,1,0:T(8,128)(2,1)}, u32[]{:S(2)}, u32[]{:S(2)}) collective-permute-start(bf16[4,512,128]{2,1,0:T(8,128)(2,1)S(1)} %shard_map.94.refs_0_), channel_id=1, source_target_pairs={{0,1},{1,0},{2,3},{3,2},{4,5},{5,4},{6,7},{7,6},{8,9},{9,8},{10,11... | collective-permute-start | bytes 1572872 | tf_op jit(solution)/shard_map/ppermute | solution.py:32
  67.6 11.5 %collective-permute-start.13 = (bf16[4,512,128]{2,1,0:T(8,128)(2,1)S(1)}, bf16[4,512,128]{2,1,0:T(8,128)(2,1)}, u32[]{:S(2)}, u32[]{:S(2)}) collective-permute-start(bf16[4,512,128]{2,1,0:T(8,128)(2,1)S(1)} %collective-permute-done.4.refs_1_), channel_id=1, source_target_pairs={{0,1},{1,0},{2,3},{3,2},{4,5},{5,4},{6,7},{7,6},{8,9},{9,8},{10,11... | collective-permute-start | bytes 1572872 | tf_op jit(solution)/shard_map/ppermute | solution.py:32
  67.7 11.5 %collective-permute-start.14 = (bf16[4,512,128]{2,1,0:T(8,128)(2,1)S(1)}, bf16[4,512,128]{2,1,0:T(8,128)(2,1)}, u32[]{:S(2)}, u32[]{:S(2)}) collective-permute-start(bf16[4,512,128]{2,1,0:T(8,128)(2,1)S(1)} %collective-permute-done.5.refs_2_), channel_id=1, source_target_pairs={{0,1},{1,0},{2,3},{3,2},{4,5},{5,4},{6,7},{7,6},{8,9},{9,8},{10,11... | collective-permute-start | bytes 1572872 | tf_op jit(solution)/shard_map/ppermute | solution.py:32
  68.9 9.1 %all-to-all-start.3 = ((f32[4,32,128]{2,1,0:T(8,128)}), f32[4,32,128]{2,1,0:T(8,128)S(1)}, u32[]{:S(2)}, u32[]{:S(2)}) async-start(f32[4,32,128]{2,1,0:T(8,128)} %shard_map.99), calls=%async_computation.3 | async-start | bytes 131072 | tf_op jit(solution)/shard_map/all_to_all | solution.py:36
  73.1 14.5 %collective-permute-start.15 = (bf16[4,512,128]{2,1,0:T(8,128)(2,1)S(1)}, bf16[4,512,128]{2,1,0:T(8,128)(2,1)}, u32[]{:S(2)}, u32[]{:S(2)}) collective-permute-start(bf16[4,512,128]{2,1,0:T(8,128)(2,1)S(1)} %collective-permute-done.7.refs_3_), channel_id=1, source_target_pairs={{0,1},{1,0},{2,3},{3,2},{4,5},{5,4},{6,7},{7,6},{8,9},{9,8},{10,11... | collective-permute-start | bytes 1572872 | tf_op jit(solution)/shard_map/ppermute | solution.py:32
  73.5 14.2 %collective-permute-start.16 = (bf16[4,512,128]{2,1,0:T(8,128)(2,1)}, bf16[4,512,128]{2,1,0:T(8,128)(2,1)}, u32[]{:S(2)}, u32[]{:S(2)}) collective-permute-start(bf16[4,512,128]{2,1,0:T(8,128)(2,1)} %copy-done.6), channel_id=1, source_target_pairs={{0,1},{1,0},{2,3},{3,2},{4,5},{5,4},{6,7},{7,6},{8,9},{9,8},{10,11... | collective-permute-start | bytes 1572872 | tf_op jit(solution)/shard_map/ppermute | solution.py:32
  78.0 9.7 %collective-permute-start.17 = (bf16[4,512,128]{2,1,0:T(8,128)(2,1)S(1)}, bf16[4,512,128]{2,1,0:T(8,128)(2,1)}, u32[]{:S(2)}, u32[]{:S(2)}) collective-permute-start(bf16[4,512,128]{2,1,0:T(8,128)(2,1)S(1)} %collective-permute-done.9.refs_5_), channel_id=1, source_target_pairs={{0,1},{1,0},{2,3},{3,2},{4,5},{5,4},{6,7},{7,6},{8,9},{9,8},{10,11... | collective-permute-start | bytes 1572872 | tf_op jit(solution)/shard_map/ppermute | solution.py:32
  79.1 8.6 %collective-permute-start.18 = (bf16[4,512,128]{2,1,0:T(8,128)(2,1)S(1)}, bf16[4,512,128]{2,1,0:T(8,128)(2,1)}, u32[]{:S(2)}, u32[]{:S(2)}) collective-permute-start(bf16[4,512,128]{2,1,0:T(8,128)(2,1)S(1)} %collective-permute-done.10.refs_6_), channel_id=1, source_target_pairs={{0,1},{1,0},{2,3},{3,2},{4,5},{5,4},{6,7},{7,6},{8,9},{9,8},{10,11... | collective-permute-start | bytes 1572872 | tf_op jit(solution)/shard_map/ppermute | solution.py:32
  79.2 8.5 %collective-permute-start.19 = (bf16[4,512,128]{2,1,0:T(8,128)(2,1)}, bf16[4,512,128]{2,1,0:T(8,128)(2,1)}, u32[]{:S(2)}, u32[]{:S(2)}) collective-permute-start(bf16[4,512,128]{2,1,0:T(8,128)(2,1)} %collective-permute-done.11.refs_7_), channel_id=1, source_target_pairs={{0,1},{1,0},{2,3},{3,2},{4,5},{5,4},{6,7},{7,6},{8,9},{9,8},{10,11... | collective-permute-start | bytes 1572872 | tf_op jit(solution)/shard_map/ppermute | solution.py:32
  80.3 18.4 %all-to-all-start.4 = ((bf16[32,32,128]{2,1,0:T(8,128)(2,1)}), bf16[32,32,128]{2,1,0:T(8,128)(2,1)S(1)}, u32[]{:S(2)}, u32[]{:S(2)}) async-start(bf16[32,32,128]{2,1,0:T(8,128)(2,1)} %shard_map.101), calls=%async_computation.4 | async-start | bytes 524288 | tf_op jit(solution)/shard_map/all_to_all | solution.py:36
  98.7 5.0 %collective-permute-start.20 = (bf16[32,32,128]{2,1,0:T(8,128)(2,1)S(1)}, bf16[32,32,128]{2,1,0:T(8,128)(2,1)S(1)}, u32[]{:S(2)}, u32[]{:S(2)}) collective-permute-start(bf16[32,32,128]{2,1,0:T(8,128)(2,1)S(1)} %all-to-all-done.4.mine_ref.refs_1_), channel_id=1, source_target_pairs={{0,1},{1,0},{2,3},{3,2},{4,5},{5,4},{6,7},{7,6},{8,9},{9,8},{10,11... | collective-permute-start | bytes 786440 | tf_op jit(solution)/shard_map/ppermute | solution.py:32
  105.1 6.0 %collective-permute-start.21 = (f32[32,224]{1,0:T(8,128)S(1)}, f32[32,224]{1,0:T(8,128)S(1)}, u32[]{:S(2)}, u32[]{:S(2)}) collective-permute-start(f32[32,224]{1,0:T(8,128)S(1)} %get-tuple-element.63.refs_4_), channel_id=1, source_target_pairs={{0,64},{64,128},{128,192},{192,0},{1,65},{65,129},{129,193},{193,1... | collective-permute-start | bytes 86024 | tf_op jit(solution)/shard_map/ppermute | solution.py:32
  105.4 5.7 %collective-permute-start.22 = (f32[32,224]{1,0:T(8,128)S(1)}, f32[32,224]{1,0:T(8,128)S(1)}, u32[]{:S(2)}, u32[]{:S(2)}) collective-permute-start(f32[32,224]{1,0:T(8,128)S(1)} %get-tuple-element.63.refs_4_), channel_id=1, source_target_pairs={{0,128},{64,192},{128,0},{192,64},{1,129},{65,193},{129,1},{193,65... | collective-permute-start | bytes 86024 | tf_op jit(solution)/shard_map/ppermute | solution.py:32
  107.4 3.8 %collective-permute-start.23 = (f32[32,224]{1,0:T(8,128)S(1)}, f32[32,224]{1,0:T(8,128)S(1)}, u32[]{:S(2)}, u32[]{:S(2)}) collective-permute-start(f32[32,224]{1,0:T(8,128)S(1)} %get-tuple-element.63.refs_4_), channel_id=1, source_target_pairs={{0,192},{64,0},{128,64},{192,128},{1,193},{65,1},{129,65},{193,129... | collective-permute-start | bytes 86024 | tf_op jit(solution)/shard_map/ppermute | solution.py:32

commit v9 on v8

--- a/solution.py
+++ b/solution.py
@@ -356,7 +356,6 @@
     left = ring(1, left)
     swap(0)
     left = exchange(left, "z")
-    left, pieces[1], pieces[7] = tie((left, pieces[1], pieces[7]))
     terms, = call(pack_kernel, [((X, tiles + Z * rank, wide), BF)], ins=[VMEM] * 3)(left, part, mine)
     terms = ring(2, terms)
     swap(1, 7)

time: 116 us -> 114 us (0.983)
  waiting for transfers between devices: 6.72 us -> 5.22 us
    all_to_all x3, waiting for transfers between devices: 5.34 us -> 2.21 us  [exchange(): return lax.all_to_all(a, axis, 0, 0)]
    ppermute x24, waiting for transfers between devices: 1.38 us -> 3.02 us  [shift(): return lax.ppermute(a, axis, [(i, (i + step) % n) for i in range(n)])]
  transfers between devices with their start and end apart: 27 -> 27, of which waited for: 4 -> 5; matrix products, arithmetic and copies ran while one was open for 0% -> 0% of each run, Pallas kernels for 20% -> 21%
where the time goes in v9:
time: 114 us; the launch traced here: 113 us
  starting transfers between devices  55.3 us (49%)
  Pallas kernels  28.7 us (25%)
  blocking collectives  21.4 us (19%)
  waiting for transfers between devices  5.22 us (5%)
  local copies, waits for them, and re-layouts  1.68 us (1%)
    ppermute x24, starting transfers between devices, shift(): return lax.ppermute(a, axis, [(i, (i + step) % n) for i in range(n)])  39.3 us
    pallas_call x13, Pallas kernels, call(): return lambda *args: run(*(placed(a, spec) for a, spec in zip(args, ins)))  28.7 us
    all_to_all x2, blocking collectives, exchange(): return lax.all_to_all(a, axis, 0, 0)  21.4 us
    all_to_all x3, starting transfers between devices, exchange(): return lax.all_to_all(a, axis, 0, 0)  15.9 us
    ppermute x24, waiting for transfers between devices, shift(): return lax.ppermute(a, axis, [(i, (i + step) % n) for i in range(n)])  3.02 us
  transfers between devices with their start and end apart: 27, of which 5 were waited for; matrix products, arithmetic and copies ran while one was open for 0% of the time, Pallas kernels for 21%

profile of v9, /device:TPU:1, one launch (start us, length us, event | category | flops | bytes accessed | tf_op | source)
XLA Modules:
  0.0 113.4 jit_solution(10160103646981344558)
XLA Ops:
  0.6 2.1 %collective-permute-start.1 = (bf16[512,128]{1,0:T(8,128)(2,1)}, bf16[512,128]{1,0:T(8,128)(2,1)S(1)}, u32[]{:S(2)}, u32[]{:S(2)}) collective-permute-start(bf16[512,128]{1,0:T(8,128)(2,1)} %cotangent_ref.1), channel_id=1, source_target_pairs={{0,16},{16,32},{32,48},{48,0},{1,17},{17,33},{33,49},{49,1},{2,18}... | collective-permute-start | bytes 393224 | tf_op jit(solution)/shard_map/ppermute | solution.py:32
  2.7 2.5 %collective-permute-start.2 = (bf16[512,128]{1,0:T(8,128)(2,1)}, bf16[512,128]{1,0:T(8,128)(2,1)S(1)}, u32[]{:S(2)}, u32[]{:S(2)}) collective-permute-start(bf16[512,128]{1,0:T(8,128)(2,1)} %cotangent_ref.1), channel_id=1, source_target_pairs={{0,32},{16,48},{32,0},{48,16},{1,33},{17,49},{33,1},{49,17},{2,34}... | collective-permute-start | bytes 393224 | tf_op jit(solution)/shard_map/ppermute | solution.py:32
  5.2 1.2 %collective-permute-start.3 = (bf16[512,128]{1,0:T(8,128)(2,1)}, bf16[512,128]{1,0:T(8,128)(2,1)S(1)}, u32[]{:S(2)}, u32[]{:S(2)}) collective-permute-start(bf16[512,128]{1,0:T(8,128)(2,1)} %cotangent_ref.1), channel_id=1, source_target_pairs={{0,48},{16,0},{32,16},{48,32},{1,49},{17,1},{33,17},{49,33},{2,50}... | collective-permute-start | bytes 393224 | tf_op jit(solution)/shard_map/ppermute | solution.py:32
  6.4 1.9 %shard_map.93 = (bf16[224,512]{1,0:T(8,128)(2,1)}, bf16[128,128]{1,0:T(8,128)(2,1)S(1)}) custom-call(bf16[224,512]{1,0:T(8,128)(2,1)} %bitcast.10, bf16[224,512]{1,0:T(8,128)(2,1)} %bitcast.12, f32[32,224]{1,0:T(8,128)} %bitcast.14), custom_call_target="tpu_custom_call" | custom-call | bytes 688128 | tf_op jit(solution)/shard_map/pallas_call | solution.py:54
  8.3 1.6 %collective-permute-start = (bf16[128,128]{1,0:T(8,128)(2,1)S(1)}, bf16[128,128]{1,0:T(8,128)(2,1)S(1)}, u32[]{:S(2)}, u32[]{:S(2)}) collective-permute-start(bf16[128,128]{1,0:T(8,128)(2,1)S(1)} %get-tuple-element.36.left_ref), channel_id=1, source_target_pairs={{0,1},{1,0},{2,3},{3,2},{4,5},{5,4},{6,7},{7,6},{8,9},{9,8},{10,11... | collective-permute-start | bytes 98312 | tf_op jit(solution)/shard_map/ppermute | solution.py:32
  9.9 0.9 collective-permute-done.theirs_ref
  10.7 0.4 collective-permute-done.2.refs_2_
  11.1 0.9 copy-done.1
  12.1 0.0 copy-start
  12.1 1.7 %collective-permute-start.4 = (bf16[4,512,128]{2,1,0:T(8,128)(2,1)S(1)}, bf16[4,512,128]{2,1,0:T(8,128)(2,1)S(1)}, u32[]{:S(2)}, u32[]{:S(2)}) collective-permute-start(bf16[4,512,128]{2,1,0:T(8,128)(2,1)S(1)} %shard_map.94.refs_0_), channel_id=1, source_target_pairs={{0,2},{2,4},{4,6},{6,8},{8,10},{10,12},{12,14},{14,0},{1,3},{3,5},... | collective-permute-start | bytes 1572872 | tf_op jit(solution)/shard_map/ppermute | solution.py:32
  13.8 4.0 %collective-permute-start.5 = (bf16[4,512,128]{2,1,0:T(8,128)(2,1)S(1)}, bf16[4,512,128]{2,1,0:T(8,128)(2,1)S(1)}, u32[]{:S(2)}, u32[]{:S(2)}) collective-permute-start(bf16[4,512,128]{2,1,0:T(8,128)(2,1)S(1)} %shard_map.94.refs_0_), channel_id=1, source_target_pairs={{0,14},{2,0},{4,2},{6,4},{8,6},{10,8},{12,10},{14,12},{1,15},{3,1}... | collective-permute-start | bytes 1572872 | tf_op jit(solution)/shard_map/ppermute | solution.py:32
  17.8 0.7 shard_map.95
  18.5 5.2 %all-to-all-start = ((bf16[8,128,128]{2,1,0:T(8,128)(2,1)}), bf16[8,128,128]{2,1,0:T(8,128)(2,1)S(1)}, u32[]{:S(2)}, u32[]{:S(2)}) async-start(bf16[8,128,128]{2,1,0:T(8,128)(2,1)} %shard_map.95), calls=%async_computation | async-start | bytes 524288 | tf_op jit(solution)/shard_map/all_to_all | solution.py:36
  23.7 2.4 %shard_map.96 = (bf16[1024,128]{1,0:T(8,128)(2,1)S(1)}, bf16[1024,128]{1,0:T(8,128)(2,1)S(1)}) custom-call(f32[32,224]{1,0:T(8,128)} %bitcast.15, bf16[224,8192]{1,0:T(8,128)(2,1)} %bitcast.8), custom_call_target="tpu_custom_call" | custom-call | flops 234881024 | bytes 3670016 | tf_op jit(solution)/shard_map/pallas_call | solution.py:54
  26.2 2.5 %collective-permute-start.6 = (bf16[1024,128]{1,0:T(8,128)(2,1)S(1)}, bf16[1024,128]{1,0:T(8,128)(2,1)S(1)}, u32[]{:S(2)}, u32[]{:S(2)}) collective-permute-start(bf16[1024,128]{1,0:T(8,128)(2,1)S(1)} %get-tuple-element.38), channel_id=1, source_target_pairs={{0,1},{1,0},{2,3},{3,2},{4,5},{5,4},{6,7},{7,6},{8,9},{9,8},{10,11... | collective-permute-start | bytes 786440 | tf_op jit(solution)/shard_map/ppermute | solution.py:32
  28.7 1.7 %collective-permute-start.7 = (bf16[4,512,128]{2,1,0:T(8,128)(2,1)S(1)}, bf16[4,512,128]{2,1,0:T(8,128)(2,1)S(1)}, u32[]{:S(2)}, u32[]{:S(2)}) collective-permute-start(bf16[4,512,128]{2,1,0:T(8,128)(2,1)S(1)} %collective-permute-done.4.refs_1_), channel_id=1, source_target_pairs={{0,2},{2,4},{4,6},{6,8},{8,10},{10,12},{12,14},{14,0},{1,3},{3,5},... | collective-permute-start | bytes 1572872 | tf_op jit(solution)/shard_map/ppermute | solution.py:32
  30.4 1.4 %collective-permute-start.8 = (bf16[4,512,128]{2,1,0:T(8,128)(2,1)S(1)}, bf16[4,512,128]{2,1,0:T(8,128)(2,1)S(1)}, u32[]{:S(2)}, u32[]{:S(2)}) collective-permute-start(bf16[4,512,128]{2,1,0:T(8,128)(2,1)S(1)} %collective-permute-done.5.refs_2_), channel_id=1, source_target_pairs={{0,14},{2,0},{4,2},{6,4},{8,6},{10,8},{12,10},{14,12},{1,15},{3,1}... | collective-permute-start | bytes 1572872 | tf_op jit(solution)/shard_map/ppermute | solution.py:32
  31.8 2.2 %all-to-all-done.left_ref = bf16[8,128,128]{2,1,0:T(8,128)(2,1)S(1)} async-done(((bf16[8,128,128]{2,1,0:T(8,128)(2,1)}), bf16[8,128,128]{2,1,0:T(8,128)(2,1)S(1)}, u32[]{:S(2)}, u32[]{:S(2)}) %all-to-all-start) | async-done | bytes 262176 | tf_op jit(solution)/shard_map/all_to_all | solution.py:36
  34.0 0.1 shard_map.97
  34.1 9.5 %all_to_all.25.terms_ref = bf16[4,384,128]{2,1,0:T(8,128)(2,1)S(1)} all-to-all(bf16[4,384,128]{2,1,0:T(8,128)(2,1)S(1)} %shard_map.97), channel_id=1, replica_groups=mesh['dp'=4,'x'=4,'z'=8,'core'=2] {'x'}, dimensions={0} | all-to-all | bytes 786432 | tf_op jit(solution)/shard_map/all_to_all | solution.py:36
  43.6 1.6 %collective-permute-done.7.refs_3_ = bf16[4,512,128]{2,1,0:T(8,128)(2,1)S(1)} collective-permute-done((bf16[4,512,128]{2,1,0:T(8,128)(2,1)S(1)}, bf16[4,512,128]{2,1,0:T(8,128)(2,1)S(1)}, u32[]{:S(2)}, u32[]{:S(2)}) %collective-permute-start.7) | collective-permute-done | bytes 524320 | tf_op jit(solution)/shard_map/ppermute | solution.py:32
  45.3 1.9 %collective-permute-start.10 = (bf16[4,512,128]{2,1,0:T(8,128)(2,1)S(1)}, bf16[4,512,128]{2,1,0:T(8,128)(2,1)S(1)}, u32[]{:S(2)}, u32[]{:S(2)}) collective-permute-start(bf16[4,512,128]{2,1,0:T(8,128)(2,1)S(1)} %collective-permute-done.8.refs_4_), channel_id=1, source_target_pairs={{0,14},{2,0},{4,2},{6,4},{8,6},{10,8},{12,10},{14,12},{1,15},{3,1}... | collective-permute-start | bytes 1572872 | tf_op jit(solution)/shard_map/ppermute | solution.py:32
  47.2 0.1 shard_map.98
  47.2 11.9 %all_to_all.26.part_ref = bf16[8,32,128]{2,1,0:T(8,128)(2,1)S(1)} all-to-all(bf16[8,32,128]{2,1,0:T(8,128)(2,1)S(1)} %get-tuple-element.43), channel_id=1, replica_groups=mesh['dp'=4,'x'=4,'z'=8,'core'=2] {'z'}, dimensions={0} | all-to-all | bytes 131072 | tf_op jit(solution)/shard_map/all_to_all | solution.py:36
  59.2 0.6 collective-permute-start.11
  59.8 6.5 %collective-permute-start.12 = (bf16[4,512,128]{2,1,0:T(8,128)(2,1)S(1)}, bf16[4,512,128]{2,1,0:T(8,128)(2,1)}, u32[]{:S(2)}, u32[]{:S(2)}) collective-permute-start(bf16[4,512,128]{2,1,0:T(8,128)(2,1)S(1)} %shard_map.94.refs_0_), channel_id=1, source_target_pairs={{0,1},{1,0},{2,3},{3,2},{4,5},{5,4},{6,7},{7,6},{8,9},{9,8},{10,11... | collective-permute-start | bytes 1572872 | tf_op jit(solution)/shard_map/ppermute | solution.py:32
  66.3 0.5 collective-permute-start.14
  66.8 0.8 shard_map.99
  67.6 4.2 %all-to-all-start.3 = ((f32[4,32,128]{2,1,0:T(8,128)}), f32[4,32,128]{2,1,0:T(8,128)S(1)}, u32[]{:S(2)}, u32[]{:S(2)}) async-start(f32[4,32,128]{2,1,0:T(8,128)} %shard_map.99), calls=%async_computation.3 | async-start | bytes 131072 | tf_op jit(solution)/shard_map/all_to_all | solution.py:36
  71.7 0.3 collective-permute-start.15
  72.0 4.5 %collective-permute-start.16 = (bf16[4,512,128]{2,1,0:T(8,128)(2,1)S(1)}, bf16[4,512,128]{2,1,0:T(8,128)(2,1)}, u32[]{:S(2)}, u32[]{:S(2)}) collective-permute-start(bf16[4,512,128]{2,1,0:T(8,128)(2,1)S(1)} %collective-permute-done.8.refs_4_), channel_id=1, source_target_pairs={{0,1},{1,0},{2,3},{3,2},{4,5},{5,4},{6,7},{7,6},{8,9},{9,8},{10,11... | collective-permute-start | bytes 1572872 | tf_op jit(solution)/shard_map/ppermute | solution.py:32
  76.6 1.1 collective-permute-start.17
  77.7 0.1 collective-permute-start.18
  77.8 0.4 collective-permute-start.19
  78.2 0.7 shard_map.101
  78.9 6.6 %all-to-all-start.4 = ((bf16[32,32,128]{2,1,0:T(8,128)(2,1)}), bf16[32,32,128]{2,1,0:T(8,128)(2,1)S(1)}, u32[]{:S(2)}, u32[]{:S(2)}) async-start(bf16[32,32,128]{2,1,0:T(8,128)(2,1)} %shard_map.101), calls=%async_computation.4 | async-start | bytes 524288 | tf_op jit(solution)/shard_map/all_to_all | solution.py:36
  85.6 0.7 copy-done.8
  86.3 10.9 %shard_map.100 = (f32[224,8192]{1,0:T(8,128)}, bf16[224,512]{1,0:T(8,128)(2,1)}, bf16[224,512]{1,0:T(8,128)(2,1)}) custom-call(bf16[4,512,128]{2,1,0:T(8,128)(2,1)} %copy-done, bf16[4,512,128]{2,1,0:T(8,128)(2,1)} %copy-done.3, bf16[4,512,128]{2,1,0:T(8,128)(2,1)} %copy-done.4, bf16[4,512,128]{2,1,0:T(8,128)(2,1)} %copy-done.5, ...), custom_call_target="tpu_custom_call" | custom-call | flops 3758096384 | bytes 31457280 | tf_op jit(solution)/shard_map/pallas_call | solution.py:54
  97.3 1.1 collective-permute-start.20
  98.4 3.2 %shard_map.102.matrix_ref.refs_0_ = f32[224,8192]{1,0:T(8,128)S(1)} custom-call(f32[224,8192]{1,0:T(8,128)} %get-tuple-element.54.source_hbm), custom_call_target="tpu_custom_call" | custom-call | tf_op jit(solution)/shard_map/pallas_call | solution.py:54
  101.6 1.3 %shard_map.103 = (f32[32,224]{1,0:T(8,128)S(1)}, f32[32,32]{1,0:T(8,128)S(1)}) custom-call(f32[224,8192]{1,0:T(8,128)S(1)} %shard_map.102.matrix_ref.refs_0_, bf16[32,32,128]{2,1,0:T(8,128)(2,1)S(1)} %all-to-all-done.4.mine_ref.refs_1_, bf16[32,32,128]{2,1,0:T(8,128)(2,1)S(1)} %collective-permute-done.20.theirs_ref.refs_2_), custom_call_target="tpu_custom_call" | custom-call | flops 117440512 | bytes 7340032 | tf_op jit(solution)/shard_map/pallas_call | solution.py:54
  102.9 0.3 collective-permute-start.21
  103.2 2.2 %collective-permute-start.22 = (f32[32,224]{1,0:T(8,128)S(1)}, f32[32,224]{1,0:T(8,128)S(1)}, u32[]{:S(2)}, u32[]{:S(2)}) collective-permute-start(f32[32,224]{1,0:T(8,128)S(1)} %get-tuple-element.57.refs_4_), channel_id=1, source_target_pairs={{0,128},{64,192},{128,0},{192,64},{1,129},{65,193},{129,1},{193,65... | collective-permute-start | bytes 86024 | tf_op jit(solution)/shard_map/ppermute | solution.py:32
  105.5 1.1 collective-permute-start.23
  106.5 2.6 %shard_map.104.refs_3_ = f32[32,32]{1,0:T(8,128)S(1)} custom-call(f32[32,32]{1,0:T(8,128)S(1)} %get-tuple-element.56.gram_ref), custom_call_target="tpu_custom_call" | custom-call | tf_op jit(solution)/shard_map/pallas_call | solution.py:54
  109.1 0.0 collective-permute-done.22.refs_6_
  109.1 0.1 collective-permute-done.23.refs_7_
  109.2 4.0 %shard_map.105 = (bf16[224,8192]{1,0:T(8,128)(2,1)}, f32[32,224]{1,0:T(8,128)}) custom-call(f32[224,8192]{1,0:T(8,128)S(1)} %shard_map.102.matrix_ref.refs_0_, bf16[32,32,128]{2,1,0:T(8,128)(2,1)S(1)} %all-to-all-done.4.mine_ref.refs_1_, bf16[32,32,128]{2,1,0:T(8,128)(2,1)S(1)} %collective-permute-done.20.theirs_ref.refs_2_, ...), custom_call_target="tpu_custom_call" | custom-call | flops 234881024 | bytes 11010048 | tf_op jit(solution)/shard_map/pallas_call | solution.py:54
  (39 shorter events, 0.1 us)
Async XLA Ops:
  0.6 10.1 %collective-permute-start.1 = (bf16[512,128]{1,0:T(8,128)(2,1)}, bf16[512,128]{1,0:T(8,128)(2,1)S(1)}, u32[]{:S(2)}, u32[]{:S(2)}) collective-permute-start(bf16[512,128]{1,0:T(8,128)(2,1)} %cotangent_ref.1), channel_id=1, source_target_pairs={{0,16},{16,32},{32,48},{48,0},{1,17},{17,33},{33,49},{49,1},{2,18}... | collective-permute-start | bytes 393224 | tf_op jit(solution)/shard_map/ppermute | solution.py:32
  2.7 8.4 %collective-permute-start.2 = (bf16[512,128]{1,0:T(8,128)(2,1)}, bf16[512,128]{1,0:T(8,128)(2,1)S(1)}, u32[]{:S(2)}, u32[]{:S(2)}) collective-permute-start(bf16[512,128]{1,0:T(8,128)(2,1)} %cotangent_ref.1), channel_id=1, source_target_pairs={{0,32},{16,48},{32,0},{48,16},{1,33},{17,49},{33,1},{49,17},{2,34}... | collective-permute-start | bytes 393224 | tf_op jit(solution)/shard_map/ppermute | solution.py:32
  5.2 5.9 %collective-permute-start.3 = (bf16[512,128]{1,0:T(8,128)(2,1)}, bf16[512,128]{1,0:T(8,128)(2,1)S(1)}, u32[]{:S(2)}, u32[]{:S(2)}) collective-permute-start(bf16[512,128]{1,0:T(8,128)(2,1)} %cotangent_ref.1), channel_id=1, source_target_pairs={{0,48},{16,0},{32,16},{48,32},{1,49},{17,1},{33,17},{49,33},{2,50}... | collective-permute-start | bytes 393224 | tf_op jit(solution)/shard_map/ppermute | solution.py:32
  8.3 2.5 %collective-permute-start = (bf16[128,128]{1,0:T(8,128)(2,1)S(1)}, bf16[128,128]{1,0:T(8,128)(2,1)S(1)}, u32[]{:S(2)}, u32[]{:S(2)}) collective-permute-start(bf16[128,128]{1,0:T(8,128)(2,1)S(1)} %get-tuple-element.36.left_ref), channel_id=1, source_target_pairs={{0,1},{1,0},{2,3},{3,2},{4,5},{5,4},{6,7},{7,6},{8,9},{9,8},{10,11... | collective-permute-start | bytes 98312 | tf_op jit(solution)/shard_map/ppermute | solution.py:32
  11.1 0.9 copy-start.1
  12.1 55.5 %copy-start = (bf16[4,512,128]{2,1,0:T(8,128)(2,1)}, bf16[4,512,128]{2,1,0:T(8,128)(2,1)S(1)}, u32[]{:S(2)}) copy-start(bf16[4,512,128]{2,1,0:T(8,128)(2,1)S(1)} %shard_map.94.refs_0_) | copy-start | bytes 1572868
  12.1 54.7 %copy-start.2 = (bf16[512,128]{1,0:T(8,128)(2,1)S(1)}, bf16[512,128]{1,0:T(8,128)(2,1)}, u32[]{:S(2)}) copy-start(bf16[512,128]{1,0:T(8,128)(2,1)} %cotangent_ref.1) | copy-start | bytes 393220
  12.1 16.6 %collective-permute-start.4 = (bf16[4,512,128]{2,1,0:T(8,128)(2,1)S(1)}, bf16[4,512,128]{2,1,0:T(8,128)(2,1)S(1)}, u32[]{:S(2)}, u32[]{:S(2)}) collective-permute-start(bf16[4,512,128]{2,1,0:T(8,128)(2,1)S(1)} %shard_map.94.refs_0_), channel_id=1, source_target_pairs={{0,2},{2,4},{4,6},{6,8},{8,10},{10,12},{12,14},{14,0},{1,3},{3,5},... | collective-permute-start | bytes 1572872 | tf_op jit(solution)/shard_map/ppermute | solution.py:32
  13.8 16.6 %collective-permute-start.5 = (bf16[4,512,128]{2,1,0:T(8,128)(2,1)S(1)}, bf16[4,512,128]{2,1,0:T(8,128)(2,1)S(1)}, u32[]{:S(2)}, u32[]{:S(2)}) collective-permute-start(bf16[4,512,128]{2,1,0:T(8,128)(2,1)S(1)} %shard_map.94.refs_0_), channel_id=1, source_target_pairs={{0,14},{2,0},{4,2},{6,4},{8,6},{10,8},{12,10},{14,12},{1,15},{3,1}... | collective-permute-start | bytes 1572872 | tf_op jit(solution)/shard_map/ppermute | solution.py:32
  18.5 15.5 %all-to-all-start = ((bf16[8,128,128]{2,1,0:T(8,128)(2,1)}), bf16[8,128,128]{2,1,0:T(8,128)(2,1)S(1)}, u32[]{:S(2)}, u32[]{:S(2)}) async-start(bf16[8,128,128]{2,1,0:T(8,128)(2,1)} %shard_map.95), calls=%async_computation | async-start | bytes 524288 | tf_op jit(solution)/shard_map/all_to_all | solution.py:36
  26.2 5.6 %collective-permute-start.6 = (bf16[1024,128]{1,0:T(8,128)(2,1)S(1)}, bf16[1024,128]{1,0:T(8,128)(2,1)S(1)}, u32[]{:S(2)}, u32[]{:S(2)}) collective-permute-start(bf16[1024,128]{1,0:T(8,128)(2,1)S(1)} %get-tuple-element.38), channel_id=1, source_target_pairs={{0,1},{1,0},{2,3},{3,2},{4,5},{5,4},{6,7},{7,6},{8,9},{9,8},{10,11... | collective-permute-start | bytes 786440 | tf_op jit(solution)/shard_map/ppermute | solution.py:32
  28.7 56.9 %copy-start.3 = (bf16[4,512,128]{2,1,0:T(8,128)(2,1)}, bf16[4,512,128]{2,1,0:T(8,128)(2,1)S(1)}, u32[]{:S(2)}) copy-start(bf16[4,512,128]{2,1,0:T(8,128)(2,1)S(1)} %collective-permute-done.4.refs_1_) | copy-start | bytes 1572868
  28.7 16.6 %collective-permute-start.7 = (bf16[4,512,128]{2,1,0:T(8,128)(2,1)S(1)}, bf16[4,512,128]{2,1,0:T(8,128)(2,1)S(1)}, u32[]{:S(2)}, u32[]{:S(2)}) collective-permute-start(bf16[4,512,128]{2,1,0:T(8,128)(2,1)S(1)} %collective-permute-done.4.refs_1_), channel_id=1, source_target_pairs={{0,2},{2,4},{4,6},{6,8},{8,10},{10,12},{12,14},{14,0},{1,3},{3,5},... | collective-permute-start | bytes 1572872 | tf_op jit(solution)/shard_map/ppermute | solution.py:32
  30.4 55.1 %copy-start.4 = (bf16[4,512,128]{2,1,0:T(8,128)(2,1)}, bf16[4,512,128]{2,1,0:T(8,128)(2,1)S(1)}, u32[]{:S(2)}) copy-start(bf16[4,512,128]{2,1,0:T(8,128)(2,1)S(1)} %collective-permute-done.5.refs_2_) | copy-start | bytes 1572868
  30.4 14.8 %collective-permute-start.8 = (bf16[4,512,128]{2,1,0:T(8,128)(2,1)S(1)}, bf16[4,512,128]{2,1,0:T(8,128)(2,1)S(1)}, u32[]{:S(2)}, u32[]{:S(2)}) collective-permute-start(bf16[4,512,128]{2,1,0:T(8,128)(2,1)S(1)} %collective-permute-done.5.refs_2_), channel_id=1, source_target_pairs={{0,14},{2,0},{4,2},{6,4},{8,6},{10,8},{12,10},{14,12},{1,15},{3,1}... | collective-permute-start | bytes 1572872 | tf_op jit(solution)/shard_map/ppermute | solution.py:32
  45.2 40.3 %copy-start.5 = (bf16[4,512,128]{2,1,0:T(8,128)(2,1)}, bf16[4,512,128]{2,1,0:T(8,128)(2,1)S(1)}, u32[]{:S(2)}) copy-start(bf16[4,512,128]{2,1,0:T(8,128)(2,1)S(1)} %collective-permute-done.7.refs_3_) | copy-start | bytes 1572868
  45.3 40.3 %copy-start.6 = (bf16[4,512,128]{2,1,0:T(8,128)(2,1)}, bf16[4,512,128]{2,1,0:T(8,128)(2,1)S(1)}, u32[]{:S(2)}) copy-start(bf16[4,512,128]{2,1,0:T(8,128)(2,1)S(1)} %collective-permute-done.8.refs_4_) | copy-start | bytes 1572868
  45.3 13.9 %collective-permute-start.10 = (bf16[4,512,128]{2,1,0:T(8,128)(2,1)S(1)}, bf16[4,512,128]{2,1,0:T(8,128)(2,1)S(1)}, u32[]{:S(2)}, u32[]{:S(2)}) collective-permute-start(bf16[4,512,128]{2,1,0:T(8,128)(2,1)S(1)} %collective-permute-done.8.refs_4_), channel_id=1, source_target_pairs={{0,14},{2,0},{4,2},{6,4},{8,6},{10,8},{12,10},{14,12},{1,15},{3,1}... | collective-permute-start | bytes 1572872 | tf_op jit(solution)/shard_map/ppermute | solution.py:32
  47.2 12.0 %collective-permute-start.9 = (bf16[4,512,128]{2,1,0:T(8,128)(2,1)S(1)}, bf16[4,512,128]{2,1,0:T(8,128)(2,1)}, u32[]{:S(2)}, u32[]{:S(2)}) collective-permute-start(bf16[4,512,128]{2,1,0:T(8,128)(2,1)S(1)} %collective-permute-done.7.refs_3_), channel_id=1, source_target_pairs={{0,2},{2,4},{4,6},{6,8},{8,10},{10,12},{12,14},{14,0},{1,3},{3,5},... | collective-permute-start | bytes 1572872 | tf_op jit(solution)/shard_map/ppermute | solution.py:32
  59.2 26.4 %copy-start.7 = (bf16[4,512,128]{2,1,0:T(8,128)(2,1)}, bf16[4,512,128]{2,1,0:T(8,128)(2,1)S(1)}, u32[]{:S(2)}) copy-start(bf16[4,512,128]{2,1,0:T(8,128)(2,1)S(1)} %collective-permute-done.10.refs_6_) | copy-start | bytes 1572868
  59.2 12.9 %collective-permute-start.11 = (bf16[4,512,128]{2,1,0:T(8,128)(2,1)}, bf16[4,512,128]{2,1,0:T(8,128)(2,1)}, u32[]{:S(2)}, u32[]{:S(2)}) collective-permute-start(bf16[4,512,128]{2,1,0:T(8,128)(2,1)} %collective-permute-done.9.refs_5_), channel_id=1, source_target_pairs={{0,2},{2,4},{4,6},{6,8},{8,10},{10,12},{12,14},{14,0},{1,3},{3,5},... | collective-permute-start | bytes 1572872 | tf_op jit(solution)/shard_map/ppermute | solution.py:32
  59.8 16.8 %collective-permute-start.12 = (bf16[4,512,128]{2,1,0:T(8,128)(2,1)S(1)}, bf16[4,512,128]{2,1,0:T(8,128)(2,1)}, u32[]{:S(2)}, u32[]{:S(2)}) collective-permute-start(bf16[4,512,128]{2,1,0:T(8,128)(2,1)S(1)} %shard_map.94.refs_0_), channel_id=1, source_target_pairs={{0,1},{1,0},{2,3},{3,2},{4,5},{5,4},{6,7},{7,6},{8,9},{9,8},{10,11... | collective-permute-start | bytes 1572872 | tf_op jit(solution)/shard_map/ppermute | solution.py:32
  66.3 11.4 %collective-permute-start.13 = (bf16[4,512,128]{2,1,0:T(8,128)(2,1)S(1)}, bf16[4,512,128]{2,1,0:T(8,128)(2,1)}, u32[]{:S(2)}, u32[]{:S(2)}) collective-permute-start(bf16[4,512,128]{2,1,0:T(8,128)(2,1)S(1)} %collective-permute-done.4.refs_1_), channel_id=1, source_target_pairs={{0,1},{1,0},{2,3},{3,2},{4,5},{5,4},{6,7},{7,6},{8,9},{9,8},{10,11... | collective-permute-start | bytes 1572872 | tf_op jit(solution)/shard_map/ppermute | solution.py:32
  66.3 11.5 %collective-permute-start.14 = (bf16[4,512,128]{2,1,0:T(8,128)(2,1)S(1)}, bf16[4,512,128]{2,1,0:T(8,128)(2,1)}, u32[]{:S(2)}, u32[]{:S(2)}) collective-permute-start(bf16[4,512,128]{2,1,0:T(8,128)(2,1)S(1)} %collective-permute-done.5.refs_2_), channel_id=1, source_target_pairs={{0,1},{1,0},{2,3},{3,2},{4,5},{5,4},{6,7},{7,6},{8,9},{9,8},{10,11... | collective-permute-start | bytes 1572872 | tf_op jit(solution)/shard_map/ppermute | solution.py:32
  67.6 9.0 %all-to-all-start.3 = ((f32[4,32,128]{2,1,0:T(8,128)}), f32[4,32,128]{2,1,0:T(8,128)S(1)}, u32[]{:S(2)}, u32[]{:S(2)}) async-start(f32[4,32,128]{2,1,0:T(8,128)} %shard_map.99), calls=%async_computation.3 | async-start | bytes 131072 | tf_op jit(solution)/shard_map/all_to_all | solution.py:36
  71.7 13.7 %collective-permute-start.15 = (bf16[4,512,128]{2,1,0:T(8,128)(2,1)S(1)}, bf16[4,512,128]{2,1,0:T(8,128)(2,1)}, u32[]{:S(2)}, u32[]{:S(2)}) collective-permute-start(bf16[4,512,128]{2,1,0:T(8,128)(2,1)S(1)} %collective-permute-done.7.refs_3_), channel_id=1, source_target_pairs={{0,1},{1,0},{2,3},{3,2},{4,5},{5,4},{6,7},{7,6},{8,9},{9,8},{10,11... | collective-permute-start | bytes 1572872 | tf_op jit(solution)/shard_map/ppermute | solution.py:32
  72.0 13.5 %collective-permute-start.16 = (bf16[4,512,128]{2,1,0:T(8,128)(2,1)S(1)}, bf16[4,512,128]{2,1,0:T(8,128)(2,1)}, u32[]{:S(2)}, u32[]{:S(2)}) collective-permute-start(bf16[4,512,128]{2,1,0:T(8,128)(2,1)S(1)} %collective-permute-done.8.refs_4_), channel_id=1, source_target_pairs={{0,1},{1,0},{2,3},{3,2},{4,5},{5,4},{6,7},{7,6},{8,9},{9,8},{10,11... | collective-permute-start | bytes 1572872 | tf_op jit(solution)/shard_map/ppermute | solution.py:32
  76.6 8.9 %collective-permute-start.17 = (bf16[4,512,128]{2,1,0:T(8,128)(2,1)}, bf16[4,512,128]{2,1,0:T(8,128)(2,1)S(1)}, u32[]{:S(2)}, u32[]{:S(2)}) collective-permute-start(bf16[4,512,128]{2,1,0:T(8,128)(2,1)} %collective-permute-done.9.refs_5_), channel_id=1, source_target_pairs={{0,1},{1,0},{2,3},{3,2},{4,5},{5,4},{6,7},{7,6},{8,9},{9,8},{10,11... | collective-permute-start | bytes 1572872 | tf_op jit(solution)/shard_map/ppermute | solution.py:32
  77.7 7.9 %collective-permute-start.18 = (bf16[4,512,128]{2,1,0:T(8,128)(2,1)S(1)}, bf16[4,512,128]{2,1,0:T(8,128)(2,1)}, u32[]{:S(2)}, u32[]{:S(2)}) collective-permute-start(bf16[4,512,128]{2,1,0:T(8,128)(2,1)S(1)} %collective-permute-done.10.refs_6_), channel_id=1, source_target_pairs={{0,1},{1,0},{2,3},{3,2},{4,5},{5,4},{6,7},{7,6},{8,9},{9,8},{10,11... | collective-permute-start | bytes 1572872 | tf_op jit(solution)/shard_map/ppermute | solution.py:32
  77.8 7.8 %collective-permute-start.19 = (bf16[4,512,128]{2,1,0:T(8,128)(2,1)}, bf16[4,512,128]{2,1,0:T(8,128)(2,1)}, u32[]{:S(2)}, u32[]{:S(2)}) collective-permute-start(bf16[4,512,128]{2,1,0:T(8,128)(2,1)} %collective-permute-done.11.refs_7_), channel_id=1, source_target_pairs={{0,1},{1,0},{2,3},{3,2},{4,5},{5,4},{6,7},{7,6},{8,9},{9,8},{10,11... | collective-permute-start | bytes 1572872 | tf_op jit(solution)/shard_map/ppermute | solution.py:32
  78.9 18.4 %all-to-all-start.4 = ((bf16[32,32,128]{2,1,0:T(8,128)(2,1)}), bf16[32,32,128]{2,1,0:T(8,128)(2,1)S(1)}, u32[]{:S(2)}, u32[]{:S(2)}) async-start(bf16[32,32,128]{2,1,0:T(8,128)(2,1)} %shard_map.101), calls=%async_computation.4 | async-start | bytes 524288 | tf_op jit(solution)/shard_map/all_to_all | solution.py:36
  85.5 0.8 copy-start.8
  97.3 4.3 %collective-permute-start.20 = (bf16[32,32,128]{2,1,0:T(8,128)(2,1)S(1)}, bf16[32,32,128]{2,1,0:T(8,128)(2,1)S(1)}, u32[]{:S(2)}, u32[]{:S(2)}) collective-permute-start(bf16[32,32,128]{2,1,0:T(8,128)(2,1)S(1)} %all-to-all-done.4.mine_ref.refs_1_), channel_id=1, source_target_pairs={{0,1},{1,0},{2,3},{3,2},{4,5},{5,4},{6,7},{7,6},{8,9},{9,8},{10,11... | collective-permute-start | bytes 786440 | tf_op jit(solution)/shard_map/ppermute | solution.py:32
  102.9 6.2 %collective-permute-start.21 = (f32[32,224]{1,0:T(8,128)S(1)}, f32[32,224]{1,0:T(8,128)S(1)}, u32[]{:S(2)}, u32[]{:S(2)}) collective-permute-start(f32[32,224]{1,0:T(8,128)S(1)} %get-tuple-element.57.refs_4_), channel_id=1, source_target_pairs={{0,64},{64,128},{128,192},{192,0},{1,65},{65,129},{129,193},{193,1... | collective-permute-start | bytes 86024 | tf_op jit(solution)/shard_map/ppermute | solution.py:32
  103.2 5.9 %collective-permute-start.22 = (f32[32,224]{1,0:T(8,128)S(1)}, f32[32,224]{1,0:T(8,128)S(1)}, u32[]{:S(2)}, u32[]{:S(2)}) collective-permute-start(f32[32,224]{1,0:T(8,128)S(1)} %get-tuple-element.57.refs_4_), channel_id=1, source_target_pairs={{0,128},{64,192},{128,0},{192,64},{1,129},{65,193},{129,1},{193,65... | collective-permute-start | bytes 86024 | tf_op jit(solution)/shard_map/ppermute | solution.py:32
  105.5 3.7 %collective-permute-start.23 = (f32[32,224]{1,0:T(8,128)S(1)}, f32[32,224]{1,0:T(8,128)S(1)}, u32[]{:S(2)}, u32[]{:S(2)}) collective-permute-start(f32[32,224]{1,0:T(8,128)S(1)} %get-tuple-element.57.refs_4_), channel_id=1, source_target_pairs={{0,192},{64,0},{128,64},{192,128},{1,193},{65,1},{129,65},{193,129... | collective-permute-start | bytes 86024 | tf_op jit(solution)/shard_map/ppermute | solution.py:32

commit v10 on v9

--- a/solution.py
+++ b/solution.py
@@ -73,8 +73,9 @@
     return copy
 
 
-def left_kernel(gate_hbm, up_hbm, q_hbm, hidden_hbm, left_ref, gate_ref, up_ref, q_ref, hidden_ref, sems):
+def left_kernel(gate_hbm, up_hbm, q_hbm, slice_hbm, hidden_hbm, left_ref, slice_ref, gate_ref, up_ref, q_ref, hidden_ref, sems):
     rank = q_ref.shape[0]
+    kept = fetch(slice_hbm, slice_ref, sems.at[4])
     for copy in [fetch(a, b, sems.at[i]) for i, (a, b) in enumerate(((gate_hbm, gate_ref), (up_hbm, up_ref), (q_hbm, q_ref)))]:
         copy.wait()
     gate = gate_ref[...].astype(F32)
@@ -86,6 +87,7 @@
     for b in range(left.shape[1] // LANES):
         left_ref[b * rank:(b + 1) * rank, :] = left[:, b * LANES:(b + 1) * LANES]
     copy.wait()
+    kept.wait()
 
 
 def chip_kernel(left_ref, theirs_ref, out_ref):
@@ -311,20 +313,20 @@
     tie = lax.optimization_barrier
 
     blocks = [cotangent] + [shift(cotangent, "x", hop, X) for hop in range(1, X)]
-    hidden, left = call(
+    hidden, left, blocks[0] = call(
         left_kernel,
-        [((rows, tokens), BF), ((tiles, LANES), BF)],
+        [((rows, tokens), BF), ((tiles, LANES), BF), ((tokens, wide), BF)],
         [
             pltpu.VMEM((rows, tokens), BF),
             pltpu.VMEM((rows, tokens), BF),
             pltpu.VMEM((rank, rows), F32),
             pltpu.VMEM((rows, tokens), BF),
-            pltpu.SemaphoreType.DMA((4,)),
+            pltpu.SemaphoreType.DMA((5,)),
         ],
-        [HBM] * 3,
-        [HBM, VMEM],
+        [HBM] * 4,
+        [HBM, VMEM, VMEM],
         moved=6 * rows * tokens,
-    )(gate.T, upward.T, start_q.T)
+    )(gate.T, upward.T, start_q.T, cotangent)
     theirs = shift(left, "core", 1, CORES)
     send, mine = call(
         error_kernel,
@@ -335,8 +337,7 @@
         moved=2 * rows * columns,
     )(start_q.T, error)
     part = shift(send, "core", 1, CORES)
-    tied = tie((left, theirs, *blocks[1:]))
-    left, theirs, blocks[1:] = tied[0], tied[1], tied[2:]
+    left, theirs, *blocks = tie((left, theirs, *blocks))
     stacked, = call(stack_kernel, [((X, tokens, wide), BF)], ins=[None] * X, outs=[None])(*blocks)
     pieces, others = {0: stacked}, {}
     steps = (0, 1, 7, 2, 6, 3, 5, 4)

time: 114 us -> 113 us (level)
  no operation moved by 1% of the time
where the time goes in v10:
time: 113 us; the launch traced here: 112 us
  starting transfers between devices  55.2 us (49%)
  Pallas kernels  28.8 us (25%)
  blocking collectives  21.5 us (19%)
  waiting for transfers between devices  5.24 us (5%)
    ppermute x24, starting transfers between devices, shift(): return lax.ppermute(a, axis, [(i, (i + step) % n) for i in range(n)])  39.3 us
    pallas_call x13, Pallas kernels, call(): return lambda *args: run(*(placed(a, spec) for a, spec in zip(args, ins)))  28.8 us
    all_to_all x2, blocking collectives, exchange(): return lax.all_to_all(a, axis, 0, 0)  21.5 us
    all_to_all x3, starting transfers between devices, exchange(): return lax.all_to_all(a, axis, 0, 0)  15.9 us
    ppermute x24, waiting for transfers between devices, shift(): return lax.ppermute(a, axis, [(i, (i + step) % n) for i in range(n)])  2.95 us
    all_to_all x3, waiting for transfers between devices, exchange(): return lax.all_to_all(a, axis, 0, 0)  2.29 us
  transfers between devices with their start and end apart: 27, of which 5 were waited for; matrix products, arithmetic and copies ran while one was open for 0% of the time, Pallas kernels for 21%

profile of v10, /device:TPU:1, one launch (start us, length us, event | category | flops | bytes accessed | tf_op | source)
XLA Modules:
  0.0 112.5 jit_solution(7596628383413309988)
XLA Ops:
  0.6 2.1 %collective-permute-start.1 = (bf16[512,128]{1,0:T(8,128)(2,1)}, bf16[512,128]{1,0:T(8,128)(2,1)S(1)}, u32[]{:S(2)}, u32[]{:S(2)}) collective-permute-start(bf16[512,128]{1,0:T(8,128)(2,1)} %cotangent_ref.1), channel_id=1, source_target_pairs={{0,16},{16,32},{32,48},{48,0},{1,17},{17,33},{33,49},{49,1},{2,18}... | collective-permute-start | bytes 393224 | tf_op jit(solution)/shard_map/ppermute | solution.py:32
  2.7 2.5 %collective-permute-start.2 = (bf16[512,128]{1,0:T(8,128)(2,1)}, bf16[512,128]{1,0:T(8,128)(2,1)S(1)}, u32[]{:S(2)}, u32[]{:S(2)}) collective-permute-start(bf16[512,128]{1,0:T(8,128)(2,1)} %cotangent_ref.1), channel_id=1, source_target_pairs={{0,32},{16,48},{32,0},{48,16},{1,33},{17,49},{33,1},{49,17},{2,34}... | collective-permute-start | bytes 393224 | tf_op jit(solution)/shard_map/ppermute | solution.py:32
  5.2 1.2 %collective-permute-start.3 = (bf16[512,128]{1,0:T(8,128)(2,1)}, bf16[512,128]{1,0:T(8,128)(2,1)S(1)}, u32[]{:S(2)}, u32[]{:S(2)}) collective-permute-start(bf16[512,128]{1,0:T(8,128)(2,1)} %cotangent_ref.1), channel_id=1, source_target_pairs={{0,48},{16,0},{32,16},{48,32},{1,49},{17,1},{33,17},{49,33},{2,50}... | collective-permute-start | bytes 393224 | tf_op jit(solution)/shard_map/ppermute | solution.py:32
  6.4 1.9 %shard_map.93 = (bf16[224,512]{1,0:T(8,128)(2,1)}, bf16[128,128]{1,0:T(8,128)(2,1)S(1)}, bf16[512,128]{1,0:T(8,128)(2,1)S(1)}) custom-call(bf16[224,512]{1,0:T(8,128)(2,1)} %bitcast.10, bf16[224,512]{1,0:T(8,128)(2,1)} %bitcast.12, f32[32,224]{1,0:T(8,128)} %bitcast.14, bf16[512,128]{1,0:T(8,128)(2,1)} %cotangent_ref.1), custom_call_target="tpu_custom_call" | custom-call | bytes 688128 | tf_op jit(solution)/shard_map/pallas_call | solution.py:54
  8.3 1.6 %collective-permute-start = (bf16[128,128]{1,0:T(8,128)(2,1)S(1)}, bf16[128,128]{1,0:T(8,128)(2,1)S(1)}, u32[]{:S(2)}, u32[]{:S(2)}) collective-permute-start(bf16[128,128]{1,0:T(8,128)(2,1)S(1)} %get-tuple-element.40.left_ref), channel_id=1, source_target_pairs={{0,1},{1,0},{2,3},{3,2},{4,5},{5,4},{6,7},{7,6},{8,9},{9,8},{10,11... | collective-permute-start | bytes 98312 | tf_op jit(solution)/shard_map/ppermute | solution.py:32
  9.9 0.9 collective-permute-done.theirs_ref
  10.8 0.3 collective-permute-done.2.refs_2_
  11.2 0.0 copy-start
  11.2 0.0 copy-start.1
  11.2 1.7 %collective-permute-start.4 = (bf16[4,512,128]{2,1,0:T(8,128)(2,1)S(1)}, bf16[4,512,128]{2,1,0:T(8,128)(2,1)S(1)}, u32[]{:S(2)}, u32[]{:S(2)}) collective-permute-start(bf16[4,512,128]{2,1,0:T(8,128)(2,1)S(1)} %shard_map.94.refs_0_), channel_id=1, source_target_pairs={{0,2},{2,4},{4,6},{6,8},{8,10},{10,12},{12,14},{14,0},{1,3},{3,5},... | collective-permute-start | bytes 1572872 | tf_op jit(solution)/shard_map/ppermute | solution.py:32
  12.9 4.0 %collective-permute-start.5 = (bf16[4,512,128]{2,1,0:T(8,128)(2,1)S(1)}, bf16[4,512,128]{2,1,0:T(8,128)(2,1)S(1)}, u32[]{:S(2)}, u32[]{:S(2)}) collective-permute-start(bf16[4,512,128]{2,1,0:T(8,128)(2,1)S(1)} %shard_map.94.refs_0_), channel_id=1, source_target_pairs={{0,14},{2,0},{4,2},{6,4},{8,6},{10,8},{12,10},{14,12},{1,15},{3,1}... | collective-permute-start | bytes 1572872 | tf_op jit(solution)/shard_map/ppermute | solution.py:32
  16.9 0.7 shard_map.95
  17.6 5.2 %all-to-all-start = ((bf16[8,128,128]{2,1,0:T(8,128)(2,1)}), bf16[8,128,128]{2,1,0:T(8,128)(2,1)S(1)}, u32[]{:S(2)}, u32[]{:S(2)}) async-start(bf16[8,128,128]{2,1,0:T(8,128)(2,1)} %shard_map.95), calls=%async_computation | async-start | bytes 524288 | tf_op jit(solution)/shard_map/all_to_all | solution.py:36
  22.8 2.4 %shard_map.96 = (bf16[1024,128]{1,0:T(8,128)(2,1)S(1)}, bf16[1024,128]{1,0:T(8,128)(2,1)S(1)}) custom-call(f32[32,224]{1,0:T(8,128)} %bitcast.15, bf16[224,8192]{1,0:T(8,128)(2,1)} %bitcast.8), custom_call_target="tpu_custom_call" | custom-call | flops 234881024 | bytes 3670016 | tf_op jit(solution)/shard_map/pallas_call | solution.py:54
  25.3 2.5 %collective-permute-start.6 = (bf16[1024,128]{1,0:T(8,128)(2,1)S(1)}, bf16[1024,128]{1,0:T(8,128)(2,1)S(1)}, u32[]{:S(2)}, u32[]{:S(2)}) collective-permute-start(bf16[1024,128]{1,0:T(8,128)(2,1)S(1)} %get-tuple-element.42), channel_id=1, source_target_pairs={{0,1},{1,0},{2,3},{3,2},{4,5},{5,4},{6,7},{7,6},{8,9},{9,8},{10,11... | collective-permute-start | bytes 786440 | tf_op jit(solution)/shard_map/ppermute | solution.py:32
  27.8 1.7 %collective-permute-start.7 = (bf16[4,512,128]{2,1,0:T(8,128)(2,1)S(1)}, bf16[4,512,128]{2,1,0:T(8,128)(2,1)S(1)}, u32[]{:S(2)}, u32[]{:S(2)}) collective-permute-start(bf16[4,512,128]{2,1,0:T(8,128)(2,1)S(1)} %collective-permute-done.4.refs_1_), channel_id=1, source_target_pairs={{0,2},{2,4},{4,6},{6,8},{8,10},{10,12},{12,14},{14,0},{1,3},{3,5},... | collective-permute-start | bytes 1572872 | tf_op jit(solution)/shard_map/ppermute | solution.py:32
  29.5 1.3 %collective-permute-start.8 = (bf16[4,512,128]{2,1,0:T(8,128)(2,1)S(1)}, bf16[4,512,128]{2,1,0:T(8,128)(2,1)S(1)}, u32[]{:S(2)}, u32[]{:S(2)}) collective-permute-start(bf16[4,512,128]{2,1,0:T(8,128)(2,1)S(1)} %collective-permute-done.5.refs_2_), channel_id=1, source_target_pairs={{0,14},{2,0},{4,2},{6,4},{8,6},{10,8},{12,10},{14,12},{1,15},{3,1}... | collective-permute-start | bytes 1572872 | tf_op jit(solution)/shard_map/ppermute | solution.py:32
  30.8 2.3 %all-to-all-done.left_ref = bf16[8,128,128]{2,1,0:T(8,128)(2,1)S(1)} async-done(((bf16[8,128,128]{2,1,0:T(8,128)(2,1)}), bf16[8,128,128]{2,1,0:T(8,128)(2,1)S(1)}, u32[]{:S(2)}, u32[]{:S(2)}) %all-to-all-start) | async-done | bytes 262176 | tf_op jit(solution)/shard_map/all_to_all | solution.py:36
  33.1 0.1 shard_map.97
  33.2 9.5 %all_to_all.25.terms_ref = bf16[4,384,128]{2,1,0:T(8,128)(2,1)S(1)} all-to-all(bf16[4,384,128]{2,1,0:T(8,128)(2,1)S(1)} %shard_map.97), channel_id=1, replica_groups=mesh['dp'=4,'x'=4,'z'=8,'core'=2] {'x'}, dimensions={0} | all-to-all | bytes 786432 | tf_op jit(solution)/shard_map/all_to_all | solution.py:36
  42.7 1.6 %collective-permute-done.7.refs_3_ = bf16[4,512,128]{2,1,0:T(8,128)(2,1)S(1)} collective-permute-done((bf16[4,512,128]{2,1,0:T(8,128)(2,1)S(1)}, bf16[4,512,128]{2,1,0:T(8,128)(2,1)S(1)}, u32[]{:S(2)}, u32[]{:S(2)}) %collective-permute-start.7) | collective-permute-done | bytes 524320 | tf_op jit(solution)/shard_map/ppermute | solution.py:32
  44.4 1.9 %collective-permute-start.10 = (bf16[4,512,128]{2,1,0:T(8,128)(2,1)S(1)}, bf16[4,512,128]{2,1,0:T(8,128)(2,1)S(1)}, u32[]{:S(2)}, u32[]{:S(2)}) collective-permute-start(bf16[4,512,128]{2,1,0:T(8,128)(2,1)S(1)} %collective-permute-done.8.refs_4_), channel_id=1, source_target_pairs={{0,14},{2,0},{4,2},{6,4},{8,6},{10,8},{12,10},{14,12},{1,15},{3,1}... | collective-permute-start | bytes 1572872 | tf_op jit(solution)/shard_map/ppermute | solution.py:32
  46.3 0.1 shard_map.98
  46.3 12.0 %all_to_all.26.part_ref = bf16[8,32,128]{2,1,0:T(8,128)(2,1)S(1)} all-to-all(bf16[8,32,128]{2,1,0:T(8,128)(2,1)S(1)} %get-tuple-element.47), channel_id=1, replica_groups=mesh['dp'=4,'x'=4,'z'=8,'core'=2] {'z'}, dimensions={0} | all-to-all | bytes 131072 | tf_op jit(solution)/shard_map/all_to_all | solution.py:36
  58.3 0.6 collective-permute-start.11
  58.9 6.4 %collective-permute-start.12 = (bf16[4,512,128]{2,1,0:T(8,128)(2,1)S(1)}, bf16[4,512,128]{2,1,0:T(8,128)(2,1)}, u32[]{:S(2)}, u32[]{:S(2)}) collective-permute-start(bf16[4,512,128]{2,1,0:T(8,128)(2,1)S(1)} %shard_map.94.refs_0_), channel_id=1, source_target_pairs={{0,1},{1,0},{2,3},{3,2},{4,5},{5,4},{6,7},{7,6},{8,9},{9,8},{10,11... | collective-permute-start | bytes 1572872 | tf_op jit(solution)/shard_map/ppermute | solution.py:32
  65.4 0.5 collective-permute-start.14
  65.9 0.8 shard_map.99
  66.7 4.2 %all-to-all-start.3 = ((f32[4,32,128]{2,1,0:T(8,128)}), f32[4,32,128]{2,1,0:T(8,128)S(1)}, u32[]{:S(2)}, u32[]{:S(2)}) async-start(f32[4,32,128]{2,1,0:T(8,128)} %shard_map.99), calls=%async_computation.3 | async-start | bytes 131072 | tf_op jit(solution)/shard_map/all_to_all | solution.py:36
  70.8 0.3 collective-permute-start.15
  71.1 4.5 %collective-permute-start.16 = (bf16[4,512,128]{2,1,0:T(8,128)(2,1)S(1)}, bf16[4,512,128]{2,1,0:T(8,128)(2,1)}, u32[]{:S(2)}, u32[]{:S(2)}) collective-permute-start(bf16[4,512,128]{2,1,0:T(8,128)(2,1)S(1)} %collective-permute-done.8.refs_4_), channel_id=1, source_target_pairs={{0,1},{1,0},{2,3},{3,2},{4,5},{5,4},{6,7},{7,6},{8,9},{9,8},{10,11... | collective-permute-start | bytes 1572872 | tf_op jit(solution)/shard_map/ppermute | solution.py:32
  75.7 1.1 collective-permute-start.17
  76.8 0.1 collective-permute-start.18
  76.8 0.4 collective-permute-start.19
  77.3 0.7 shard_map.101
  78.0 6.6 %all-to-all-start.4 = ((bf16[32,32,128]{2,1,0:T(8,128)(2,1)}), bf16[32,32,128]{2,1,0:T(8,128)(2,1)S(1)}, u32[]{:S(2)}, u32[]{:S(2)}) async-start(bf16[32,32,128]{2,1,0:T(8,128)(2,1)} %shard_map.101), calls=%async_computation.4 | async-start | bytes 524288 | tf_op jit(solution)/shard_map/all_to_all | solution.py:36
  84.7 0.7 copy-done.7
  85.4 10.9 %shard_map.100 = (f32[224,8192]{1,0:T(8,128)}, bf16[224,512]{1,0:T(8,128)(2,1)}, bf16[224,512]{1,0:T(8,128)(2,1)}) custom-call(bf16[4,512,128]{2,1,0:T(8,128)(2,1)} %copy-done, bf16[4,512,128]{2,1,0:T(8,128)(2,1)} %copy-done.2, bf16[4,512,128]{2,1,0:T(8,128)(2,1)} %copy-done.3, bf16[4,512,128]{2,1,0:T(8,128)(2,1)} %copy-done.4, ...), custom_call_target="tpu_custom_call" | custom-call | flops 3758096384 | bytes 31457280 | tf_op jit(solution)/shard_map/pallas_call | solution.py:54
  96.3 1.2 %collective-permute-start.20 = (bf16[32,32,128]{2,1,0:T(8,128)(2,1)S(1)}, bf16[32,32,128]{2,1,0:T(8,128)(2,1)S(1)}, u32[]{:S(2)}, u32[]{:S(2)}) collective-permute-start(bf16[32,32,128]{2,1,0:T(8,128)(2,1)S(1)} %all-to-all-done.4.mine_ref.refs_1_), channel_id=1, source_target_pairs={{0,1},{1,0},{2,3},{3,2},{4,5},{5,4},{6,7},{7,6},{8,9},{9,8},{10,11... | collective-permute-start | bytes 786440 | tf_op jit(solution)/shard_map/ppermute | solution.py:32
  97.5 3.2 %shard_map.102.matrix_ref.refs_0_ = f32[224,8192]{1,0:T(8,128)S(1)} custom-call(f32[224,8192]{1,0:T(8,128)} %get-tuple-element.58.source_hbm), custom_call_target="tpu_custom_call" | custom-call | tf_op jit(solution)/shard_map/pallas_call | solution.py:54
  100.7 1.3 %shard_map.103 = (f32[32,224]{1,0:T(8,128)S(1)}, f32[32,32]{1,0:T(8,128)S(1)}) custom-call(f32[224,8192]{1,0:T(8,128)S(1)} %shard_map.102.matrix_ref.refs_0_, bf16[32,32,128]{2,1,0:T(8,128)(2,1)S(1)} %all-to-all-done.4.mine_ref.refs_1_, bf16[32,32,128]{2,1,0:T(8,128)(2,1)S(1)} %collective-permute-done.20.theirs_ref.refs_2_), custom_call_target="tpu_custom_call" | custom-call | flops 117440512 | bytes 7340032 | tf_op jit(solution)/shard_map/pallas_call | solution.py:54
  102.0 0.3 collective-permute-start.21
  102.3 2.2 %collective-permute-start.22 = (f32[32,224]{1,0:T(8,128)S(1)}, f32[32,224]{1,0:T(8,128)S(1)}, u32[]{:S(2)}, u32[]{:S(2)}) collective-permute-start(f32[32,224]{1,0:T(8,128)S(1)} %get-tuple-element.61.refs_4_), channel_id=1, source_target_pairs={{0,128},{64,192},{128,0},{192,64},{1,129},{65,193},{129,1},{193,65... | collective-permute-start | bytes 86024 | tf_op jit(solution)/shard_map/ppermute | solution.py:32
  104.6 1.1 collective-permute-start.23
  105.6 2.6 %shard_map.104.refs_3_ = f32[32,32]{1,0:T(8,128)S(1)} custom-call(f32[32,32]{1,0:T(8,128)S(1)} %get-tuple-element.60.gram_ref), custom_call_target="tpu_custom_call" | custom-call | tf_op jit(solution)/shard_map/pallas_call | solution.py:54
  108.2 0.0 collective-permute-done.22.refs_6_
  108.2 0.1 collective-permute-done.23.refs_7_
  108.3 4.0 %shard_map.105 = (bf16[224,8192]{1,0:T(8,128)(2,1)}, f32[32,224]{1,0:T(8,128)}) custom-call(f32[224,8192]{1,0:T(8,128)S(1)} %shard_map.102.matrix_ref.refs_0_, bf16[32,32,128]{2,1,0:T(8,128)(2,1)S(1)} %all-to-all-done.4.mine_ref.refs_1_, bf16[32,32,128]{2,1,0:T(8,128)(2,1)S(1)} %collective-permute-done.20.theirs_ref.refs_2_, ...), custom_call_target="tpu_custom_call" | custom-call | flops 234881024 | bytes 11010048 | tf_op jit(solution)/shard_map/pallas_call | solution.py:54
  (37 shorter events, 0.1 us)
Async XLA Ops:
  0.6 10.1 %collective-permute-start.1 = (bf16[512,128]{1,0:T(8,128)(2,1)}, bf16[512,128]{1,0:T(8,128)(2,1)S(1)}, u32[]{:S(2)}, u32[]{:S(2)}) collective-permute-start(bf16[512,128]{1,0:T(8,128)(2,1)} %cotangent_ref.1), channel_id=1, source_target_pairs={{0,16},{16,32},{32,48},{48,0},{1,17},{17,33},{33,49},{49,1},{2,18}... | collective-permute-start | bytes 393224 | tf_op jit(solution)/shard_map/ppermute | solution.py:32
  2.7 8.4 %collective-permute-start.2 = (bf16[512,128]{1,0:T(8,128)(2,1)}, bf16[512,128]{1,0:T(8,128)(2,1)S(1)}, u32[]{:S(2)}, u32[]{:S(2)}) collective-permute-start(bf16[512,128]{1,0:T(8,128)(2,1)} %cotangent_ref.1), channel_id=1, source_target_pairs={{0,32},{16,48},{32,0},{48,16},{1,33},{17,49},{33,1},{49,17},{2,34}... | collective-permute-start | bytes 393224 | tf_op jit(solution)/shard_map/ppermute | solution.py:32
  5.2 5.9 %collective-permute-start.3 = (bf16[512,128]{1,0:T(8,128)(2,1)}, bf16[512,128]{1,0:T(8,128)(2,1)S(1)}, u32[]{:S(2)}, u32[]{:S(2)}) collective-permute-start(bf16[512,128]{1,0:T(8,128)(2,1)} %cotangent_ref.1), channel_id=1, source_target_pairs={{0,48},{16,0},{32,16},{48,32},{1,49},{17,1},{33,17},{49,33},{2,50}... | collective-permute-start | bytes 393224 | tf_op jit(solution)/shard_map/ppermute | solution.py:32
  8.3 2.5 %collective-permute-start = (bf16[128,128]{1,0:T(8,128)(2,1)S(1)}, bf16[128,128]{1,0:T(8,128)(2,1)S(1)}, u32[]{:S(2)}, u32[]{:S(2)}) collective-permute-start(bf16[128,128]{1,0:T(8,128)(2,1)S(1)} %get-tuple-element.40.left_ref), channel_id=1, source_target_pairs={{0,1},{1,0},{2,3},{3,2},{4,5},{5,4},{6,7},{7,6},{8,9},{9,8},{10,11... | collective-permute-start | bytes 98312 | tf_op jit(solution)/shard_map/ppermute | solution.py:32
  11.2 55.5 %copy-start = (bf16[4,512,128]{2,1,0:T(8,128)(2,1)}, bf16[4,512,128]{2,1,0:T(8,128)(2,1)S(1)}, u32[]{:S(2)}) copy-start(bf16[4,512,128]{2,1,0:T(8,128)(2,1)S(1)} %shard_map.94.refs_0_) | copy-start | bytes 1572868
  11.2 54.7 %copy-start.1 = (bf16[512,128]{1,0:T(8,128)(2,1)S(1)}, bf16[512,128]{1,0:T(8,128)(2,1)}, u32[]{:S(2)}) copy-start(bf16[512,128]{1,0:T(8,128)(2,1)} %cotangent_ref.1) | copy-start | bytes 393220
  11.2 16.6 %collective-permute-start.4 = (bf16[4,512,128]{2,1,0:T(8,128)(2,1)S(1)}, bf16[4,512,128]{2,1,0:T(8,128)(2,1)S(1)}, u32[]{:S(2)}, u32[]{:S(2)}) collective-permute-start(bf16[4,512,128]{2,1,0:T(8,128)(2,1)S(1)} %shard_map.94.refs_0_), channel_id=1, source_target_pairs={{0,2},{2,4},{4,6},{6,8},{8,10},{10,12},{12,14},{14,0},{1,3},{3,5},... | collective-permute-start | bytes 1572872 | tf_op jit(solution)/shard_map/ppermute | solution.py:32
  12.9 16.6 %collective-permute-start.5 = (bf16[4,512,128]{2,1,0:T(8,128)(2,1)S(1)}, bf16[4,512,128]{2,1,0:T(8,128)(2,1)S(1)}, u32[]{:S(2)}, u32[]{:S(2)}) collective-permute-start(bf16[4,512,128]{2,1,0:T(8,128)(2,1)S(1)} %shard_map.94.refs_0_), channel_id=1, source_target_pairs={{0,14},{2,0},{4,2},{6,4},{8,6},{10,8},{12,10},{14,12},{1,15},{3,1}... | collective-permute-start | bytes 1572872 | tf_op jit(solution)/shard_map/ppermute | solution.py:32
  17.6 15.5 %all-to-all-start = ((bf16[8,128,128]{2,1,0:T(8,128)(2,1)}), bf16[8,128,128]{2,1,0:T(8,128)(2,1)S(1)}, u32[]{:S(2)}, u32[]{:S(2)}) async-start(bf16[8,128,128]{2,1,0:T(8,128)(2,1)} %shard_map.95), calls=%async_computation | async-start | bytes 524288 | tf_op jit(solution)/shard_map/all_to_all | solution.py:36
  25.3 5.5 %collective-permute-start.6 = (bf16[1024,128]{1,0:T(8,128)(2,1)S(1)}, bf16[1024,128]{1,0:T(8,128)(2,1)S(1)}, u32[]{:S(2)}, u32[]{:S(2)}) collective-permute-start(bf16[1024,128]{1,0:T(8,128)(2,1)S(1)} %get-tuple-element.42), channel_id=1, source_target_pairs={{0,1},{1,0},{2,3},{3,2},{4,5},{5,4},{6,7},{7,6},{8,9},{9,8},{10,11... | collective-permute-start | bytes 786440 | tf_op jit(solution)/shard_map/ppermute | solution.py:32
  27.8 56.9 %copy-start.2 = (bf16[4,512,128]{2,1,0:T(8,128)(2,1)}, bf16[4,512,128]{2,1,0:T(8,128)(2,1)S(1)}, u32[]{:S(2)}) copy-start(bf16[4,512,128]{2,1,0:T(8,128)(2,1)S(1)} %collective-permute-done.4.refs_1_) | copy-start | bytes 1572868
  27.8 16.6 %collective-permute-start.7 = (bf16[4,512,128]{2,1,0:T(8,128)(2,1)S(1)}, bf16[4,512,128]{2,1,0:T(8,128)(2,1)S(1)}, u32[]{:S(2)}, u32[]{:S(2)}) collective-permute-start(bf16[4,512,128]{2,1,0:T(8,128)(2,1)S(1)} %collective-permute-done.4.refs_1_), channel_id=1, source_target_pairs={{0,2},{2,4},{4,6},{6,8},{8,10},{10,12},{12,14},{14,0},{1,3},{3,5},... | collective-permute-start | bytes 1572872 | tf_op jit(solution)/shard_map/ppermute | solution.py:32
  29.5 55.1 %copy-start.3 = (bf16[4,512,128]{2,1,0:T(8,128)(2,1)}, bf16[4,512,128]{2,1,0:T(8,128)(2,1)S(1)}, u32[]{:S(2)}) copy-start(bf16[4,512,128]{2,1,0:T(8,128)(2,1)S(1)} %collective-permute-done.5.refs_2_) | copy-start | bytes 1572868
  29.5 14.8 %collective-permute-start.8 = (bf16[4,512,128]{2,1,0:T(8,128)(2,1)S(1)}, bf16[4,512,128]{2,1,0:T(8,128)(2,1)S(1)}, u32[]{:S(2)}, u32[]{:S(2)}) collective-permute-start(bf16[4,512,128]{2,1,0:T(8,128)(2,1)S(1)} %collective-permute-done.5.refs_2_), channel_id=1, source_target_pairs={{0,14},{2,0},{4,2},{6,4},{8,6},{10,8},{12,10},{14,12},{1,15},{3,1}... | collective-permute-start | bytes 1572872 | tf_op jit(solution)/shard_map/ppermute | solution.py:32
  44.3 40.3 %copy-start.4 = (bf16[4,512,128]{2,1,0:T(8,128)(2,1)}, bf16[4,512,128]{2,1,0:T(8,128)(2,1)S(1)}, u32[]{:S(2)}) copy-start(bf16[4,512,128]{2,1,0:T(8,128)(2,1)S(1)} %collective-permute-done.7.refs_3_) | copy-start | bytes 1572868
  44.4 40.3 %copy-start.5 = (bf16[4,512,128]{2,1,0:T(8,128)(2,1)}, bf16[4,512,128]{2,1,0:T(8,128)(2,1)S(1)}, u32[]{:S(2)}) copy-start(bf16[4,512,128]{2,1,0:T(8,128)(2,1)S(1)} %collective-permute-done.8.refs_4_) | copy-start | bytes 1572868
  44.4 13.9 %collective-permute-start.10 = (bf16[4,512,128]{2,1,0:T(8,128)(2,1)S(1)}, bf16[4,512,128]{2,1,0:T(8,128)(2,1)S(1)}, u32[]{:S(2)}, u32[]{:S(2)}) collective-permute-start(bf16[4,512,128]{2,1,0:T(8,128)(2,1)S(1)} %collective-permute-done.8.refs_4_), channel_id=1, source_target_pairs={{0,14},{2,0},{4,2},{6,4},{8,6},{10,8},{12,10},{14,12},{1,15},{3,1}... | collective-permute-start | bytes 1572872 | tf_op jit(solution)/shard_map/ppermute | solution.py:32
  46.3 12.0 %collective-permute-start.9 = (bf16[4,512,128]{2,1,0:T(8,128)(2,1)S(1)}, bf16[4,512,128]{2,1,0:T(8,128)(2,1)}, u32[]{:S(2)}, u32[]{:S(2)}) collective-permute-start(bf16[4,512,128]{2,1,0:T(8,128)(2,1)S(1)} %collective-permute-done.7.refs_3_), channel_id=1, source_target_pairs={{0,2},{2,4},{4,6},{6,8},{8,10},{10,12},{12,14},{14,0},{1,3},{3,5},... | collective-permute-start | bytes 1572872 | tf_op jit(solution)/shard_map/ppermute | solution.py:32
  58.3 26.4 %copy-start.6 = (bf16[4,512,128]{2,1,0:T(8,128)(2,1)}, bf16[4,512,128]{2,1,0:T(8,128)(2,1)S(1)}, u32[]{:S(2)}) copy-start(bf16[4,512,128]{2,1,0:T(8,128)(2,1)S(1)} %collective-permute-done.10.refs_6_) | copy-start | bytes 1572868
  58.3 12.8 %collective-permute-start.11 = (bf16[4,512,128]{2,1,0:T(8,128)(2,1)}, bf16[4,512,128]{2,1,0:T(8,128)(2,1)}, u32[]{:S(2)}, u32[]{:S(2)}) collective-permute-start(bf16[4,512,128]{2,1,0:T(8,128)(2,1)} %collective-permute-done.9.refs_5_), channel_id=1, source_target_pairs={{0,2},{2,4},{4,6},{6,8},{8,10},{10,12},{12,14},{14,0},{1,3},{3,5},... | collective-permute-start | bytes 1572872 | tf_op jit(solution)/shard_map/ppermute | solution.py:32
  58.9 16.7 %collective-permute-start.12 = (bf16[4,512,128]{2,1,0:T(8,128)(2,1)S(1)}, bf16[4,512,128]{2,1,0:T(8,128)(2,1)}, u32[]{:S(2)}, u32[]{:S(2)}) collective-permute-start(bf16[4,512,128]{2,1,0:T(8,128)(2,1)S(1)} %shard_map.94.refs_0_), channel_id=1, source_target_pairs={{0,1},{1,0},{2,3},{3,2},{4,5},{5,4},{6,7},{7,6},{8,9},{9,8},{10,11... | collective-permute-start | bytes 1572872 | tf_op jit(solution)/shard_map/ppermute | solution.py:32
  65.4 11.4 %collective-permute-start.13 = (bf16[4,512,128]{2,1,0:T(8,128)(2,1)S(1)}, bf16[4,512,128]{2,1,0:T(8,128)(2,1)}, u32[]{:S(2)}, u32[]{:S(2)}) collective-permute-start(bf16[4,512,128]{2,1,0:T(8,128)(2,1)S(1)} %collective-permute-done.4.refs_1_), channel_id=1, source_target_pairs={{0,1},{1,0},{2,3},{3,2},{4,5},{5,4},{6,7},{7,6},{8,9},{9,8},{10,11... | collective-permute-start | bytes 1572872 | tf_op jit(solution)/shard_map/ppermute | solution.py:32
  65.4 11.5 %collective-permute-start.14 = (bf16[4,512,128]{2,1,0:T(8,128)(2,1)S(1)}, bf16[4,512,128]{2,1,0:T(8,128)(2,1)}, u32[]{:S(2)}, u32[]{:S(2)}) collective-permute-start(bf16[4,512,128]{2,1,0:T(8,128)(2,1)S(1)} %collective-permute-done.5.refs_2_), channel_id=1, source_target_pairs={{0,1},{1,0},{2,3},{3,2},{4,5},{5,4},{6,7},{7,6},{8,9},{9,8},{10,11... | collective-permute-start | bytes 1572872 | tf_op jit(solution)/shard_map/ppermute | solution.py:32
  66.7 9.0 %all-to-all-start.3 = ((f32[4,32,128]{2,1,0:T(8,128)}), f32[4,32,128]{2,1,0:T(8,128)S(1)}, u32[]{:S(2)}, u32[]{:S(2)}) async-start(f32[4,32,128]{2,1,0:T(8,128)} %shard_map.99), calls=%async_computation.3 | async-start | bytes 131072 | tf_op jit(solution)/shard_map/all_to_all | solution.py:36
  70.8 13.7 %collective-permute-start.15 = (bf16[4,512,128]{2,1,0:T(8,128)(2,1)S(1)}, bf16[4,512,128]{2,1,0:T(8,128)(2,1)}, u32[]{:S(2)}, u32[]{:S(2)}) collective-permute-start(bf16[4,512,128]{2,1,0:T(8,128)(2,1)S(1)} %collective-permute-done.7.refs_3_), channel_id=1, source_target_pairs={{0,1},{1,0},{2,3},{3,2},{4,5},{5,4},{6,7},{7,6},{8,9},{9,8},{10,11... | collective-permute-start | bytes 1572872 | tf_op jit(solution)/shard_map/ppermute | solution.py:32
  71.1 13.5 %collective-permute-start.16 = (bf16[4,512,128]{2,1,0:T(8,128)(2,1)S(1)}, bf16[4,512,128]{2,1,0:T(8,128)(2,1)}, u32[]{:S(2)}, u32[]{:S(2)}) collective-permute-start(bf16[4,512,128]{2,1,0:T(8,128)(2,1)S(1)} %collective-permute-done.8.refs_4_), channel_id=1, source_target_pairs={{0,1},{1,0},{2,3},{3,2},{4,5},{5,4},{6,7},{7,6},{8,9},{9,8},{10,11... | collective-permute-start | bytes 1572872 | tf_op jit(solution)/shard_map/ppermute | solution.py:32
  75.7 8.9 %collective-permute-start.17 = (bf16[4,512,128]{2,1,0:T(8,128)(2,1)}, bf16[4,512,128]{2,1,0:T(8,128)(2,1)S(1)}, u32[]{:S(2)}, u32[]{:S(2)}) collective-permute-start(bf16[4,512,128]{2,1,0:T(8,128)(2,1)} %collective-permute-done.9.refs_5_), channel_id=1, source_target_pairs={{0,1},{1,0},{2,3},{3,2},{4,5},{5,4},{6,7},{7,6},{8,9},{9,8},{10,11... | collective-permute-start | bytes 1572872 | tf_op jit(solution)/shard_map/ppermute | solution.py:32
  76.8 7.9 %collective-permute-start.18 = (bf16[4,512,128]{2,1,0:T(8,128)(2,1)S(1)}, bf16[4,512,128]{2,1,0:T(8,128)(2,1)}, u32[]{:S(2)}, u32[]{:S(2)}) collective-permute-start(bf16[4,512,128]{2,1,0:T(8,128)(2,1)S(1)} %collective-permute-done.10.refs_6_), channel_id=1, source_target_pairs={{0,1},{1,0},{2,3},{3,2},{4,5},{5,4},{6,7},{7,6},{8,9},{9,8},{10,11... | collective-permute-start | bytes 1572872 | tf_op jit(solution)/shard_map/ppermute | solution.py:32
  76.8 7.8 %collective-permute-start.19 = (bf16[4,512,128]{2,1,0:T(8,128)(2,1)}, bf16[4,512,128]{2,1,0:T(8,128)(2,1)}, u32[]{:S(2)}, u32[]{:S(2)}) collective-permute-start(bf16[4,512,128]{2,1,0:T(8,128)(2,1)} %collective-permute-done.11.refs_7_), channel_id=1, source_target_pairs={{0,1},{1,0},{2,3},{3,2},{4,5},{5,4},{6,7},{7,6},{8,9},{9,8},{10,11... | collective-permute-start | bytes 1572872 | tf_op jit(solution)/shard_map/ppermute | solution.py:32
  78.0 18.3 %all-to-all-start.4 = ((bf16[32,32,128]{2,1,0:T(8,128)(2,1)}), bf16[32,32,128]{2,1,0:T(8,128)(2,1)S(1)}, u32[]{:S(2)}, u32[]{:S(2)}) async-start(bf16[32,32,128]{2,1,0:T(8,128)(2,1)} %shard_map.101), calls=%async_computation.4 | async-start | bytes 524288 | tf_op jit(solution)/shard_map/all_to_all | solution.py:36
  84.6 0.8 copy-start.7
  96.3 4.3 %collective-permute-start.20 = (bf16[32,32,128]{2,1,0:T(8,128)(2,1)S(1)}, bf16[32,32,128]{2,1,0:T(8,128)(2,1)S(1)}, u32[]{:S(2)}, u32[]{:S(2)}) collective-permute-start(bf16[32,32,128]{2,1,0:T(8,128)(2,1)S(1)} %all-to-all-done.4.mine_ref.refs_1_), channel_id=1, source_target_pairs={{0,1},{1,0},{2,3},{3,2},{4,5},{5,4},{6,7},{7,6},{8,9},{9,8},{10,11... | collective-permute-start | bytes 786440 | tf_op jit(solution)/shard_map/ppermute | solution.py:32
  102.0 6.2 %collective-permute-start.21 = (f32[32,224]{1,0:T(8,128)S(1)}, f32[32,224]{1,0:T(8,128)S(1)}, u32[]{:S(2)}, u32[]{:S(2)}) collective-permute-start(f32[32,224]{1,0:T(8,128)S(1)} %get-tuple-element.61.refs_4_), channel_id=1, source_target_pairs={{0,64},{64,128},{128,192},{192,0},{1,65},{65,129},{129,193},{193,1... | collective-permute-start | bytes 86024 | tf_op jit(solution)/shard_map/ppermute | solution.py:32
  102.3 5.9 %collective-permute-start.22 = (f32[32,224]{1,0:T(8,128)S(1)}, f32[32,224]{1,0:T(8,128)S(1)}, u32[]{:S(2)}, u32[]{:S(2)}) collective-permute-start(f32[32,224]{1,0:T(8,128)S(1)} %get-tuple-element.61.refs_4_), channel_id=1, source_target_pairs={{0,128},{64,192},{128,0},{192,64},{1,129},{65,193},{129,1},{193,65... | collective-permute-start | bytes 86024 | tf_op jit(solution)/shard_map/ppermute | solution.py:32
  104.6 3.7 %collective-permute-start.23 = (f32[32,224]{1,0:T(8,128)S(1)}, f32[32,224]{1,0:T(8,128)S(1)}, u32[]{:S(2)}, u32[]{:S(2)}) collective-permute-start(f32[32,224]{1,0:T(8,128)S(1)} %get-tuple-element.61.refs_4_), channel_id=1, source_target_pairs={{0,192},{64,0},{128,64},{192,128},{1,193},{65,1},{129,65},{193,129... | collective-permute-start | bytes 86024 | tf_op jit(solution)/shard_map/ppermute | solution.py:32

commit v11 on v10

--- a/solution.py
+++ b/solution.py
@@ -373,6 +373,7 @@
     terms = exchange(terms, "dp")
     terms, pieces[4] = tie((terms, pieces[4]))
     mine, = call(spread_kernel, [((X * Z, rank, wide), BF)], ins=[VMEM])(terms)
+    mine, pieces[4] = tie((mine, pieces[4]))
     mine = exchange(mine, ("x", "z"))
     swap(4)
     matrix, d_gate, d_up = use_pieces(

time: 113 us -> 114 us (level)
  waiting for transfers between devices: 5.24 us -> 9.76 us
  blocking collectives: 21.5 us -> 19.5 us
    ppermute x24, waiting for transfers between devices: 2.95 us -> 8.86 us  [shift(): return lax.ppermute(a, axis, [(i, (i + step) % n) for i in range(n)])]
    all_to_all x2, blocking collectives: 21.5 us -> 19.5 us  [exchange(): return lax.all_to_all(a, axis, 0, 0)]
    all_to_all x3, starting transfers between devices: 15.9 us -> 14.2 us  [exchange(): return lax.all_to_all(a, axis, 0, 0)]
    all_to_all x3, waiting for transfers between devices: 2.29 us -> 0.9 us  [exchange(): return lax.all_to_all(a, axis, 0, 0)]
  transfers between devices with their start and end apart: 27 -> 27, of which waited for: 5 -> 7; matrix products, arithmetic and copies ran while one was open for 0% -> 0% of each run, Pallas kernels for 21% -> 21%
where the time goes in v11:
time: 114 us; the launch traced here: 113 us
  starting transfers between devices  54.2 us (48%)
  Pallas kernels  28.8 us (25%)
  blocking collectives  19.5 us (17%)
  waiting for transfers between devices  9.76 us (9%)
    ppermute x24, starting transfers between devices, shift(): return lax.ppermute(a, axis, [(i, (i + step) % n) for i in range(n)])  40 us
    pallas_call x13, Pallas kernels, call(): return lambda *args: run(*(placed(a, spec) for a, spec in zip(args, ins)))  28.8 us
    all_to_all x2, blocking collectives, exchange(): return lax.all_to_all(a, axis, 0, 0)  19.5 us
    all_to_all x3, starting transfers between devices, exchange(): return lax.all_to_all(a, axis, 0, 0)  14.2 us
    ppermute x24, waiting for transfers between devices, shift(): return lax.ppermute(a, axis, [(i, (i + step) % n) for i in range(n)])  8.86 us
  transfers between devices with their start and end apart: 27, of which 7 were waited for; matrix products, arithmetic and copies ran while one was open for 0% of the time, Pallas kernels for 21%

profile of v11, /device:TPU:1, one launch (start us, length us, event | category | flops | bytes accessed | tf_op | source)
XLA Modules:
  0.0 113.3 jit_solution(12594408080442462353)
XLA Ops:
  0.6 3.7 %collective-permute-start.2 = (bf16[512,128]{1,0:T(8,128)(2,1)}, bf16[512,128]{1,0:T(8,128)(2,1)S(1)}, u32[]{:S(2)}, u32[]{:S(2)}) collective-permute-start(bf16[512,128]{1,0:T(8,128)(2,1)} %cotangent_ref.1), channel_id=1, source_target_pairs={{0,32},{16,48},{32,0},{48,16},{1,33},{17,49},{33,1},{49,17},{2,34}... | collective-permute-start | bytes 393224 | tf_op jit(solution)/shard_map/ppermute | solution.py:32
  4.3 0.3 collective-permute-start.1
  4.6 2.4 %collective-permute-start.3 = (bf16[512,128]{1,0:T(8,128)(2,1)}, bf16[512,128]{1,0:T(8,128)(2,1)S(1)}, u32[]{:S(2)}, u32[]{:S(2)}) collective-permute-start(bf16[512,128]{1,0:T(8,128)(2,1)} %cotangent_ref.1), channel_id=1, source_target_pairs={{0,48},{16,0},{32,16},{48,32},{1,49},{17,1},{33,17},{49,33},{2,50}... | collective-permute-start | bytes 393224 | tf_op jit(solution)/shard_map/ppermute | solution.py:32
  7.0 1.9 %shard_map.93 = (bf16[224,512]{1,0:T(8,128)(2,1)}, bf16[128,128]{1,0:T(8,128)(2,1)S(1)}, bf16[512,128]{1,0:T(8,128)(2,1)S(1)}) custom-call(bf16[224,512]{1,0:T(8,128)(2,1)} %bitcast.10, bf16[224,512]{1,0:T(8,128)(2,1)} %bitcast.12, f32[32,224]{1,0:T(8,128)} %bitcast.14, bf16[512,128]{1,0:T(8,128)(2,1)} %cotangent_ref.1), custom_call_target="tpu_custom_call" | custom-call | bytes 688128 | tf_op jit(solution)/shard_map/pallas_call | solution.py:54
  8.9 1.6 %collective-permute-start = (bf16[128,128]{1,0:T(8,128)(2,1)S(1)}, bf16[128,128]{1,0:T(8,128)(2,1)S(1)}, u32[]{:S(2)}, u32[]{:S(2)}) collective-permute-start(bf16[128,128]{1,0:T(8,128)(2,1)S(1)} %get-tuple-element.42.left_ref), channel_id=1, source_target_pairs={{0,1},{1,0},{2,3},{3,2},{4,5},{5,4},{6,7},{7,6},{8,9},{9,8},{10,11... | collective-permute-start | bytes 98312 | tf_op jit(solution)/shard_map/ppermute | solution.py:32
  10.5 0.9 collective-permute-done.theirs_ref
  11.4 0.3 collective-permute-done.1.refs_1_
  11.7 0.0 collective-permute-done.3.refs_3_
  11.7 0.0 copy-start
  11.8 0.0 copy-start.1
  11.8 5.3 %collective-permute-start.5 = (bf16[4,512,128]{2,1,0:T(8,128)(2,1)S(1)}, bf16[4,512,128]{2,1,0:T(8,128)(2,1)S(1)}, u32[]{:S(2)}, u32[]{:S(2)}) collective-permute-start(bf16[4,512,128]{2,1,0:T(8,128)(2,1)S(1)} %shard_map.94.refs_0_), channel_id=1, source_target_pairs={{0,14},{2,0},{4,2},{6,4},{8,6},{10,8},{12,10},{14,12},{1,15},{3,1}... | collective-permute-start | bytes 1572872 | tf_op jit(solution)/shard_map/ppermute | solution.py:32
  17.1 0.0 collective-permute-start.4
  17.1 0.7 shard_map.95
  17.8 4.1 %all-to-all-start = ((bf16[8,128,128]{2,1,0:T(8,128)(2,1)}), bf16[8,128,128]{2,1,0:T(8,128)(2,1)S(1)}, u32[]{:S(2)}, u32[]{:S(2)}) async-start(bf16[8,128,128]{2,1,0:T(8,128)(2,1)} %shard_map.95), calls=%async_computation | async-start | bytes 524288 | tf_op jit(solution)/shard_map/all_to_all | solution.py:36
  21.9 2.4 %shard_map.96 = (bf16[1024,128]{1,0:T(8,128)(2,1)S(1)}, bf16[1024,128]{1,0:T(8,128)(2,1)S(1)}) custom-call(f32[32,224]{1,0:T(8,128)} %bitcast.15, bf16[224,8192]{1,0:T(8,128)(2,1)} %bitcast.8), custom_call_target="tpu_custom_call" | custom-call | flops 234881024 | bytes 3670016 | tf_op jit(solution)/shard_map/pallas_call | solution.py:54
  24.4 1.8 %collective-permute-start.6 = (bf16[1024,128]{1,0:T(8,128)(2,1)S(1)}, bf16[1024,128]{1,0:T(8,128)(2,1)S(1)}, u32[]{:S(2)}, u32[]{:S(2)}) collective-permute-start(bf16[1024,128]{1,0:T(8,128)(2,1)S(1)} %get-tuple-element.44), channel_id=1, source_target_pairs={{0,1},{1,0},{2,3},{3,2},{4,5},{5,4},{6,7},{7,6},{8,9},{9,8},{10,11... | collective-permute-start | bytes 786440 | tf_op jit(solution)/shard_map/ppermute | solution.py:32
  26.2 4.2 %collective-permute-done.5.refs_2_ = bf16[4,512,128]{2,1,0:T(8,128)(2,1)S(1)} collective-permute-done((bf16[4,512,128]{2,1,0:T(8,128)(2,1)S(1)}, bf16[4,512,128]{2,1,0:T(8,128)(2,1)S(1)}, u32[]{:S(2)}, u32[]{:S(2)}) %collective-permute-start.5) | collective-permute-done | bytes 524320 | tf_op jit(solution)/shard_map/ppermute | solution.py:32
  30.5 3.8 %collective-permute-start.8 = (bf16[4,512,128]{2,1,0:T(8,128)(2,1)S(1)}, bf16[4,512,128]{2,1,0:T(8,128)(2,1)S(1)}, u32[]{:S(2)}, u32[]{:S(2)}) collective-permute-start(bf16[4,512,128]{2,1,0:T(8,128)(2,1)S(1)} %collective-permute-done.5.refs_2_), channel_id=1, source_target_pairs={{0,14},{2,0},{4,2},{6,4},{8,6},{10,8},{12,10},{14,12},{1,15},{3,1}... | collective-permute-start | bytes 1572872 | tf_op jit(solution)/shard_map/ppermute | solution.py:32
  34.3 0.9 all-to-all-done.left_ref
  35.2 0.1 shard_map.97
  35.3 9.3 %all_to_all.25.terms_ref = bf16[4,384,128]{2,1,0:T(8,128)(2,1)S(1)} all-to-all(bf16[4,384,128]{2,1,0:T(8,128)(2,1)S(1)} %shard_map.97), channel_id=1, replica_groups=mesh['dp'=4,'x'=4,'z'=8,'core'=2] {'x'}, dimensions={0} | all-to-all | bytes 786432 | tf_op jit(solution)/shard_map/all_to_all | solution.py:36
  44.5 1.8 %collective-permute-done.7.refs_3_ = bf16[4,512,128]{2,1,0:T(8,128)(2,1)S(1)} collective-permute-done((bf16[4,512,128]{2,1,0:T(8,128)(2,1)S(1)}, bf16[4,512,128]{2,1,0:T(8,128)(2,1)S(1)}, u32[]{:S(2)}, u32[]{:S(2)}) %collective-permute-start.7) | collective-permute-done | bytes 524320 | tf_op jit(solution)/shard_map/ppermute | solution.py:32
  46.3 0.3 collective-permute-start.9
  46.7 2.4 %collective-permute-start.10 = (bf16[4,512,128]{2,1,0:T(8,128)(2,1)S(1)}, bf16[4,512,128]{2,1,0:T(8,128)(2,1)S(1)}, u32[]{:S(2)}, u32[]{:S(2)}) collective-permute-start(bf16[4,512,128]{2,1,0:T(8,128)(2,1)S(1)} %collective-permute-done.8.refs_4_), channel_id=1, source_target_pairs={{0,14},{2,0},{4,2},{6,4},{8,6},{10,8},{12,10},{14,12},{1,15},{3,1}... | collective-permute-start | bytes 1572872 | tf_op jit(solution)/shard_map/ppermute | solution.py:32
  49.0 0.1 shard_map.98
  49.1 10.3 %all_to_all.26.part_ref = bf16[8,32,128]{2,1,0:T(8,128)(2,1)S(1)} all-to-all(bf16[8,32,128]{2,1,0:T(8,128)(2,1)S(1)} %get-tuple-element.49), channel_id=1, replica_groups=mesh['dp'=4,'x'=4,'z'=8,'core'=2] {'z'}, dimensions={0} | all-to-all | bytes 131072 | tf_op jit(solution)/shard_map/all_to_all | solution.py:36
  59.4 0.2 collective-permute-start.11
  59.5 6.6 %collective-permute-start.12 = (bf16[4,512,128]{2,1,0:T(8,128)(2,1)S(1)}, bf16[4,512,128]{2,1,0:T(8,128)(2,1)}, u32[]{:S(2)}, u32[]{:S(2)}) collective-permute-start(bf16[4,512,128]{2,1,0:T(8,128)(2,1)S(1)} %shard_map.94.refs_0_), channel_id=1, source_target_pairs={{0,1},{1,0},{2,3},{3,2},{4,5},{5,4},{6,7},{7,6},{8,9},{9,8},{10,11... | collective-permute-start | bytes 1572872 | tf_op jit(solution)/shard_map/ppermute | solution.py:32
  66.2 0.6 collective-permute-start.14
  66.8 0.8 shard_map.99
  67.6 4.2 %all-to-all-start.3 = ((f32[4,32,128]{2,1,0:T(8,128)}), f32[4,32,128]{2,1,0:T(8,128)S(1)}, u32[]{:S(2)}, u32[]{:S(2)}) async-start(f32[4,32,128]{2,1,0:T(8,128)} %shard_map.99), calls=%async_computation.3 | async-start | bytes 131072 | tf_op jit(solution)/shard_map/all_to_all | solution.py:36
  71.8 0.8 collective-permute-start.15
  72.6 4.0 %collective-permute-start.16 = (bf16[4,512,128]{2,1,0:T(8,128)(2,1)S(1)}, bf16[4,512,128]{2,1,0:T(8,128)(2,1)}, u32[]{:S(2)}, u32[]{:S(2)}) collective-permute-start(bf16[4,512,128]{2,1,0:T(8,128)(2,1)S(1)} %collective-permute-done.8.refs_4_), channel_id=1, source_target_pairs={{0,1},{1,0},{2,3},{3,2},{4,5},{5,4},{6,7},{7,6},{8,9},{9,8},{10,11... | collective-permute-start | bytes 1572872 | tf_op jit(solution)/shard_map/ppermute | solution.py:32
  76.6 0.7 shard_map.100
  77.3 1.7 %collective-permute-start.17 = (bf16[4,512,128]{2,1,0:T(8,128)(2,1)S(1)}, bf16[4,512,128]{2,1,0:T(8,128)(2,1)}, u32[]{:S(2)}, u32[]{:S(2)}) collective-permute-start(bf16[4,512,128]{2,1,0:T(8,128)(2,1)S(1)} %collective-permute-done.9.refs_5_), channel_id=1, source_target_pairs={{0,1},{1,0},{2,3},{3,2},{4,5},{5,4},{6,7},{7,6},{8,9},{9,8},{10,11... | collective-permute-start | bytes 1572872 | tf_op jit(solution)/shard_map/ppermute | solution.py:32
  79.0 0.1 collective-permute-start.18
  79.1 0.4 collective-permute-start.19
  79.5 6.0 %all-to-all-start.4 = ((bf16[32,32,128]{2,1,0:T(8,128)(2,1)}), bf16[32,32,128]{2,1,0:T(8,128)(2,1)S(1)}, u32[]{:S(2)}, u32[]{:S(2)}) async-start(bf16[32,32,128]{2,1,0:T(8,128)(2,1)} %shard_map.100), calls=%async_computation.4 | async-start | bytes 524288 | tf_op jit(solution)/shard_map/all_to_all | solution.py:36
  85.5 10.9 %shard_map.101 = (f32[224,8192]{1,0:T(8,128)}, bf16[224,512]{1,0:T(8,128)(2,1)}, bf16[224,512]{1,0:T(8,128)(2,1)}) custom-call(bf16[4,512,128]{2,1,0:T(8,128)(2,1)} %copy-done, bf16[4,512,128]{2,1,0:T(8,128)(2,1)} %copy-done.3, bf16[4,512,128]{2,1,0:T(8,128)(2,1)} %copy-done.2, bf16[4,512,128]{2,1,0:T(8,128)(2,1)} %copy-done.5, ...), custom_call_target="tpu_custom_call" | custom-call | flops 3758096384 | bytes 31457280 | tf_op jit(solution)/shard_map/pallas_call | solution.py:54
  96.5 1.9 %collective-permute-start.20 = (bf16[32,32,128]{2,1,0:T(8,128)(2,1)S(1)}, bf16[32,32,128]{2,1,0:T(8,128)(2,1)S(1)}, u32[]{:S(2)}, u32[]{:S(2)}) collective-permute-start(bf16[32,32,128]{2,1,0:T(8,128)(2,1)S(1)} %all-to-all-done.4.mine_ref.refs_1_), channel_id=1, source_target_pairs={{0,1},{1,0},{2,3},{3,2},{4,5},{5,4},{6,7},{7,6},{8,9},{9,8},{10,11... | collective-permute-start | bytes 786440 | tf_op jit(solution)/shard_map/ppermute | solution.py:32
  98.4 3.2 %shard_map.102.matrix_ref.refs_0_ = f32[224,8192]{1,0:T(8,128)S(1)} custom-call(f32[224,8192]{1,0:T(8,128)} %get-tuple-element.62.source_hbm), custom_call_target="tpu_custom_call" | custom-call | tf_op jit(solution)/shard_map/pallas_call | solution.py:54
  101.6 1.3 %shard_map.103 = (f32[32,224]{1,0:T(8,128)S(1)}, f32[32,32]{1,0:T(8,128)S(1)}) custom-call(f32[224,8192]{1,0:T(8,128)S(1)} %shard_map.102.matrix_ref.refs_0_, bf16[32,32,128]{2,1,0:T(8,128)(2,1)S(1)} %all-to-all-done.4.mine_ref.refs_1_, bf16[32,32,128]{2,1,0:T(8,128)(2,1)S(1)} %collective-permute-done.20.theirs_ref.refs_2_), custom_call_target="tpu_custom_call" | custom-call | flops 117440512 | bytes 7340032 | tf_op jit(solution)/shard_map/pallas_call | solution.py:54
  102.8 0.9 collective-permute-start.23
  103.8 1.2 %collective-permute-start.22 = (f32[32,224]{1,0:T(8,128)S(1)}, f32[32,224]{1,0:T(8,128)S(1)}, u32[]{:S(2)}, u32[]{:S(2)}) collective-permute-start(f32[32,224]{1,0:T(8,128)S(1)} %get-tuple-element.65.refs_4_), channel_id=1, source_target_pairs={{0,128},{64,192},{128,0},{192,64},{1,129},{65,193},{129,1},{193,65... | collective-permute-start | bytes 86024 | tf_op jit(solution)/shard_map/ppermute | solution.py:32
  105.0 2.6 %shard_map.104.refs_3_ = f32[32,32]{1,0:T(8,128)S(1)} custom-call(f32[32,32]{1,0:T(8,128)S(1)} %get-tuple-element.64.gram_ref), custom_call_target="tpu_custom_call" | custom-call | tf_op jit(solution)/shard_map/pallas_call | solution.py:54
  107.6 0.5 collective-permute-done.22.refs_6_
  108.1 1.1 collective-permute-done.21.refs_5_
  109.2 4.0 %shard_map.105 = (bf16[224,8192]{1,0:T(8,128)(2,1)}, f32[32,224]{1,0:T(8,128)}) custom-call(f32[224,8192]{1,0:T(8,128)S(1)} %shard_map.102.matrix_ref.refs_0_, bf16[32,32,128]{2,1,0:T(8,128)(2,1)S(1)} %all-to-all-done.4.mine_ref.refs_1_, bf16[32,32,128]{2,1,0:T(8,128)(2,1)S(1)} %collective-permute-done.20.theirs_ref.refs_2_, ...), custom_call_target="tpu_custom_call" | custom-call | flops 234881024 | bytes 11010048 | tf_op jit(solution)/shard_map/pallas_call | solution.py:54
  (37 shorter events, 0.1 us)
Async XLA Ops:
  0.6 10.8 %collective-permute-start.2 = (bf16[512,128]{1,0:T(8,128)(2,1)}, bf16[512,128]{1,0:T(8,128)(2,1)S(1)}, u32[]{:S(2)}, u32[]{:S(2)}) collective-permute-start(bf16[512,128]{1,0:T(8,128)(2,1)} %cotangent_ref.1), channel_id=1, source_target_pairs={{0,32},{16,48},{32,0},{48,16},{1,33},{17,49},{33,1},{49,17},{2,34}... | collective-permute-start | bytes 393224 | tf_op jit(solution)/shard_map/ppermute | solution.py:32
  4.3 7.4 %collective-permute-start.1 = (bf16[512,128]{1,0:T(8,128)(2,1)}, bf16[512,128]{1,0:T(8,128)(2,1)S(1)}, u32[]{:S(2)}, u32[]{:S(2)}) collective-permute-start(bf16[512,128]{1,0:T(8,128)(2,1)} %cotangent_ref.1), channel_id=1, source_target_pairs={{0,16},{16,32},{32,48},{48,0},{1,17},{17,33},{33,49},{49,1},{2,18}... | collective-permute-start | bytes 393224 | tf_op jit(solution)/shard_map/ppermute | solution.py:32
  4.6 7.1 %collective-permute-start.3 = (bf16[512,128]{1,0:T(8,128)(2,1)}, bf16[512,128]{1,0:T(8,128)(2,1)S(1)}, u32[]{:S(2)}, u32[]{:S(2)}) collective-permute-start(bf16[512,128]{1,0:T(8,128)(2,1)} %cotangent_ref.1), channel_id=1, source_target_pairs={{0,48},{16,0},{32,16},{48,32},{1,49},{17,1},{33,17},{49,33},{2,50}... | collective-permute-start | bytes 393224 | tf_op jit(solution)/shard_map/ppermute | solution.py:32
  8.9 2.5 %collective-permute-start = (bf16[128,128]{1,0:T(8,128)(2,1)S(1)}, bf16[128,128]{1,0:T(8,128)(2,1)S(1)}, u32[]{:S(2)}, u32[]{:S(2)}) collective-permute-start(bf16[128,128]{1,0:T(8,128)(2,1)S(1)} %get-tuple-element.42.left_ref), channel_id=1, source_target_pairs={{0,1},{1,0},{2,3},{3,2},{4,5},{5,4},{6,7},{7,6},{8,9},{9,8},{10,11... | collective-permute-start | bytes 98312 | tf_op jit(solution)/shard_map/ppermute | solution.py:32
  11.7 55.9 %copy-start = (bf16[4,512,128]{2,1,0:T(8,128)(2,1)}, bf16[4,512,128]{2,1,0:T(8,128)(2,1)S(1)}, u32[]{:S(2)}) copy-start(bf16[4,512,128]{2,1,0:T(8,128)(2,1)S(1)} %shard_map.94.refs_0_) | copy-start | bytes 1572868
  11.8 55.1 %copy-start.1 = (bf16[512,128]{1,0:T(8,128)(2,1)S(1)}, bf16[512,128]{1,0:T(8,128)(2,1)}, u32[]{:S(2)}) copy-start(bf16[512,128]{1,0:T(8,128)(2,1)} %cotangent_ref.1) | copy-start | bytes 393220
  11.8 18.7 %collective-permute-start.5 = (bf16[4,512,128]{2,1,0:T(8,128)(2,1)S(1)}, bf16[4,512,128]{2,1,0:T(8,128)(2,1)S(1)}, u32[]{:S(2)}, u32[]{:S(2)}) collective-permute-start(bf16[4,512,128]{2,1,0:T(8,128)(2,1)S(1)} %shard_map.94.refs_0_), channel_id=1, source_target_pairs={{0,14},{2,0},{4,2},{6,4},{8,6},{10,8},{12,10},{14,12},{1,15},{3,1}... | collective-permute-start | bytes 1572872 | tf_op jit(solution)/shard_map/ppermute | solution.py:32
  17.1 17.1 %collective-permute-start.4 = (bf16[4,512,128]{2,1,0:T(8,128)(2,1)S(1)}, bf16[4,512,128]{2,1,0:T(8,128)(2,1)S(1)}, u32[]{:S(2)}, u32[]{:S(2)}) collective-permute-start(bf16[4,512,128]{2,1,0:T(8,128)(2,1)S(1)} %shard_map.94.refs_0_), channel_id=1, source_target_pairs={{0,2},{2,4},{4,6},{6,8},{8,10},{10,12},{12,14},{14,0},{1,3},{3,5},... | collective-permute-start | bytes 1572872 | tf_op jit(solution)/shard_map/ppermute | solution.py:32
  17.8 17.3 %all-to-all-start = ((bf16[8,128,128]{2,1,0:T(8,128)(2,1)}), bf16[8,128,128]{2,1,0:T(8,128)(2,1)S(1)}, u32[]{:S(2)}, u32[]{:S(2)}) async-start(bf16[8,128,128]{2,1,0:T(8,128)(2,1)} %shard_map.95), calls=%async_computation | async-start | bytes 524288 | tf_op jit(solution)/shard_map/all_to_all | solution.py:36
  24.4 9.9 %collective-permute-start.6 = (bf16[1024,128]{1,0:T(8,128)(2,1)S(1)}, bf16[1024,128]{1,0:T(8,128)(2,1)S(1)}, u32[]{:S(2)}, u32[]{:S(2)}) collective-permute-start(bf16[1024,128]{1,0:T(8,128)(2,1)S(1)} %get-tuple-element.44), channel_id=1, source_target_pairs={{0,1},{1,0},{2,3},{3,2},{4,5},{5,4},{6,7},{7,6},{8,9},{9,8},{10,11... | collective-permute-start | bytes 786440 | tf_op jit(solution)/shard_map/ppermute | solution.py:32
  30.4 55.0 %copy-start.2 = (bf16[4,512,128]{2,1,0:T(8,128)(2,1)}, bf16[4,512,128]{2,1,0:T(8,128)(2,1)S(1)}, u32[]{:S(2)}) copy-start(bf16[4,512,128]{2,1,0:T(8,128)(2,1)S(1)} %collective-permute-done.5.refs_2_) | copy-start | bytes 1572868
  30.5 14.1 %collective-permute-start.8 = (bf16[4,512,128]{2,1,0:T(8,128)(2,1)S(1)}, bf16[4,512,128]{2,1,0:T(8,128)(2,1)S(1)}, u32[]{:S(2)}, u32[]{:S(2)}) collective-permute-start(bf16[4,512,128]{2,1,0:T(8,128)(2,1)S(1)} %collective-permute-done.5.refs_2_), channel_id=1, source_target_pairs={{0,14},{2,0},{4,2},{6,4},{8,6},{10,8},{12,10},{14,12},{1,15},{3,1}... | collective-permute-start | bytes 1572872 | tf_op jit(solution)/shard_map/ppermute | solution.py:32
  34.3 51.2 %copy-start.3 = (bf16[4,512,128]{2,1,0:T(8,128)(2,1)}, bf16[4,512,128]{2,1,0:T(8,128)(2,1)S(1)}, u32[]{:S(2)}) copy-start(bf16[4,512,128]{2,1,0:T(8,128)(2,1)S(1)} %collective-permute-done.4.refs_1_) | copy-start | bytes 1572868
  34.3 12.1 %collective-permute-start.7 = (bf16[4,512,128]{2,1,0:T(8,128)(2,1)S(1)}, bf16[4,512,128]{2,1,0:T(8,128)(2,1)S(1)}, u32[]{:S(2)}, u32[]{:S(2)}) collective-permute-start(bf16[4,512,128]{2,1,0:T(8,128)(2,1)S(1)} %collective-permute-done.4.refs_1_), channel_id=1, source_target_pairs={{0,2},{2,4},{4,6},{6,8},{8,10},{10,12},{12,14},{14,0},{1,3},{3,5},... | collective-permute-start | bytes 1572872 | tf_op jit(solution)/shard_map/ppermute | solution.py:32
  44.5 41.0 %copy-start.4 = (bf16[4,512,128]{2,1,0:T(8,128)(2,1)}, bf16[4,512,128]{2,1,0:T(8,128)(2,1)S(1)}, u32[]{:S(2)}) copy-start(bf16[4,512,128]{2,1,0:T(8,128)(2,1)S(1)} %collective-permute-done.8.refs_4_) | copy-start | bytes 1572868
  46.3 39.2 %copy-start.5 = (bf16[4,512,128]{2,1,0:T(8,128)(2,1)}, bf16[4,512,128]{2,1,0:T(8,128)(2,1)S(1)}, u32[]{:S(2)}) copy-start(bf16[4,512,128]{2,1,0:T(8,128)(2,1)S(1)} %collective-permute-done.7.refs_3_) | copy-start | bytes 1572868
  46.3 13.0 %collective-permute-start.9 = (bf16[4,512,128]{2,1,0:T(8,128)(2,1)S(1)}, bf16[4,512,128]{2,1,0:T(8,128)(2,1)S(1)}, u32[]{:S(2)}, u32[]{:S(2)}) collective-permute-start(bf16[4,512,128]{2,1,0:T(8,128)(2,1)S(1)} %collective-permute-done.7.refs_3_), channel_id=1, source_target_pairs={{0,2},{2,4},{4,6},{6,8},{8,10},{10,12},{12,14},{14,0},{1,3},{3,5},... | collective-permute-start | bytes 1572872 | tf_op jit(solution)/shard_map/ppermute | solution.py:32
  46.7 12.7 %collective-permute-start.10 = (bf16[4,512,128]{2,1,0:T(8,128)(2,1)S(1)}, bf16[4,512,128]{2,1,0:T(8,128)(2,1)S(1)}, u32[]{:S(2)}, u32[]{:S(2)}) collective-permute-start(bf16[4,512,128]{2,1,0:T(8,128)(2,1)S(1)} %collective-permute-done.8.refs_4_), channel_id=1, source_target_pairs={{0,14},{2,0},{4,2},{6,4},{8,6},{10,8},{12,10},{14,12},{1,15},{3,1}... | collective-permute-start | bytes 1572872 | tf_op jit(solution)/shard_map/ppermute | solution.py:32
  59.4 26.2 %copy-start.6 = (bf16[4,512,128]{2,1,0:T(8,128)(2,1)}, bf16[4,512,128]{2,1,0:T(8,128)(2,1)S(1)}, u32[]{:S(2)}) copy-start(bf16[4,512,128]{2,1,0:T(8,128)(2,1)S(1)} %collective-permute-done.9.refs_5_) | copy-start | bytes 1572868
  59.4 6.8 %copy-start.7 = (bf16[4,512,128]{2,1,0:T(8,128)(2,1)}, bf16[4,512,128]{2,1,0:T(8,128)(2,1)S(1)}, u32[]{:S(2)}) copy-start(bf16[4,512,128]{2,1,0:T(8,128)(2,1)S(1)} %collective-permute-done.10.refs_6_) | copy-start | bytes 1572868
  59.4 13.2 %collective-permute-start.11 = (bf16[4,512,128]{2,1,0:T(8,128)(2,1)S(1)}, bf16[4,512,128]{2,1,0:T(8,128)(2,1)}, u32[]{:S(2)}, u32[]{:S(2)}) collective-permute-start(bf16[4,512,128]{2,1,0:T(8,128)(2,1)S(1)} %collective-permute-done.9.refs_5_), channel_id=1, source_target_pairs={{0,2},{2,4},{4,6},{6,8},{8,10},{10,12},{12,14},{14,0},{1,3},{3,5},... | collective-permute-start | bytes 1572872 | tf_op jit(solution)/shard_map/ppermute | solution.py:32
  59.5 17.8 %collective-permute-start.12 = (bf16[4,512,128]{2,1,0:T(8,128)(2,1)S(1)}, bf16[4,512,128]{2,1,0:T(8,128)(2,1)}, u32[]{:S(2)}, u32[]{:S(2)}) collective-permute-start(bf16[4,512,128]{2,1,0:T(8,128)(2,1)S(1)} %shard_map.94.refs_0_), channel_id=1, source_target_pairs={{0,1},{1,0},{2,3},{3,2},{4,5},{5,4},{6,7},{7,6},{8,9},{9,8},{10,11... | collective-permute-start | bytes 1572872 | tf_op jit(solution)/shard_map/ppermute | solution.py:32
  66.2 12.8 %collective-permute-start.14 = (bf16[4,512,128]{2,1,0:T(8,128)(2,1)S(1)}, bf16[4,512,128]{2,1,0:T(8,128)(2,1)}, u32[]{:S(2)}, u32[]{:S(2)}) collective-permute-start(bf16[4,512,128]{2,1,0:T(8,128)(2,1)S(1)} %collective-permute-done.5.refs_2_), channel_id=1, source_target_pairs={{0,1},{1,0},{2,3},{3,2},{4,5},{5,4},{6,7},{7,6},{8,9},{9,8},{10,11... | collective-permute-start | bytes 1572872 | tf_op jit(solution)/shard_map/ppermute | solution.py:32
  66.8 12.2 %collective-permute-start.13 = (bf16[4,512,128]{2,1,0:T(8,128)(2,1)S(1)}, bf16[4,512,128]{2,1,0:T(8,128)(2,1)}, u32[]{:S(2)}, u32[]{:S(2)}) collective-permute-start(bf16[4,512,128]{2,1,0:T(8,128)(2,1)S(1)} %collective-permute-done.4.refs_1_), channel_id=1, source_target_pairs={{0,1},{1,0},{2,3},{3,2},{4,5},{5,4},{6,7},{7,6},{8,9},{9,8},{10,11... | collective-permute-start | bytes 1572872 | tf_op jit(solution)/shard_map/ppermute | solution.py:32
  67.6 8.9 %all-to-all-start.3 = ((f32[4,32,128]{2,1,0:T(8,128)}), f32[4,32,128]{2,1,0:T(8,128)S(1)}, u32[]{:S(2)}, u32[]{:S(2)}) async-start(f32[4,32,128]{2,1,0:T(8,128)} %shard_map.99), calls=%async_computation.3 | async-start | bytes 131072 | tf_op jit(solution)/shard_map/all_to_all | solution.py:36
  71.8 13.6 %collective-permute-start.15 = (bf16[4,512,128]{2,1,0:T(8,128)(2,1)S(1)}, bf16[4,512,128]{2,1,0:T(8,128)(2,1)}, u32[]{:S(2)}, u32[]{:S(2)}) collective-permute-start(bf16[4,512,128]{2,1,0:T(8,128)(2,1)S(1)} %collective-permute-done.7.refs_3_), channel_id=1, source_target_pairs={{0,1},{1,0},{2,3},{3,2},{4,5},{5,4},{6,7},{7,6},{8,9},{9,8},{10,11... | collective-permute-start | bytes 1572872 | tf_op jit(solution)/shard_map/ppermute | solution.py:32
  72.6 12.9 %collective-permute-start.16 = (bf16[4,512,128]{2,1,0:T(8,128)(2,1)S(1)}, bf16[4,512,128]{2,1,0:T(8,128)(2,1)}, u32[]{:S(2)}, u32[]{:S(2)}) collective-permute-start(bf16[4,512,128]{2,1,0:T(8,128)(2,1)S(1)} %collective-permute-done.8.refs_4_), channel_id=1, source_target_pairs={{0,1},{1,0},{2,3},{3,2},{4,5},{5,4},{6,7},{7,6},{8,9},{9,8},{10,11... | collective-permute-start | bytes 1572872 | tf_op jit(solution)/shard_map/ppermute | solution.py:32
  77.3 8.2 %collective-permute-start.17 = (bf16[4,512,128]{2,1,0:T(8,128)(2,1)S(1)}, bf16[4,512,128]{2,1,0:T(8,128)(2,1)}, u32[]{:S(2)}, u32[]{:S(2)}) collective-permute-start(bf16[4,512,128]{2,1,0:T(8,128)(2,1)S(1)} %collective-permute-done.9.refs_5_), channel_id=1, source_target_pairs={{0,1},{1,0},{2,3},{3,2},{4,5},{5,4},{6,7},{7,6},{8,9},{9,8},{10,11... | collective-permute-start | bytes 1572872 | tf_op jit(solution)/shard_map/ppermute | solution.py:32
  79.0 6.5 %collective-permute-start.18 = (bf16[4,512,128]{2,1,0:T(8,128)(2,1)}, bf16[4,512,128]{2,1,0:T(8,128)(2,1)}, u32[]{:S(2)}, u32[]{:S(2)}) collective-permute-start(bf16[4,512,128]{2,1,0:T(8,128)(2,1)} %copy-done.7), channel_id=1, source_target_pairs={{0,1},{1,0},{2,3},{3,2},{4,5},{5,4},{6,7},{7,6},{8,9},{9,8},{10,11... | collective-permute-start | bytes 1572872 | tf_op jit(solution)/shard_map/ppermute | solution.py:32
  79.1 6.4 %collective-permute-start.19 = (bf16[4,512,128]{2,1,0:T(8,128)(2,1)}, bf16[4,512,128]{2,1,0:T(8,128)(2,1)}, u32[]{:S(2)}, u32[]{:S(2)}) collective-permute-start(bf16[4,512,128]{2,1,0:T(8,128)(2,1)} %collective-permute-done.11.refs_7_), channel_id=1, source_target_pairs={{0,1},{1,0},{2,3},{3,2},{4,5},{5,4},{6,7},{7,6},{8,9},{9,8},{10,11... | collective-permute-start | bytes 1572872 | tf_op jit(solution)/shard_map/ppermute | solution.py:32
  79.5 17.0 %all-to-all-start.4 = ((bf16[32,32,128]{2,1,0:T(8,128)(2,1)}), bf16[32,32,128]{2,1,0:T(8,128)(2,1)S(1)}, u32[]{:S(2)}, u32[]{:S(2)}) async-start(bf16[32,32,128]{2,1,0:T(8,128)(2,1)} %shard_map.100), calls=%async_computation.4 | async-start | bytes 524288 | tf_op jit(solution)/shard_map/all_to_all | solution.py:36
  96.5 5.1 %collective-permute-start.20 = (bf16[32,32,128]{2,1,0:T(8,128)(2,1)S(1)}, bf16[32,32,128]{2,1,0:T(8,128)(2,1)S(1)}, u32[]{:S(2)}, u32[]{:S(2)}) collective-permute-start(bf16[32,32,128]{2,1,0:T(8,128)(2,1)S(1)} %all-to-all-done.4.mine_ref.refs_1_), channel_id=1, source_target_pairs={{0,1},{1,0},{2,3},{3,2},{4,5},{5,4},{6,7},{7,6},{8,9},{9,8},{10,11... | collective-permute-start | bytes 786440 | tf_op jit(solution)/shard_map/ppermute | solution.py:32
  102.8 4.7 %collective-permute-start.23 = (f32[32,224]{1,0:T(8,128)S(1)}, f32[32,224]{1,0:T(8,128)S(1)}, u32[]{:S(2)}, u32[]{:S(2)}) collective-permute-start(f32[32,224]{1,0:T(8,128)S(1)} %get-tuple-element.65.refs_4_), channel_id=1, source_target_pairs={{0,192},{64,0},{128,64},{192,128},{1,193},{65,1},{129,65},{193,129... | collective-permute-start | bytes 86024 | tf_op jit(solution)/shard_map/ppermute | solution.py:32
  103.8 4.3 %collective-permute-start.22 = (f32[32,224]{1,0:T(8,128)S(1)}, f32[32,224]{1,0:T(8,128)S(1)}, u32[]{:S(2)}, u32[]{:S(2)}) collective-permute-start(f32[32,224]{1,0:T(8,128)S(1)} %get-tuple-element.65.refs_4_), channel_id=1, source_target_pairs={{0,128},{64,192},{128,0},{192,64},{1,129},{65,193},{129,1},{193,65... | collective-permute-start | bytes 86024 | tf_op jit(solution)/shard_map/ppermute | solution.py:32
  105.0 4.2 %collective-permute-start.21 = (f32[32,224]{1,0:T(8,128)S(1)}, f32[32,224]{1,0:T(8,128)S(1)}, u32[]{:S(2)}, u32[]{:S(2)}) collective-permute-start(f32[32,224]{1,0:T(8,128)S(1)} %get-tuple-element.65.refs_4_), channel_id=1, source_target_pairs={{0,64},{64,128},{128,192},{192,0},{1,65},{65,129},{129,193},{193,1... | collective-permute-start | bytes 86024 | tf_op jit(solution)/shard_map/ppermute | solution.py:32
